TPU v7x, 32 devices: a whole 2x2x4 slice. The times are simulated.
32 devices in a mesh: dp: 4 (over y, x), row: 2 (over core), col: 4 (over z).
Axes of the slice: x: 2, y: 2, z: 4, core: 2. Of those that a mesh axis runs over, the one named last changes fastest.
Arguments:
- partials: bfloat16 [4, 2, 4, 2, 1024, 8192], P('dp', None, None, 'row', None, 'col'), may hold values from -40 to 40
- params: float32 [2, 8192, 8192], P(None, ('dp', 'row'), 'col'), may hold values from -4 to 4
- row_factor: float32 [2, 8192], P(None, ('dp', 'row')), may hold values from 0.05 to 500
- col_factor: float32 [2, 8192], P(None, 'col'), may hold values from 0.05 to 500
Outputs:
- new_params: float32 [2, 8192, 8192], P(None, ('dp', 'row'), 'col')
- update: float32 [2, 8192, 8192], P(None, ('dp', 'row'), 'col')
- new_rows: float32 [2, 8192], P(None, ('dp', 'row'))
- new_columns: float32 [2, 8192], P(None, 'col')
All inputs are finite; a program needn't handle non-finite values.
Results may differ from a plain program's by a relative error of at most 0.0003.
Values sent between devices are 32-bit elements; how exact they have to be, the bound alone decides.
No kernel may reach another device: no remote copies, remote signals or barrier semaphores. Data moves between devices by JAX's collectives and lax.ppermute only.
A program may use at most 256 MiB of HBM per device.

v0:
```python
import jax
import jax.numpy as jnp
from jax import lax
from jax.sharding import PartitionSpec as P

decay_rate = 1.0 - 2.0 ** (-0.8)
tiny_eps = 1e-30
clip_limit = 1.0
learn_rate = 0.01


def per_device(partials, params, row_factor, col_factor):
    block_cols = params.shape[2]
    extent = block_cols * lax.axis_size("col")
    pieces = partials[0, :, :, 0].astype(jnp.float32)
    summed = lax.psum_scatter(pieces, "dp", scatter_dimension=1, tiled=True)[:, 0]
    squares = summed * summed
    row_local = jnp.sum(squares, axis=2)
    own_cols = jnp.sum(squares, axis=1)
    row_total = lax.psum(row_local, "col")
    col_total = lax.psum(own_cols, ("dp", "row"))
    row_new = decay_rate * row_factor + (1.0 - decay_rate) * (row_total / extent + tiny_eps)
    col_new = decay_rate * col_factor + (1.0 - decay_rate) * (col_total / extent + tiny_eps)
    level_sum = lax.psum(jnp.sum(row_new, axis=1), ("dp", "row"))
    row_level = level_sum / extent
    second = row_new[:, :, None] * col_new[:, None, :] / row_level[:, None, None]
    scaled = summed * lax.rsqrt(second)
    total = lax.psum(jnp.sum(scaled * scaled, axis=(1, 2)), ("dp", "row", "col"))
    spread = jnp.sqrt(total / (extent * extent))
    scaled = scaled / jnp.maximum(1.0, spread / clip_limit)[:, None, None]
    return (params - learn_rate * scaled, scaled, row_new, col_new)


def solution(mesh):
    placed = (
        P("dp", None, None, "row", None, "col"),
        P(None, ("dp", "row"), "col"),
        P(None, ("dp", "row")),
        P(None, "col"),
    )
    return jax.shard_map(
        per_device,
        mesh=mesh,
        in_specs=placed,
        out_specs=(
            P(None, ("dp", "row"), "col"),
            P(None, ("dp", "row"), "col"),
            P(None, ("dp", "row")),
            P(None, "col"),
        ),
        check_vma=False,
    )
```

profile of v0, /device:TPU:0, one launch (start us, length us, event | category | flops | bytes accessed | tf_op | source)
XLA Modules:
  0.0 718.1 jit_solution(18126380962517987446)
XLA Ops:
  7.2 0.0 reduce-scatter.4.cloned.1.call-start
  7.2 32.4 %bitcast_convert_fusion = f32[2,4,1024,2048]{3,2,0,1:T(8,128)} fusion(bf16[1,2,4,1,1024,2048]{5,4,3,2,1,0:T(8,128)(2,1)} %param.4), kind=kLoop, calls=%fused_computation | loop fusion | flops 16777216 | bytes 100663296 | tf_op jit(solution)/shard_map/convert_element_type | solution.py:15
  39.6 0.0 reduce-scatter.4.cloned.1.call-update
  39.7 0.0 copy-start.3
  39.7 0.0 copy-start.2
  39.7 561.1 %reduce-scatter.4.cloned.1.call-done = f32[2,1,1024,2048]{3,2,0,1:T(8,128)} async-done(((f32[2,4,1024,2048]{3,2,0,1:T(8,128)}), f32[2,1,1024,2048]{3,2,0,1:T(8,128)}) %reduce-scatter.4.cloned.1.call-update) | async-done | bytes 16777232
  600.8 7.7 %fusion = (f32[2,2048]{1,0:T(2,128)S(1)}, f32[2,1024]{1,0:T(2,128)S(1)}) fusion(f32[2,1,1024,2048]{3,2,0,1:T(8,128)} %reduce-scatter.4.cloned.1.call-done), kind=kLoop, calls=%fused_computation.5 | loop fusion | flops 12576768 | bytes 16801792 | tf_op jit(solution)/shard_map/reduce_sum | solution.py:19
  608.5 11.9 %psum.28 = f32[2,1024]{1,0:T(2,128)S(1)} all-reduce(f32[2,1024]{1,0:T(2,128)S(1)} %get-tuple-element.5), channel_id=1, replica_groups=mesh['dp'=4,'row'=2,'col'=4] {'col'}, use_global_device_ids=true, to_apply=%region_2.0 | all-reduce | flops 2048 | bytes 16384 | tf_op jit(solution)/shard_map/psum | solution.py:20
  620.4 0.0 copy-done.3
  620.4 0.1 fusion.2
  620.5 0.0 copy-start.1
  620.5 22.3 %all-reduce.1 = (f32[2]{0:T(128)S(1)}, f32[2,2048]{1,0:T(2,128)S(1)}) all-reduce(f32[2]{0:T(128)S(1)} %get-tuple-element.10, f32[2,2048]{1,0:T(2,128)S(1)} %get-tuple-element.4), channel_id=1, replica_groups=mesh['dp'=4,'row'=2,'col'=4] {'dp','row'}, use_global_device_ids=true, to_apply=%region_6.0 | all-reduce | flops 4098 | bytes 32784 | tf_op jit(solution)/shard_map/psum | solution.py:24
  642.9 0.0 copy-done.2
  642.9 0.0 copy-start
  642.9 8.8 %multiply_reduce_fusion = f32[2]{0:T(128)S(1)} fusion(f32[2]{0:T(128)S(1)} %broadcast_multiply_fusion, f32[2,2048]{1,0:T(2,128)S(1)} %multiply_add_fusion, f32[2,1024]{1,0:T(2,128)S(1)} %get-tuple-element.11, f32[2,1,1024,2048]{3,2,0,1:T(8,128)} %reduce-scatter.4.cloned.1.call-done), kind=kLoop, calls=%fused_computation.4 | loop fusion | flops 20971518 | bytes 16801808 | tf_op jit(solution)/shard_map/reduce_sum | solution.py:28
  651.7 36.9 %psum.31 = f32[2]{0:T(128)S(1)} all-reduce(f32[2]{0:T(128)S(1)} %multiply_reduce_fusion), channel_id=1, replica_groups=mesh['dp'=4,'row'=2,'col'=4] {'dp','row','col'}, use_global_device_ids=true, to_apply=%region_8.0 | all-reduce | flops 2 | bytes 16 | tf_op jit(solution)/shard_map/psum | solution.py:28
  688.6 22.7 %multiply_subtract_fusion = (f32[2,1024,2048]{2,1,0:T(8,128)}, f32[2,1024,2048]{2,1,0:T(8,128)}) fusion(f32[2,1024,2048]{2,1,0:T(8,128)} %param.5, f32[2]{0:T(128)S(1)} %sqrt_maximum_fusion, f32[2]{0:T(128)S(1)} %broadcast_multiply_fusion, f32[2,2048]{1,0:T(2,128)S(1)} %multiply_add_fusion, f32[2,1024]{1,0:T(2,128)S(1)} %get-tuple-element.11, ...), kind=kLoop, calls=%fused_computation.3 | loop fusion | flops 25165824 | bytes 67133456 | tf_op jit(solution)/shard_map/sub | solution.py:31
  711.2 0.0 copy-done.1
  711.3 0.0 copy-done
  (3 shorter events, 0.0 us)
Async XLA Ops:
  7.2 593.6 %reduce-scatter.4.cloned.1.call-start = ((), (), s32[]{:S(2)}) async-start(), calls=%async_computation.1 | async-start | bytes 83886080
  39.7 580.7 %copy-start.3 = (f32[2,1024]{1,0:T(2,128)S(1)}, f32[2,1024]{1,0:T(2,128)}, u32[]{:S(2)}) copy-start(f32[2,1024]{1,0:T(2,128)} %param.6) | copy-start | bytes 24580
  39.7 603.2 %copy-start.2 = (f32[2,2048]{1,0:T(2,128)S(1)}, f32[2,2048]{1,0:T(2,128)}, u32[]{:S(2)}) copy-start(f32[2,2048]{1,0:T(2,128)} %param.7) | copy-start | bytes 49156
  620.5 90.7 %copy-start.1 = (f32[2,1024]{1,0:T(2,128)}, f32[2,1024]{1,0:T(2,128)S(1)}, u32[]{:S(2)}) copy-start(f32[2,1024]{1,0:T(2,128)S(1)} %get-tuple-element.11) | copy-start | bytes 24580
  642.9 68.3 %copy-start = (f32[2,2048]{1,0:T(2,128)}, f32[2,2048]{1,0:T(2,128)S(1)}, u32[]{:S(2)}) copy-start(f32[2,2048]{1,0:T(2,128)S(1)} %multiply_add_fusion) | copy-start | bytes 49156
Sparse Core Ops, SparseCore 0:
  39.8 560.9 reduce-scatter.3
where the time goes:
time: 719 us; the launch traced here: 718 us
  waiting for transfers between devices  561 us (78%)
  other arithmetic  71.7 us (10%)
  blocking collectives  71.1 us (10%)
  between operations  14.1 us (2%)
    unnamed x2, waiting for transfers between devices  561 us
    psum x1, blocking collectives, per_device(): lax.psum(jnp.sum(scaled * scaled, axis=(1, 2)), ('dp', 'row', 'col'))  36.9 us
    convert_element_type x1, other arithmetic, per_device(): pieces = partials[0, :, :, 0].astype(jnp.float32)  32.4 us
    sub x1, other arithmetic, per_device(): return (params - learn_rate * scaled, scaled, row_new, col_new)  22.7 us
    psum x1, blocking collectives, per_device(): level_sum = lax.psum(jnp.sum(row_new, axis=1), ('dp', 'row'))  22.3 us
  transfers between devices with their start and end apart: 1, of which 1 were waited for; matrix products, arithmetic and copies ran while one was open for 0% of the time, Pallas kernels for 0%

commit v1 on v0

v1 whole, which is shorter than its diff:
```python
import jax
import jax.numpy as jnp
from jax import lax
from jax.sharding import PartitionSpec as P

decay_rate = 1.0 - 2.0 ** (-0.8)
tiny_eps = 1e-30
clip_limit = 1.0
learn_rate = 0.01

chunks = 2
in_flight = 2


def swap(x, axes, mask):
    size = lax.axis_size(axes)
    return lax.ppermute(x, axes, [(i, i ^ mask) for i in range(size)])


def exchange_sum(x, axes):
    size = lax.axis_size(axes)
    got = [x] + [swap(x, axes, mask) for mask in range(1, size)]
    while len(got) > 1:
        got = [got[i] + got[i + 1] for i in range(0, len(got), 2)]
    return got[0]


def per_device(partials, params, row_factor, col_factor):
    mats, rows, block_cols = params.shape
    extent = block_cols * lax.axis_size("col")
    me = lax.axis_index("dp")
    part = rows // (2 * chunks)

    def piece(m, mask, start):
        block = lax.dynamic_slice(
            partials,
            (0, m, me ^ mask, 0, start, 0),
            (1, 1, 1, 1, part, block_cols),
        )
        return block.reshape(part, block_cols).astype(jnp.float32)

    sent = {1: [], 2: []}

    def send(x, mask):
        queue = sent[mask]
        if len(queue) >= in_flight:
            x, _ = lax.optimization_barrier((x, queue[-in_flight]))
        queue.append(swap(x, "dp", mask))
        return queue[-1]

    steps = [(m, chunk) for m in range(mats) for chunk in range(chunks)]
    halves = ((1, 2), (2, 1))

    def start_of(chunk, half):
        return (2 * chunk + half) * part

    def send_passed(m, chunk):
        return [send(piece(m, 3, start_of(chunk, h)), first) for h, (first, _) in enumerate(halves)]

    blocks = [[] for _ in range(mats)]
    passed = send_passed(*steps[0])
    for k, (m, chunk) in enumerate(steps):
        if k + 1 < len(steps):
            later = send_passed(*steps[k + 1])
        direct = [send(piece(m, first, start_of(chunk, h)), first) for h, (first, _) in enumerate(halves)]
        hop = [
            send(passed[h] + piece(m, second, start_of(chunk, h)), second)
            for h, (_, second) in enumerate(halves)
        ]
        for h in range(2):
            blocks[m].append(piece(m, 0, start_of(chunk, h)) + direct[h] + hop[h])
        passed = later

    new_params, update, new_rows, new_columns = [], [], [], []
    for m in range(mats):
        summed = jnp.concatenate(blocks[m], axis=0)
        squares = summed * summed
        row_total = exchange_sum(jnp.sum(squares, axis=1), "col")
        col_total = exchange_sum(jnp.sum(squares, axis=0), ("dp", "row"))
        row_new = decay_rate * row_factor[m] + (1.0 - decay_rate) * (row_total / extent + tiny_eps)
        col_new = decay_rate * col_factor[m] + (1.0 - decay_rate) * (col_total / extent + tiny_eps)
        weighted = squares * (1.0 / row_new)[:, None] * (1.0 / col_new)[None, :]
        pair = jnp.stack([jnp.sum(weighted), jnp.sum(row_new)])
        pair = exchange_sum(pair, ("dp", "row"))
        row_level = pair[1] / extent
        total = exchange_sum(pair[0], "col") * row_level
        spread = jnp.sqrt(total / (extent * extent))
        factor = jnp.sqrt(row_level) / jnp.maximum(1.0, spread / clip_limit)
        step = summed * (lax.rsqrt(row_new) * factor)[:, None] * lax.rsqrt(col_new)[None, :]
        new_params.append(params[m] - learn_rate * step)
        update.append(step)
        new_rows.append(row_new)
        new_columns.append(col_new)
    return tuple(jnp.stack(x) for x in (new_params, update, new_rows, new_columns))


def solution(mesh):
    placed = (
        P("dp", None, None, "row", None, "col"),
        P(None, ("dp", "row"), "col"),
        P(None, ("dp", "row")),
        P(None, "col"),
    )
    return jax.shard_map(
        per_device,
        mesh=mesh,
        in_specs=placed,
        out_specs=(
            P(None, ("dp", "row"), "col"),
            P(None, ("dp", "row"), "col"),
            P(None, ("dp", "row")),
            P(None, "col"),
        ),
        check_vma=False,
    )
```

time: 719 us -> 753 us (1.047)
  starting transfers between devices: 0.04 us -> 73.1 us
  blocking collectives: 71.1 us -> 0 us
  other arithmetic: 71.7 us -> 113 us
    unnamed x2 -> x0, waiting for transfers between devices: 561 us -> none
    ppermute x0 -> x64, waiting for transfers between devices: none -> 554 us  [swap(): return lax.ppermute(x, axes, [(i, i ^ mask) for i in range(size)])]
    ppermute x0 -> x64, starting transfers between devices: none -> 73.1 us  [swap(): return lax.ppermute(x, axes, [(i, i ^ mask) for i in range(size)])]
    psum x3 -> x0, blocking collectives: 71.1 us -> none  [the longest x1 36.9 us: per_device(): lax.psum(jnp.sum(scaled * scaled, axis=(1, 2)), ('dp', 'row', 'col'))]
    add x1 -> x6, other arithmetic: 0.02 us -> 40.8 us  [the longest x2 26.1 us: per_device(): blocks[m].append(piece(m, 0, start_of(chunk, h)) + direct[h] + hop[h])]
    another operation x0 -> x5, other arithmetic: none -> 25.1 us  [the longest x3 22.4 us: per_device(): jnp.stack(x)]
    convert_element_type x1, other arithmetic: 32.4 us -> 14 us  [piece(): return block.reshape(part, block_cols).astype(jnp.float32)]
    reduce_sum x3 -> x6, other arithmetic: 16.6 us -> 12.4 us  [the longest x4 10.3 us: per_device(): pair = jnp.stack([jnp.sum(weighted), jnp.sum(row_new)])]
  transfers between devices with their start and end apart: 1 -> 64, of which waited for: 1 -> 20; matrix products, arithmetic and copies ran while one was open for 0% -> 4% of each run, Pallas kernels for 0% -> 0%
where the time goes in v1:
time: 753 us
  waiting for transfers between devices  554 us (74%)
  other arithmetic  113 us (15%)
  starting transfers between devices  73.1 us (10%)
  between operations  7.55 us (1%)
    ppermute x64, waiting for transfers between devices, swap(): return lax.ppermute(x, axes, [(i, i ^ mask) for i in range(size)])  554 us
    ppermute x64, starting transfers between devices, swap(): return lax.ppermute(x, axes, [(i, i ^ mask) for i in range(size)])  73.1 us
    add x2, other arithmetic, per_device(): blocks[m].append(piece(m, 0, start_of(chunk, h)) + direct[h] + hop[h])  26.1 us
    another operation x3, other arithmetic, per_device(): jnp.stack(x)  22.4 us
    sub x1, other arithmetic, per_device(): new_params.append(params[m] - learn_rate * step)  21 us
  transfers between devices with their start and end apart: 64, of which 20 were waited for; matrix products, arithmetic and copies ran while one was open for 4% of the time, Pallas kernels for 0%

profile of v1, /device:TPU:0, one launch (start us, length us, event | category | flops | bytes accessed | tf_op | source)
XLA Modules:
  0.0 753.2 jit_solution(7041841456715818157)
XLA Ops:
  0.7 14.0 %bitcast_convert_fusion.5 = (f32[256,2048]{1,0:T(8,128)}, f32[256,2048]{1,0:T(8,128)}, f32[256,2048]{1,0:T(8,128)}, f32[256,2048]{1,0:T(8,128)S(1)}, f32[256,204...) fusion(bf16[1,2,4,1,1024,2048]{5,4,3,2,1,0:T(8,128)(2,1)} %para, ...), kind=kLoop, calls=%fused_computation.41 | loop fusion | flops 8388608 | bytes 50331660 | tf_op jit(solution)/shard_map/convert_element_type | solution.py:40
  14.6 3.0 collective-permute-start.4
  17.6 45.6 %collective-permute-done.4 = f32[256,2048]{1,0:T(8,128)S(1)} collective-permute-done((f32[256,2048]{1,0:T(8,128)S(1)}, f32[256,2048]{1,0:T(8,128)S(1)}, u32[]{:S(2)}, u32[]{:S(2)}) %collective-permute-start.4) | collective-permute-done | bytes 2097184 | tf_op jit(solution)/shard_map/ppermute | solution.py:17
  67.0 43.3 %collective-permute-done.5 = f32[256,2048]{1,0:T(8,128)S(1)} collective-permute-done((f32[256,2048]{1,0:T(8,128)}, f32[256,2048]{1,0:T(8,128)S(1)}, u32[]{:S(2)}, u32[]{:S(2)}) %collective-permute-start.5) | collective-permute-done | bytes 2097184 | tf_op jit(solution)/shard_map/ppermute | solution.py:17
  113.9 42.6 %collective-permute-done = f32[256,2048]{1,0:T(8,128)} collective-permute-done((f32[256,2048]{1,0:T(8,128)}, f32[256,2048]{1,0:T(8,128)}, u32[]{:S(2)}, u32[]{:S(2)}) %collective-permute-start) | collective-permute-done | bytes 2097184 | tf_op jit(solution)/shard_map/ppermute | solution.py:17
  156.5 2.7 collective-permute-done.9
  159.2 9.2 %convert_add_fusion.10 = (f32[256,2048]{1,0:T(8,128)}, f32[256,2048]{1,0:T(8,128)}, f32[256,2048]{1,0:T(8,128)}, f32[256,2048]{1,0:T(8,128)}) fusion(f32[256,2048]{1,0:T(8,128)} %collective-permute-done.6, bf16[1,2,4,1,1024,2048]{5,4,3,2,1,0:T(8,128)(2,1)} %param.4, s32[]{:T(128)S(6)} %select_n.11, f32[256,2048]{1,0:T(8,128)} %collective-permute-done.9, ...), kind=kLoop, calls=%fused_computation.27 | loop fusion | flops 4194304 | bytes 20971528 | tf_op jit(solution)/shard_map/add | solution.py:67
  169.8 31.7 %collective-permute-done.2 = f32[256,2048]{1,0:T(8,128)S(1)} collective-permute-done((f32[256,2048]{1,0:T(8,128)}, f32[256,2048]{1,0:T(8,128)S(1)}, u32[]{:S(2)}, u32[]{:S(2)}) %collective-permute-start.2) | collective-permute-done | bytes 2097184 | tf_op jit(solution)/shard_map/ppermute | solution.py:17
  202.6 11.6 %collective-permute-done.7 = f32[256,2048]{1,0:T(8,128)S(1)} collective-permute-done((f32[256,2048]{1,0:T(8,128)}, f32[256,2048]{1,0:T(8,128)S(1)}, u32[]{:S(2)}, u32[]{:S(2)}) %collective-permute-start.7) | collective-permute-done | bytes 2097184 | tf_op jit(solution)/shard_map/ppermute | solution.py:17
  217.1 33.2 %collective-permute-done.3 = f32[256,2048]{1,0:T(8,128)S(1)} collective-permute-done((f32[256,2048]{1,0:T(8,128)}, f32[256,2048]{1,0:T(8,128)S(1)}, u32[]{:S(2)}, u32[]{:S(2)}) %collective-permute-start.3) | collective-permute-done | bytes 2097184 | tf_op jit(solution)/shard_map/ppermute | solution.py:17
  251.3 8.8 %collective-permute-done.8 = f32[256,2048]{1,0:T(8,128)S(1)} collective-permute-done((f32[256,2048]{1,0:T(8,128)}, f32[256,2048]{1,0:T(8,128)S(1)}, u32[]{:S(2)}, u32[]{:S(2)}) %collective-permute-start.8) | collective-permute-done | bytes 2097184 | tf_op jit(solution)/shard_map/ppermute | solution.py:17
  262.2 33.0 %collective-permute-done.10 = f32[256,2048]{1,0:T(8,128)S(1)} collective-permute-done((f32[256,2048]{1,0:T(8,128)}, f32[256,2048]{1,0:T(8,128)S(1)}, u32[]{:S(2)}, u32[]{:S(2)}) %collective-permute-start.10) | collective-permute-done | bytes 2097184 | tf_op jit(solution)/shard_map/ppermute | solution.py:17
  296.3 43.8 %collective-permute-done.11 = f32[256,2048]{1,0:T(8,128)S(1)} collective-permute-done((f32[256,2048]{1,0:T(8,128)}, f32[256,2048]{1,0:T(8,128)S(1)}, u32[]{:S(2)}, u32[]{:S(2)}) %collective-permute-start.11) | collective-permute-done | bytes 2097184 | tf_op jit(solution)/shard_map/ppermute | solution.py:17
  342.7 11.0 %collective-permute-done.1 = f32[256,2048]{1,0:T(8,128)S(1)} collective-permute-done((f32[256,2048]{1,0:T(8,128)S(1)}, f32[256,2048]{1,0:T(8,128)S(1)}, u32[]{:S(2)}, u32[]{:S(2)}) %collective-permute-start.1) | collective-permute-done | bytes 2097184 | tf_op jit(solution)/shard_map/ppermute | solution.py:17
  355.1 30.0 %collective-permute-done.37 = f32[256,2048]{1,0:T(8,128)S(1)} collective-permute-done((f32[256,2048]{1,0:T(8,128)S(1)}, f32[256,2048]{1,0:T(8,128)S(1)}, u32[]{:S(2)}, u32[]{:S(2)}) %collective-permute-start.37) | collective-permute-done | bytes 2097184 | tf_op jit(solution)/shard_map/ppermute | solution.py:17
  386.5 43.5 %collective-permute-done.35 = f32[256,2048]{1,0:T(8,128)S(1)} collective-permute-done((f32[256,2048]{1,0:T(8,128)S(1)}, f32[256,2048]{1,0:T(8,128)S(1)}, u32[]{:S(2)}, u32[]{:S(2)}) %collective-permute-start.35) | collective-permute-done | bytes 2097184 | tf_op jit(solution)/shard_map/ppermute | solution.py:17
  430.0 2.8 convert_add_fusion
  435.2 6.5 collective-permute-done.12
  441.7 29.9 %collective-permute-done.42 = f32[256,2048]{1,0:T(8,128)} collective-permute-done((f32[256,2048]{1,0:T(8,128)}, f32[256,2048]{1,0:T(8,128)}, u32[]{:S(2)}, u32[]{:S(2)}) %collective-permute-start.42) | collective-permute-done | bytes 2097184 | tf_op jit(solution)/shard_map/ppermute | solution.py:17
  471.6 9.4 %collective-permute-done.43 = f32[256,2048]{1,0:T(8,128)} collective-permute-done((f32[256,2048]{1,0:T(8,128)}, f32[256,2048]{1,0:T(8,128)}, u32[]{:S(2)}, u32[]{:S(2)}) %collective-permute-start.43) | collective-permute-done | bytes 2097184 | tf_op jit(solution)/shard_map/ppermute | solution.py:17
  480.9 18.1 %fusion.9 = (f32[256,2048]{1,0:T(8,128)S(1)}, f32[256,2048]{1,0:T(8,128)}, f32[256,2048]{1,0:T(8,128)}, f32[256,2048]{1,0:T(8,128)}, f32[256,2048]{1,0:T(8,128)}...) fusion(f32[256,2048]{1,0:T(8,128)} %copy-done.16, f32[256,2048]{1,0:T(8,128)} %copy-done.20, ...), kind=kLoop, calls=%fused_computation.35 | loop fusion | flops 11010048 | bytes 52428812 | tf_op jit(solution)/shard_map/add | solution.py:71
  501.3 43.6 %collective-permute-done.13 = f32[256,2048]{1,0:T(8,128)} collective-permute-done((f32[256,2048]{1,0:T(8,128)}, f32[256,2048]{1,0:T(8,128)}, u32[]{:S(2)}, u32[]{:S(2)}) %collective-permute-start.13) | collective-permute-done | bytes 2097184 | tf_op jit(solution)/shard_map/ppermute | solution.py:17
  547.0 43.6 %collective-permute-done.34 = f32[256,2048]{1,0:T(8,128)} collective-permute-done((f32[256,2048]{1,0:T(8,128)}, f32[256,2048]{1,0:T(8,128)}, u32[]{:S(2)}, u32[]{:S(2)}) %collective-permute-start.34) | collective-permute-done | bytes 2097184 | tf_op jit(solution)/shard_map/ppermute | solution.py:17
  592.7 38.6 %collective-permute-done.40 = f32[256,2048]{1,0:T(8,128)} collective-permute-done((f32[256,2048]{1,0:T(8,128)}, f32[256,2048]{1,0:T(8,128)}, u32[]{:S(2)}, u32[]{:S(2)}) %collective-permute-start.40) | collective-permute-done | bytes 2097184 | tf_op jit(solution)/shard_map/ppermute | solution.py:17
  631.3 8.1 %fusion.6 = (f32[256,2048]{1,0:T(8,128)S(1)}, f32[256,2048]{1,0:T(8,128)S(1)}, f32[256,2048]{1,0:T(8,128)S(1)}) fusion(f32[256,2048]{1,0:T(8,128)} %collective-permute-done.13, f32[256,2048]{1,0:T(8,128)} %copy-done.11, bf16[1,2,4,1,1024,2048]{5,4,3,2,1,0:T(8,128)(2,1)} %param.4, s32[]{:T(128)S(6)} %select_n.8, f32[256,2048]{1,0:T(8,128)} %copy-done.23, ...), kind=kLoop, calls=%fused_computation.26 | loop fusion | flops 4718592 | bytes 22020100 | tf_op jit(solution)/shard_map/add | solution.py:71
  647.0 2.6 collective-permute-start.16
  665.0 5.8 multiply_reduce_fusion
  678.2 3.2 multiply_reduce_fusion.1
  693.6 2.6 collective-permute-start.63
  700.0 2.6 collective-permute-start.33
  711.0 21.0 %multiply_subtract_fusion.1 = (f32[1,1024,2048]{2,1,0:T(8,128)}, f32[1,1024,2048]{2,1,0:T(8,128)}, f32[1,1024,2048]{2,1,0:T(8,128)}, f32[1,1024,2048]{2,1,0:T(8,128)}) fusion(f32[2,1024,2048]{2,1,0:T(8,128)} %param.5, f32[2048]{0:T(1024)S(1)} %rsqrt.13, f32[1024]{0:T(1024)S(1)} %rsqrt_multiply_fusion.1, f32[1,256,2048]{2,1,0:T(8,128)} %bitcast.125, ...), kind=kLoop, calls=%fused_computation.10 | loop fusion | flops 29360128 | bytes 67133440 | tf_op jit(solution)/shard_map/sub | solution.py:90
  732.1 21.1 %pad_maximum_fusion = (f32[2,1024,2048]{2,1,0:T(8,128)}, f32[2,1024,2048]{2,1,0:T(8,128)}) fusion(f32[1,1024,2048]{2,1,0:T(8,128)} %get-tuple-element.91, f32[1,1024,2048]{2,1,0:T(8,128)} %get-tuple-element.48, f32[1,1024,2048]{2,1,0:T(8,128)} %get-tuple-element.92, f32[1,1024,2048]{2,1,0:T(8,128)} %get-tuple-element.49), kind=kLoop, calls=%fused_computation | loop fusion | flops 8388608 | bytes 67108864 | tf_op jit(solution)/shard_map/stack | solution.py:94
  (181 shorter events, 79.3 us)
Async XLA Ops:
  14.6 48.7 %collective-permute-start.4 = (f32[256,2048]{1,0:T(8,128)S(1)}, f32[256,2048]{1,0:T(8,128)S(1)}, u32[]{:S(2)}, u32[]{:S(2)}) collective-permute-start(f32[256,2048]{1,0:T(8,128)S(1)} %get-tuple-element.81), channel_id=1, source_target_pairs={{0,16},{8,24},{16,0},{24,8},{1,17},{9,25},{17,1},{25,9},{2,18},{10... | collective-permute-start | bytes 6291464 | tf_op jit(solution)/shard_map/ppermute | solution.py:17
  63.3 47.0 %collective-permute-start.5 = (f32[256,2048]{1,0:T(8,128)}, f32[256,2048]{1,0:T(8,128)S(1)}, u32[]{:S(2)}, u32[]{:S(2)}) collective-permute-start(f32[256,2048]{1,0:T(8,128)} %get-tuple-element.26), channel_id=1, source_target_pairs={{0,16},{8,24},{16,0},{24,8},{1,17},{9,25},{17,1},{25,9},{2,18},{10... | collective-permute-start | bytes 6291464 | tf_op jit(solution)/shard_map/ppermute | solution.py:17
  65.0 48.9 %collective-permute-start.6 = (f32[256,2048]{1,0:T(8,128)}, f32[256,2048]{1,0:T(8,128)}, u32[]{:S(2)}, u32[]{:S(2)}) collective-permute-start(f32[256,2048]{1,0:T(8,128)} %get-tuple-element.80), channel_id=1, source_target_pairs={{0,8},{8,0},{16,24},{24,16},{1,9},{9,1},{17,25},{25,17},{2,10},{10... | collective-permute-start | bytes 6291464 | tf_op jit(solution)/shard_map/ppermute | solution.py:17
  66.5 90.0 %collective-permute-start = (f32[256,2048]{1,0:T(8,128)}, f32[256,2048]{1,0:T(8,128)}, u32[]{:S(2)}, u32[]{:S(2)}) collective-permute-start(f32[256,2048]{1,0:T(8,128)} %get-tuple-element.84), channel_id=1, source_target_pairs={{0,8},{8,0},{16,24},{24,16},{1,9},{9,1},{17,25},{25,17},{2,10},{10... | collective-permute-start | bytes 6291464 | tf_op jit(solution)/shard_map/ppermute | solution.py:17
  110.3 48.9 %collective-permute-start.9 = (f32[256,2048]{1,0:T(8,128)}, f32[256,2048]{1,0:T(8,128)}, u32[]{:S(2)}, u32[]{:S(2)}) collective-permute-start(f32[256,2048]{1,0:T(8,128)} %get-tuple-element.29), channel_id=1, source_target_pairs={{0,16},{8,24},{16,0},{24,8},{1,17},{9,25},{17,1},{25,9},{2,18},{10... | collective-permute-start | bytes 6291464 | tf_op jit(solution)/shard_map/ppermute | solution.py:17
  111.7 89.7 %collective-permute-start.2 = (f32[256,2048]{1,0:T(8,128)}, f32[256,2048]{1,0:T(8,128)S(1)}, u32[]{:S(2)}, u32[]{:S(2)}) collective-permute-start(f32[256,2048]{1,0:T(8,128)} %get-tuple-element.83), channel_id=1, source_target_pairs={{0,16},{8,24},{16,0},{24,8},{1,17},{9,25},{17,1},{25,9},{2,18},{10... | collective-permute-start | bytes 6291464 | tf_op jit(solution)/shard_map/ppermute | solution.py:17
  168.4 45.8 %collective-permute-start.7 = (f32[256,2048]{1,0:T(8,128)}, f32[256,2048]{1,0:T(8,128)S(1)}, u32[]{:S(2)}, u32[]{:S(2)}) collective-permute-start(f32[256,2048]{1,0:T(8,128)} %get-tuple-element.27), channel_id=1, source_target_pairs={{0,8},{8,0},{16,24},{24,16},{1,9},{9,1},{17,25},{25,17},{2,10},{10... | collective-permute-start | bytes 6291464 | tf_op jit(solution)/shard_map/ppermute | solution.py:17
  201.5 48.8 %collective-permute-start.3 = (f32[256,2048]{1,0:T(8,128)}, f32[256,2048]{1,0:T(8,128)S(1)}, u32[]{:S(2)}, u32[]{:S(2)}) collective-permute-start(f32[256,2048]{1,0:T(8,128)} %get-tuple-element.25), channel_id=1, source_target_pairs={{0,16},{8,24},{16,0},{24,8},{1,17},{9,25},{17,1},{25,9},{2,18},{10... | collective-permute-start | bytes 6291464 | tf_op jit(solution)/shard_map/ppermute | solution.py:17
  214.2 46.0 %collective-permute-start.8 = (f32[256,2048]{1,0:T(8,128)}, f32[256,2048]{1,0:T(8,128)S(1)}, u32[]{:S(2)}, u32[]{:S(2)}) collective-permute-start(f32[256,2048]{1,0:T(8,128)} %get-tuple-element.28), channel_id=1, source_target_pairs={{0,8},{8,0},{16,24},{24,16},{1,9},{9,1},{17,25},{25,17},{2,10},{10... | collective-permute-start | bytes 6291464 | tf_op jit(solution)/shard_map/ppermute | solution.py:17
  215.6 79.6 %collective-permute-start.10 = (f32[256,2048]{1,0:T(8,128)}, f32[256,2048]{1,0:T(8,128)S(1)}, u32[]{:S(2)}, u32[]{:S(2)}) collective-permute-start(f32[256,2048]{1,0:T(8,128)} %get-tuple-element.30), channel_id=1, source_target_pairs={{0,16},{8,24},{16,0},{24,8},{1,17},{9,25},{17,1},{25,9},{2,18},{10... | collective-permute-start | bytes 6291464 | tf_op jit(solution)/shard_map/ppermute | solution.py:17
  250.2 89.9 %collective-permute-start.11 = (f32[256,2048]{1,0:T(8,128)}, f32[256,2048]{1,0:T(8,128)S(1)}, u32[]{:S(2)}, u32[]{:S(2)}) collective-permute-start(f32[256,2048]{1,0:T(8,128)} %get-tuple-element.31), channel_id=1, source_target_pairs={{0,16},{8,24},{16,0},{24,8},{1,17},{9,25},{17,1},{25,9},{2,18},{10... | collective-permute-start | bytes 6291464 | tf_op jit(solution)/shard_map/ppermute | solution.py:17
  260.2 81.1 %collective-permute-start.38 = (f32[256,2048]{1,0:T(8,128)S(1)}, f32[256,2048]{1,0:T(8,128)S(1)}, u32[]{:S(2)}, u32[]{:S(2)}) collective-permute-start(f32[256,2048]{1,0:T(8,128)S(1)} %copy-done.15), channel_id=1, source_target_pairs={{0,8},{8,0},{16,24},{24,16},{1,9},{9,1},{17,25},{25,17},{2,10},{10... | collective-permute-start | bytes 6291464 | tf_op jit(solution)/shard_map/ppermute | solution.py:17
  261.6 92.1 %collective-permute-start.1 = (f32[256,2048]{1,0:T(8,128)S(1)}, f32[256,2048]{1,0:T(8,128)S(1)}, u32[]{:S(2)}, u32[]{:S(2)}) collective-permute-start(f32[256,2048]{1,0:T(8,128)S(1)} %copy-done.13), channel_id=1, source_target_pairs={{0,8},{8,0},{16,24},{24,16},{1,9},{9,1},{17,25},{25,17},{2,10},{10... | collective-permute-start | bytes 6291464 | tf_op jit(solution)/shard_map/ppermute | solution.py:17
  295.2 89.9 %collective-permute-start.37 = (f32[256,2048]{1,0:T(8,128)S(1)}, f32[256,2048]{1,0:T(8,128)S(1)}, u32[]{:S(2)}, u32[]{:S(2)}) collective-permute-start(f32[256,2048]{1,0:T(8,128)S(1)} %get-tuple-element.37), channel_id=1, source_target_pairs={{0,16},{8,24},{16,0},{24,8},{1,17},{9,25},{17,1},{25,9},{2,18},{10... | collective-permute-start | bytes 6291464 | tf_op jit(solution)/shard_map/ppermute | solution.py:17
  340.1 89.9 %collective-permute-start.35 = (f32[256,2048]{1,0:T(8,128)S(1)}, f32[256,2048]{1,0:T(8,128)S(1)}, u32[]{:S(2)}, u32[]{:S(2)}) collective-permute-start(f32[256,2048]{1,0:T(8,128)S(1)} %get-tuple-element.35), channel_id=1, source_target_pairs={{0,16},{8,24},{16,0},{24,8},{1,17},{9,25},{17,1},{25,9},{2,18},{10... | collective-permute-start | bytes 6291464 | tf_op jit(solution)/shard_map/ppermute | solution.py:17
  341.2 91.6 %collective-permute-start.39 = (f32[256,2048]{1,0:T(8,128)}, f32[256,2048]{1,0:T(8,128)S(1)}, u32[]{:S(2)}, u32[]{:S(2)}) collective-permute-start(f32[256,2048]{1,0:T(8,128)} %get-tuple-element.39), channel_id=1, source_target_pairs={{0,8},{8,0},{16,24},{24,16},{1,9},{9,1},{17,25},{25,17},{2,10},{10... | collective-permute-start | bytes 6291464 | tf_op jit(solution)/shard_map/ppermute | solution.py:17
  353.7 88.0 %collective-permute-start.12 = (f32[256,2048]{1,0:T(8,128)}, f32[256,2048]{1,0:T(8,128)}, u32[]{:S(2)}, u32[]{:S(2)}) collective-permute-start(f32[256,2048]{1,0:T(8,128)} %get-tuple-element.32), channel_id=1, source_target_pairs={{0,8},{8,0},{16,24},{24,16},{1,9},{9,1},{17,25},{25,17},{2,10},{10... | collective-permute-start | bytes 6291464 | tf_op jit(solution)/shard_map/ppermute | solution.py:17
  385.1 86.5 %collective-permute-start.42 = (f32[256,2048]{1,0:T(8,128)}, f32[256,2048]{1,0:T(8,128)}, u32[]{:S(2)}, u32[]{:S(2)}) collective-permute-start(f32[256,2048]{1,0:T(8,128)} %get-tuple-element.42), channel_id=1, source_target_pairs={{0,16},{8,24},{16,0},{24,8},{1,17},{9,25},{17,1},{25,9},{2,18},{10... | collective-permute-start | bytes 6291464 | tf_op jit(solution)/shard_map/ppermute | solution.py:17
  434.1 46.8 %collective-permute-start.43 = (f32[256,2048]{1,0:T(8,128)}, f32[256,2048]{1,0:T(8,128)}, u32[]{:S(2)}, u32[]{:S(2)}) collective-permute-start(f32[256,2048]{1,0:T(8,128)} %convert_add_fusion), channel_id=1, source_target_pairs={{0,8},{8,0},{16,24},{24,16},{1,9},{9,1},{17,25},{25,17},{2,10},{10... | collective-permute-start | bytes 6291464 | tf_op jit(solution)/shard_map/ppermute | solution.py:17
  499.0 45.9 %collective-permute-start.13 = (f32[256,2048]{1,0:T(8,128)}, f32[256,2048]{1,0:T(8,128)}, u32[]{:S(2)}, u32[]{:S(2)}) collective-permute-start(f32[256,2048]{1,0:T(8,128)} %get-tuple-element.33), channel_id=1, source_target_pairs={{0,8},{8,0},{16,24},{24,16},{1,9},{9,1},{17,25},{25,17},{2,10},{10... | collective-permute-start | bytes 6291464 | tf_op jit(solution)/shard_map/ppermute | solution.py:17
  500.6 44.9 %collective-permute-start.36 = (f32[256,2048]{1,0:T(8,128)}, f32[256,2048]{1,0:T(8,128)}, u32[]{:S(2)}, u32[]{:S(2)}) collective-permute-start(f32[256,2048]{1,0:T(8,128)} %get-tuple-element.36), channel_id=1, source_target_pairs={{0,16},{8,24},{16,0},{24,8},{1,17},{9,25},{17,1},{25,9},{2,18},{10... | collective-permute-start | bytes 6291464 | tf_op jit(solution)/shard_map/ppermute | solution.py:17
  544.9 45.8 %collective-permute-start.34 = (f32[256,2048]{1,0:T(8,128)}, f32[256,2048]{1,0:T(8,128)}, u32[]{:S(2)}, u32[]{:S(2)}) collective-permute-start(f32[256,2048]{1,0:T(8,128)} %get-tuple-element.34), channel_id=1, source_target_pairs={{0,8},{8,0},{16,24},{24,16},{1,9},{9,1},{17,25},{25,17},{2,10},{10... | collective-permute-start | bytes 6291464 | tf_op jit(solution)/shard_map/ppermute | solution.py:17
  545.5 45.9 %collective-permute-start.41 = (f32[256,2048]{1,0:T(8,128)}, f32[256,2048]{1,0:T(8,128)S(1)}, u32[]{:S(2)}, u32[]{:S(2)}) collective-permute-start(f32[256,2048]{1,0:T(8,128)} %get-tuple-element.41), channel_id=1, source_target_pairs={{0,16},{8,24},{16,0},{24,8},{1,17},{9,25},{17,1},{25,9},{2,18},{10... | collective-permute-start | bytes 6291464 | tf_op jit(solution)/shard_map/ppermute | solution.py:17
  590.7 40.6 %collective-permute-start.40 = (f32[256,2048]{1,0:T(8,128)}, f32[256,2048]{1,0:T(8,128)}, u32[]{:S(2)}, u32[]{:S(2)}) collective-permute-start(f32[256,2048]{1,0:T(8,128)} %get-tuple-element.40), channel_id=1, source_target_pairs={{0,8},{8,0},{16,24},{24,16},{1,9},{9,1},{17,25},{25,17},{2,10},{10... | collective-permute-start | bytes 6291464 | tf_op jit(solution)/shard_map/ppermute | solution.py:17
  659.7 11.1 %collective-permute-start.23 = (f32[2048]{0:T(1024)S(1)}, f32[2048]{0:T(1024)S(1)}, u32[]{:S(2)}, u32[]{:S(2)}) collective-permute-start(f32[2048]{0:T(1024)S(1)} %get-tuple-element.45), channel_id=1, source_target_pairs={{0,28},{4,24},{8,20},{12,16},{16,12},{20,8},{24,4},{28,0},{1,29},{... | collective-permute-start | bytes 24584 | tf_op jit(solution)/shard_map/ppermute | solution.py:17
  660.8 10.8 %collective-permute-start.22 = (f32[2048]{0:T(1024)S(1)}, f32[2048]{0:T(1024)S(1)}, u32[]{:S(2)}, u32[]{:S(2)}) collective-permute-start(f32[2048]{0:T(1024)S(1)} %get-tuple-element.45), channel_id=1, source_target_pairs={{0,24},{4,28},{8,16},{12,20},{16,8},{20,12},{24,0},{28,4},{1,25},{... | collective-permute-start | bytes 24584 | tf_op jit(solution)/shard_map/ppermute | solution.py:17
  662.3 10.9 %collective-permute-start.21 = (f32[2048]{0:T(1024)S(1)}, f32[2048]{0:T(1024)S(1)}, u32[]{:S(2)}, u32[]{:S(2)}) collective-permute-start(f32[2048]{0:T(1024)S(1)} %get-tuple-element.45), channel_id=1, source_target_pairs={{0,20},{4,16},{8,28},{12,24},{16,4},{20,0},{24,12},{28,8},{1,21},{... | collective-permute-start | bytes 24584 | tf_op jit(solution)/shard_map/ppermute | solution.py:17
  662.5 12.2 %collective-permute-start.20 = (f32[2048]{0:T(1024)S(1)}, f32[2048]{0:T(1024)S(1)}, u32[]{:S(2)}, u32[]{:S(2)}) collective-permute-start(f32[2048]{0:T(1024)S(1)} %get-tuple-element.45), channel_id=1, source_target_pairs={{0,16},{4,20},{8,24},{12,28},{16,0},{20,4},{24,8},{28,12},{1,17},{... | collective-permute-start | bytes 24584 | tf_op jit(solution)/shard_map/ppermute | solution.py:17
  664.2 11.4 %collective-permute-start.19 = (f32[2048]{0:T(1024)S(1)}, f32[2048]{0:T(1024)S(1)}, u32[]{:S(2)}, u32[]{:S(2)}) collective-permute-start(f32[2048]{0:T(1024)S(1)} %get-tuple-element.45), channel_id=1, source_target_pairs={{0,12},{4,8},{8,4},{12,0},{16,28},{20,24},{24,20},{28,16},{1,13},{... | collective-permute-start | bytes 24584 | tf_op jit(solution)/shard_map/ppermute | solution.py:17
  676.6 10.5 %collective-permute-start.55 = (f32[2]{0:T(128)S(1)}, f32[2]{0:T(128)S(1)}, u32[]{:S(2)}, u32[]{:S(2)}) collective-permute-start(f32[2]{0:T(128)S(1)} %pad_maximum_fusion.5), channel_id=1, source_target_pairs={{0,8},{4,12},{8,0},{12,4},{16,24},{20,28},{24,16},{28,20},{1,9},{5... | collective-permute-start | bytes 32 | tf_op jit(solution)/shard_map/ppermute | solution.py:17
  693.6 13.5 %collective-permute-start.63 = (f32[]{:T(128)}, f32[]{:T(128)}, u32[]{:S(2)}, u32[]{:S(2)}) collective-permute-start(f32[]{:T(128)} %bitcast.51), channel_id=1, source_target_pairs={{0,3},{1,2},{2,1},{3,0},{4,7},{5,6},{6,5},{7,4},{8,11},{9,10},{10,... | collective-permute-start | bytes 20 | tf_op jit(solution)/shard_map/ppermute | solution.py:17
  696.2 10.9 %collective-permute-start.62 = (f32[]{:T(128)}, f32[]{:T(128)}, u32[]{:S(2)}, u32[]{:S(2)}) collective-permute-start(f32[]{:T(128)} %bitcast.51), channel_id=1, source_target_pairs={{0,2},{1,3},{2,0},{3,1},{4,6},{5,7},{6,4},{7,5},{8,10},{9,11},{10,... | collective-permute-start | bytes 20 | tf_op jit(solution)/shard_map/ppermute | solution.py:17
  (59 other events, 1885.9 us)

commit v2 on v0

v2 whole, which is shorter than its diff:
```python
import functools

import jax
import jax.numpy as jnp
from jax import lax
from jax.experimental import pallas as pl
from jax.experimental.pallas import tpu as pltpu
from jax.sharding import PartitionSpec as P

decay_rate = 1.0 - 2.0 ** (-0.8)
tiny_eps = 1e-30
clip_limit = 1.0
learn_rate = 0.01

lanes = 128
sublanes = 8
blocks_of_matrix = 8
tile_rows = 16


def swap(x, axes, mask):
    size = lax.axis_size(axes)
    return lax.ppermute(x, axes, [(i, i ^ mask) for i in range(size)])


def exchange_sum(x, axes):
    size = lax.axis_size(axes)
    got = [x] + [swap(x, axes, mask) for mask in range(1, size)]
    while len(got) > 1:
        got = [got[i] + got[i + 1] for i in range(0, len(got), 2)]
    return got[0]


def pairwise_sum(x, axes):
    mask = 1
    while mask < lax.axis_size(axes):
        x = x + swap(x, axes, mask)
        mask *= 2
    return x


def step_kernel(takes, finishes, sends, starts, *refs):
    refs = list(refs[1:])
    take = lambda yes: refs.pop(0) if yes else None
    got = [take(takes or finishes) for _ in range(2)]
    mine = take(finishes)
    direct = [take(sends) for _ in range(2)]
    relay = [take(sends) for _ in range(2)]
    onward = take(starts)
    cols_in, summed_in, rows_in = take(True), take(finishes), take(finishes)
    out = [take(sends or starts) for _ in range(2)]
    cols_out, summed_out, rows_out = take(True), take(finishes), take(finishes)
    tail_slot = 2 if finishes else 0
    out_slot = 2 if sends else 0

    @pl.when(pl.program_id(0) == 0)
    def _():
        cols_out[...] = cols_in[...]

    f32 = jnp.float32
    for half in range(2):
        if starts:
            out[half][out_slot] = onward[half].astype(f32)
        if sends:
            out[half][0] = direct[half][...].astype(f32)
            out[1 - half][1] = got[half][tail_slot] + relay[half][...].astype(f32)
        if finishes:
            total = mine[half].astype(f32) + got[half][0] + got[1 - half][1]
            summed_out[half] = total
            squares = total * total
            rows_out[half] = sum(
                squares[:, i : i + lanes] for i in range(0, squares.shape[1], lanes)
            )
            cols_out[...] += sum(
                squares[i : i + sublanes] for i in range(0, squares.shape[0], sublanes)
            )


def step(j, total_blocks, me, partials, got, cols, summed, rows):
    mats, _, count, _, part, width = partials.shape
    tile = min(tile_rows, part)
    finishes = j >= 2
    takes = 0 <= j < total_blocks
    sends = takes
    starts = j + 2 < total_blocks
    f32 = jnp.float32

    def piece_spec(block, mask, half):
        m, b = divmod(block, count)
        if half is None:
            return pl.BlockSpec(
                (None, None, None, 2, tile, width),
                lambda t, at: (m, at[0] ^ mask, b, 0, t, 0),
            )
        return pl.BlockSpec(
            (None, None, None, None, tile, width),
            lambda t, at: (m, at[0] ^ mask, b, half, t, 0),
        )

    def message_spec(slots):
        return pl.BlockSpec((slots, tile, width), lambda t, at: (0, t, 0))

    operands, in_specs = [], []

    def add(x, spec):
        operands.append(x)
        in_specs.append(spec)

    if j >= 0:
        for x in got:
            add(x, message_spec(x.shape[0]))
    if finishes:
        add(partials, piece_spec(j - 2, 0, None))
    if sends:
        for half, mask in ((0, 1), (1, 2)):
            add(partials, piece_spec(j, mask, half))
        for half, mask in ((0, 2), (1, 1)):
            add(partials, piece_spec(j, mask, half))
    if starts:
        add(partials, piece_spec(j + 2, 3, None))
    m, b = divmod(max(j - 2, 0), count)
    cols_spec = pl.BlockSpec((None, sublanes, width), lambda t, at: (m, 0, 0))
    done_spec = lambda size: pl.BlockSpec(
        (None, None, 2, tile, size), lambda t, at: (m, b, 0, t, 0)
    )
    add(cols, cols_spec)
    aliases = {len(operands): 2 if sends or starts else 0}
    if finishes:
        for x in (summed, rows):
            add(x, pl.BlockSpec(memory_space=pl.ANY))
            aliases[len(operands)] = max(aliases.values()) + 1

    slots = (2 if sends else 0) + (1 if starts else 0)
    out_shape, out_specs = [], []
    if slots:
        for _ in range(2):
            out_shape.append(jax.ShapeDtypeStruct((slots, part, width), f32))
            out_specs.append(message_spec(slots))
    out_shape.append(jax.ShapeDtypeStruct(cols.shape, f32))
    out_specs.append(cols_spec)
    if finishes:
        for x in (summed, rows):
            out_shape.append(jax.ShapeDtypeStruct(x.shape, f32))
            out_specs.append(done_spec(x.shape[-1]))
    moved = part * width * (4 * (2 * slots + 8) + 2 * 8)
    result = pl.pallas_call(
        functools.partial(step_kernel, takes, finishes, sends, starts),
        out_shape=out_shape,
        grid_spec=pltpu.PrefetchScalarGridSpec(
            num_scalar_prefetch=1,
            grid=(part // tile,),
            in_specs=in_specs,
            out_specs=out_specs,
        ),
        input_output_aliases=aliases,
        compiler_params=pltpu.CompilerParams(vmem_limit_bytes=24 * 1024 * 1024),
        cost_estimate=pl.CostEstimate(
            flops=part * width * 20, bytes_accessed=moved, transcendentals=0
        ),
        name="step",
    )(me, *operands)
    sent = result[:2] if slots else None
    rest = result[2:] if slots else result
    return (sent, rest[0]) + ((rest[1], rest[2]) if finishes else (summed, rows))


def per_device(partials, params, row_factor, col_factor):
    mats, rows, block_cols = params.shape
    extent = block_cols * lax.axis_size("col")
    me = lax.axis_index("dp").astype(jnp.int32).reshape(1)
    count = blocks_of_matrix
    while rows % (2 * count * 16):
        count //= 2
    part = rows // (2 * count)
    total_blocks = mats * count
    pieces = partials.reshape(mats, partials.shape[2], count, 2, part, block_cols)

    cols = jnp.zeros((mats, sublanes, block_cols), jnp.float32)
    summed = jnp.zeros((mats, count, 2, part, block_cols), jnp.float32)
    row_parts = jnp.zeros((mats, count, 2, part, lanes), jnp.float32)
    flying = {}
    for j in range(-2, total_blocks + 2):
        got = flying.pop(j, None)
        sent, cols, summed, row_parts = step(
            j, total_blocks, me, pieces, got, cols, summed, row_parts
        )
        if sent is not None:
            flying[j + 2] = [swap(sent[0], "dp", 1), swap(sent[1], "dp", 2)]

    summed = summed.reshape(params.shape)
    row_total = exchange_sum(jnp.sum(row_parts.reshape(mats, rows, lanes), axis=2), "col")
    row_new = decay_rate * row_factor + (1.0 - decay_rate) * (row_total / extent + tiny_eps)
    weighted = jnp.sum(summed * summed * (1.0 / row_new)[:, :, None], axis=1)
    level = jnp.broadcast_to(jnp.sum(row_new, axis=1)[:, None], (mats, lanes))
    sums = jnp.concatenate([jnp.sum(cols, axis=1), weighted, level], axis=1)
    sums = pairwise_sum(sums, ("dp", "row"))
    col_total, weighted = sums[:, :block_cols], sums[:, block_cols : 2 * block_cols]
    row_level = sums[:, 2 * block_cols] / extent
    col_new = decay_rate * col_factor + (1.0 - decay_rate) * (col_total / extent + tiny_eps)
    total = exchange_sum(jnp.sum(weighted / col_new, axis=1), "col") * row_level
    spread = jnp.sqrt(total / (extent * extent))
    factor = jnp.sqrt(row_level) / jnp.maximum(1.0, spread / clip_limit)
    by_row = lax.rsqrt(row_new) * factor[:, None]
    update = summed * by_row[:, :, None] * lax.rsqrt(col_new)[:, None, :]
    return (params - learn_rate * update, update, row_new, col_new)


def solution(mesh):
    placed = (
        P("dp", None, None, "row", None, "col"),
        P(None, ("dp", "row"), "col"),
        P(None, ("dp", "row")),
        P(None, "col"),
    )
    return jax.shard_map(
        per_device,
        mesh=mesh,
        in_specs=placed,
        out_specs=(
            P(None, ("dp", "row"), "col"),
            P(None, ("dp", "row"), "col"),
            P(None, ("dp", "row")),
            P(None, "col"),
        ),
        check_vma=False,
    )
```

time: 719 us -> 613 us (0.85)
  waiting for transfers between devices: 561 us -> 453 us
  blocking collectives: 71.1 us -> 0 us
  Pallas kernels: 0 us -> 58.7 us
  starting transfers between devices: 0.04 us -> 50.7 us
  other arithmetic: 71.7 us -> 32.1 us
  local copies, waits for them, and re-layouts: 0.02 us -> 16.9 us
  between operations: 14.1 us -> 0.97 us
    unnamed x2 -> x0, waiting for transfers between devices: 561 us -> none
    ppermute x0 -> x45, waiting for transfers between devices: none -> 453 us  [swap(): return lax.ppermute(x, axes, [(i, i ^ mask) for i in range(size)])]
    psum x3 -> x0, blocking collectives: 71.1 us -> none  [the longest x1 36.9 us: per_device(): lax.psum(jnp.sum(scaled * scaled, axis=(1, 2)), ('dp', 'row', 'col'))]
    pallas_call x0 -> x20, Pallas kernels: none -> 58.7 us  [step(): pl.pallas_call(functools.partial(step_kernel, takes, finishes, sends, sta...]
    ppermute x0 -> x45, starting transfers between devices: none -> 50.7 us  [swap(): return lax.ppermute(x, axes, [(i, i ^ mask) for i in range(size)])]
    convert_element_type x1 -> x0, other arithmetic: 32.4 us -> none  [per_device(): pieces = partials[0, :, :, 0].astype(jnp.float32)]
    unnamed x8 -> x28, local copies, waits for them, and re-layouts: 0.02 us -> 14.4 us
    reduce_sum x3 -> x5, other arithmetic: 16.6 us -> 9.4 us  [the longest x1 7.51 us: per_device(): weighted = jnp.sum(summed * summed * (1.0 / row_new)[:, :, None], axis=1)]
  transfers between devices with their start and end apart: 1 -> 45, of which waited for: 1 -> 43; matrix products, arithmetic and copies ran while one was open for 0% -> 0% of each run, Pallas kernels for 0% -> 9%
where the time goes in v2:
time: 613 us; the launch traced here: 612 us
  waiting for transfers between devices  453 us (74%)
  Pallas kernels  58.7 us (10%)
  starting transfers between devices  50.7 us (8%)
  other arithmetic  32.1 us (5%)
  local copies, waits for them, and re-layouts  16.9 us (3%)
    ppermute x45, waiting for transfers between devices, swap(): return lax.ppermute(x, axes, [(i, i ^ mask) for i in range(size)])  453 us
    pallas_call x20, Pallas kernels, step(): pl.pallas_call(functools.partial(step_kernel, takes, finishes, sends, sta...  58.7 us
    ppermute x45, starting transfers between devices, swap(): return lax.ppermute(x, axes, [(i, i ^ mask) for i in range(size)])  50.7 us
    sub x1, other arithmetic, per_device(): return (params - learn_rate * update, update, row_new, col_new)  22.4 us
    unnamed x28, local copies, waits for them, and re-layouts  14.4 us
  transfers between devices with their start and end apart: 45, of which 43 were waited for; matrix products, arithmetic and copies ran while one was open for 0% of the time, Pallas kernels for 9%

profile of v2, /device:TPU:0, one launch (start us, length us, event | category | flops | bytes accessed | tf_op | source)
XLA Modules:
  0.0 612.1 jit_solution(15469277249225951465)
XLA Ops:
  9.8 8.6 %collective-permute-done.2.refs_1_ = f32[1,64,2048]{2,1,0:T(8,128)S(1)} collective-permute-done((f32[1,64,2048]{2,1,0:T(8,128)S(1)}, f32[1,64,2048]{2,1,0:T(8,128)S(1)}, u32[]{:S(2)}, u32[]{:S(2)}) %collective-permute-start.2) | collective-permute-done | bytes 524320 | tf_op jit(solution)/shard_map/ppermute | solution.py:23
  25.2 4.4 collective-permute-done.refs_1_
  31.7 3.8 step.23
  37.6 25.8 %collective-permute-done.6.refs_1_ = f32[3,64,2048]{2,1,0:T(8,128)S(1)} collective-permute-done((f32[3,64,2048]{2,1,0:T(8,128)S(1)}, f32[3,64,2048]{2,1,0:T(8,128)S(1)}, u32[]{:S(2)}, u32[]{:S(2)}) %collective-permute-start.6) | collective-permute-done | bytes 1572896 | tf_op jit(solution)/shard_map/ppermute | solution.py:23
  71.7 3.1 step.24
  77.5 19.6 %collective-permute-done.4.refs_1_ = f32[3,64,2048]{2,1,0:T(8,128)} collective-permute-done((f32[3,64,2048]{2,1,0:T(8,128)S(1)}, f32[3,64,2048]{2,1,0:T(8,128)}, u32[]{:S(2)}, u32[]{:S(2)}) %collective-permute-start.4) | collective-permute-done | bytes 1572896 | tf_op jit(solution)/shard_map/ppermute | solution.py:23
  99.2 3.5 step.25
  104.9 25.9 %collective-permute-done.10.refs_1_ = f32[3,64,2048]{2,1,0:T(8,128)S(1)} collective-permute-done((f32[3,64,2048]{2,1,0:T(8,128)S(1)}, f32[3,64,2048]{2,1,0:T(8,128)S(1)}, u32[]{:S(2)}, u32[]{:S(2)}) %collective-permute-start.10) | collective-permute-done | bytes 1572896 | tf_op jit(solution)/shard_map/ppermute | solution.py:23
  132.8 3.1 step.26
  138.1 26.3 %collective-permute-done.8.refs_1_ = f32[3,64,2048]{2,1,0:T(8,128)S(1)} collective-permute-done((f32[3,64,2048]{2,1,0:T(8,128)S(1)}, f32[3,64,2048]{2,1,0:T(8,128)S(1)}, u32[]{:S(2)}, u32[]{:S(2)}) %collective-permute-start.8) | collective-permute-done | bytes 1572896 | tf_op jit(solution)/shard_map/ppermute | solution.py:23
  166.6 3.1 step.27
  171.8 26.3 %collective-permute-done.14.refs_1_ = f32[3,64,2048]{2,1,0:T(8,128)S(1)} collective-permute-done((f32[3,64,2048]{2,1,0:T(8,128)S(1)}, f32[3,64,2048]{2,1,0:T(8,128)S(1)}, u32[]{:S(2)}, u32[]{:S(2)}) %collective-permute-start.14) | collective-permute-done | bytes 1572896 | tf_op jit(solution)/shard_map/ppermute | solution.py:23
  200.3 3.1 step.28
  205.5 26.3 %collective-permute-done.12.refs_1_ = f32[3,64,2048]{2,1,0:T(8,128)S(1)} collective-permute-done((f32[3,64,2048]{2,1,0:T(8,128)S(1)}, f32[3,64,2048]{2,1,0:T(8,128)S(1)}, u32[]{:S(2)}, u32[]{:S(2)}) %collective-permute-start.12) | collective-permute-done | bytes 1572896 | tf_op jit(solution)/shard_map/ppermute | solution.py:23
  234.0 3.1 step.29
  239.2 26.3 %collective-permute-done.18.refs_1_ = f32[3,64,2048]{2,1,0:T(8,128)S(1)} collective-permute-done((f32[3,64,2048]{2,1,0:T(8,128)S(1)}, f32[3,64,2048]{2,1,0:T(8,128)S(1)}, u32[]{:S(2)}, u32[]{:S(2)}) %collective-permute-start.18) | collective-permute-done | bytes 1572896 | tf_op jit(solution)/shard_map/ppermute | solution.py:23
  267.7 3.1 step.30
  272.9 26.3 %collective-permute-done.16.refs_1_ = f32[3,64,2048]{2,1,0:T(8,128)S(1)} collective-permute-done((f32[3,64,2048]{2,1,0:T(8,128)S(1)}, f32[3,64,2048]{2,1,0:T(8,128)S(1)}, u32[]{:S(2)}, u32[]{:S(2)}) %collective-permute-start.16) | collective-permute-done | bytes 1572896 | tf_op jit(solution)/shard_map/ppermute | solution.py:23
  301.4 3.1 step.31
  306.6 26.3 %collective-permute-done.22.refs_1_ = f32[3,64,2048]{2,1,0:T(8,128)S(1)} collective-permute-done((f32[3,64,2048]{2,1,0:T(8,128)S(1)}, f32[3,64,2048]{2,1,0:T(8,128)S(1)}, u32[]{:S(2)}, u32[]{:S(2)}) %collective-permute-start.22) | collective-permute-done | bytes 1572896 | tf_op jit(solution)/shard_map/ppermute | solution.py:23
  340.3 26.3 %collective-permute-done.20.refs_1_ = f32[3,64,2048]{2,1,0:T(8,128)S(1)} collective-permute-done((f32[3,64,2048]{2,1,0:T(8,128)S(1)}, f32[3,64,2048]{2,1,0:T(8,128)S(1)}, u32[]{:S(2)}, u32[]{:S(2)}) %collective-permute-start.20) | collective-permute-done | bytes 1572896 | tf_op jit(solution)/shard_map/ppermute | solution.py:23
  374.1 26.3 %collective-permute-done.26.refs_1_ = f32[3,64,2048]{2,1,0:T(8,128)S(1)} collective-permute-done((f32[3,64,2048]{2,1,0:T(8,128)S(1)}, f32[3,64,2048]{2,1,0:T(8,128)S(1)}, u32[]{:S(2)}, u32[]{:S(2)}) %collective-permute-start.26) | collective-permute-done | bytes 1572896 | tf_op jit(solution)/shard_map/ppermute | solution.py:23
  407.8 26.3 %collective-permute-done.24.refs_1_ = f32[3,64,2048]{2,1,0:T(8,128)S(1)} collective-permute-done((f32[3,64,2048]{2,1,0:T(8,128)S(1)}, f32[3,64,2048]{2,1,0:T(8,128)S(1)}, u32[]{:S(2)}, u32[]{:S(2)}) %collective-permute-start.24) | collective-permute-done | bytes 1572896 | tf_op jit(solution)/shard_map/ppermute | solution.py:23
  441.5 26.3 %collective-permute-done.30.refs_1_ = f32[3,64,2048]{2,1,0:T(8,128)S(1)} collective-permute-done((f32[3,64,2048]{2,1,0:T(8,128)S(1)}, f32[3,64,2048]{2,1,0:T(8,128)S(1)}, u32[]{:S(2)}, u32[]{:S(2)}) %collective-permute-start.30) | collective-permute-done | bytes 1572896 | tf_op jit(solution)/shard_map/ppermute | solution.py:23
  476.1 25.4 %collective-permute-done.28.refs_1_ = f32[3,64,2048]{2,1,0:T(8,128)S(1)} collective-permute-done((f32[3,64,2048]{2,1,0:T(8,128)S(1)}, f32[3,64,2048]{2,1,0:T(8,128)S(1)}, u32[]{:S(2)}, u32[]{:S(2)}) %collective-permute-start.28) | collective-permute-done | bytes 1572896 | tf_op jit(solution)/shard_map/ppermute | solution.py:23
  508.6 15.4 %collective-permute-done.34.refs_1_ = f32[2,64,2048]{2,1,0:T(8,128)S(1)} collective-permute-done((f32[2,64,2048]{2,1,0:T(8,128)S(1)}, f32[2,64,2048]{2,1,0:T(8,128)S(1)}, u32[]{:S(2)}, u32[]{:S(2)}) %collective-permute-start.34) | collective-permute-done | bytes 1048608 | tf_op jit(solution)/shard_map/ppermute | solution.py:23
  529.6 16.0 %collective-permute-done.32.refs_1_ = f32[2,64,2048]{2,1,0:T(8,128)S(1)} collective-permute-done((f32[2,64,2048]{2,1,0:T(8,128)S(1)}, f32[2,64,2048]{2,1,0:T(8,128)S(1)}, u32[]{:S(2)}, u32[]{:S(2)}) %collective-permute-start.32) | collective-permute-done | bytes 1048608 | tf_op jit(solution)/shard_map/ppermute | solution.py:23
  549.6 5.8 copy-done
  558.0 3.6 collective-permute-start.38
  566.4 7.5 %multiply_reduce_fusion = f32[2,2048]{1,0:T(2,128)S(1)} fusion(f32[2,8,2,64,2048]{4,3,2,1,0:T(8,128)} %copy-done, f32[2,8,2,64]{3,2,1,0:T(2,128)S(1)} %mul.77), kind=kLoop, calls=%fused_computation.3 | loop fusion | flops 12578816 | bytes 16801792 | tf_op jit(solution)/shard_map/reduce_sum | solution.py:193
  575.9 3.4 collective-permute-done.40
  589.7 22.4 %multiply_subtract_fusion = (f32[2,1024,2048]{2,1,0:T(8,128)}, f32[2,1024,2048]{2,1,0:T(8,128)}) fusion(f32[2,1024,2048]{2,1,0:T(8,128)} %param.5, f32[2,2048]{1,0:T(2,128)S(1)} %rsqrt.7, f32[2,1024]{1,0:T(2,128)S(1)} %rsqrt_multiply_fusion, f32[2,8,2,64,2048]{4,3,2,1,0:T(8,128)} %copy-done), kind=kLoop, calls=%fused_computation.2 | loop fusion | flops 16777216 | bytes 67133440 | tf_op jit(solution)/shard_map/sub | solution.py:205
  (127 shorter events, 134.6 us)
Async XLA Ops:
  23.1 40.2 %collective-permute-start.6 = (f32[3,64,2048]{2,1,0:T(8,128)S(1)}, f32[3,64,2048]{2,1,0:T(8,128)S(1)}, u32[]{:S(2)}, u32[]{:S(2)}) collective-permute-start(f32[3,64,2048]{2,1,0:T(8,128)S(1)} %get-tuple-element.101), channel_id=1, source_target_pairs={{0,8},{8,0},{16,24},{24,16},{1,9},{9,1},{17,25},{25,17},{2,10},{10... | collective-permute-start | bytes 4718600 | tf_op jit(solution)/shard_map/ppermute | solution.py:23
  23.2 42.2 %collective-permute-start.7 = (f32[3,64,2048]{2,1,0:T(8,128)S(1)}, f32[3,64,2048]{2,1,0:T(8,128)S(1)}, u32[]{:S(2)}, u32[]{:S(2)}) collective-permute-start(f32[3,64,2048]{2,1,0:T(8,128)S(1)} %get-tuple-element.102), channel_id=1, source_target_pairs={{0,16},{8,24},{16,0},{24,8},{1,17},{9,25},{17,1},{25,9},{2,18},{10... | collective-permute-start | bytes 4718600 | tf_op jit(solution)/shard_map/ppermute | solution.py:23
  35.5 61.7 %collective-permute-start.4 = (f32[3,64,2048]{2,1,0:T(8,128)S(1)}, f32[3,64,2048]{2,1,0:T(8,128)}, u32[]{:S(2)}, u32[]{:S(2)}) collective-permute-start(f32[3,64,2048]{2,1,0:T(8,128)S(1)} %get-tuple-element.99), channel_id=1, source_target_pairs={{0,8},{8,0},{16,24},{24,16},{1,9},{9,1},{17,25},{25,17},{2,10},{10... | collective-permute-start | bytes 4718600 | tf_op jit(solution)/shard_map/ppermute | solution.py:23
  35.5 63.7 %collective-permute-start.5 = (f32[3,64,2048]{2,1,0:T(8,128)}, f32[3,64,2048]{2,1,0:T(8,128)}, u32[]{:S(2)}, u32[]{:S(2)}) collective-permute-start(f32[3,64,2048]{2,1,0:T(8,128)} %get-tuple-element.100), channel_id=1, source_target_pairs={{0,16},{8,24},{16,0},{24,8},{1,17},{9,25},{17,1},{25,9},{2,18},{10... | collective-permute-start | bytes 4718600 | tf_op jit(solution)/shard_map/ppermute | solution.py:23
  74.8 55.9 %collective-permute-start.10 = (f32[3,64,2048]{2,1,0:T(8,128)S(1)}, f32[3,64,2048]{2,1,0:T(8,128)S(1)}, u32[]{:S(2)}, u32[]{:S(2)}) collective-permute-start(f32[3,64,2048]{2,1,0:T(8,128)S(1)} %get-tuple-element.109), channel_id=1, source_target_pairs={{0,8},{8,0},{16,24},{24,16},{1,9},{9,1},{17,25},{25,17},{2,10},{10... | collective-permute-start | bytes 4718600 | tf_op jit(solution)/shard_map/ppermute | solution.py:23
  76.0 56.9 %collective-permute-start.11 = (f32[3,64,2048]{2,1,0:T(8,128)S(1)}, f32[3,64,2048]{2,1,0:T(8,128)S(1)}, u32[]{:S(2)}, u32[]{:S(2)}) collective-permute-start(f32[3,64,2048]{2,1,0:T(8,128)S(1)} %get-tuple-element.110), channel_id=1, source_target_pairs={{0,16},{8,24},{16,0},{24,8},{1,17},{9,25},{17,1},{25,9},{2,18},{10... | collective-permute-start | bytes 4718600 | tf_op jit(solution)/shard_map/ppermute | solution.py:23
  102.8 61.7 %collective-permute-start.8 = (f32[3,64,2048]{2,1,0:T(8,128)S(1)}, f32[3,64,2048]{2,1,0:T(8,128)S(1)}, u32[]{:S(2)}, u32[]{:S(2)}) collective-permute-start(f32[3,64,2048]{2,1,0:T(8,128)S(1)} %get-tuple-element.107), channel_id=1, source_target_pairs={{0,8},{8,0},{16,24},{24,16},{1,9},{9,1},{17,25},{25,17},{2,10},{10... | collective-permute-start | bytes 4718600 | tf_op jit(solution)/shard_map/ppermute | solution.py:23
  102.9 63.7 %collective-permute-start.9 = (f32[3,64,2048]{2,1,0:T(8,128)S(1)}, f32[3,64,2048]{2,1,0:T(8,128)S(1)}, u32[]{:S(2)}, u32[]{:S(2)}) collective-permute-start(f32[3,64,2048]{2,1,0:T(8,128)S(1)} %get-tuple-element.108), channel_id=1, source_target_pairs={{0,16},{8,24},{16,0},{24,8},{1,17},{9,25},{17,1},{25,9},{2,18},{10... | collective-permute-start | bytes 4718600 | tf_op jit(solution)/shard_map/ppermute | solution.py:23
  136.0 62.2 %collective-permute-start.14 = (f32[3,64,2048]{2,1,0:T(8,128)S(1)}, f32[3,64,2048]{2,1,0:T(8,128)S(1)}, u32[]{:S(2)}, u32[]{:S(2)}) collective-permute-start(f32[3,64,2048]{2,1,0:T(8,128)S(1)} %get-tuple-element.119), channel_id=1, source_target_pairs={{0,8},{8,0},{16,24},{24,16},{1,9},{9,1},{17,25},{25,17},{2,10},{10... | collective-permute-start | bytes 4718600 | tf_op jit(solution)/shard_map/ppermute | solution.py:23
  136.1 64.2 %collective-permute-start.15 = (f32[3,64,2048]{2,1,0:T(8,128)S(1)}, f32[3,64,2048]{2,1,0:T(8,128)S(1)}, u32[]{:S(2)}, u32[]{:S(2)}) collective-permute-start(f32[3,64,2048]{2,1,0:T(8,128)S(1)} %get-tuple-element.120), channel_id=1, source_target_pairs={{0,16},{8,24},{16,0},{24,8},{1,17},{9,25},{17,1},{25,9},{2,18},{10... | collective-permute-start | bytes 4718600 | tf_op jit(solution)/shard_map/ppermute | solution.py:23
  169.7 62.2 %collective-permute-start.12 = (f32[3,64,2048]{2,1,0:T(8,128)S(1)}, f32[3,64,2048]{2,1,0:T(8,128)S(1)}, u32[]{:S(2)}, u32[]{:S(2)}) collective-permute-start(f32[3,64,2048]{2,1,0:T(8,128)S(1)} %get-tuple-element.117), channel_id=1, source_target_pairs={{0,8},{8,0},{16,24},{24,16},{1,9},{9,1},{17,25},{25,17},{2,10},{10... | collective-permute-start | bytes 4718600 | tf_op jit(solution)/shard_map/ppermute | solution.py:23
  169.8 64.2 %collective-permute-start.13 = (f32[3,64,2048]{2,1,0:T(8,128)S(1)}, f32[3,64,2048]{2,1,0:T(8,128)S(1)}, u32[]{:S(2)}, u32[]{:S(2)}) collective-permute-start(f32[3,64,2048]{2,1,0:T(8,128)S(1)} %get-tuple-element.118), channel_id=1, source_target_pairs={{0,16},{8,24},{16,0},{24,8},{1,17},{9,25},{17,1},{25,9},{2,18},{10... | collective-permute-start | bytes 4718600 | tf_op jit(solution)/shard_map/ppermute | solution.py:23
  203.4 62.2 %collective-permute-start.18 = (f32[3,64,2048]{2,1,0:T(8,128)S(1)}, f32[3,64,2048]{2,1,0:T(8,128)S(1)}, u32[]{:S(2)}, u32[]{:S(2)}) collective-permute-start(f32[3,64,2048]{2,1,0:T(8,128)S(1)} %get-tuple-element.129), channel_id=1, source_target_pairs={{0,8},{8,0},{16,24},{24,16},{1,9},{9,1},{17,25},{25,17},{2,10},{10... | collective-permute-start | bytes 4718600 | tf_op jit(solution)/shard_map/ppermute | solution.py:23
  203.5 64.2 %collective-permute-start.19 = (f32[3,64,2048]{2,1,0:T(8,128)S(1)}, f32[3,64,2048]{2,1,0:T(8,128)S(1)}, u32[]{:S(2)}, u32[]{:S(2)}) collective-permute-start(f32[3,64,2048]{2,1,0:T(8,128)S(1)} %get-tuple-element.130), channel_id=1, source_target_pairs={{0,16},{8,24},{16,0},{24,8},{1,17},{9,25},{17,1},{25,9},{2,18},{10... | collective-permute-start | bytes 4718600 | tf_op jit(solution)/shard_map/ppermute | solution.py:23
  237.1 62.2 %collective-permute-start.16 = (f32[3,64,2048]{2,1,0:T(8,128)S(1)}, f32[3,64,2048]{2,1,0:T(8,128)S(1)}, u32[]{:S(2)}, u32[]{:S(2)}) collective-permute-start(f32[3,64,2048]{2,1,0:T(8,128)S(1)} %get-tuple-element.127), channel_id=1, source_target_pairs={{0,8},{8,0},{16,24},{24,16},{1,9},{9,1},{17,25},{25,17},{2,10},{10... | collective-permute-start | bytes 4718600 | tf_op jit(solution)/shard_map/ppermute | solution.py:23
  237.2 64.2 %collective-permute-start.17 = (f32[3,64,2048]{2,1,0:T(8,128)S(1)}, f32[3,64,2048]{2,1,0:T(8,128)S(1)}, u32[]{:S(2)}, u32[]{:S(2)}) collective-permute-start(f32[3,64,2048]{2,1,0:T(8,128)S(1)} %get-tuple-element.128), channel_id=1, source_target_pairs={{0,16},{8,24},{16,0},{24,8},{1,17},{9,25},{17,1},{25,9},{2,18},{10... | collective-permute-start | bytes 4718600 | tf_op jit(solution)/shard_map/ppermute | solution.py:23
  270.8 62.2 %collective-permute-start.22 = (f32[3,64,2048]{2,1,0:T(8,128)S(1)}, f32[3,64,2048]{2,1,0:T(8,128)S(1)}, u32[]{:S(2)}, u32[]{:S(2)}) collective-permute-start(f32[3,64,2048]{2,1,0:T(8,128)S(1)} %get-tuple-element.139), channel_id=1, source_target_pairs={{0,8},{8,0},{16,24},{24,16},{1,9},{9,1},{17,25},{25,17},{2,10},{10... | collective-permute-start | bytes 4718600 | tf_op jit(solution)/shard_map/ppermute | solution.py:23
  270.9 64.2 %collective-permute-start.23 = (f32[3,64,2048]{2,1,0:T(8,128)S(1)}, f32[3,64,2048]{2,1,0:T(8,128)S(1)}, u32[]{:S(2)}, u32[]{:S(2)}) collective-permute-start(f32[3,64,2048]{2,1,0:T(8,128)S(1)} %get-tuple-element.140), channel_id=1, source_target_pairs={{0,16},{8,24},{16,0},{24,8},{1,17},{9,25},{17,1},{25,9},{2,18},{10... | collective-permute-start | bytes 4718600 | tf_op jit(solution)/shard_map/ppermute | solution.py:23
  304.5 62.2 %collective-permute-start.20 = (f32[3,64,2048]{2,1,0:T(8,128)S(1)}, f32[3,64,2048]{2,1,0:T(8,128)S(1)}, u32[]{:S(2)}, u32[]{:S(2)}) collective-permute-start(f32[3,64,2048]{2,1,0:T(8,128)S(1)} %get-tuple-element.137), channel_id=1, source_target_pairs={{0,8},{8,0},{16,24},{24,16},{1,9},{9,1},{17,25},{25,17},{2,10},{10... | collective-permute-start | bytes 4718600 | tf_op jit(solution)/shard_map/ppermute | solution.py:23
  304.6 64.2 %collective-permute-start.21 = (f32[3,64,2048]{2,1,0:T(8,128)S(1)}, f32[3,64,2048]{2,1,0:T(8,128)S(1)}, u32[]{:S(2)}, u32[]{:S(2)}) collective-permute-start(f32[3,64,2048]{2,1,0:T(8,128)S(1)} %get-tuple-element.138), channel_id=1, source_target_pairs={{0,16},{8,24},{16,0},{24,8},{1,17},{9,25},{17,1},{25,9},{2,18},{10... | collective-permute-start | bytes 4718600 | tf_op jit(solution)/shard_map/ppermute | solution.py:23
  338.2 62.2 %collective-permute-start.26 = (f32[3,64,2048]{2,1,0:T(8,128)S(1)}, f32[3,64,2048]{2,1,0:T(8,128)S(1)}, u32[]{:S(2)}, u32[]{:S(2)}) collective-permute-start(f32[3,64,2048]{2,1,0:T(8,128)S(1)} %get-tuple-element.149), channel_id=1, source_target_pairs={{0,8},{8,0},{16,24},{24,16},{1,9},{9,1},{17,25},{25,17},{2,10},{10... | collective-permute-start | bytes 4718600 | tf_op jit(solution)/shard_map/ppermute | solution.py:23
  338.3 64.2 %collective-permute-start.27 = (f32[3,64,2048]{2,1,0:T(8,128)S(1)}, f32[3,64,2048]{2,1,0:T(8,128)S(1)}, u32[]{:S(2)}, u32[]{:S(2)}) collective-permute-start(f32[3,64,2048]{2,1,0:T(8,128)S(1)} %get-tuple-element.150), channel_id=1, source_target_pairs={{0,16},{8,24},{16,0},{24,8},{1,17},{9,25},{17,1},{25,9},{2,18},{10... | collective-permute-start | bytes 4718600 | tf_op jit(solution)/shard_map/ppermute | solution.py:23
  371.9 62.2 %collective-permute-start.24 = (f32[3,64,2048]{2,1,0:T(8,128)S(1)}, f32[3,64,2048]{2,1,0:T(8,128)S(1)}, u32[]{:S(2)}, u32[]{:S(2)}) collective-permute-start(f32[3,64,2048]{2,1,0:T(8,128)S(1)} %get-tuple-element.147), channel_id=1, source_target_pairs={{0,8},{8,0},{16,24},{24,16},{1,9},{9,1},{17,25},{25,17},{2,10},{10... | collective-permute-start | bytes 4718600 | tf_op jit(solution)/shard_map/ppermute | solution.py:23
  372.0 64.2 %collective-permute-start.25 = (f32[3,64,2048]{2,1,0:T(8,128)S(1)}, f32[3,64,2048]{2,1,0:T(8,128)S(1)}, u32[]{:S(2)}, u32[]{:S(2)}) collective-permute-start(f32[3,64,2048]{2,1,0:T(8,128)S(1)} %get-tuple-element.148), channel_id=1, source_target_pairs={{0,16},{8,24},{16,0},{24,8},{1,17},{9,25},{17,1},{25,9},{2,18},{10... | collective-permute-start | bytes 4718600 | tf_op jit(solution)/shard_map/ppermute | solution.py:23
  405.6 62.2 %collective-permute-start.30 = (f32[3,64,2048]{2,1,0:T(8,128)S(1)}, f32[3,64,2048]{2,1,0:T(8,128)S(1)}, u32[]{:S(2)}, u32[]{:S(2)}) collective-permute-start(f32[3,64,2048]{2,1,0:T(8,128)S(1)} %get-tuple-element.159), channel_id=1, source_target_pairs={{0,8},{8,0},{16,24},{24,16},{1,9},{9,1},{17,25},{25,17},{2,10},{10... | collective-permute-start | bytes 4718600 | tf_op jit(solution)/shard_map/ppermute | solution.py:23
  405.7 64.2 %collective-permute-start.31 = (f32[3,64,2048]{2,1,0:T(8,128)S(1)}, f32[3,64,2048]{2,1,0:T(8,128)S(1)}, u32[]{:S(2)}, u32[]{:S(2)}) collective-permute-start(f32[3,64,2048]{2,1,0:T(8,128)S(1)} %get-tuple-element.160), channel_id=1, source_target_pairs={{0,16},{8,24},{16,0},{24,8},{1,17},{9,25},{17,1},{25,9},{2,18},{10... | collective-permute-start | bytes 4718600 | tf_op jit(solution)/shard_map/ppermute | solution.py:23
  439.4 62.2 %collective-permute-start.28 = (f32[3,64,2048]{2,1,0:T(8,128)S(1)}, f32[3,64,2048]{2,1,0:T(8,128)S(1)}, u32[]{:S(2)}, u32[]{:S(2)}) collective-permute-start(f32[3,64,2048]{2,1,0:T(8,128)S(1)} %get-tuple-element.157), channel_id=1, source_target_pairs={{0,8},{8,0},{16,24},{24,16},{1,9},{9,1},{17,25},{25,17},{2,10},{10... | collective-permute-start | bytes 4718600 | tf_op jit(solution)/shard_map/ppermute | solution.py:23
  439.5 64.2 %collective-permute-start.29 = (f32[3,64,2048]{2,1,0:T(8,128)S(1)}, f32[3,64,2048]{2,1,0:T(8,128)S(1)}, u32[]{:S(2)}, u32[]{:S(2)}) collective-permute-start(f32[3,64,2048]{2,1,0:T(8,128)S(1)} %get-tuple-element.158), channel_id=1, source_target_pairs={{0,16},{8,24},{16,0},{24,8},{1,17},{9,25},{17,1},{25,9},{2,18},{10... | collective-permute-start | bytes 4718600 | tf_op jit(solution)/shard_map/ppermute | solution.py:23
  474.0 50.0 %collective-permute-start.34 = (f32[2,64,2048]{2,1,0:T(8,128)S(1)}, f32[2,64,2048]{2,1,0:T(8,128)S(1)}, u32[]{:S(2)}, u32[]{:S(2)}) collective-permute-start(f32[2,64,2048]{2,1,0:T(8,128)S(1)} %get-tuple-element.169), channel_id=1, source_target_pairs={{0,8},{8,0},{16,24},{24,16},{1,9},{9,1},{17,25},{25,17},{2,10},{10... | collective-permute-start | bytes 3145736 | tf_op jit(solution)/shard_map/ppermute | solution.py:23
  474.1 52.0 %collective-permute-start.35 = (f32[2,64,2048]{2,1,0:T(8,128)S(1)}, f32[2,64,2048]{2,1,0:T(8,128)S(1)}, u32[]{:S(2)}, u32[]{:S(2)}) collective-permute-start(f32[2,64,2048]{2,1,0:T(8,128)S(1)} %get-tuple-element.170), channel_id=1, source_target_pairs={{0,16},{8,24},{16,0},{24,8},{1,17},{9,25},{17,1},{25,9},{2,18},{10... | collective-permute-start | bytes 3145736 | tf_op jit(solution)/shard_map/ppermute | solution.py:23
  506.5 39.2 %collective-permute-start.32 = (f32[2,64,2048]{2,1,0:T(8,128)S(1)}, f32[2,64,2048]{2,1,0:T(8,128)S(1)}, u32[]{:S(2)}, u32[]{:S(2)}) collective-permute-start(f32[2,64,2048]{2,1,0:T(8,128)S(1)} %get-tuple-element.167), channel_id=1, source_target_pairs={{0,8},{8,0},{16,24},{24,16},{1,9},{9,1},{17,25},{25,17},{2,10},{10... | collective-permute-start | bytes 3145736 | tf_op jit(solution)/shard_map/ppermute | solution.py:23
  506.6 40.5 %collective-permute-start.33 = (f32[2,64,2048]{2,1,0:T(8,128)S(1)}, f32[2,64,2048]{2,1,0:T(8,128)S(1)}, u32[]{:S(2)}, u32[]{:S(2)}) collective-permute-start(f32[2,64,2048]{2,1,0:T(8,128)S(1)} %get-tuple-element.168), channel_id=1, source_target_pairs={{0,16},{8,24},{16,0},{24,8},{1,17},{9,25},{17,1},{25,9},{2,18},{10... | collective-permute-start | bytes 3145736 | tf_op jit(solution)/shard_map/ppermute | solution.py:23
  (27 other events, 263.2 us)

commit v3 on v2

v3 whole, which is shorter than its diff:
```python
import functools

import jax
import jax.numpy as jnp
from jax import lax
from jax.experimental import pallas as pl
from jax.experimental.pallas import tpu as pltpu
from jax.sharding import PartitionSpec as P

decay_rate = 1.0 - 2.0 ** (-0.8)
tiny_eps = 1e-30
clip_limit = 1.0
learn_rate = 0.01

lanes = 128
sublanes = 8
blocks_of_matrix = 4
tile_rows = 16
finish_rows = 64
f32 = jnp.float32


def swap(x, axes, mask):
    size = lax.axis_size(axes)
    return lax.ppermute(x, axes, [(i, i ^ mask) for i in range(size)])


def exchange_sum(x, axes):
    size = lax.axis_size(axes)
    got = [x] + [swap(x, axes, mask) for mask in range(1, size)]
    while len(got) > 1:
        got = [got[i] + got[i + 1] for i in range(0, len(got), 2)]
    return got[0]


def pairwise_sum(x, axes):
    mask = 1
    while mask < lax.axis_size(axes):
        x = x + swap(x, axes, mask)
        mask *= 2
    return x


def tie(*xs):
    return lax.optimization_barrier(xs)


def params_of(mib):
    return pltpu.CompilerParams(vmem_limit_bytes=mib * 1024 * 1024)


def step_kernel(takes, finishes, first, sends, starts, *refs):
    refs = list(refs[1:])
    take = lambda yes: refs.pop(0) if yes else None
    got = [take(takes or finishes) for _ in range(2)]
    mine = take(finishes)
    direct = [take(sends) for _ in range(2)]
    relay = [take(sends) for _ in range(2)]
    onward = take(starts)
    again = finishes and not first
    cols_in, _, _ = take(again), take(again), take(again)
    out = [take(sends or starts) for _ in range(2)]
    cols_out, summed_out, rows_out = take(finishes), take(finishes), take(finishes)
    row_parts = take(finishes)
    tail_slot = 2 if finishes else 0
    out_slot = 2 if sends else 0
    t = pl.program_id(0)

    if finishes:

        @pl.when(t == 0)
        def _():
            cols_out[...] = jnp.zeros_like(cols_out) if first else cols_in[...]

    for half in range(2):
        if starts:
            out[half][out_slot] = onward[half].astype(f32)
        if sends:
            out[half][0] = direct[half][...].astype(f32)
            out[1 - half][1] = got[half][tail_slot] + relay[half][...].astype(f32)
        if finishes:
            total = mine[half].astype(f32) + got[half][0] + got[1 - half][1]
            summed_out[half] = total
            squares = total * total
            tile, width = squares.shape
            part = row_parts.shape[0] // 2
            row_parts[pl.ds(pl.multiple_of(half * part + t * tile, sublanes), tile)] = sum(
                squares[:, i : i + lanes] for i in range(0, width, lanes)
            )
            cols_out[...] += sum(squares[i : i + sublanes] for i in range(0, tile, sublanes))

    if finishes:

        @pl.when(t == pl.num_programs(0) - 1)
        def _():
            rows_out[...] = lax.dot_general(
                jnp.ones((sublanes, lanes), f32),
                row_parts[...],
                (((1,), (1,)), ((), ())),
                precision=lax.Precision.HIGHEST,
                preferred_element_type=f32,
            )


def step(j, total_blocks, me, partials, got, sums):
    mats, _, count, _, part, width = partials.shape
    tile = min(tile_rows, part)
    finishes = j >= 2
    takes = 0 <= j < total_blocks
    sends = takes
    starts = j + 2 < total_blocks
    b = (j - 2) % count
    first = finishes and b == 0

    def piece_spec(block, mask, half):
        m, b = divmod(block, count)
        if half is None:
            return pl.BlockSpec(
                (None, None, None, 2, tile, width),
                lambda t, at: (m, at[0] ^ mask, b, 0, t, 0),
            )
        return pl.BlockSpec(
            (None, None, None, None, tile, width),
            lambda t, at: (m, at[0] ^ mask, b, half, t, 0),
        )

    def message_spec(slots):
        return pl.BlockSpec((slots, tile, width), lambda t, at: (0, t, 0))

    operands, in_specs = [], []

    def add(x, spec):
        operands.append(x)
        in_specs.append(spec)

    if j >= 0:
        for x in got:
            add(x, message_spec(x.shape[0]))
    if finishes:
        add(partials, piece_spec(j - 2, 0, None))
    if sends:
        for half, mask in ((0, 1), (1, 2)):
            add(partials, piece_spec(j, mask, half))
        for half, mask in ((0, 2), (1, 1)):
            add(partials, piece_spec(j, mask, half))
    if starts:
        add(partials, piece_spec(j + 2, 3, None))

    slots = (2 if sends else 0) + (1 if starts else 0)
    out_shape, out_specs, scratch, aliases = [], [], [], {}
    if slots:
        for _ in range(2):
            out_shape.append(jax.ShapeDtypeStruct((slots, part, width), f32))
            out_specs.append(message_spec(slots))
    if finishes:
        cols_spec = pl.BlockSpec((sublanes, width), lambda t, at: (0, 0))
        if not first:
            add(sums[0], cols_spec)
            for i in (1, 2):
                aliases[1 + len(operands)] = len(out_shape) + i
                add(sums[i], pl.BlockSpec(memory_space=pl.ANY))
        out_shape.append(jax.ShapeDtypeStruct((sublanes, width), f32))
        out_specs.append(cols_spec)
        out_shape.append(jax.ShapeDtypeStruct((count, 2, part, width), f32))
        out_specs.append(pl.BlockSpec((None, 2, tile, width), lambda t, at: (b, 0, t, 0)))
        out_shape.append(jax.ShapeDtypeStruct((count, sublanes, 2 * part), f32))
        out_specs.append(pl.BlockSpec((None, sublanes, 2 * part), lambda t, at: (b, 0, 0)))
        scratch.append(pltpu.VMEM((2 * part, lanes), f32))
    moved = part * width * (4 * (2 * slots + 8) + 2 * 8)
    result = pl.pallas_call(
        functools.partial(step_kernel, takes, finishes, first, sends, starts),
        out_shape=out_shape,
        grid_spec=pltpu.PrefetchScalarGridSpec(
            num_scalar_prefetch=1,
            grid=(part // tile,),
            in_specs=in_specs,
            out_specs=out_specs,
            scratch_shapes=scratch,
        ),
        input_output_aliases=aliases,
        compiler_params=params_of(24),
        cost_estimate=pl.CostEstimate(
            flops=part * width * 20, bytes_accessed=moved, transcendentals=0
        ),
        name="step",
    )(me, *operands)
    sent = result[:2] if slots else None
    return sent, tuple(result[2:] if slots else result) if finishes else None


def weighted_kernel(extent, totals, factor, cols, summed, rows_out, stats, weighted, level):
    i = pl.program_id(0)

    @pl.when(i == 0)
    def _():
        weighted[...] = jnp.zeros_like(weighted)
        level[...] = jnp.zeros_like(level)

    row_new = decay_rate * factor[...] + (1.0 - decay_rate) * (totals[...] / extent + tiny_eps)
    rows_out[...] = row_new
    level[...] += row_new
    inverse = jnp.transpose(1.0 / row_new)[:, 0:1]
    part = summed.shape[1]
    for half in range(2):
        for r in range(0, part, sublanes):
            x = summed[half, r : r + sublanes]
            at = half * part + r
            weighted[...] += x * x * inverse[at : at + sublanes]

    @pl.when(i == pl.num_programs(0) - 1)
    def _():
        stats[...] = jnp.zeros_like(stats)
        stats[0:1] = jnp.sum(cols[...], axis=0, keepdims=True)
        stats[1:2] = jnp.sum(weighted[...], axis=0, keepdims=True)
        total = jnp.sum(level[0:1], axis=1, keepdims=True)
        stats[2:3] = jnp.broadcast_to(total, (1, stats.shape[1]))


def weighted_sums(extent, totals, factor, cols, summed):
    count, _, part, width = summed.shape
    along = pl.BlockSpec((None, sublanes, 2 * part), lambda i: (i, 0, 0))
    whole = pl.BlockSpec((sublanes, width), lambda i: (0, 0))
    return pl.pallas_call(
        functools.partial(weighted_kernel, extent),
        grid=(count,),
        in_specs=[
            along,
            pl.BlockSpec((None, 1, 2 * part), lambda i: (i, 0, 0)),
            whole,
            pl.BlockSpec((None, 2, part, width), lambda i: (i, 0, 0, 0)),
        ],
        out_specs=[along, whole],
        out_shape=[
            jax.ShapeDtypeStruct(totals.shape, f32),
            jax.ShapeDtypeStruct((sublanes, width), f32),
        ],
        scratch_shapes=[pltpu.VMEM((sublanes, width), f32), pltpu.VMEM((sublanes, 2 * part), f32)],
        compiler_params=params_of(16),
        cost_estimate=pl.CostEstimate(
            flops=3 * summed.size, bytes_accessed=4 * summed.size, transcendentals=0
        ),
        name="weighted",
    )(totals, factor.reshape(count, 1, 2 * part), cols, summed)


def finish_kernel(m, tile, by_row, by_col, summed, params, *refs):
    new_params, update, column = refs[-3:]
    count, _, part, width = summed.shape
    for i in range(count):
        column[i] = jnp.transpose(by_row[i])

    def body(x, p, new_p, moved):
        i, half, t = (pl.program_id(axis) for axis in range(3))
        start = pl.multiple_of(half * part + t * tile, sublanes)
        y = x[...] * column[i, pl.ds(start, tile)][:, 0:1] * by_col[...]
        moved[...] = y
        new_p[...] = p[...] - learn_rate * y

    of_sum = pl.BlockSpec((None, None, tile, width), lambda i, h, t: (i, h, t, 0))
    of_matrix = pl.BlockSpec((None, None, None, tile, width), lambda i, h, t: (m, i, h, t, 0))
    pltpu.emit_pipeline(
        body,
        grid=(count, 2, part // tile),
        in_specs=[of_sum, of_matrix],
        out_specs=[of_matrix] * 2,
    )(summed, params, new_params, update)


def finish(m, by_row, by_col, summed, params, outs):
    count, _, part, width = summed.shape
    held = () if outs is None else outs
    in_hbm = pl.BlockSpec(memory_space=pltpu.HBM)
    return pl.pallas_call(
        functools.partial(finish_kernel, m, min(part, finish_rows)),
        in_specs=[
            pl.BlockSpec(memory_space=pltpu.VMEM),
            pl.BlockSpec(memory_space=pltpu.VMEM),
            pl.BlockSpec(memory_space=pl.ANY),
            in_hbm,
        ]
        + [in_hbm] * len(held),
        out_specs=[in_hbm] * 2,
        out_shape=[jax.ShapeDtypeStruct(params.shape, f32)] * 2,
        scratch_shapes=[pltpu.VMEM((count, 2 * part, sublanes), f32)],
        input_output_aliases={4 + i: i for i in range(len(held))},
        compiler_params=params_of(44),
        cost_estimate=pl.CostEstimate(
            flops=4 * summed.size, bytes_accessed=16 * summed.size, transcendentals=0
        ),
        name="finish",
    )(by_row, by_col, summed, params, *held)


def per_device(partials, params, row_factor, col_factor):
    mats, rows, block_cols = params.shape
    extent = block_cols * lax.axis_size("col")
    me = lax.axis_index("dp").astype(jnp.int32).reshape(1)
    count = blocks_of_matrix
    part = rows // (2 * count)
    total_blocks = mats * count
    pieces = partials.reshape(mats, partials.shape[2], count, 2, part, block_cols)
    blocked = params.reshape(mats, count, 2, part, block_cols)

    new_rows, new_columns = [], []

    def row_stage(m, sums):
        cols, summed, rows_along = sums
        totals = exchange_sum(rows_along, "col")
        row_new, stats = weighted_sums(extent, totals, row_factor[m], cols, summed)
        new_rows.append(row_new[:, 0].reshape(rows))
        return row_new, stats

    def col_stage(m, stats):
        col_new = decay_rate * col_factor[m : m + 1] + (1.0 - decay_rate) * (
            stats[0:1] / extent + tiny_eps
        )
        new_columns.append(col_new)
        return col_new, stats[2, 0] / extent, jnp.sum(stats[1:2] / col_new)

    def last_stage(row_new, col_new, row_level, total):
        spread = jnp.sqrt(total * row_level / (extent * extent))
        factor = jnp.sqrt(row_level) / jnp.maximum(1.0, spread / clip_limit)
        return lax.rsqrt(row_new) * factor, lax.rsqrt(col_new)

    flying = {}
    sums = None
    row_news, stats, summeds = [], [], []
    for j in range(-2, total_blocks + 2):
        m, b = divmod(j - 2, count)
        got = flying.pop(j, None)
        sent, sums = step(j, total_blocks, me, pieces, got, sums)
        if sums:
            me, *sums = tie(me, *sums)
        else:
            me, *sent = tie(me, *sent)
        if sent is not None:
            flying[j + 2] = [swap(sent[0], "dp", 1), swap(sent[1], "dp", 2)]
        if 0 <= m < mats - 1 and b == count - 1:
            row_new, own = row_stage(m, sums)
            me, own = tie(me, pairwise_sum(own, "row"))
            row_news.append(row_new)
            stats.append(own)
            summeds.append(sums[1])
        if j == total_blocks:
            earlier = [exchange_sum(own, "dp") for own in tie(*stats, me)[:-1]]

    ready = []
    for m, own in enumerate(earlier):
        own, *sums = tie(own, *sums)
        col_new, row_level, total = col_stage(m, own)
        ready.append((row_news[m], col_new, row_level, exchange_sum(total, "col")))
    row_new, own = row_stage(mats - 1, sums)
    own = pairwise_sum(own, "row")
    outs = None
    for m, values in enumerate(ready):
        own, *values = tie(own, *values)
        outs = finish(m, *last_stage(*values), summeds[m], blocked, outs)
    own = exchange_sum(own, "dp")
    col_new, row_level, total = col_stage(mats - 1, own)
    if outs is not None:
        total, *outs = tie(total, *outs)
    by_row, by_col = last_stage(row_new, col_new, row_level, exchange_sum(total, "col"))
    new_params, update = finish(mats - 1, by_row, by_col, sums[1], blocked, outs)
    return (
        new_params.reshape(params.shape),
        update.reshape(params.shape),
        jnp.stack(new_rows),
        jnp.concatenate(new_columns, axis=0),
    )


def solution(mesh):
    placed = (
        P("dp", None, None, "row", None, "col"),
        P(None, ("dp", "row"), "col"),
        P(None, ("dp", "row")),
        P(None, "col"),
    )
    return jax.shard_map(
        per_device,
        mesh=mesh,
        in_specs=placed,
        out_specs=(
            P(None, ("dp", "row"), "col"),
            P(None, ("dp", "row"), "col"),
            P(None, ("dp", "row")),
            P(None, "col"),
        ),
        check_vma=False,
    )
```

time: 613 us -> 636 us (1.038)
  Pallas kernels: 58.7 us -> 101 us
  other arithmetic: 32.1 us -> 2.68 us
  waiting for transfers between devices: 453 us -> 461 us
  between operations: 0.97 us -> 7.76 us
    pallas_call x20 -> x16, Pallas kernels: 58.7 us -> 101 us  [the longest x12 68.9 us: step(): pl.pallas_call(functools.partial(step_kernel, takes, finishes, first, sen...]
    sub x1 -> x0, other arithmetic: 22.4 us -> none  [per_device(): return (params - learn_rate * update, update, row_new, col_new)]
    ppermute x45 -> x40, waiting for transfers between devices: 453 us -> 461 us  [swap(): return lax.ppermute(x, axes, [(i, i ^ mask) for i in range(size)])]
    reduce_sum x5 -> x2, other arithmetic: 9.4 us -> 1.32 us  [col_stage(): return (col_new, stats[2, 0] / extent, jnp.sum(stats[1:2] / col_new))]
    ppermute x45 -> x40, starting transfers between devices: 50.7 us -> 47.1 us  [swap(): return lax.ppermute(x, axes, [(i, i ^ mask) for i in range(size)])]
    unnamed x28 -> x14, local copies, waits for them, and re-layouts: 14.4 us -> 13.4 us
  transfers between devices with their start and end apart: 45 -> 40, of which waited for: 43 -> 28; matrix products, arithmetic and copies ran while one was open for 0% -> 0% of each run, Pallas kernels for 9% -> 13%
where the time goes in v3:
time: 636 us; the launch traced here: 634 us
  waiting for transfers between devices  461 us (72%)
  Pallas kernels  101 us (16%)
  starting transfers between devices  47.1 us (7%)
  local copies, waits for them, and re-layouts  14.5 us (2%)
  between operations  7.76 us (1%)
    ppermute x40, waiting for transfers between devices, swap(): return lax.ppermute(x, axes, [(i, i ^ mask) for i in range(size)])  461 us
    pallas_call x12, Pallas kernels, step(): pl.pallas_call(functools.partial(step_kernel, takes, finishes, first, sen...  68.9 us
    ppermute x40, starting transfers between devices, swap(): return lax.ppermute(x, axes, [(i, i ^ mask) for i in range(size)])  47.1 us
    pallas_call x2, Pallas kernels, finish(): pl.pallas_call(functools.partial(finish_kernel, m, min(part, finish_rows)...  28.7 us
    unnamed x14, local copies, waits for them, and re-layouts  13.4 us
  transfers between devices with their start and end apart: 40, of which 28 were waited for; matrix products, arithmetic and copies ran while one was open for 0% of the time, Pallas kernels for 13%

profile of v3, /device:TPU:0, one launch (start us, length us, event | category | flops | bytes accessed | tf_op | source)
XLA Modules:
  0.0 634.0 jit_solution(7804893365578931107)
XLA Ops:
  0.6 3.9 step.12
  9.0 3.9 step.13
  13.6 17.9 %collective-permute-done.refs_1_ = f32[1,128,2048]{2,1,0:T(8,128)S(1)} collective-permute-done((f32[1,128,2048]{2,1,0:T(8,128)S(1)}, f32[1,128,2048]{2,1,0:T(8,128)S(1)}, u32[]{:S(2)}, u32[]{:S(2)}) %collective-permute-start) | collective-permute-done | bytes 1048608 | tf_op jit(solution)/shard_map/ppermute | solution.py:25
  33.6 5.0 step.14
  40.8 13.2 %collective-permute-done.2.refs_1_ = f32[1,128,2048]{2,1,0:T(8,128)S(1)} collective-permute-done((f32[1,128,2048]{2,1,0:T(8,128)S(1)}, f32[1,128,2048]{2,1,0:T(8,128)S(1)}, u32[]{:S(2)}, u32[]{:S(2)}) %collective-permute-start.2) | collective-permute-done | bytes 1048608 | tf_op jit(solution)/shard_map/ppermute | solution.py:25
  56.1 6.3 step.15
  64.5 56.9 %collective-permute-done.4.refs_1_ = f32[3,128,2048]{2,1,0:T(8,128)S(1)} collective-permute-done((f32[3,128,2048]{2,1,0:T(8,128)S(1)}, f32[3,128,2048]{2,1,0:T(8,128)S(1)}, u32[]{:S(2)}, u32[]{:S(2)}) %collective-permute-start.4) | collective-permute-done | bytes 3145760 | tf_op jit(solution)/shard_map/ppermute | solution.py:25
  123.5 8.1 %step.16 = (f32[3,128,2048]{2,1,0:T(8,128)}, f32[3,128,2048]{2,1,0:T(8,128)}, f32[8,2048]{1,0:T(8,128)S(1)}, f32[4,2,128,2048]{3,2,1,0:T(8,128)S(1)}, f32[4,8,256]{2,1,0:T(8,128)S(1)}) custom-call(s32[1]{0:T(128)} %bitcast.refs_0_, f32[3,128,2048]{2,1,0:T(8,128)S(1)} %collective-permute-done.4.refs_1_, f32[3,128,2048]{2,1,0:T(8,128)S(1)} %collective-permute-done.5.refs_2_, ...), custom_call_target="tpu_custom_call" | custom-call | flops 5242880 | bytes 18874368 | tf_op jit(solution)/shard_map/step/pallas_call | solution.py:170
  133.6 55.2 %collective-permute-done.6.refs_1_ = f32[3,128,2048]{2,1,0:T(8,128)S(1)} collective-permute-done((f32[3,128,2048]{2,1,0:T(8,128)}, f32[3,128,2048]{2,1,0:T(8,128)S(1)}, u32[]{:S(2)}, u32[]{:S(2)}) %collective-permute-start.6) | collective-permute-done | bytes 3145760 | tf_op jit(solution)/shard_map/ppermute | solution.py:25
  190.9 7.1 %step.17 = (f32[3,128,2048]{2,1,0:T(8,128)}, f32[3,128,2048]{2,1,0:T(8,128)S(1)}, f32[8,2048]{1,0:T(8,128)S(1)}, f32[4,2,128,2048]{3,2,1,0:T(8,128)S(1)}, f32[4,8,256]{2,1,0:T(8,128)S(1)}) custom-call(s32[1]{0:T(128)} %bitcast.refs_0_, f32[3,128,2048]{2,1,0:T(8,128)S(1)} %collective-permute-done.6.refs_1_, ...), custom_call_target="tpu_custom_call", output_to_operand_aliasing={{3}: (10, {}), {4}: (11, {})} | custom-call | flops 5242880 | bytes 18874368 | tf_op jit(solution)/shard_map/step/pallas_call | solution.py:170
  200.0 56.2 %collective-permute-done.8.refs_1_ = f32[3,128,2048]{2,1,0:T(8,128)S(1)} collective-permute-done((f32[3,128,2048]{2,1,0:T(8,128)}, f32[3,128,2048]{2,1,0:T(8,128)S(1)}, u32[]{:S(2)}, u32[]{:S(2)}) %collective-permute-start.8) | collective-permute-done | bytes 3145760 | tf_op jit(solution)/shard_map/ppermute | solution.py:25
  258.3 7.1 %step.18 = (f32[3,128,2048]{2,1,0:T(8,128)}, f32[3,128,2048]{2,1,0:T(8,128)S(1)}, f32[8,2048]{1,0:T(8,128)S(1)}, f32[4,2,128,2048]{3,2,1,0:T(8,128)S(1)}, f32[4,8,256]{2,1,0:T(8,128)S(1)}) custom-call(s32[1]{0:T(128)} %bitcast.refs_0_, f32[3,128,2048]{2,1,0:T(8,128)S(1)} %collective-permute-done.8.refs_1_, ...), custom_call_target="tpu_custom_call", output_to_operand_aliasing={{3}: (10, {}), {4}: (11, {})} | custom-call | flops 5242880 | bytes 18874368 | tf_op jit(solution)/shard_map/step/pallas_call | solution.py:170
  267.4 56.2 %collective-permute-done.10.refs_1_ = f32[3,128,2048]{2,1,0:T(8,128)S(1)} collective-permute-done((f32[3,128,2048]{2,1,0:T(8,128)}, f32[3,128,2048]{2,1,0:T(8,128)S(1)}, u32[]{:S(2)}, u32[]{:S(2)}) %collective-permute-start.10) | collective-permute-done | bytes 3145760 | tf_op jit(solution)/shard_map/ppermute | solution.py:25
  325.7 7.2 %step.19 = (f32[3,128,2048]{2,1,0:T(8,128)S(1)}, f32[3,128,2048]{2,1,0:T(8,128)}, f32[8,2048]{1,0:T(8,128)S(1)}, f32[4,2,128,2048]{3,2,1,0:T(8,128)S(1)}, f32[4,8,256]{2,1,0:T(8,128)S(1)}) custom-call(s32[1]{0:T(128)} %bitcast.refs_0_, f32[3,128,2048]{2,1,0:T(8,128)S(1)} %collective-permute-done.10.refs_1_, ...), custom_call_target="tpu_custom_call", output_to_operand_aliasing={{3}: (10, {}), {4}: (11, {})} | custom-call | flops 5242880 | bytes 18874368 | tf_op jit(solution)/shard_map/step/pallas_call | solution.py:170
  335.0 3.6 collective-permute-start.14
  341.5 4.0 collective-permute-done.13
  352.3 38.7 %collective-permute-done.16.refs_1_ = f32[3,128,2048]{2,1,0:T(8,128)S(1)} collective-permute-done((f32[3,128,2048]{2,1,0:T(8,128)}, f32[3,128,2048]{2,1,0:T(8,128)S(1)}, u32[]{:S(2)}, u32[]{:S(2)}) %collective-permute-start.16) | collective-permute-done | bytes 3145760 | tf_op jit(solution)/shard_map/ppermute | solution.py:25
  393.1 5.6 step.20
  400.9 57.6 %collective-permute-done.18.refs_1_ = f32[3,128,2048]{2,1,0:T(8,128)S(1)} collective-permute-done((f32[3,128,2048]{2,1,0:T(8,128)S(1)}, f32[3,128,2048]{2,1,0:T(8,128)S(1)}, u32[]{:S(2)}, u32[]{:S(2)}) %collective-permute-start.18) | collective-permute-done | bytes 3145760 | tf_op jit(solution)/shard_map/ppermute | solution.py:25
  460.6 5.6 step.21
  468.3 35.1 %collective-permute-done.20.refs_1_ = f32[2,128,2048]{2,1,0:T(8,128)S(1)} collective-permute-done((f32[2,128,2048]{2,1,0:T(8,128)S(1)}, f32[2,128,2048]{2,1,0:T(8,128)S(1)}, u32[]{:S(2)}, u32[]{:S(2)}) %collective-permute-start.20) | collective-permute-done | bytes 2097184 | tf_op jit(solution)/shard_map/ppermute | solution.py:25
  505.5 4.6 step.22
  513.7 34.6 %collective-permute-done.25.refs_1_ = f32[2,128,2048]{2,1,0:T(8,128)S(1)} collective-permute-done((f32[2,128,2048]{2,1,0:T(8,128)S(1)}, f32[2,128,2048]{2,1,0:T(8,128)S(1)}, u32[]{:S(2)}, u32[]{:S(2)}) %collective-permute-start.25) | collective-permute-done | bytes 2097184 | tf_op jit(solution)/shard_map/ppermute | solution.py:25
  551.1 4.6 step.23
  555.7 3.3 copy-done.2
  559.1 3.7 collective-permute-start.29
  564.7 3.6 collective-permute-start.33
  577.8 3.4 copy-done.3
  587.9 3.4 copy-done.1
  591.2 14.4 %finish.2 = (f32[2,4,2,128,2048]{4,3,2,1,0:T(8,128)}, f32[2,4,2,128,2048]{4,3,2,1,0:T(8,128)}) custom-call(f32[4,8,256]{2,1,0:T(8,128)S(1)} %rsqrt_multiply_fusion.by_row, f32[1,2048]{1,0:T(1,128)S(1)} %rsqrt.14.by_col, f32[4,2,128,2048]{3,2,1,0:T(8,128)S(1)} %copy-done.1, f32[2,4,2,128,2048]{4,3,2,1,0:T(8,128)} %bitcast.61), custom_call_target="tpu_custom_call" | custom-call | flops 8388608 | bytes 33554432 | tf_op jit(solution)/shard_map/finish/pallas_call | solution.py:273
  616.3 3.4 copy-done.4
  619.7 14.4 %finish.3 = (f32[2,4,2,128,2048]{4,3,2,1,0:T(8,128)}, f32[2,4,2,128,2048]{4,3,2,1,0:T(8,128)}) custom-call(f32[4,8,256]{2,1,0:T(8,128)S(1)} %rsqrt_multiply_fusion.1.by_row, f32[1,2048]{1,0:T(1,128)S(1)} %get-tuple-element.224.by_col, f32[4,2,128,2048]{3,2,1,0:T(8,128)S(1)} %copy-done.4, ...), custom_call_target="tpu_custom_call", output_to_operand_aliasing={{0}: (4, {}), {1}: (5, {})} | custom-call | flops 8388608 | bytes 33554432 | tf_op jit(solution)/shard_map/finish/pallas_call | solution.py:273
  (97 shorter events, 78.6 us)
Async XLA Ops:
  4.5 27.0 %collective-permute-start = (f32[1,128,2048]{2,1,0:T(8,128)S(1)}, f32[1,128,2048]{2,1,0:T(8,128)S(1)}, u32[]{:S(2)}, u32[]{:S(2)}) collective-permute-start(f32[1,128,2048]{2,1,0:T(8,128)S(1)} %get-tuple-element.120), channel_id=1, source_target_pairs={{0,8},{8,0},{16,24},{24,16},{1,9},{9,1},{17,25},{25,17},{2,10},{10... | collective-permute-start | bytes 3145736 | tf_op jit(solution)/shard_map/ppermute | solution.py:25
  7.5 26.1 %collective-permute-start.1 = (f32[1,128,2048]{2,1,0:T(8,128)S(1)}, f32[1,128,2048]{2,1,0:T(8,128)S(1)}, u32[]{:S(2)}, u32[]{:S(2)}) collective-permute-start(f32[1,128,2048]{2,1,0:T(8,128)S(1)} %get-tuple-element.121), channel_id=1, source_target_pairs={{0,16},{8,24},{16,0},{24,8},{1,17},{9,25},{17,1},{25,9},{2,18},{10... | collective-permute-start | bytes 3145736 | tf_op jit(solution)/shard_map/ppermute | solution.py:25
  12.9 41.1 %collective-permute-start.2 = (f32[1,128,2048]{2,1,0:T(8,128)S(1)}, f32[1,128,2048]{2,1,0:T(8,128)S(1)}, u32[]{:S(2)}, u32[]{:S(2)}) collective-permute-start(f32[1,128,2048]{2,1,0:T(8,128)S(1)} %get-tuple-element.125), channel_id=1, source_target_pairs={{0,8},{8,0},{16,24},{24,16},{1,9},{9,1},{17,25},{25,17},{2,10},{10... | collective-permute-start | bytes 3145736 | tf_op jit(solution)/shard_map/ppermute | solution.py:25
  13.5 42.6 %collective-permute-start.3 = (f32[1,128,2048]{2,1,0:T(8,128)S(1)}, f32[1,128,2048]{2,1,0:T(8,128)S(1)}, u32[]{:S(2)}, u32[]{:S(2)}) collective-permute-start(f32[1,128,2048]{2,1,0:T(8,128)S(1)} %get-tuple-element.126), channel_id=1, source_target_pairs={{0,16},{8,24},{16,0},{24,8},{1,17},{9,25},{17,1},{25,9},{2,18},{10... | collective-permute-start | bytes 3145736 | tf_op jit(solution)/shard_map/ppermute | solution.py:25
  38.6 82.8 %collective-permute-start.4 = (f32[3,128,2048]{2,1,0:T(8,128)S(1)}, f32[3,128,2048]{2,1,0:T(8,128)S(1)}, u32[]{:S(2)}, u32[]{:S(2)}) collective-permute-start(f32[3,128,2048]{2,1,0:T(8,128)S(1)} %get-tuple-element.130), channel_id=1, source_target_pairs={{0,8},{8,0},{16,24},{24,16},{1,9},{9,1},{17,25},{25,17},{2,10},{10... | collective-permute-start | bytes 9437192 | tf_op jit(solution)/shard_map/ppermute | solution.py:25
  38.7 84.8 %collective-permute-start.5 = (f32[3,128,2048]{2,1,0:T(8,128)S(1)}, f32[3,128,2048]{2,1,0:T(8,128)S(1)}, u32[]{:S(2)}, u32[]{:S(2)}) collective-permute-start(f32[3,128,2048]{2,1,0:T(8,128)S(1)} %get-tuple-element.131), channel_id=1, source_target_pairs={{0,16},{8,24},{16,0},{24,8},{1,17},{9,25},{17,1},{25,9},{2,18},{10... | collective-permute-start | bytes 9437192 | tf_op jit(solution)/shard_map/ppermute | solution.py:25
  62.4 126.4 %collective-permute-start.6 = (f32[3,128,2048]{2,1,0:T(8,128)}, f32[3,128,2048]{2,1,0:T(8,128)S(1)}, u32[]{:S(2)}, u32[]{:S(2)}) collective-permute-start(f32[3,128,2048]{2,1,0:T(8,128)} %get-tuple-element.136), channel_id=1, source_target_pairs={{0,8},{8,0},{16,24},{24,16},{1,9},{9,1},{17,25},{25,17},{2,10},{10... | collective-permute-start | bytes 9437192 | tf_op jit(solution)/shard_map/ppermute | solution.py:25
  62.5 128.4 %collective-permute-start.7 = (f32[3,128,2048]{2,1,0:T(8,128)S(1)}, f32[3,128,2048]{2,1,0:T(8,128)S(1)}, u32[]{:S(2)}, u32[]{:S(2)}) collective-permute-start(f32[3,128,2048]{2,1,0:T(8,128)S(1)} %get-tuple-element.137), channel_id=1, source_target_pairs={{0,16},{8,24},{16,0},{24,8},{1,17},{9,25},{17,1},{25,9},{2,18},{10... | collective-permute-start | bytes 9437192 | tf_op jit(solution)/shard_map/ppermute | solution.py:25
  131.6 124.6 %collective-permute-start.8 = (f32[3,128,2048]{2,1,0:T(8,128)}, f32[3,128,2048]{2,1,0:T(8,128)S(1)}, u32[]{:S(2)}, u32[]{:S(2)}) collective-permute-start(f32[3,128,2048]{2,1,0:T(8,128)} %get-tuple-element.145), channel_id=1, source_target_pairs={{0,8},{8,0},{16,24},{24,16},{1,9},{9,1},{17,25},{25,17},{2,10},{10... | collective-permute-start | bytes 9437192 | tf_op jit(solution)/shard_map/ppermute | solution.py:25
  131.6 126.7 %collective-permute-start.9 = (f32[3,128,2048]{2,1,0:T(8,128)}, f32[3,128,2048]{2,1,0:T(8,128)S(1)}, u32[]{:S(2)}, u32[]{:S(2)}) collective-permute-start(f32[3,128,2048]{2,1,0:T(8,128)} %get-tuple-element.146), channel_id=1, source_target_pairs={{0,16},{8,24},{16,0},{24,8},{1,17},{9,25},{17,1},{25,9},{2,18},{10... | collective-permute-start | bytes 9437192 | tf_op jit(solution)/shard_map/ppermute | solution.py:25
  198.0 125.7 %collective-permute-start.10 = (f32[3,128,2048]{2,1,0:T(8,128)}, f32[3,128,2048]{2,1,0:T(8,128)S(1)}, u32[]{:S(2)}, u32[]{:S(2)}) collective-permute-start(f32[3,128,2048]{2,1,0:T(8,128)} %get-tuple-element.154), channel_id=1, source_target_pairs={{0,8},{8,0},{16,24},{24,16},{1,9},{9,1},{17,25},{25,17},{2,10},{10... | collective-permute-start | bytes 9437192 | tf_op jit(solution)/shard_map/ppermute | solution.py:25
  198.0 127.7 %collective-permute-start.11 = (f32[3,128,2048]{2,1,0:T(8,128)S(1)}, f32[3,128,2048]{2,1,0:T(8,128)S(1)}, u32[]{:S(2)}, u32[]{:S(2)}) collective-permute-start(f32[3,128,2048]{2,1,0:T(8,128)S(1)} %get-tuple-element.155), channel_id=1, source_target_pairs={{0,16},{8,24},{16,0},{24,8},{1,17},{9,25},{17,1},{25,9},{2,18},{10... | collective-permute-start | bytes 9437192 | tf_op jit(solution)/shard_map/ppermute | solution.py:25
  265.4 125.7 %collective-permute-start.16 = (f32[3,128,2048]{2,1,0:T(8,128)}, f32[3,128,2048]{2,1,0:T(8,128)S(1)}, u32[]{:S(2)}, u32[]{:S(2)}) collective-permute-start(f32[3,128,2048]{2,1,0:T(8,128)} %get-tuple-element.169), channel_id=1, source_target_pairs={{0,8},{8,0},{16,24},{24,16},{1,9},{9,1},{17,25},{25,17},{2,10},{10... | collective-permute-start | bytes 9437192 | tf_op jit(solution)/shard_map/ppermute | solution.py:25
  265.4 127.7 %collective-permute-start.17 = (f32[3,128,2048]{2,1,0:T(8,128)S(1)}, f32[3,128,2048]{2,1,0:T(8,128)S(1)}, u32[]{:S(2)}, u32[]{:S(2)}) collective-permute-start(f32[3,128,2048]{2,1,0:T(8,128)S(1)} %get-tuple-element.170), channel_id=1, source_target_pairs={{0,16},{8,24},{16,0},{24,8},{1,17},{9,25},{17,1},{25,9},{2,18},{10... | collective-permute-start | bytes 9437192 | tf_op jit(solution)/shard_map/ppermute | solution.py:25
  332.9 125.6 %collective-permute-start.18 = (f32[3,128,2048]{2,1,0:T(8,128)S(1)}, f32[3,128,2048]{2,1,0:T(8,128)S(1)}, u32[]{:S(2)}, u32[]{:S(2)}) collective-permute-start(f32[3,128,2048]{2,1,0:T(8,128)S(1)} %get-tuple-element.175), channel_id=1, source_target_pairs={{0,8},{8,0},{16,24},{24,16},{1,9},{9,1},{17,25},{25,17},{2,10},{10... | collective-permute-start | bytes 9437192 | tf_op jit(solution)/shard_map/ppermute | solution.py:25
  332.9 127.6 %collective-permute-start.19 = (f32[3,128,2048]{2,1,0:T(8,128)}, f32[3,128,2048]{2,1,0:T(8,128)S(1)}, u32[]{:S(2)}, u32[]{:S(2)}) collective-permute-start(f32[3,128,2048]{2,1,0:T(8,128)} %get-tuple-element.176), channel_id=1, source_target_pairs={{0,16},{8,24},{16,0},{24,8},{1,17},{9,25},{17,1},{25,9},{2,18},{10... | collective-permute-start | bytes 9437192 | tf_op jit(solution)/shard_map/ppermute | solution.py:25
  398.7 104.7 %collective-permute-start.20 = (f32[2,128,2048]{2,1,0:T(8,128)S(1)}, f32[2,128,2048]{2,1,0:T(8,128)S(1)}, u32[]{:S(2)}, u32[]{:S(2)}) collective-permute-start(f32[2,128,2048]{2,1,0:T(8,128)S(1)} %get-tuple-element.184), channel_id=1, source_target_pairs={{0,8},{8,0},{16,24},{24,16},{1,9},{9,1},{17,25},{25,17},{2,10},{10... | collective-permute-start | bytes 6291464 | tf_op jit(solution)/shard_map/ppermute | solution.py:25
  398.8 106.7 %collective-permute-start.21 = (f32[2,128,2048]{2,1,0:T(8,128)S(1)}, f32[2,128,2048]{2,1,0:T(8,128)S(1)}, u32[]{:S(2)}, u32[]{:S(2)}) collective-permute-start(f32[2,128,2048]{2,1,0:T(8,128)S(1)} %get-tuple-element.185), channel_id=1, source_target_pairs={{0,16},{8,24},{16,0},{24,8},{1,17},{9,25},{17,1},{25,9},{2,18},{10... | collective-permute-start | bytes 6291464 | tf_op jit(solution)/shard_map/ppermute | solution.py:25
  466.1 82.2 %collective-permute-start.25 = (f32[2,128,2048]{2,1,0:T(8,128)S(1)}, f32[2,128,2048]{2,1,0:T(8,128)S(1)}, u32[]{:S(2)}, u32[]{:S(2)}) collective-permute-start(f32[2,128,2048]{2,1,0:T(8,128)S(1)} %get-tuple-element.194), channel_id=1, source_target_pairs={{0,8},{8,0},{16,24},{24,16},{1,9},{9,1},{17,25},{25,17},{2,10},{10... | collective-permute-start | bytes 6291464 | tf_op jit(solution)/shard_map/ppermute | solution.py:25
  466.2 84.8 %collective-permute-start.26 = (f32[2,128,2048]{2,1,0:T(8,128)S(1)}, f32[2,128,2048]{2,1,0:T(8,128)S(1)}, u32[]{:S(2)}, u32[]{:S(2)}) collective-permute-start(f32[2,128,2048]{2,1,0:T(8,128)S(1)} %get-tuple-element.195), channel_id=1, source_target_pairs={{0,16},{8,24},{16,0},{24,8},{1,17},{9,25},{17,1},{25,9},{2,18},{10... | collective-permute-start | bytes 6291464 | tf_op jit(solution)/shard_map/ppermute | solution.py:25
  510.1 48.9 %collective-permute-start.24 = (f32[8,2048]{1,0:T(8,128)S(1)}, f32[8,2048]{1,0:T(8,128)S(1)}, u32[]{:S(2)}, u32[]{:S(2)}) collective-permute-start(f32[8,2048]{1,0:T(8,128)S(1)} %add.75), channel_id=1, source_target_pairs={{0,24},{8,16},{16,8},{24,0},{1,25},{9,17},{17,9},{25,1},{2,26},{10... | collective-permute-start | bytes 196616 | tf_op jit(solution)/shard_map/ppermute | solution.py:25
  511.7 47.3 %collective-permute-start.23 = (f32[8,2048]{1,0:T(8,128)S(1)}, f32[8,2048]{1,0:T(8,128)S(1)}, u32[]{:S(2)}, u32[]{:S(2)}) collective-permute-start(f32[8,2048]{1,0:T(8,128)S(1)} %add.75), channel_id=1, source_target_pairs={{0,16},{8,24},{16,0},{24,8},{1,17},{9,25},{17,1},{25,9},{2,18},{10... | collective-permute-start | bytes 196616 | tf_op jit(solution)/shard_map/ppermute | solution.py:25
  511.8 47.2 %collective-permute-start.22 = (f32[8,2048]{1,0:T(8,128)S(1)}, f32[8,2048]{1,0:T(8,128)S(1)}, u32[]{:S(2)}, u32[]{:S(2)}) collective-permute-start(f32[8,2048]{1,0:T(8,128)S(1)} %add.75), channel_id=1, source_target_pairs={{0,8},{8,0},{16,24},{24,16},{1,9},{9,1},{17,25},{25,17},{2,10},{10... | collective-permute-start | bytes 196616 | tf_op jit(solution)/shard_map/ppermute | solution.py:25
  559.1 18.7 %collective-permute-start.29 = (f32[4,8,256]{2,1,0:T(8,128)S(1)}, f32[4,8,256]{2,1,0:T(8,128)S(1)}, u32[]{:S(2)}, u32[]{:S(2)}) collective-permute-start(f32[4,8,256]{2,1,0:T(8,128)S(1)} %get-tuple-element.205), channel_id=1, source_target_pairs={{0,3},{1,2},{2,1},{3,0},{4,7},{5,6},{6,5},{7,4},{8,11},{9,10},{10,... | collective-permute-start | bytes 98312 | tf_op jit(solution)/shard_map/ppermute | solution.py:25
  562.7 15.1 %collective-permute-start.28 = (f32[4,8,256]{2,1,0:T(8,128)S(1)}, f32[4,8,256]{2,1,0:T(8,128)S(1)}, u32[]{:S(2)}, u32[]{:S(2)}) collective-permute-start(f32[4,8,256]{2,1,0:T(8,128)S(1)} %get-tuple-element.205), channel_id=1, source_target_pairs={{0,2},{1,3},{2,0},{3,1},{4,6},{5,7},{6,4},{7,5},{8,10},{9,11},{10,... | collective-permute-start | bytes 98312 | tf_op jit(solution)/shard_map/ppermute | solution.py:25
  562.7 15.1 %collective-permute-start.27 = (f32[4,8,256]{2,1,0:T(8,128)S(1)}, f32[4,8,256]{2,1,0:T(8,128)S(1)}, u32[]{:S(2)}, u32[]{:S(2)}) collective-permute-start(f32[4,8,256]{2,1,0:T(8,128)S(1)} %get-tuple-element.205), channel_id=1, source_target_pairs={{0,1},{1,0},{2,3},{3,2},{4,5},{5,4},{6,7},{7,6},{8,9},{9,8},{10,11... | collective-permute-start | bytes 98312 | tf_op jit(solution)/shard_map/ppermute | solution.py:25
  564.7 8.5 %collective-permute-start.33 = (f32[]{:T(128)}, f32[]{:T(128)}, u32[]{:S(2)}, u32[]{:S(2)}) collective-permute-start(f32[]{:T(128)} %get-tuple-element.226), channel_id=1, source_target_pairs={{0,3},{1,2},{2,1},{3,0},{4,7},{5,6},{6,5},{7,4},{8,11},{9,10},{10,... | collective-permute-start | bytes 20 | tf_op jit(solution)/shard_map/ppermute | solution.py:25
  584.1 21.5 %collective-permute-start.36 = (f32[8,2048]{1,0:T(8,128)S(1)}, f32[8,2048]{1,0:T(8,128)S(1)}, u32[]{:S(2)}, u32[]{:S(2)}) collective-permute-start(f32[8,2048]{1,0:T(8,128)S(1)} %add.82), channel_id=1, source_target_pairs={{0,24},{8,16},{16,8},{24,0},{1,25},{9,17},{17,9},{25,1},{2,26},{10... | collective-permute-start | bytes 196616 | tf_op jit(solution)/shard_map/ppermute | solution.py:25
  585.7 19.9 %collective-permute-start.35 = (f32[8,2048]{1,0:T(8,128)S(1)}, f32[8,2048]{1,0:T(8,128)S(1)}, u32[]{:S(2)}, u32[]{:S(2)}) collective-permute-start(f32[8,2048]{1,0:T(8,128)S(1)} %add.82), channel_id=1, source_target_pairs={{0,16},{8,24},{16,0},{24,8},{1,17},{9,25},{17,1},{25,9},{2,18},{10... | collective-permute-start | bytes 196616 | tf_op jit(solution)/shard_map/ppermute | solution.py:25
  585.8 19.8 %collective-permute-start.34 = (f32[8,2048]{1,0:T(8,128)S(1)}, f32[8,2048]{1,0:T(8,128)S(1)}, u32[]{:S(2)}, u32[]{:S(2)}) collective-permute-start(f32[8,2048]{1,0:T(8,128)S(1)} %add.82), channel_id=1, source_target_pairs={{0,8},{8,0},{16,24},{24,16},{1,9},{9,1},{17,25},{25,17},{2,10},{10... | collective-permute-start | bytes 196616 | tf_op jit(solution)/shard_map/ppermute | solution.py:25
  607.6 7.3 %collective-permute-start.39 = (f32[]{:T(128)}, f32[]{:T(128)}, u32[]{:S(2)}, u32[]{:S(2)}) collective-permute-start(f32[]{:T(128)} %fusion.4), channel_id=1, source_target_pairs={{0,3},{1,2},{2,1},{3,0},{4,7},{5,6},{6,5},{7,4},{8,11},{9,10},{10,... | collective-permute-start | bytes 20 | tf_op jit(solution)/shard_map/ppermute | solution.py:25
  607.8 7.1 %collective-permute-start.38 = (f32[]{:T(128)}, f32[]{:T(128)}, u32[]{:S(2)}, u32[]{:S(2)}) collective-permute-start(f32[]{:T(128)} %fusion.4), channel_id=1, source_target_pairs={{0,2},{1,3},{2,0},{3,1},{4,6},{5,7},{6,4},{7,5},{8,10},{9,11},{10,... | collective-permute-start | bytes 20 | tf_op jit(solution)/shard_map/ppermute | solution.py:25
  (15 other events, 190.3 us)

commit v4 on v3

v4 whole, which is shorter than its diff:
```python
import functools

import jax
import jax.numpy as jnp
from jax import lax
from jax.experimental import pallas as pl
from jax.experimental.pallas import tpu as pltpu
from jax.sharding import PartitionSpec as P

decay_rate = 1.0 - 2.0 ** (-0.8)
tiny_eps = 1e-30
clip_limit = 1.0
learn_rate = 0.01

lanes = 128
sublanes = 8
blocks_of_matrix = 8
tile_rows = 16
finish_rows = 64
f32 = jnp.float32


def swap(x, axes, mask):
    size = lax.axis_size(axes)
    return lax.ppermute(x, axes, [(i, i ^ mask) for i in range(size)])


def exchange(x, axes):
    return [x] + [swap(x, axes, mask) for mask in range(1, lax.axis_size(axes))]


def tree_sum(got):
    while len(got) > 1:
        got = [got[i] + got[i + 1] for i in range(0, len(got), 2)]
    return got[0]


def pairwise_sum(x, axes):
    mask = 1
    while mask < lax.axis_size(axes):
        x = x + swap(x, axes, mask)
        mask *= 2
    return x


def tie(*xs):
    return lax.optimization_barrier(xs)


def params_of(mib):
    return pltpu.CompilerParams(vmem_limit_bytes=mib * 1024 * 1024)


def step_kernel(takes, finishes, first, sends, starts, brings, carries, *refs):
    refs = list(refs[1:])
    take = lambda yes: refs.pop(0) if yes else None
    got = [take(takes or finishes) for _ in range(2)]
    mine = take(finishes)
    direct = [take(sends) for _ in range(2)]
    relay = [take(sends) for _ in range(2)]
    onward = take(starts)
    again = finishes and not first
    cols_in, _, _ = take(again), take(again), take(again)
    stats_in = take(brings is not None or carries is not None)
    out = [take(sends or starts) for _ in range(2)]
    cols_out, summed_out, rows_out = take(finishes), take(finishes), take(finishes)
    stats_out = take(brings is not None)
    row_parts = take(finishes)
    t = pl.program_id(0)
    tile, width = (onward if starts else mine if finishes else direct[0]).shape[-2:]
    part = tile * pl.num_programs(0)

    def rows_of(slot):
        return pl.ds(pl.multiple_of(slot * part + t * tile, sublanes), tile)

    @pl.when(t == 0)
    def _():
        if finishes:
            cols_out[...] = jnp.zeros_like(cols_out) if first else cols_in[...]
        if brings is not None:
            stats_out[...] = stats_in[...] + got[brings][got[brings].shape[0] - sublanes :]
        if carries is not None:
            stats = stats_in if brings is None else stats_out
            out[carries][out[carries].shape[0] - sublanes :] = stats[...]

    for half in range(2):
        if starts:
            out[half][rows_of(2 if sends else 0)] = onward[half].astype(f32)
        if sends:
            out[half][rows_of(0)] = direct[half][...].astype(f32)
            passed = got[half][rows_of(2 if finishes else 0)]
            out[1 - half][rows_of(1)] = passed + relay[half][...].astype(f32)
        if finishes:
            total = mine[half].astype(f32) + got[half][rows_of(0)] + got[1 - half][rows_of(1)]
            summed_out[half] = total
            squares = total * total
            row_parts[rows_of(half)] = sum(squares[:, i : i + lanes] for i in range(0, width, lanes))
            cols_out[...] += sum(squares[i : i + sublanes] for i in range(0, tile, sublanes))

    if finishes:

        @pl.when(t == pl.num_programs(0) - 1)
        def _():
            rows_out[...] = lax.dot_general(
                jnp.ones((sublanes, lanes), f32),
                row_parts[...],
                (((1,), (1,)), ((), ())),
                precision=lax.Precision.HIGHEST,
                preferred_element_type=f32,
            )


def step(j, total_blocks, me, partials, got, sums, stats, brings, carries):
    mats, _, count, _, part, width = partials.shape
    tile = min(tile_rows, part)
    finishes = j >= 2
    takes = 0 <= j < total_blocks
    sends = takes
    starts = j + 2 < total_blocks
    b = (j - 2) % count
    first = finishes and b == 0

    def piece_spec(block, mask, half):
        m, b = divmod(block, count)
        if half is None:
            return pl.BlockSpec(
                (None, None, None, 2, tile, width),
                lambda t, at: (m, at[0] ^ mask, b, 0, t, 0),
            )
        return pl.BlockSpec(
            (None, None, None, None, tile, width),
            lambda t, at: (m, at[0] ^ mask, b, half, t, 0),
        )

    in_vmem = pl.BlockSpec(memory_space=pltpu.VMEM)
    operands, in_specs = [], []

    def add(x, spec):
        operands.append(x)
        in_specs.append(spec)

    if j >= 0:
        for x in got:
            add(x, in_vmem)
    if finishes:
        add(partials, piece_spec(j - 2, 0, None))
    if sends:
        for half, mask in ((0, 1), (1, 2)):
            add(partials, piece_spec(j, mask, half))
        for half, mask in ((0, 2), (1, 1)):
            add(partials, piece_spec(j, mask, half))
    if starts:
        add(partials, piece_spec(j + 2, 3, None))

    slots = (2 if sends else 0) + (1 if starts else 0)
    out_shape, out_specs, scratch, aliases = [], [], [], {}
    if slots:
        for link in range(2):
            size = slots * part + (sublanes if link == carries else 0)
            out_shape.append(jax.ShapeDtypeStruct((size, width), f32))
            out_specs.append(in_vmem)
    cols_spec = pl.BlockSpec((sublanes, width), lambda t, at: (0, 0))
    if finishes:
        if not first:
            add(sums[0], cols_spec)
            for i in (1, 2):
                aliases[1 + len(operands)] = len(out_shape) + i
                add(sums[i], pl.BlockSpec(memory_space=pl.ANY))
        out_shape.append(jax.ShapeDtypeStruct((sublanes, width), f32))
        out_specs.append(cols_spec)
        out_shape.append(jax.ShapeDtypeStruct((count, 2, part, width), f32))
        out_specs.append(pl.BlockSpec((None, 2, tile, width), lambda t, at: (b, 0, t, 0)))
        out_shape.append(jax.ShapeDtypeStruct((count, sublanes, 2 * part), f32))
        out_specs.append(pl.BlockSpec((None, sublanes, 2 * part), lambda t, at: (b, 0, 0)))
        scratch.append(pltpu.VMEM((2 * part, lanes), f32))
    if brings is not None or carries is not None:
        add(stats, cols_spec)
    if brings is not None:
        out_shape.append(jax.ShapeDtypeStruct((sublanes, width), f32))
        out_specs.append(cols_spec)
    moved = part * width * (4 * (2 * slots + 8) + 2 * 8)
    result = pl.pallas_call(
        functools.partial(step_kernel, takes, finishes, first, sends, starts, brings, carries),
        out_shape=out_shape,
        grid_spec=pltpu.PrefetchScalarGridSpec(
            num_scalar_prefetch=1,
            grid=(part // tile,),
            in_specs=in_specs,
            out_specs=out_specs,
            scratch_shapes=scratch,
        ),
        input_output_aliases=aliases,
        compiler_params=params_of(34),
        cost_estimate=pl.CostEstimate(
            flops=part * width * 20, bytes_accessed=moved, transcendentals=0
        ),
        name="step",
    )(me, *operands)
    sent = list(result[:2]) if slots else None
    rest = list(result[2:] if slots else result)
    return sent, rest[:3] if finishes else None, rest[3] if brings is not None else stats


def weighted_kernel(extent, factor, cols, summed, *refs):
    *totals, rows_out, stats, weighted, level = refs
    i = pl.program_id(0)

    @pl.when(i == 0)
    def _():
        weighted[...] = jnp.zeros_like(weighted)
        level[...] = jnp.zeros_like(level)

    total = tree_sum([x[...] for x in totals])
    row_new = decay_rate * factor[...] + (1.0 - decay_rate) * (total / extent + tiny_eps)
    rows_out[...] = row_new
    level[...] += row_new
    inverse = jnp.transpose(1.0 / row_new)[:, 0:1]
    part = summed.shape[1]
    for half in range(2):
        for r in range(0, part, sublanes):
            x = summed[half, r : r + sublanes]
            at = half * part + r
            weighted[...] += x * x * inverse[at : at + sublanes]

    @pl.when(i == pl.num_programs(0) - 1)
    def _():
        stats[...] = jnp.zeros_like(stats)
        stats[0:1] = jnp.sum(cols[...], axis=0, keepdims=True)
        stats[1:2] = jnp.sum(weighted[...], axis=0, keepdims=True)
        total = jnp.sum(level[0:1], axis=1, keepdims=True)
        stats[2:3] = jnp.broadcast_to(total, (1, stats.shape[1]))


def weighted_sums(extent, totals, factor, cols, summed):
    count, _, part, width = summed.shape
    along = pl.BlockSpec((None, sublanes, 2 * part), lambda i: (i, 0, 0))
    whole = pl.BlockSpec((sublanes, width), lambda i: (0, 0))
    return pl.pallas_call(
        functools.partial(weighted_kernel, extent),
        grid=(count,),
        in_specs=[
            pl.BlockSpec((None, 1, 2 * part), lambda i: (i, 0, 0)),
            whole,
            pl.BlockSpec((None, 2, part, width), lambda i: (i, 0, 0, 0)),
        ]
        + [along] * len(totals),
        out_specs=[along, whole],
        out_shape=[
            jax.ShapeDtypeStruct(totals[0].shape, f32),
            jax.ShapeDtypeStruct((sublanes, width), f32),
        ],
        scratch_shapes=[pltpu.VMEM((sublanes, width), f32), pltpu.VMEM((sublanes, 2 * part), f32)],
        compiler_params=params_of(16),
        cost_estimate=pl.CostEstimate(
            flops=3 * summed.size, bytes_accessed=4 * summed.size, transcendentals=0
        ),
        name="weighted",
    )(factor.reshape(count, 1, 2 * part), cols, summed, *totals)


def column_kernel(extent, factor, *refs):
    *parts, cols_out, pair = refs
    stats = tree_sum([x[...] for x in parts])
    col_new = decay_rate * factor[...] + (1.0 - decay_rate) * (stats[0:1] / extent + tiny_eps)
    cols_out[...] = col_new
    total = jnp.sum(stats[1:2] / col_new, axis=1, keepdims=True)
    pair[...] = jnp.zeros_like(pair)
    pair[0:1] = jnp.broadcast_to(total, (1, lanes))
    pair[1:2] = stats[2:3, :lanes] / extent


def column_stage(extent, factor, parts):
    return pl.pallas_call(
        functools.partial(column_kernel, extent),
        in_specs=[pl.BlockSpec(memory_space=pltpu.VMEM)] * (1 + len(parts)),
        out_specs=[pl.BlockSpec(memory_space=pltpu.VMEM)] * 2,
        out_shape=[
            jax.ShapeDtypeStruct(factor.shape, f32),
            jax.ShapeDtypeStruct((sublanes, lanes), f32),
        ],
        name="column",
    )(factor, *parts)


def finish_kernel(m, tile, extent, partners, row_new, col_new, summed, params, *refs):
    pairs, (new_params, update, column, by_col) = refs[:partners], refs[-4:]
    count, _, part, width = summed.shape
    row_level = pairs[0][1:2, 0:1]
    total = tree_sum([x[0:1, 0:1] for x in pairs]) * row_level
    spread = jnp.sqrt(total / (extent * extent))
    factor = jnp.sqrt(row_level) / jnp.maximum(1.0, spread / clip_limit)
    by_col[...] = lax.rsqrt(col_new[...])
    for i in range(count):
        column[i] = jnp.transpose(lax.rsqrt(row_new[i]) * factor)

    def body(x, p, new_p, moved):
        i, half, t = (pl.program_id(axis) for axis in range(3))
        start = pl.multiple_of(half * part + t * tile, sublanes)
        y = x[...] * column[i, pl.ds(start, tile)][:, 0:1] * by_col[...]
        moved[...] = y
        new_p[...] = p[...] - learn_rate * y

    of_sum = pl.BlockSpec((None, None, tile, width), lambda i, h, t: (i, h, t, 0))
    of_matrix = pl.BlockSpec((None, None, None, tile, width), lambda i, h, t: (m, i, h, t, 0))
    pltpu.emit_pipeline(
        body,
        grid=(count, 2, part // tile),
        in_specs=[of_sum, of_matrix],
        out_specs=[of_matrix] * 2,
    )(summed, params, new_params, update)


def finish(m, extent, row_new, col_new, pairs, summed, params, outs, mib):
    count, _, part, width = summed.shape
    held = () if outs is None else outs
    in_hbm = pl.BlockSpec(memory_space=pltpu.HBM)
    in_vmem = pl.BlockSpec(memory_space=pltpu.VMEM)
    return pl.pallas_call(
        functools.partial(finish_kernel, m, min(part, finish_rows), extent, len(pairs)),
        in_specs=[in_vmem, in_vmem, pl.BlockSpec(memory_space=pl.ANY), in_hbm]
        + [in_vmem] * len(pairs)
        + [in_hbm] * len(held),
        out_specs=[in_hbm] * 2,
        out_shape=[jax.ShapeDtypeStruct(params.shape, f32)] * 2,
        scratch_shapes=[
            pltpu.VMEM((count, 2 * part, sublanes), f32),
            pltpu.VMEM((1, width), f32),
        ],
        input_output_aliases={4 + len(pairs) + i: i for i in range(len(held))},
        compiler_params=params_of(mib),
        cost_estimate=pl.CostEstimate(
            flops=4 * summed.size, bytes_accessed=16 * summed.size, transcendentals=0
        ),
        name="finish",
    )(row_new, col_new, summed, params, *pairs, *held)


def per_device(partials, params, row_factor, col_factor):
    mats, rows, block_cols = params.shape
    extent = block_cols * lax.axis_size("col")
    me = lax.axis_index("dp").astype(jnp.int32).reshape(1)
    count = blocks_of_matrix
    part = rows // (2 * count)
    total_blocks = mats * count
    pieces = partials.reshape(mats, partials.shape[2], count, 2, part, block_cols)
    blocked = params.reshape(mats, count, 2, part, block_cols)
    new_rows, new_columns = [], []

    def row_stage(m, sums):
        cols, summed, rows_along = sums
        row_new, stats = weighted_sums(
            extent, exchange(rows_along, "col"), row_factor[m], cols, summed
        )
        new_rows.append(row_new[:, 0].reshape(rows))
        return row_new, pairwise_sum(stats, "row")

    def col_stage(m, parts):
        col_new, pair = column_stage(extent, col_factor[m : m + 1], parts)
        new_columns.append(col_new)
        return col_new, exchange(pair, "col")

    flying = {}
    sums = stats = outs = None
    last = {}
    for j in range(-2, total_blocks + 2):
        m, b = divmod(j - 2, count)
        since = b + 1 if m >= 1 else None
        carries = {1: 0, 3: 1}.get(since)
        brings = {3: 0, 5: 1}.get(since)
        got = flying.pop(j, None)
        sent, sums, stats = step(
            j, total_blocks, me, pieces, got, sums, stats, brings, carries
        )
        if sent is not None:
            flying[j + 2] = [swap(sent[0], "dp", 1), swap(sent[1], "dp", 2)]
        if sums:
            me, *sums = tie(me, *sums)
        else:
            me, *_ = tie(me, *sent)
        if 0 <= m < mats - 1 and b == count - 1:
            row_new, stats = row_stage(m, sums)
            last = dict(m=m, row_new=row_new, summed=sums[1])
            me, stats = tie(me, stats)
        if since == 5:
            stats, me = tie(stats, me)
            col_new, pairs = col_stage(last["m"], [stats])
            outs = finish(
                last["m"], extent, last["row_new"], col_new, pairs, last["summed"], blocked, outs, 36
            )
            me, *outs = tie(me, *outs)

    row_new, stats = row_stage(mats - 1, sums)
    col_new, pairs = col_stage(mats - 1, exchange(stats, "dp"))
    new_params, update = finish(
        mats - 1, extent, row_new, col_new, pairs, sums[1], blocked, outs, 44
    )
    return (
        new_params.reshape(params.shape),
        update.reshape(params.shape),
        jnp.stack(new_rows),
        jnp.concatenate(new_columns, axis=0),
    )


def solution(mesh):
    placed = (
        P("dp", None, None, "row", None, "col"),
        P(None, ("dp", "row"), "col"),
        P(None, ("dp", "row")),
        P(None, "col"),
    )
    return jax.shard_map(
        per_device,
        mesh=mesh,
        in_specs=placed,
        out_specs=(
            P(None, ("dp", "row"), "col"),
            P(None, ("dp", "row"), "col"),
            P(None, ("dp", "row")),
            P(None, "col"),
        ),
        check_vma=False,
    )
```

time: 636 us -> 599 us (0.942)
  waiting for transfers between devices: 461 us -> 422 us
  starting transfers between devices: 47.1 us -> 61.9 us
  Pallas kernels: 101 us -> 93.9 us
  between operations: 7.76 us -> 0.93 us
    ppermute x40 -> x53, waiting for transfers between devices: 461 us -> 422 us  [swap(): return lax.ppermute(x, axes, [(i, i ^ mask) for i in range(size)])]
    ppermute x40 -> x53, starting transfers between devices: 47.1 us -> 61.9 us  [swap(): return lax.ppermute(x, axes, [(i, i ^ mask) for i in range(size)])]
    pallas_call x12 -> x20, Pallas kernels: 68.9 us -> 56.8 us  [step(): pl.pallas_call(functools.partial(step_kernel, takes, finishes, first, sen...]
    unnamed x14 -> x40, local copies, waits for them, and re-layouts: 13.4 us -> 16.1 us
  transfers between devices with their start and end apart: 40 -> 53, of which waited for: 28 -> 46; matrix products, arithmetic and copies ran while one was open for 0% -> 0% of each run, Pallas kernels for 13% -> 12%
where the time goes in v4:
time: 599 us; the launch traced here: 597 us
  waiting for transfers between devices  422 us (70%)
  Pallas kernels  93.9 us (16%)
  starting transfers between devices  61.9 us (10%)
  local copies, waits for them, and re-layouts  16.7 us (3%)
    ppermute x53, waiting for transfers between devices, swap(): return lax.ppermute(x, axes, [(i, i ^ mask) for i in range(size)])  422 us
    ppermute x53, starting transfers between devices, swap(): return lax.ppermute(x, axes, [(i, i ^ mask) for i in range(size)])  61.9 us
    pallas_call x20, Pallas kernels, step(): pl.pallas_call(functools.partial(step_kernel, takes, finishes, first, sen...  56.8 us
    pallas_call x2, Pallas kernels, finish(): pl.pallas_call(functools.partial(finish_kernel, m, min(part, finish_rows)...  29.7 us
    unnamed x40, local copies, waits for them, and re-layouts  16.1 us
  transfers between devices with their start and end apart: 53, of which 46 were waited for; matrix products, arithmetic and copies ran while one was open for 0% of the time, Pallas kernels for 12%

profile of v4, /device:TPU:0, one launch (start us, length us, event | category | flops | bytes accessed | tf_op | source)
XLA Modules:
  0.0 597.0 jit_solution(1105300325181539401)
XLA Ops:
  2.6 3.0 collective-permute-start
  9.8 8.6 %collective-permute-done.refs_1_ = f32[64,2048]{1,0:T(8,128)S(1)} collective-permute-done((f32[64,2048]{1,0:T(8,128)S(1)}, f32[64,2048]{1,0:T(8,128)S(1)}, u32[]{:S(2)}, u32[]{:S(2)}) %collective-permute-start) | collective-permute-done | bytes 524320 | tf_op jit(solution)/shard_map/ppermute | solution.py:25
  25.1 4.5 collective-permute-done.2.refs_1_
  36.3 27.0 %collective-permute-done.4.refs_1_ = f32[192,2048]{1,0:T(8,128)S(1)} collective-permute-done((f32[192,2048]{1,0:T(8,128)S(1)}, f32[192,2048]{1,0:T(8,128)S(1)}, u32[]{:S(2)}, u32[]{:S(2)}) %collective-permute-start.4) | collective-permute-done | bytes 1572896 | tf_op jit(solution)/shard_map/ppermute | solution.py:25
  65.4 3.0 step.24
  70.5 26.5 %collective-permute-done.6.refs_1_ = f32[192,2048]{1,0:T(8,128)S(1)} collective-permute-done((f32[192,2048]{1,0:T(8,128)S(1)}, f32[192,2048]{1,0:T(8,128)S(1)}, u32[]{:S(2)}, u32[]{:S(2)}) %collective-permute-start.6) | collective-permute-done | bytes 1572896 | tf_op jit(solution)/shard_map/ppermute | solution.py:25
  99.1 3.0 step.25
  104.2 26.5 %collective-permute-done.8.refs_1_ = f32[192,2048]{1,0:T(8,128)S(1)} collective-permute-done((f32[192,2048]{1,0:T(8,128)S(1)}, f32[192,2048]{1,0:T(8,128)S(1)}, u32[]{:S(2)}, u32[]{:S(2)}) %collective-permute-start.8) | collective-permute-done | bytes 1572896 | tf_op jit(solution)/shard_map/ppermute | solution.py:25
  137.9 26.5 %collective-permute-done.10.refs_1_ = f32[192,2048]{1,0:T(8,128)S(1)} collective-permute-done((f32[192,2048]{1,0:T(8,128)S(1)}, f32[192,2048]{1,0:T(8,128)S(1)}, u32[]{:S(2)}, u32[]{:S(2)}) %collective-permute-start.10) | collective-permute-done | bytes 1572896 | tf_op jit(solution)/shard_map/ppermute | solution.py:25
  171.7 26.5 %collective-permute-done.12.refs_1_ = f32[192,2048]{1,0:T(8,128)S(1)} collective-permute-done((f32[192,2048]{1,0:T(8,128)S(1)}, f32[192,2048]{1,0:T(8,128)S(1)}, u32[]{:S(2)}, u32[]{:S(2)}) %collective-permute-start.12) | collective-permute-done | bytes 1572896 | tf_op jit(solution)/shard_map/ppermute | solution.py:25
  205.4 26.5 %collective-permute-done.14.refs_1_ = f32[192,2048]{1,0:T(8,128)S(1)} collective-permute-done((f32[192,2048]{1,0:T(8,128)S(1)}, f32[192,2048]{1,0:T(8,128)S(1)}, u32[]{:S(2)}, u32[]{:S(2)}) %collective-permute-start.14) | collective-permute-done | bytes 1572896 | tf_op jit(solution)/shard_map/ppermute | solution.py:25
  239.1 26.5 %collective-permute-done.16.refs_1_ = f32[192,2048]{1,0:T(8,128)S(1)} collective-permute-done((f32[192,2048]{1,0:T(8,128)S(1)}, f32[192,2048]{1,0:T(8,128)S(1)}, u32[]{:S(2)}, u32[]{:S(2)}) %collective-permute-start.16) | collective-permute-done | bytes 1572896 | tf_op jit(solution)/shard_map/ppermute | solution.py:25
  272.8 26.5 %collective-permute-done.18.refs_1_ = f32[192,2048]{1,0:T(8,128)S(1)} collective-permute-done((f32[192,2048]{1,0:T(8,128)S(1)}, f32[192,2048]{1,0:T(8,128)S(1)}, u32[]{:S(2)}, u32[]{:S(2)}) %collective-permute-start.18) | collective-permute-done | bytes 1572896 | tf_op jit(solution)/shard_map/ppermute | solution.py:25
  306.5 3.6 collective-permute-start.22
  313.1 4.0 collective-permute-done.21.refs_2_
  324.3 8.7 %collective-permute-done.24.refs_1_ = f32[192,2048]{1,0:T(8,128)S(1)} collective-permute-done((f32[192,2048]{1,0:T(8,128)S(1)}, f32[192,2048]{1,0:T(8,128)S(1)}, u32[]{:S(2)}, u32[]{:S(2)}) %collective-permute-start.24) | collective-permute-done | bytes 1572896 | tf_op jit(solution)/shard_map/ppermute | solution.py:25
  335.1 3.0 step.32
  340.2 26.5 %collective-permute-done.26.refs_1_ = f32[192,2048]{1,0:T(8,128)S(1)} collective-permute-done((f32[192,2048]{1,0:T(8,128)S(1)}, f32[192,2048]{1,0:T(8,128)S(1)}, u32[]{:S(2)}, u32[]{:S(2)}) %collective-permute-start.26) | collective-permute-done | bytes 1572896 | tf_op jit(solution)/shard_map/ppermute | solution.py:25
  373.9 28.6 %collective-permute-done.29.refs_2_ = f32[192,2048]{1,0:T(8,128)S(1)} collective-permute-done((f32[192,2048]{1,0:T(8,128)S(1)}, f32[192,2048]{1,0:T(8,128)S(1)}, u32[]{:S(2)}, u32[]{:S(2)}) %collective-permute-start.29) | collective-permute-done | bytes 1572896 | tf_op jit(solution)/shard_map/ppermute | solution.py:25
  402.5 3.1 step.34
  408.5 27.0 %collective-permute-done.30.refs_1_ = f32[192,2048]{1,0:T(8,128)S(1)} collective-permute-done((f32[192,2048]{1,0:T(8,128)S(1)}, f32[192,2048]{1,0:T(8,128)S(1)}, u32[]{:S(2)}, u32[]{:S(2)}) %collective-permute-start.30) | collective-permute-done | bytes 1572896 | tf_op jit(solution)/shard_map/ppermute | solution.py:25
  436.2 4.6 step.35
  444.3 24.8 %collective-permute-done.32.refs_1_ = f32[192,2048]{1,0:T(8,128)S(1)} collective-permute-done((f32[192,2048]{1,0:T(8,128)S(1)}, f32[192,2048]{1,0:T(8,128)S(1)}, u32[]{:S(2)}, u32[]{:S(2)}) %collective-permute-start.32) | collective-permute-done | bytes 1572896 | tf_op jit(solution)/shard_map/ppermute | solution.py:25
  474.1 3.3 copy-done.2
  481.6 3.6 collective-permute-start.36
  491.4 3.4 copy-done.1
  496.2 15.3 %finish.2 = (f32[2,8,2,64,2048]{4,3,2,1,0:T(8,128)}, f32[2,8,2,64,2048]{4,3,2,1,0:T(8,128)}) custom-call(f32[8,8,128]{2,1,0:T(8,128)S(1)} %get-tuple-element.304.row_new, f32[1,2048]{1,0:T(1,128)S(1)} %copy-done.7, f32[8,2,64,2048]{3,2,1,0:T(8,128)S(1)} %copy-done.1, f32[2,8,2,64,2048]{4,3,2,1,0:T(8,128)} %bitcast.109, f32[8,128]{1,0:T(8,128)S(1)} %copy-done.10, ...), custom_call_target="tpu_custom_call" | custom-call | flops 8388608 | bytes 33554432 | tf_op jit(solution)/shard_map/finish/pallas_call | solution.py:318
  515.4 10.0 %collective-permute-done.39.refs_1_ = f32[128,2048]{1,0:T(8,128)S(1)} collective-permute-done((f32[128,2048]{1,0:T(8,128)}, f32[128,2048]{1,0:T(8,128)S(1)}, u32[]{:S(2)}, u32[]{:S(2)}) %collective-permute-start.39) | collective-permute-done | bytes 1048608 | tf_op jit(solution)/shard_map/ppermute | solution.py:25
  529.9 17.2 %collective-permute-done.41.refs_1_ = f32[128,2048]{1,0:T(8,128)S(1)} collective-permute-done((f32[128,2048]{1,0:T(8,128)S(1)}, f32[128,2048]{1,0:T(8,128)S(1)}, u32[]{:S(2)}, u32[]{:S(2)}) %collective-permute-start.41) | collective-permute-done | bytes 1048608 | tf_op jit(solution)/shard_map/ppermute | solution.py:25
  550.9 3.7 collective-permute-start.45
  577.8 3.4 copy-done.5
  582.6 14.4 %finish.3 = (f32[2,8,2,64,2048]{4,3,2,1,0:T(8,128)}, f32[2,8,2,64,2048]{4,3,2,1,0:T(8,128)}) custom-call(f32[8,8,128]{2,1,0:T(8,128)S(1)} %get-tuple-element.340.row_new, f32[1,2048]{1,0:T(1,128)S(1)} %copy-done.9, f32[8,2,64,2048]{3,2,1,0:T(8,128)S(1)} %copy-done.5, f32[2,8,2,64,2048]{4,3,2,1,0:T(8,128)} %bitcast.110, ...), custom_call_target="tpu_custom_call", output_to_operand_aliasing={{0}: (8, {}), {1}: (9, {})} | custom-call | flops 8388608 | bytes 33554432 | tf_op jit(solution)/shard_map/finish/pallas_call | solution.py:318
  (148 shorter events, 153.4 us)
Async XLA Ops:
  22.9 40.4 %collective-permute-start.4 = (f32[192,2048]{1,0:T(8,128)S(1)}, f32[192,2048]{1,0:T(8,128)S(1)}, u32[]{:S(2)}, u32[]{:S(2)}) collective-permute-start(f32[192,2048]{1,0:T(8,128)S(1)} %get-tuple-element.182), channel_id=1, source_target_pairs={{0,8},{8,0},{16,24},{24,16},{1,9},{9,1},{17,25},{25,17},{2,10},{10... | collective-permute-start | bytes 4718600 | tf_op jit(solution)/shard_map/ppermute | solution.py:25
  23.1 42.4 %collective-permute-start.5 = (f32[192,2048]{1,0:T(8,128)S(1)}, f32[192,2048]{1,0:T(8,128)S(1)}, u32[]{:S(2)}, u32[]{:S(2)}) collective-permute-start(f32[192,2048]{1,0:T(8,128)S(1)} %get-tuple-element.183), channel_id=1, source_target_pairs={{0,16},{8,24},{16,0},{24,8},{1,17},{9,25},{17,1},{25,9},{2,18},{10... | collective-permute-start | bytes 4718600 | tf_op jit(solution)/shard_map/ppermute | solution.py:25
  34.2 62.8 %collective-permute-start.6 = (f32[192,2048]{1,0:T(8,128)S(1)}, f32[192,2048]{1,0:T(8,128)S(1)}, u32[]{:S(2)}, u32[]{:S(2)}) collective-permute-start(f32[192,2048]{1,0:T(8,128)S(1)} %get-tuple-element.185), channel_id=1, source_target_pairs={{0,8},{8,0},{16,24},{24,16},{1,9},{9,1},{17,25},{25,17},{2,10},{10... | collective-permute-start | bytes 4718600 | tf_op jit(solution)/shard_map/ppermute | solution.py:25
  34.3 64.8 %collective-permute-start.7 = (f32[192,2048]{1,0:T(8,128)S(1)}, f32[192,2048]{1,0:T(8,128)S(1)}, u32[]{:S(2)}, u32[]{:S(2)}) collective-permute-start(f32[192,2048]{1,0:T(8,128)S(1)} %get-tuple-element.186), channel_id=1, source_target_pairs={{0,16},{8,24},{16,0},{24,8},{1,17},{9,25},{17,1},{25,9},{2,18},{10... | collective-permute-start | bytes 4718600 | tf_op jit(solution)/shard_map/ppermute | solution.py:25
  68.4 62.3 %collective-permute-start.8 = (f32[192,2048]{1,0:T(8,128)S(1)}, f32[192,2048]{1,0:T(8,128)S(1)}, u32[]{:S(2)}, u32[]{:S(2)}) collective-permute-start(f32[192,2048]{1,0:T(8,128)S(1)} %get-tuple-element.199), channel_id=1, source_target_pairs={{0,8},{8,0},{16,24},{24,16},{1,9},{9,1},{17,25},{25,17},{2,10},{10... | collective-permute-start | bytes 4718600 | tf_op jit(solution)/shard_map/ppermute | solution.py:25
  68.5 64.3 %collective-permute-start.9 = (f32[192,2048]{1,0:T(8,128)S(1)}, f32[192,2048]{1,0:T(8,128)S(1)}, u32[]{:S(2)}, u32[]{:S(2)}) collective-permute-start(f32[192,2048]{1,0:T(8,128)S(1)} %get-tuple-element.200), channel_id=1, source_target_pairs={{0,16},{8,24},{16,0},{24,8},{1,17},{9,25},{17,1},{25,9},{2,18},{10... | collective-permute-start | bytes 4718600 | tf_op jit(solution)/shard_map/ppermute | solution.py:25
  102.1 62.3 %collective-permute-start.10 = (f32[192,2048]{1,0:T(8,128)S(1)}, f32[192,2048]{1,0:T(8,128)S(1)}, u32[]{:S(2)}, u32[]{:S(2)}) collective-permute-start(f32[192,2048]{1,0:T(8,128)S(1)} %get-tuple-element.208), channel_id=1, source_target_pairs={{0,8},{8,0},{16,24},{24,16},{1,9},{9,1},{17,25},{25,17},{2,10},{10... | collective-permute-start | bytes 4718600 | tf_op jit(solution)/shard_map/ppermute | solution.py:25
  102.2 64.3 %collective-permute-start.11 = (f32[192,2048]{1,0:T(8,128)S(1)}, f32[192,2048]{1,0:T(8,128)S(1)}, u32[]{:S(2)}, u32[]{:S(2)}) collective-permute-start(f32[192,2048]{1,0:T(8,128)S(1)} %get-tuple-element.209), channel_id=1, source_target_pairs={{0,16},{8,24},{16,0},{24,8},{1,17},{9,25},{17,1},{25,9},{2,18},{10... | collective-permute-start | bytes 4718600 | tf_op jit(solution)/shard_map/ppermute | solution.py:25
  135.8 62.3 %collective-permute-start.12 = (f32[192,2048]{1,0:T(8,128)S(1)}, f32[192,2048]{1,0:T(8,128)S(1)}, u32[]{:S(2)}, u32[]{:S(2)}) collective-permute-start(f32[192,2048]{1,0:T(8,128)S(1)} %get-tuple-element.217), channel_id=1, source_target_pairs={{0,8},{8,0},{16,24},{24,16},{1,9},{9,1},{17,25},{25,17},{2,10},{10... | collective-permute-start | bytes 4718600 | tf_op jit(solution)/shard_map/ppermute | solution.py:25
  135.9 64.3 %collective-permute-start.13 = (f32[192,2048]{1,0:T(8,128)S(1)}, f32[192,2048]{1,0:T(8,128)S(1)}, u32[]{:S(2)}, u32[]{:S(2)}) collective-permute-start(f32[192,2048]{1,0:T(8,128)S(1)} %get-tuple-element.218), channel_id=1, source_target_pairs={{0,16},{8,24},{16,0},{24,8},{1,17},{9,25},{17,1},{25,9},{2,18},{10... | collective-permute-start | bytes 4718600 | tf_op jit(solution)/shard_map/ppermute | solution.py:25
  169.5 62.3 %collective-permute-start.14 = (f32[192,2048]{1,0:T(8,128)S(1)}, f32[192,2048]{1,0:T(8,128)S(1)}, u32[]{:S(2)}, u32[]{:S(2)}) collective-permute-start(f32[192,2048]{1,0:T(8,128)S(1)} %get-tuple-element.226), channel_id=1, source_target_pairs={{0,8},{8,0},{16,24},{24,16},{1,9},{9,1},{17,25},{25,17},{2,10},{10... | collective-permute-start | bytes 4718600 | tf_op jit(solution)/shard_map/ppermute | solution.py:25
  169.6 64.3 %collective-permute-start.15 = (f32[192,2048]{1,0:T(8,128)S(1)}, f32[192,2048]{1,0:T(8,128)S(1)}, u32[]{:S(2)}, u32[]{:S(2)}) collective-permute-start(f32[192,2048]{1,0:T(8,128)S(1)} %get-tuple-element.227), channel_id=1, source_target_pairs={{0,16},{8,24},{16,0},{24,8},{1,17},{9,25},{17,1},{25,9},{2,18},{10... | collective-permute-start | bytes 4718600 | tf_op jit(solution)/shard_map/ppermute | solution.py:25
  203.2 62.3 %collective-permute-start.16 = (f32[192,2048]{1,0:T(8,128)S(1)}, f32[192,2048]{1,0:T(8,128)S(1)}, u32[]{:S(2)}, u32[]{:S(2)}) collective-permute-start(f32[192,2048]{1,0:T(8,128)S(1)} %get-tuple-element.235), channel_id=1, source_target_pairs={{0,8},{8,0},{16,24},{24,16},{1,9},{9,1},{17,25},{25,17},{2,10},{10... | collective-permute-start | bytes 4718600 | tf_op jit(solution)/shard_map/ppermute | solution.py:25
  203.3 64.3 %collective-permute-start.17 = (f32[192,2048]{1,0:T(8,128)S(1)}, f32[192,2048]{1,0:T(8,128)S(1)}, u32[]{:S(2)}, u32[]{:S(2)}) collective-permute-start(f32[192,2048]{1,0:T(8,128)S(1)} %get-tuple-element.236), channel_id=1, source_target_pairs={{0,16},{8,24},{16,0},{24,8},{1,17},{9,25},{17,1},{25,9},{2,18},{10... | collective-permute-start | bytes 4718600 | tf_op jit(solution)/shard_map/ppermute | solution.py:25
  236.9 62.3 %collective-permute-start.18 = (f32[192,2048]{1,0:T(8,128)S(1)}, f32[192,2048]{1,0:T(8,128)S(1)}, u32[]{:S(2)}, u32[]{:S(2)}) collective-permute-start(f32[192,2048]{1,0:T(8,128)S(1)} %get-tuple-element.244), channel_id=1, source_target_pairs={{0,8},{8,0},{16,24},{24,16},{1,9},{9,1},{17,25},{25,17},{2,10},{10... | collective-permute-start | bytes 4718600 | tf_op jit(solution)/shard_map/ppermute | solution.py:25
  237.1 64.3 %collective-permute-start.19 = (f32[192,2048]{1,0:T(8,128)S(1)}, f32[192,2048]{1,0:T(8,128)S(1)}, u32[]{:S(2)}, u32[]{:S(2)}) collective-permute-start(f32[192,2048]{1,0:T(8,128)S(1)} %get-tuple-element.245), channel_id=1, source_target_pairs={{0,16},{8,24},{16,0},{24,8},{1,17},{9,25},{17,1},{25,9},{2,18},{10... | collective-permute-start | bytes 4718600 | tf_op jit(solution)/shard_map/ppermute | solution.py:25
  270.7 62.3 %collective-permute-start.24 = (f32[192,2048]{1,0:T(8,128)S(1)}, f32[192,2048]{1,0:T(8,128)S(1)}, u32[]{:S(2)}, u32[]{:S(2)}) collective-permute-start(f32[192,2048]{1,0:T(8,128)S(1)} %get-tuple-element.258), channel_id=1, source_target_pairs={{0,8},{8,0},{16,24},{24,16},{1,9},{9,1},{17,25},{25,17},{2,10},{10... | collective-permute-start | bytes 4718600 | tf_op jit(solution)/shard_map/ppermute | solution.py:25
  270.8 64.3 %collective-permute-start.25 = (f32[192,2048]{1,0:T(8,128)S(1)}, f32[192,2048]{1,0:T(8,128)S(1)}, u32[]{:S(2)}, u32[]{:S(2)}) collective-permute-start(f32[192,2048]{1,0:T(8,128)S(1)} %get-tuple-element.259), channel_id=1, source_target_pairs={{0,16},{8,24},{16,0},{24,8},{1,17},{9,25},{17,1},{25,9},{2,18},{10... | collective-permute-start | bytes 4718600 | tf_op jit(solution)/shard_map/ppermute | solution.py:25
  304.4 62.3 %collective-permute-start.26 = (f32[192,2048]{1,0:T(8,128)S(1)}, f32[192,2048]{1,0:T(8,128)S(1)}, u32[]{:S(2)}, u32[]{:S(2)}) collective-permute-start(f32[192,2048]{1,0:T(8,128)S(1)} %get-tuple-element.265), channel_id=1, source_target_pairs={{0,8},{8,0},{16,24},{24,16},{1,9},{9,1},{17,25},{25,17},{2,10},{10... | collective-permute-start | bytes 4718600 | tf_op jit(solution)/shard_map/ppermute | solution.py:25
  304.5 64.3 %collective-permute-start.27 = (f32[192,2048]{1,0:T(8,128)S(1)}, f32[192,2048]{1,0:T(8,128)S(1)}, u32[]{:S(2)}, u32[]{:S(2)}) collective-permute-start(f32[192,2048]{1,0:T(8,128)S(1)} %get-tuple-element.266), channel_id=1, source_target_pairs={{0,16},{8,24},{16,0},{24,8},{1,17},{9,25},{17,1},{25,9},{2,18},{10... | collective-permute-start | bytes 4718600 | tf_op jit(solution)/shard_map/ppermute | solution.py:25
  338.1 64.4 %collective-permute-start.28 = (f32[200,2048]{1,0:T(8,128)S(1)}, f32[200,2048]{1,0:T(8,128)S(1)}, u32[]{:S(2)}, u32[]{:S(2)}) collective-permute-start(f32[200,2048]{1,0:T(8,128)S(1)} %get-tuple-element.274), channel_id=1, source_target_pairs={{0,8},{8,0},{16,24},{24,16},{1,9},{9,1},{17,25},{25,17},{2,10},{10... | collective-permute-start | bytes 4915208 | tf_op jit(solution)/shard_map/ppermute | solution.py:25
  338.2 64.3 %collective-permute-start.29 = (f32[192,2048]{1,0:T(8,128)S(1)}, f32[192,2048]{1,0:T(8,128)S(1)}, u32[]{:S(2)}, u32[]{:S(2)}) collective-permute-start(f32[192,2048]{1,0:T(8,128)S(1)} %get-tuple-element.275), channel_id=1, source_target_pairs={{0,16},{8,24},{16,0},{24,8},{1,17},{9,25},{17,1},{25,9},{2,18},{10... | collective-permute-start | bytes 4718600 | tf_op jit(solution)/shard_map/ppermute | solution.py:25
  371.8 63.7 %collective-permute-start.30 = (f32[192,2048]{1,0:T(8,128)S(1)}, f32[192,2048]{1,0:T(8,128)S(1)}, u32[]{:S(2)}, u32[]{:S(2)}) collective-permute-start(f32[192,2048]{1,0:T(8,128)S(1)} %get-tuple-element.283), channel_id=1, source_target_pairs={{0,8},{8,0},{16,24},{24,16},{1,9},{9,1},{17,25},{25,17},{2,10},{10... | collective-permute-start | bytes 4718600 | tf_op jit(solution)/shard_map/ppermute | solution.py:25
  371.9 64.3 %collective-permute-start.31 = (f32[192,2048]{1,0:T(8,128)S(1)}, f32[192,2048]{1,0:T(8,128)S(1)}, u32[]{:S(2)}, u32[]{:S(2)}) collective-permute-start(f32[192,2048]{1,0:T(8,128)S(1)} %get-tuple-element.284), channel_id=1, source_target_pairs={{0,16},{8,24},{16,0},{24,8},{1,17},{9,25},{17,1},{25,9},{2,18},{10... | collective-permute-start | bytes 4718600 | tf_op jit(solution)/shard_map/ppermute | solution.py:25
  405.6 65.7 %collective-permute-start.33 = (f32[200,2048]{1,0:T(8,128)S(1)}, f32[200,2048]{1,0:T(8,128)S(1)}, u32[]{:S(2)}, u32[]{:S(2)}) collective-permute-start(f32[200,2048]{1,0:T(8,128)S(1)} %get-tuple-element.293), channel_id=1, source_target_pairs={{0,16},{8,24},{16,0},{24,8},{1,17},{9,25},{17,1},{25,9},{2,18},{10... | collective-permute-start | bytes 4915208 | tf_op jit(solution)/shard_map/ppermute | solution.py:25
  407.1 62.1 %collective-permute-start.32 = (f32[192,2048]{1,0:T(8,128)S(1)}, f32[192,2048]{1,0:T(8,128)S(1)}, u32[]{:S(2)}, u32[]{:S(2)}) collective-permute-start(f32[192,2048]{1,0:T(8,128)S(1)} %get-tuple-element.292), channel_id=1, source_target_pairs={{0,8},{8,0},{16,24},{24,16},{1,9},{9,1},{17,25},{25,17},{2,10},{10... | collective-permute-start | bytes 4718600 | tf_op jit(solution)/shard_map/ppermute | solution.py:25
  440.8 70.7 %collective-permute-start.37 = (f32[192,2048]{1,0:T(8,128)}, f32[192,2048]{1,0:T(8,128)S(1)}, u32[]{:S(2)}, u32[]{:S(2)}) collective-permute-start(f32[192,2048]{1,0:T(8,128)} %get-tuple-element.311), channel_id=1, source_target_pairs={{0,8},{8,0},{16,24},{24,16},{1,9},{9,1},{17,25},{25,17},{2,10},{10... | collective-permute-start | bytes 4718600 | tf_op jit(solution)/shard_map/ppermute | solution.py:25
  442.2 69.3 %collective-permute-start.38 = (f32[192,2048]{1,0:T(8,128)}, f32[192,2048]{1,0:T(8,128)S(1)}, u32[]{:S(2)}, u32[]{:S(2)}) collective-permute-start(f32[192,2048]{1,0:T(8,128)} %get-tuple-element.312), channel_id=1, source_target_pairs={{0,16},{8,24},{16,0},{24,8},{1,17},{9,25},{17,1},{25,9},{2,18},{10... | collective-permute-start | bytes 4718600 | tf_op jit(solution)/shard_map/ppermute | solution.py:25
  487.2 38.2 %collective-permute-start.39 = (f32[128,2048]{1,0:T(8,128)}, f32[128,2048]{1,0:T(8,128)S(1)}, u32[]{:S(2)}, u32[]{:S(2)}) collective-permute-start(f32[128,2048]{1,0:T(8,128)} %copy-done.13), channel_id=1, source_target_pairs={{0,8},{8,0},{16,24},{24,16},{1,9},{9,1},{17,25},{25,17},{2,10},{10... | collective-permute-start | bytes 3145736 | tf_op jit(solution)/shard_map/ppermute | solution.py:25
  489.9 37.6 %collective-permute-start.40 = (f32[128,2048]{1,0:T(8,128)}, f32[128,2048]{1,0:T(8,128)S(1)}, u32[]{:S(2)}, u32[]{:S(2)}) collective-permute-start(f32[128,2048]{1,0:T(8,128)} %copy-done.12), channel_id=1, source_target_pairs={{0,16},{8,24},{16,0},{24,8},{1,17},{9,25},{17,1},{25,9},{2,18},{10... | collective-permute-start | bytes 3145736 | tf_op jit(solution)/shard_map/ppermute | solution.py:25
  514.3 32.7 %collective-permute-start.41 = (f32[128,2048]{1,0:T(8,128)S(1)}, f32[128,2048]{1,0:T(8,128)S(1)}, u32[]{:S(2)}, u32[]{:S(2)}) collective-permute-start(f32[128,2048]{1,0:T(8,128)S(1)} %get-tuple-element.329), channel_id=1, source_target_pairs={{0,8},{8,0},{16,24},{24,16},{1,9},{9,1},{17,25},{25,17},{2,10},{10... | collective-permute-start | bytes 3145736 | tf_op jit(solution)/shard_map/ppermute | solution.py:25
  514.9 33.6 %collective-permute-start.42 = (f32[128,2048]{1,0:T(8,128)S(1)}, f32[128,2048]{1,0:T(8,128)S(1)}, u32[]{:S(2)}, u32[]{:S(2)}) collective-permute-start(f32[128,2048]{1,0:T(8,128)S(1)} %get-tuple-element.330), channel_id=1, source_target_pairs={{0,16},{8,24},{16,0},{24,8},{1,17},{9,25},{17,1},{25,9},{2,18},{10... | collective-permute-start | bytes 3145736 | tf_op jit(solution)/shard_map/ppermute | solution.py:25
  (41 other events, 318.0 us)

commit v5 on v4

--- a/solution.py
+++ b/solution.py
@@ -16,7 +16,6 @@
 sublanes = 8
 blocks_of_matrix = 8
 tile_rows = 16
-finish_rows = 64
 f32 = jnp.float32
 
 
@@ -278,61 +277,58 @@
             jax.ShapeDtypeStruct(factor.shape, f32),
             jax.ShapeDtypeStruct((sublanes, lanes), f32),
         ],
+        compiler_params=params_of(4),
         name="column",
     )(factor, *parts)
 
 
-def finish_kernel(m, tile, extent, partners, row_new, col_new, summed, params, *refs):
-    pairs, (new_params, update, column, by_col) = refs[:partners], refs[-4:]
+def finish_kernel(m, extent, row_new, col_new, total, pair, summed, params, *refs):
+    new_params, update, column, by_col = refs[-4:]
     count, _, part, width = summed.shape
-    row_level = pairs[0][1:2, 0:1]
-    total = tree_sum([x[0:1, 0:1] for x in pairs]) * row_level
-    spread = jnp.sqrt(total / (extent * extent))
+    row_level = pair[1:2, 0:1]
+    spread = jnp.sqrt(total[0:1, 0:1] * row_level / (extent * extent))
     factor = jnp.sqrt(row_level) / jnp.maximum(1.0, spread / clip_limit)
     by_col[...] = lax.rsqrt(col_new[...])
     for i in range(count):
         column[i] = jnp.transpose(lax.rsqrt(row_new[i]) * factor)
 
-    def body(x, p, new_p, moved):
-        i, half, t = (pl.program_id(axis) for axis in range(3))
-        start = pl.multiple_of(half * part + t * tile, sublanes)
-        y = x[...] * column[i, pl.ds(start, tile)][:, 0:1] * by_col[...]
-        moved[...] = y
-        new_p[...] = p[...] - learn_rate * y
-
-    of_sum = pl.BlockSpec((None, None, tile, width), lambda i, h, t: (i, h, t, 0))
-    of_matrix = pl.BlockSpec((None, None, None, tile, width), lambda i, h, t: (m, i, h, t, 0))
+    def body(p, new_p, moved):
+        i = pl.program_id(0)
+        for half in range(2):
+            for r in range(0, part, sublanes):
+                at = half * part + r
+                mine = column[i, at : at + sublanes][:, 0:1]
+                y = summed[i, half, r : r + sublanes] * mine * by_col[...]
+                moved[half, r : r + sublanes] = y
+                new_p[half, r : r + sublanes] = p[half, r : r + sublanes] - learn_rate * y
+
+    of_matrix = pl.BlockSpec((None, None, 2, part, width), lambda i: (m, i, 0, 0, 0))
     pltpu.emit_pipeline(
-        body,
-        grid=(count, 2, part // tile),
-        in_specs=[of_sum, of_matrix],
-        out_specs=[of_matrix] * 2,
-    )(summed, params, new_params, update)
-
-
-def finish(m, extent, row_new, col_new, pairs, summed, params, outs, mib):
+        body, grid=(count,), in_specs=[of_matrix], out_specs=[of_matrix] * 2
+    )(params, new_params, update)
+
+
+def finish(m, extent, row_new, col_new, pair, summed, params, outs, mib):
     count, _, part, width = summed.shape
     held = () if outs is None else outs
     in_hbm = pl.BlockSpec(memory_space=pltpu.HBM)
     in_vmem = pl.BlockSpec(memory_space=pltpu.VMEM)
     return pl.pallas_call(
-        functools.partial(finish_kernel, m, min(part, finish_rows), extent, len(pairs)),
-        in_specs=[in_vmem, in_vmem, pl.BlockSpec(memory_space=pl.ANY), in_hbm]
-        + [in_vmem] * len(pairs)
-        + [in_hbm] * len(held),
+        functools.partial(finish_kernel, m, extent),
+        in_specs=[in_vmem] * 5 + [in_hbm] * (1 + len(held)),
         out_specs=[in_hbm] * 2,
         out_shape=[jax.ShapeDtypeStruct(params.shape, f32)] * 2,
         scratch_shapes=[
             pltpu.VMEM((count, 2 * part, sublanes), f32),
             pltpu.VMEM((1, width), f32),
         ],
-        input_output_aliases={4 + len(pairs) + i: i for i in range(len(held))},
+        input_output_aliases={6 + i: i for i in range(len(held))},
         compiler_params=params_of(mib),
         cost_estimate=pl.CostEstimate(
             flops=4 * summed.size, bytes_accessed=16 * summed.size, transcendentals=0
         ),
         name="finish",
-    )(row_new, col_new, summed, params, *pairs, *held)
+    )(row_new, col_new, *pair, summed, params, *held)
 
 
 def per_device(partials, params, row_factor, col_factor):
@@ -349,7 +345,7 @@
     def row_stage(m, sums):
         cols, summed, rows_along = sums
         row_new, stats = weighted_sums(
-            extent, exchange(rows_along, "col"), row_factor[m], cols, summed
+            extent, [pairwise_sum(rows_along, "col")], row_factor[m], cols, summed
         )
         new_rows.append(row_new[:, 0].reshape(rows))
         return row_new, pairwise_sum(stats, "row")
@@ -357,7 +353,8 @@
     def col_stage(m, parts):
         col_new, pair = column_stage(extent, col_factor[m : m + 1], parts)
         new_columns.append(col_new)
-        return col_new, exchange(pair, "col")
+        total = pairwise_sum(pair[0:1], "col")
+        return col_new, (total, pair)
 
     flying = {}
     sums = stats = outs = None

time: 599 us -> 590 us (0.985)
  waiting for transfers between devices: 422 us -> 441 us
  local copies, waits for them, and re-layouts: 16.7 us -> 0.06 us
  Pallas kernels: 93.9 us -> 84.8 us
    ppermute x53 -> x49, waiting for transfers between devices: 422 us -> 441 us  [swap(): return lax.ppermute(x, axes, [(i, i ^ mask) for i in range(size)])]
    unnamed x40 -> x10, local copies, waits for them, and re-layouts: 16.1 us -> 0.02 us
    pallas_call x2, Pallas kernels: 29.7 us -> 21.8 us  [finish(): pl.pallas_call(functools.partial(finish_kernel, m, extent), in_specs=[in_...]
    ppermute x53 -> x49, starting transfers between devices: 61.9 us -> 60.9 us  [swap(): return lax.ppermute(x, axes, [(i, i ^ mask) for i in range(size)])]
  transfers between devices with their start and end apart: 53 -> 49, of which waited for: 46 -> 47; matrix products, arithmetic and copies ran while one was open for 0% -> 0% of each run, Pallas kernels for 12% -> 11%
where the time goes in v5:
time: 590 us; the launch traced here: 589 us
  waiting for transfers between devices  441 us (75%)
  Pallas kernels  84.8 us (14%)
  starting transfers between devices  60.9 us (10%)
    ppermute x49, waiting for transfers between devices, swap(): return lax.ppermute(x, axes, [(i, i ^ mask) for i in range(size)])  441 us
    ppermute x49, starting transfers between devices, swap(): return lax.ppermute(x, axes, [(i, i ^ mask) for i in range(size)])  60.9 us
    pallas_call x20, Pallas kernels, step(): pl.pallas_call(functools.partial(step_kernel, takes, finishes, first, sen...  58.6 us
    pallas_call x2, Pallas kernels, finish(): pl.pallas_call(functools.partial(finish_kernel, m, extent), in_specs=[in_...  21.8 us
  transfers between devices with their start and end apart: 49, of which 47 were waited for; matrix products, arithmetic and copies ran while one was open for 0% of the time, Pallas kernels for 11%

profile of v5, /device:TPU:0, one launch (start us, length us, event | category | flops | bytes accessed | tf_op | source)
XLA Modules:
  0.0 588.6 jit_solution(5157105640991222257)
XLA Ops:
  2.6 3.0 collective-permute-start
  9.8 8.6 %collective-permute-done.refs_1_ = f32[64,2048]{1,0:T(8,128)S(1)} collective-permute-done((f32[64,2048]{1,0:T(8,128)S(1)}, f32[64,2048]{1,0:T(8,128)S(1)}, u32[]{:S(2)}, u32[]{:S(2)}) %collective-permute-start) | collective-permute-done | bytes 524320 | tf_op jit(solution)/shard_map/ppermute | solution.py:24
  25.1 4.5 collective-permute-done.2.refs_1_
  36.3 27.0 %collective-permute-done.4.refs_1_ = f32[192,2048]{1,0:T(8,128)S(1)} collective-permute-done((f32[192,2048]{1,0:T(8,128)S(1)}, f32[192,2048]{1,0:T(8,128)S(1)}, u32[]{:S(2)}, u32[]{:S(2)}) %collective-permute-start.4) | collective-permute-done | bytes 1572896 | tf_op jit(solution)/shard_map/ppermute | solution.py:24
  65.4 3.0 step.24
  70.5 26.5 %collective-permute-done.6.refs_1_ = f32[192,2048]{1,0:T(8,128)S(1)} collective-permute-done((f32[192,2048]{1,0:T(8,128)S(1)}, f32[192,2048]{1,0:T(8,128)S(1)}, u32[]{:S(2)}, u32[]{:S(2)}) %collective-permute-start.6) | collective-permute-done | bytes 1572896 | tf_op jit(solution)/shard_map/ppermute | solution.py:24
  104.2 26.5 %collective-permute-done.8.refs_1_ = f32[192,2048]{1,0:T(8,128)S(1)} collective-permute-done((f32[192,2048]{1,0:T(8,128)S(1)}, f32[192,2048]{1,0:T(8,128)S(1)}, u32[]{:S(2)}, u32[]{:S(2)}) %collective-permute-start.8) | collective-permute-done | bytes 1572896 | tf_op jit(solution)/shard_map/ppermute | solution.py:24
  132.8 3.0 step.26
  138.0 26.5 %collective-permute-done.10.refs_1_ = f32[192,2048]{1,0:T(8,128)S(1)} collective-permute-done((f32[192,2048]{1,0:T(8,128)S(1)}, f32[192,2048]{1,0:T(8,128)S(1)}, u32[]{:S(2)}, u32[]{:S(2)}) %collective-permute-start.10) | collective-permute-done | bytes 1572896 | tf_op jit(solution)/shard_map/ppermute | solution.py:24
  166.5 3.0 step.27
  171.7 26.5 %collective-permute-done.12.refs_1_ = f32[192,2048]{1,0:T(8,128)S(1)} collective-permute-done((f32[192,2048]{1,0:T(8,128)S(1)}, f32[192,2048]{1,0:T(8,128)S(1)}, u32[]{:S(2)}, u32[]{:S(2)}) %collective-permute-start.12) | collective-permute-done | bytes 1572896 | tf_op jit(solution)/shard_map/ppermute | solution.py:24
  200.2 3.0 step.28
  205.4 26.5 %collective-permute-done.14.refs_1_ = f32[192,2048]{1,0:T(8,128)S(1)} collective-permute-done((f32[192,2048]{1,0:T(8,128)S(1)}, f32[192,2048]{1,0:T(8,128)S(1)}, u32[]{:S(2)}, u32[]{:S(2)}) %collective-permute-start.14) | collective-permute-done | bytes 1572896 | tf_op jit(solution)/shard_map/ppermute | solution.py:24
  233.9 3.0 step.29
  239.1 26.5 %collective-permute-done.16.refs_1_ = f32[192,2048]{1,0:T(8,128)S(1)} collective-permute-done((f32[192,2048]{1,0:T(8,128)S(1)}, f32[192,2048]{1,0:T(8,128)S(1)}, u32[]{:S(2)}, u32[]{:S(2)}) %collective-permute-start.16) | collective-permute-done | bytes 1572896 | tf_op jit(solution)/shard_map/ppermute | solution.py:24
  267.7 3.0 step.30
  272.8 26.5 %collective-permute-done.18.refs_1_ = f32[192,2048]{1,0:T(8,128)S(1)} collective-permute-done((f32[192,2048]{1,0:T(8,128)S(1)}, f32[192,2048]{1,0:T(8,128)S(1)}, u32[]{:S(2)}, u32[]{:S(2)}) %collective-permute-start.18) | collective-permute-done | bytes 1572896 | tf_op jit(solution)/shard_map/ppermute | solution.py:24
  301.4 3.0 step.31
  318.6 14.3 %collective-permute-done.23.refs_1_ = f32[192,2048]{1,0:T(8,128)S(1)} collective-permute-done((f32[192,2048]{1,0:T(8,128)S(1)}, f32[192,2048]{1,0:T(8,128)S(1)}, u32[]{:S(2)}, u32[]{:S(2)}) %collective-permute-start.23) | collective-permute-done | bytes 1572896 | tf_op jit(solution)/shard_map/ppermute | solution.py:24
  335.1 3.0 step.32
  340.2 26.5 %collective-permute-done.25.refs_1_ = f32[192,2048]{1,0:T(8,128)S(1)} collective-permute-done((f32[192,2048]{1,0:T(8,128)S(1)}, f32[192,2048]{1,0:T(8,128)S(1)}, u32[]{:S(2)}, u32[]{:S(2)}) %collective-permute-start.25) | collective-permute-done | bytes 1572896 | tf_op jit(solution)/shard_map/ppermute | solution.py:24
  373.9 28.6 %collective-permute-done.28.refs_2_ = f32[192,2048]{1,0:T(8,128)S(1)} collective-permute-done((f32[192,2048]{1,0:T(8,128)S(1)}, f32[192,2048]{1,0:T(8,128)S(1)}, u32[]{:S(2)}, u32[]{:S(2)}) %collective-permute-start.28) | collective-permute-done | bytes 1572896 | tf_op jit(solution)/shard_map/ppermute | solution.py:24
  402.5 3.1 step.34
  408.5 27.0 %collective-permute-done.29.refs_1_ = f32[192,2048]{1,0:T(8,128)S(1)} collective-permute-done((f32[192,2048]{1,0:T(8,128)S(1)}, f32[192,2048]{1,0:T(8,128)S(1)}, u32[]{:S(2)}, u32[]{:S(2)}) %collective-permute-start.29) | collective-permute-done | bytes 1572896 | tf_op jit(solution)/shard_map/ppermute | solution.py:24
  436.2 4.6 step.35
  443.7 25.5 %collective-permute-done.31.refs_1_ = f32[192,2048]{1,0:T(8,128)S(1)} collective-permute-done((f32[192,2048]{1,0:T(8,128)S(1)}, f32[192,2048]{1,0:T(8,128)S(1)}, u32[]{:S(2)}, u32[]{:S(2)}) %collective-permute-start.31) | collective-permute-done | bytes 1572896 | tf_op jit(solution)/shard_map/ppermute | solution.py:24
  471.3 4.6 step.36
  484.3 10.9 %finish.2 = (f32[2,8,2,64,2048]{4,3,2,1,0:T(8,128)}, f32[2,8,2,64,2048]{4,3,2,1,0:T(8,128)}) custom-call(f32[8,8,128]{2,1,0:T(8,128)S(1)} %get-tuple-element.304.row_new, f32[1,2048]{1,0:T(1,128)S(1)} %get-tuple-element.306.col_new, f32[1,128]{1,0:T(1,128)S(1)} %add.34.total, f32[8,128]{1,0:T(8,128)S(1)} %get-tuple-element.307.pair, ...), custom_call_target="tpu_custom_call" | custom-call | flops 8388608 | bytes 33554432 | tf_op jit(solution)/shard_map/finish/pallas_call | solution.py:316
  495.2 7.7 %collective-permute-done.35.refs_1_ = f32[192,2048]{1,0:T(8,128)S(1)} collective-permute-done((f32[192,2048]{1,0:T(8,128)}, f32[192,2048]{1,0:T(8,128)S(1)}, u32[]{:S(2)}, u32[]{:S(2)}) %collective-permute-start.35) | collective-permute-done | bytes 1572896 | tf_op jit(solution)/shard_map/ppermute | solution.py:24
  509.9 15.5 %collective-permute-done.37.refs_1_ = f32[128,2048]{1,0:T(8,128)S(1)} collective-permute-done((f32[128,2048]{1,0:T(8,128)}, f32[128,2048]{1,0:T(8,128)S(1)}, u32[]{:S(2)}, u32[]{:S(2)}) %collective-permute-start.37) | collective-permute-done | bytes 1048608 | tf_op jit(solution)/shard_map/ppermute | solution.py:24
  529.9 17.2 %collective-permute-done.39.refs_1_ = f32[128,2048]{1,0:T(8,128)S(1)} collective-permute-done((f32[128,2048]{1,0:T(8,128)S(1)}, f32[128,2048]{1,0:T(8,128)S(1)}, u32[]{:S(2)}, u32[]{:S(2)}) %collective-permute-start.39) | collective-permute-done | bytes 1048608 | tf_op jit(solution)/shard_map/ppermute | solution.py:24
  577.7 10.9 %finish.3 = (f32[2,8,2,64,2048]{4,3,2,1,0:T(8,128)}, f32[2,8,2,64,2048]{4,3,2,1,0:T(8,128)}) custom-call(f32[8,8,128]{2,1,0:T(8,128)S(1)} %get-tuple-element.340.row_new, f32[1,2048]{1,0:T(1,128)S(1)} %get-tuple-element.342.col_new, f32[1,128]{1,0:T(1,128)S(1)} %add.39.total, ...), custom_call_target="tpu_custom_call", output_to_operand_aliasing={{0}: (6, {}), {1}: (7, {})} | custom-call | flops 8388608 | bytes 33554432 | tf_op jit(solution)/shard_map/finish/pallas_call | solution.py:316
  (121 shorter events, 138.8 us)
Async XLA Ops:
  22.9 40.4 %collective-permute-start.4 = (f32[192,2048]{1,0:T(8,128)S(1)}, f32[192,2048]{1,0:T(8,128)S(1)}, u32[]{:S(2)}, u32[]{:S(2)}) collective-permute-start(f32[192,2048]{1,0:T(8,128)S(1)} %get-tuple-element.182), channel_id=1, source_target_pairs={{0,8},{8,0},{16,24},{24,16},{1,9},{9,1},{17,25},{25,17},{2,10},{10... | collective-permute-start | bytes 4718600 | tf_op jit(solution)/shard_map/ppermute | solution.py:24
  23.1 42.4 %collective-permute-start.5 = (f32[192,2048]{1,0:T(8,128)S(1)}, f32[192,2048]{1,0:T(8,128)S(1)}, u32[]{:S(2)}, u32[]{:S(2)}) collective-permute-start(f32[192,2048]{1,0:T(8,128)S(1)} %get-tuple-element.183), channel_id=1, source_target_pairs={{0,16},{8,24},{16,0},{24,8},{1,17},{9,25},{17,1},{25,9},{2,18},{10... | collective-permute-start | bytes 4718600 | tf_op jit(solution)/shard_map/ppermute | solution.py:24
  34.2 62.8 %collective-permute-start.6 = (f32[192,2048]{1,0:T(8,128)S(1)}, f32[192,2048]{1,0:T(8,128)S(1)}, u32[]{:S(2)}, u32[]{:S(2)}) collective-permute-start(f32[192,2048]{1,0:T(8,128)S(1)} %get-tuple-element.185), channel_id=1, source_target_pairs={{0,8},{8,0},{16,24},{24,16},{1,9},{9,1},{17,25},{25,17},{2,10},{10... | collective-permute-start | bytes 4718600 | tf_op jit(solution)/shard_map/ppermute | solution.py:24
  34.3 64.8 %collective-permute-start.7 = (f32[192,2048]{1,0:T(8,128)S(1)}, f32[192,2048]{1,0:T(8,128)S(1)}, u32[]{:S(2)}, u32[]{:S(2)}) collective-permute-start(f32[192,2048]{1,0:T(8,128)S(1)} %get-tuple-element.186), channel_id=1, source_target_pairs={{0,16},{8,24},{16,0},{24,8},{1,17},{9,25},{17,1},{25,9},{2,18},{10... | collective-permute-start | bytes 4718600 | tf_op jit(solution)/shard_map/ppermute | solution.py:24
  68.4 62.3 %collective-permute-start.8 = (f32[192,2048]{1,0:T(8,128)S(1)}, f32[192,2048]{1,0:T(8,128)S(1)}, u32[]{:S(2)}, u32[]{:S(2)}) collective-permute-start(f32[192,2048]{1,0:T(8,128)S(1)} %get-tuple-element.199), channel_id=1, source_target_pairs={{0,8},{8,0},{16,24},{24,16},{1,9},{9,1},{17,25},{25,17},{2,10},{10... | collective-permute-start | bytes 4718600 | tf_op jit(solution)/shard_map/ppermute | solution.py:24
  68.5 64.3 %collective-permute-start.9 = (f32[192,2048]{1,0:T(8,128)S(1)}, f32[192,2048]{1,0:T(8,128)S(1)}, u32[]{:S(2)}, u32[]{:S(2)}) collective-permute-start(f32[192,2048]{1,0:T(8,128)S(1)} %get-tuple-element.200), channel_id=1, source_target_pairs={{0,16},{8,24},{16,0},{24,8},{1,17},{9,25},{17,1},{25,9},{2,18},{10... | collective-permute-start | bytes 4718600 | tf_op jit(solution)/shard_map/ppermute | solution.py:24
  102.1 62.3 %collective-permute-start.10 = (f32[192,2048]{1,0:T(8,128)S(1)}, f32[192,2048]{1,0:T(8,128)S(1)}, u32[]{:S(2)}, u32[]{:S(2)}) collective-permute-start(f32[192,2048]{1,0:T(8,128)S(1)} %get-tuple-element.208), channel_id=1, source_target_pairs={{0,8},{8,0},{16,24},{24,16},{1,9},{9,1},{17,25},{25,17},{2,10},{10... | collective-permute-start | bytes 4718600 | tf_op jit(solution)/shard_map/ppermute | solution.py:24
  102.2 64.3 %collective-permute-start.11 = (f32[192,2048]{1,0:T(8,128)S(1)}, f32[192,2048]{1,0:T(8,128)S(1)}, u32[]{:S(2)}, u32[]{:S(2)}) collective-permute-start(f32[192,2048]{1,0:T(8,128)S(1)} %get-tuple-element.209), channel_id=1, source_target_pairs={{0,16},{8,24},{16,0},{24,8},{1,17},{9,25},{17,1},{25,9},{2,18},{10... | collective-permute-start | bytes 4718600 | tf_op jit(solution)/shard_map/ppermute | solution.py:24
  135.8 62.3 %collective-permute-start.12 = (f32[192,2048]{1,0:T(8,128)S(1)}, f32[192,2048]{1,0:T(8,128)S(1)}, u32[]{:S(2)}, u32[]{:S(2)}) collective-permute-start(f32[192,2048]{1,0:T(8,128)S(1)} %get-tuple-element.217), channel_id=1, source_target_pairs={{0,8},{8,0},{16,24},{24,16},{1,9},{9,1},{17,25},{25,17},{2,10},{10... | collective-permute-start | bytes 4718600 | tf_op jit(solution)/shard_map/ppermute | solution.py:24
  135.9 64.3 %collective-permute-start.13 = (f32[192,2048]{1,0:T(8,128)S(1)}, f32[192,2048]{1,0:T(8,128)S(1)}, u32[]{:S(2)}, u32[]{:S(2)}) collective-permute-start(f32[192,2048]{1,0:T(8,128)S(1)} %get-tuple-element.218), channel_id=1, source_target_pairs={{0,16},{8,24},{16,0},{24,8},{1,17},{9,25},{17,1},{25,9},{2,18},{10... | collective-permute-start | bytes 4718600 | tf_op jit(solution)/shard_map/ppermute | solution.py:24
  169.5 62.3 %collective-permute-start.14 = (f32[192,2048]{1,0:T(8,128)S(1)}, f32[192,2048]{1,0:T(8,128)S(1)}, u32[]{:S(2)}, u32[]{:S(2)}) collective-permute-start(f32[192,2048]{1,0:T(8,128)S(1)} %get-tuple-element.226), channel_id=1, source_target_pairs={{0,8},{8,0},{16,24},{24,16},{1,9},{9,1},{17,25},{25,17},{2,10},{10... | collective-permute-start | bytes 4718600 | tf_op jit(solution)/shard_map/ppermute | solution.py:24
  169.6 64.3 %collective-permute-start.15 = (f32[192,2048]{1,0:T(8,128)S(1)}, f32[192,2048]{1,0:T(8,128)S(1)}, u32[]{:S(2)}, u32[]{:S(2)}) collective-permute-start(f32[192,2048]{1,0:T(8,128)S(1)} %get-tuple-element.227), channel_id=1, source_target_pairs={{0,16},{8,24},{16,0},{24,8},{1,17},{9,25},{17,1},{25,9},{2,18},{10... | collective-permute-start | bytes 4718600 | tf_op jit(solution)/shard_map/ppermute | solution.py:24
  203.2 62.3 %collective-permute-start.16 = (f32[192,2048]{1,0:T(8,128)S(1)}, f32[192,2048]{1,0:T(8,128)S(1)}, u32[]{:S(2)}, u32[]{:S(2)}) collective-permute-start(f32[192,2048]{1,0:T(8,128)S(1)} %get-tuple-element.235), channel_id=1, source_target_pairs={{0,8},{8,0},{16,24},{24,16},{1,9},{9,1},{17,25},{25,17},{2,10},{10... | collective-permute-start | bytes 4718600 | tf_op jit(solution)/shard_map/ppermute | solution.py:24
  203.3 64.3 %collective-permute-start.17 = (f32[192,2048]{1,0:T(8,128)S(1)}, f32[192,2048]{1,0:T(8,128)S(1)}, u32[]{:S(2)}, u32[]{:S(2)}) collective-permute-start(f32[192,2048]{1,0:T(8,128)S(1)} %get-tuple-element.236), channel_id=1, source_target_pairs={{0,16},{8,24},{16,0},{24,8},{1,17},{9,25},{17,1},{25,9},{2,18},{10... | collective-permute-start | bytes 4718600 | tf_op jit(solution)/shard_map/ppermute | solution.py:24
  236.9 62.3 %collective-permute-start.18 = (f32[192,2048]{1,0:T(8,128)S(1)}, f32[192,2048]{1,0:T(8,128)S(1)}, u32[]{:S(2)}, u32[]{:S(2)}) collective-permute-start(f32[192,2048]{1,0:T(8,128)S(1)} %get-tuple-element.244), channel_id=1, source_target_pairs={{0,8},{8,0},{16,24},{24,16},{1,9},{9,1},{17,25},{25,17},{2,10},{10... | collective-permute-start | bytes 4718600 | tf_op jit(solution)/shard_map/ppermute | solution.py:24
  237.1 64.3 %collective-permute-start.19 = (f32[192,2048]{1,0:T(8,128)S(1)}, f32[192,2048]{1,0:T(8,128)S(1)}, u32[]{:S(2)}, u32[]{:S(2)}) collective-permute-start(f32[192,2048]{1,0:T(8,128)S(1)} %get-tuple-element.245), channel_id=1, source_target_pairs={{0,16},{8,24},{16,0},{24,8},{1,17},{9,25},{17,1},{25,9},{2,18},{10... | collective-permute-start | bytes 4718600 | tf_op jit(solution)/shard_map/ppermute | solution.py:24
  270.7 62.3 %collective-permute-start.23 = (f32[192,2048]{1,0:T(8,128)S(1)}, f32[192,2048]{1,0:T(8,128)S(1)}, u32[]{:S(2)}, u32[]{:S(2)}) collective-permute-start(f32[192,2048]{1,0:T(8,128)S(1)} %get-tuple-element.258), channel_id=1, source_target_pairs={{0,8},{8,0},{16,24},{24,16},{1,9},{9,1},{17,25},{25,17},{2,10},{10... | collective-permute-start | bytes 4718600 | tf_op jit(solution)/shard_map/ppermute | solution.py:24
  270.8 64.3 %collective-permute-start.24 = (f32[192,2048]{1,0:T(8,128)S(1)}, f32[192,2048]{1,0:T(8,128)S(1)}, u32[]{:S(2)}, u32[]{:S(2)}) collective-permute-start(f32[192,2048]{1,0:T(8,128)S(1)} %get-tuple-element.259), channel_id=1, source_target_pairs={{0,16},{8,24},{16,0},{24,8},{1,17},{9,25},{17,1},{25,9},{2,18},{10... | collective-permute-start | bytes 4718600 | tf_op jit(solution)/shard_map/ppermute | solution.py:24
  304.4 62.3 %collective-permute-start.25 = (f32[192,2048]{1,0:T(8,128)S(1)}, f32[192,2048]{1,0:T(8,128)S(1)}, u32[]{:S(2)}, u32[]{:S(2)}) collective-permute-start(f32[192,2048]{1,0:T(8,128)S(1)} %get-tuple-element.265), channel_id=1, source_target_pairs={{0,8},{8,0},{16,24},{24,16},{1,9},{9,1},{17,25},{25,17},{2,10},{10... | collective-permute-start | bytes 4718600 | tf_op jit(solution)/shard_map/ppermute | solution.py:24
  304.5 64.3 %collective-permute-start.26 = (f32[192,2048]{1,0:T(8,128)S(1)}, f32[192,2048]{1,0:T(8,128)S(1)}, u32[]{:S(2)}, u32[]{:S(2)}) collective-permute-start(f32[192,2048]{1,0:T(8,128)S(1)} %get-tuple-element.266), channel_id=1, source_target_pairs={{0,16},{8,24},{16,0},{24,8},{1,17},{9,25},{17,1},{25,9},{2,18},{10... | collective-permute-start | bytes 4718600 | tf_op jit(solution)/shard_map/ppermute | solution.py:24
  338.1 64.4 %collective-permute-start.27 = (f32[200,2048]{1,0:T(8,128)S(1)}, f32[200,2048]{1,0:T(8,128)S(1)}, u32[]{:S(2)}, u32[]{:S(2)}) collective-permute-start(f32[200,2048]{1,0:T(8,128)S(1)} %get-tuple-element.274), channel_id=1, source_target_pairs={{0,8},{8,0},{16,24},{24,16},{1,9},{9,1},{17,25},{25,17},{2,10},{10... | collective-permute-start | bytes 4915208 | tf_op jit(solution)/shard_map/ppermute | solution.py:24
  338.2 64.3 %collective-permute-start.28 = (f32[192,2048]{1,0:T(8,128)S(1)}, f32[192,2048]{1,0:T(8,128)S(1)}, u32[]{:S(2)}, u32[]{:S(2)}) collective-permute-start(f32[192,2048]{1,0:T(8,128)S(1)} %get-tuple-element.275), channel_id=1, source_target_pairs={{0,16},{8,24},{16,0},{24,8},{1,17},{9,25},{17,1},{25,9},{2,18},{10... | collective-permute-start | bytes 4718600 | tf_op jit(solution)/shard_map/ppermute | solution.py:24
  371.8 63.7 %collective-permute-start.29 = (f32[192,2048]{1,0:T(8,128)S(1)}, f32[192,2048]{1,0:T(8,128)S(1)}, u32[]{:S(2)}, u32[]{:S(2)}) collective-permute-start(f32[192,2048]{1,0:T(8,128)S(1)} %get-tuple-element.283), channel_id=1, source_target_pairs={{0,8},{8,0},{16,24},{24,16},{1,9},{9,1},{17,25},{25,17},{2,10},{10... | collective-permute-start | bytes 4718600 | tf_op jit(solution)/shard_map/ppermute | solution.py:24
  371.9 64.3 %collective-permute-start.30 = (f32[192,2048]{1,0:T(8,128)S(1)}, f32[192,2048]{1,0:T(8,128)S(1)}, u32[]{:S(2)}, u32[]{:S(2)}) collective-permute-start(f32[192,2048]{1,0:T(8,128)S(1)} %get-tuple-element.284), channel_id=1, source_target_pairs={{0,16},{8,24},{16,0},{24,8},{1,17},{9,25},{17,1},{25,9},{2,18},{10... | collective-permute-start | bytes 4718600 | tf_op jit(solution)/shard_map/ppermute | solution.py:24
  405.6 65.7 %collective-permute-start.32 = (f32[200,2048]{1,0:T(8,128)S(1)}, f32[200,2048]{1,0:T(8,128)S(1)}, u32[]{:S(2)}, u32[]{:S(2)}) collective-permute-start(f32[200,2048]{1,0:T(8,128)S(1)} %get-tuple-element.293), channel_id=1, source_target_pairs={{0,16},{8,24},{16,0},{24,8},{1,17},{9,25},{17,1},{25,9},{2,18},{10... | collective-permute-start | bytes 4915208 | tf_op jit(solution)/shard_map/ppermute | solution.py:24
  407.1 62.1 %collective-permute-start.31 = (f32[192,2048]{1,0:T(8,128)S(1)}, f32[192,2048]{1,0:T(8,128)S(1)}, u32[]{:S(2)}, u32[]{:S(2)}) collective-permute-start(f32[192,2048]{1,0:T(8,128)S(1)} %get-tuple-element.292), channel_id=1, source_target_pairs={{0,8},{8,0},{16,24},{24,16},{1,9},{9,1},{17,25},{25,17},{2,10},{10... | collective-permute-start | bytes 4718600 | tf_op jit(solution)/shard_map/ppermute | solution.py:24
  440.8 62.1 %collective-permute-start.35 = (f32[192,2048]{1,0:T(8,128)}, f32[192,2048]{1,0:T(8,128)S(1)}, u32[]{:S(2)}, u32[]{:S(2)}) collective-permute-start(f32[192,2048]{1,0:T(8,128)} %get-tuple-element.311), channel_id=1, source_target_pairs={{0,8},{8,0},{16,24},{24,16},{1,9},{9,1},{17,25},{25,17},{2,10},{10... | collective-permute-start | bytes 4718600 | tf_op jit(solution)/shard_map/ppermute | solution.py:24
  442.2 62.8 %collective-permute-start.36 = (f32[192,2048]{1,0:T(8,128)}, f32[192,2048]{1,0:T(8,128)S(1)}, u32[]{:S(2)}, u32[]{:S(2)}) collective-permute-start(f32[192,2048]{1,0:T(8,128)} %get-tuple-element.312), channel_id=1, source_target_pairs={{0,16},{8,24},{16,0},{24,8},{1,17},{9,25},{17,1},{25,9},{2,18},{10... | collective-permute-start | bytes 4718600 | tf_op jit(solution)/shard_map/ppermute | solution.py:24
  482.2 43.2 %collective-permute-start.37 = (f32[128,2048]{1,0:T(8,128)}, f32[128,2048]{1,0:T(8,128)S(1)}, u32[]{:S(2)}, u32[]{:S(2)}) collective-permute-start(f32[128,2048]{1,0:T(8,128)} %get-tuple-element.320), channel_id=1, source_target_pairs={{0,8},{8,0},{16,24},{24,16},{1,9},{9,1},{17,25},{25,17},{2,10},{10... | collective-permute-start | bytes 3145736 | tf_op jit(solution)/shard_map/ppermute | solution.py:24
  482.7 44.7 %collective-permute-start.38 = (f32[128,2048]{1,0:T(8,128)S(1)}, f32[128,2048]{1,0:T(8,128)S(1)}, u32[]{:S(2)}, u32[]{:S(2)}) collective-permute-start(f32[128,2048]{1,0:T(8,128)S(1)} %get-tuple-element.321), channel_id=1, source_target_pairs={{0,16},{8,24},{16,0},{24,8},{1,17},{9,25},{17,1},{25,9},{2,18},{10... | collective-permute-start | bytes 3145736 | tf_op jit(solution)/shard_map/ppermute | solution.py:24
  507.8 39.3 %collective-permute-start.39 = (f32[128,2048]{1,0:T(8,128)S(1)}, f32[128,2048]{1,0:T(8,128)S(1)}, u32[]{:S(2)}, u32[]{:S(2)}) collective-permute-start(f32[128,2048]{1,0:T(8,128)S(1)} %get-tuple-element.329), channel_id=1, source_target_pairs={{0,8},{8,0},{16,24},{24,16},{1,9},{9,1},{17,25},{25,17},{2,10},{10... | collective-permute-start | bytes 3145736 | tf_op jit(solution)/shard_map/ppermute | solution.py:24
  507.9 40.6 %collective-permute-start.40 = (f32[128,2048]{1,0:T(8,128)S(1)}, f32[128,2048]{1,0:T(8,128)S(1)}, u32[]{:S(2)}, u32[]{:S(2)}) collective-permute-start(f32[128,2048]{1,0:T(8,128)S(1)} %get-tuple-element.330), channel_id=1, source_target_pairs={{0,16},{8,24},{16,0},{24,8},{1,17},{9,25},{17,1},{25,9},{2,18},{10... | collective-permute-start | bytes 3145736 | tf_op jit(solution)/shard_map/ppermute | solution.py:24
  (22 other events, 238.8 us)

commit v6 on v4

--- a/solution.py
+++ b/solution.py
@@ -16,7 +16,6 @@
 sublanes = 8
 blocks_of_matrix = 8
 tile_rows = 16
-finish_rows = 64
 f32 = jnp.float32
 
 
@@ -51,7 +50,7 @@
     return pltpu.CompilerParams(vmem_limit_bytes=mib * 1024 * 1024)
 
 
-def step_kernel(takes, finishes, first, sends, starts, brings, carries, *refs):
+def step_kernel(takes, finishes, b, sends, starts, brings, carries, *refs):
     refs = list(refs[1:])
     take = lambda yes: refs.pop(0) if yes else None
     got = [take(takes or finishes) for _ in range(2)]
@@ -59,11 +58,12 @@
     direct = [take(sends) for _ in range(2)]
     relay = [take(sends) for _ in range(2)]
     onward = take(starts)
+    first = b == 0
     again = finishes and not first
-    cols_in, _, _ = take(again), take(again), take(again)
+    cols_in, rows_in, _ = take(again), take(again), take(again)
     stats_in = take(brings is not None or carries is not None)
     out = [take(sends or starts) for _ in range(2)]
-    cols_out, summed_out, rows_out = take(finishes), take(finishes), take(finishes)
+    cols_out, rows_out, summed_out = take(finishes), take(finishes), take(finishes)
     stats_out = take(brings is not None)
     row_parts = take(finishes)
     t = pl.program_id(0)
@@ -77,11 +77,13 @@
     def _():
         if finishes:
             cols_out[...] = jnp.zeros_like(cols_out) if first else cols_in[...]
+            rows_out[...] = jnp.zeros_like(rows_out) if first else rows_in[...]
         if brings is not None:
-            stats_out[...] = stats_in[...] + got[brings][got[brings].shape[0] - sublanes :]
+            brought = got[brings][got[brings].shape[0] - sublanes :, : stats_in.shape[1]]
+            stats_out[...] = stats_in[...] + brought
         if carries is not None:
             stats = stats_in if brings is None else stats_out
-            out[carries][out[carries].shape[0] - sublanes :] = stats[...]
+            out[carries][out[carries].shape[0] - sublanes :, : stats.shape[1]] = stats[...]
 
     for half in range(2):
         if starts:
@@ -101,13 +103,14 @@
 
         @pl.when(t == pl.num_programs(0) - 1)
         def _():
-            rows_out[...] = lax.dot_general(
+            along = lax.dot_general(
                 jnp.ones((sublanes, lanes), f32),
                 row_parts[...],
                 (((1,), (1,)), ((), ())),
                 precision=lax.Precision.HIGHEST,
                 preferred_element_type=f32,
             )
+            rows_out[b : b + 1] = along[0:1]
 
 
 def step(j, total_blocks, me, partials, got, sums, stats, brings, carries):
@@ -159,28 +162,29 @@
             size = slots * part + (sublanes if link == carries else 0)
             out_shape.append(jax.ShapeDtypeStruct((size, width), f32))
             out_specs.append(in_vmem)
-    cols_spec = pl.BlockSpec((sublanes, width), lambda t, at: (0, 0))
+    whole = lambda *shape: pl.BlockSpec(shape, lambda t, at: (0,) * len(shape))
     if finishes:
+        rows_shape = (count, 2 * part)
         if not first:
-            add(sums[0], cols_spec)
-            for i in (1, 2):
-                aliases[1 + len(operands)] = len(out_shape) + i
-                add(sums[i], pl.BlockSpec(memory_space=pl.ANY))
+            add(sums[0], whole(sublanes, width))
+            add(sums[1], whole(*rows_shape))
+            aliases[1 + len(operands)] = len(out_shape) + 2
+            add(sums[2], pl.BlockSpec(memory_space=pl.ANY))
         out_shape.append(jax.ShapeDtypeStruct((sublanes, width), f32))
-        out_specs.append(cols_spec)
+        out_specs.append(whole(sublanes, width))
+        out_shape.append(jax.ShapeDtypeStruct(rows_shape, f32))
+        out_specs.append(whole(*rows_shape))
         out_shape.append(jax.ShapeDtypeStruct((count, 2, part, width), f32))
         out_specs.append(pl.BlockSpec((None, 2, tile, width), lambda t, at: (b, 0, t, 0)))
-        out_shape.append(jax.ShapeDtypeStruct((count, sublanes, 2 * part), f32))
-        out_specs.append(pl.BlockSpec((None, sublanes, 2 * part), lambda t, at: (b, 0, 0)))
         scratch.append(pltpu.VMEM((2 * part, lanes), f32))
     if brings is not None or carries is not None:
-        add(stats, cols_spec)
+        add(stats, whole(*stats.shape))
     if brings is not None:
-        out_shape.append(jax.ShapeDtypeStruct((sublanes, width), f32))
-        out_specs.append(cols_spec)
+        out_shape.append(jax.ShapeDtypeStruct(stats.shape, f32))
+        out_specs.append(whole(*stats.shape))
     moved = part * width * (4 * (2 * slots + 8) + 2 * 8)
     result = pl.pallas_call(
-        functools.partial(step_kernel, takes, finishes, first, sends, starts, brings, carries),
+        functools.partial(step_kernel, takes, finishes, b, sends, starts, brings, carries),
         out_shape=out_shape,
         grid_spec=pltpu.PrefetchScalarGridSpec(
             num_scalar_prefetch=1,
@@ -202,71 +206,57 @@
 
 
 def weighted_kernel(extent, factor, cols, summed, *refs):
-    *totals, rows_out, stats, weighted, level = refs
-    i = pl.program_id(0)
-
-    @pl.when(i == 0)
-    def _():
-        weighted[...] = jnp.zeros_like(weighted)
-        level[...] = jnp.zeros_like(level)
-
+    *totals, rows_out, stats, weighted = refs
+    count, _, part, width = summed.shape
     total = tree_sum([x[...] for x in totals])
     row_new = decay_rate * factor[...] + (1.0 - decay_rate) * (total / extent + tiny_eps)
     rows_out[...] = row_new
-    level[...] += row_new
-    inverse = jnp.transpose(1.0 / row_new)[:, 0:1]
-    part = summed.shape[1]
-    for half in range(2):
-        for r in range(0, part, sublanes):
-            x = summed[half, r : r + sublanes]
-            at = half * part + r
-            weighted[...] += x * x * inverse[at : at + sublanes]
-
-    @pl.when(i == pl.num_programs(0) - 1)
-    def _():
-        stats[...] = jnp.zeros_like(stats)
-        stats[0:1] = jnp.sum(cols[...], axis=0, keepdims=True)
-        stats[1:2] = jnp.sum(weighted[...], axis=0, keepdims=True)
-        total = jnp.sum(level[0:1], axis=1, keepdims=True)
-        stats[2:3] = jnp.broadcast_to(total, (1, stats.shape[1]))
+    inverse = jnp.transpose(1.0 / row_new)
+    weighted[...] = jnp.zeros_like(weighted)
+    for i in range(count):
+        for r in range(0, 2 * part, sublanes):
+            half, at = divmod(r, part)
+            x = summed[i, half, at : at + sublanes]
+            weighted[...] += x * x * inverse[r : r + sublanes, i : i + 1]
+    size = width // sublanes
+    for at, x in ((0, cols), (size, weighted)):
+        sums = jnp.sum(x[...], axis=0, keepdims=True)
+        for k in range(sublanes):
+            stats[k : k + 1, at : at + size] = sums[:, k * size : (k + 1) * size]
+    level = jnp.sum(jnp.sum(row_new, axis=0, keepdims=True), axis=1, keepdims=True)
+    stats[:, 2 * size :] = jnp.broadcast_to(level, (sublanes, lanes))
 
 
 def weighted_sums(extent, totals, factor, cols, summed):
-    count, _, part, width = summed.shape
-    along = pl.BlockSpec((None, sublanes, 2 * part), lambda i: (i, 0, 0))
-    whole = pl.BlockSpec((sublanes, width), lambda i: (0, 0))
+    width = summed.shape[-1]
+    in_vmem = pl.BlockSpec(memory_space=pltpu.VMEM)
     return pl.pallas_call(
         functools.partial(weighted_kernel, extent),
-        grid=(count,),
-        in_specs=[
-            pl.BlockSpec((None, 1, 2 * part), lambda i: (i, 0, 0)),
-            whole,
-            pl.BlockSpec((None, 2, part, width), lambda i: (i, 0, 0, 0)),
-        ]
-        + [along] * len(totals),
-        out_specs=[along, whole],
+        in_specs=[in_vmem] * (3 + len(totals)),
+        out_specs=[in_vmem] * 2,
         out_shape=[
             jax.ShapeDtypeStruct(totals[0].shape, f32),
-            jax.ShapeDtypeStruct((sublanes, width), f32),
+            jax.ShapeDtypeStruct((sublanes, 2 * width // sublanes + lanes), f32),
         ],
-        scratch_shapes=[pltpu.VMEM((sublanes, width), f32), pltpu.VMEM((sublanes, 2 * part), f32)],
+        scratch_shapes=[pltpu.VMEM((sublanes, width), f32)],
         compiler_params=params_of(16),
         cost_estimate=pl.CostEstimate(
             flops=3 * summed.size, bytes_accessed=4 * summed.size, transcendentals=0
         ),
         name="weighted",
-    )(factor.reshape(count, 1, 2 * part), cols, summed, *totals)
+    )(factor.reshape(totals[0].shape), cols, summed, *totals)
 
 
 def column_kernel(extent, factor, *refs):
     *parts, cols_out, pair = refs
     stats = tree_sum([x[...] for x in parts])
-    col_new = decay_rate * factor[...] + (1.0 - decay_rate) * (stats[0:1] / extent + tiny_eps)
+    size = factor.shape[1]
+    col_new = decay_rate * factor[...] + (1.0 - decay_rate) * (stats[:, :size] / extent + tiny_eps)
     cols_out[...] = col_new
-    total = jnp.sum(stats[1:2] / col_new, axis=1, keepdims=True)
-    pair[...] = jnp.zeros_like(pair)
+    total = jnp.sum(stats[:, size : 2 * size] / col_new, axis=0, keepdims=True)
+    total = jnp.sum(total, axis=1, keepdims=True)
+    pair[...] = stats[:, 2 * size :] / extent
     pair[0:1] = jnp.broadcast_to(total, (1, lanes))
-    pair[1:2] = stats[2:3, :lanes] / extent
 
 
 def column_stage(extent, factor, parts):
@@ -278,52 +268,60 @@
             jax.ShapeDtypeStruct(factor.shape, f32),
             jax.ShapeDtypeStruct((sublanes, lanes), f32),
         ],
+        compiler_params=params_of(4),
         name="column",
     )(factor, *parts)
 
 
-def finish_kernel(m, tile, extent, partners, row_new, col_new, summed, params, *refs):
+def finish_kernel(m, extent, partners, staged, row_new, col_new, summed, params, *refs):
     pairs, (new_params, update, column, by_col) = refs[:partners], refs[-4:]
     count, _, part, width = summed.shape
     row_level = pairs[0][1:2, 0:1]
     total = tree_sum([x[0:1, 0:1] for x in pairs]) * row_level
     spread = jnp.sqrt(total / (extent * extent))
     factor = jnp.sqrt(row_level) / jnp.maximum(1.0, spread / clip_limit)
-    by_col[...] = lax.rsqrt(col_new[...])
+    by_row = jnp.transpose(lax.rsqrt(row_new[...]) * factor)
     for i in range(count):
-        column[i] = jnp.transpose(lax.rsqrt(row_new[i]) * factor)
-
-    def body(x, p, new_p, moved):
-        i, half, t = (pl.program_id(axis) for axis in range(3))
-        start = pl.multiple_of(half * part + t * tile, sublanes)
-        y = x[...] * column[i, pl.ds(start, tile)][:, 0:1] * by_col[...]
-        moved[...] = y
-        new_p[...] = p[...] - learn_rate * y
-
-    of_sum = pl.BlockSpec((None, None, tile, width), lambda i, h, t: (i, h, t, 0))
-    of_matrix = pl.BlockSpec((None, None, None, tile, width), lambda i, h, t: (m, i, h, t, 0))
+        column[i] = jnp.broadcast_to(by_row[:, i : i + 1], column.shape[1:])
+    size = width // sublanes
+    for k in range(sublanes):
+        by_col[:, k * size : (k + 1) * size] = lax.rsqrt(col_new[k : k + 1])
+
+    def body(*blocks):
+        i = pl.program_id(0)
+        new_p, moved = blocks[-2:]
+        for half in range(2):
+            for r in range(0, part, sublanes):
+                at = half * part + r
+                mine = column[i, at : at + sublanes][:, 0:1]
+                y = summed[i, half, r : r + sublanes] * mine * by_col[...]
+                moved[half, r : r + sublanes] = y
+                p = params[i, half, r : r + sublanes] if staged else blocks[0][half, r : r + sublanes]
+                new_p[half, r : r + sublanes] = p - learn_rate * y
+
+    of_matrix = pl.BlockSpec((None, None, 2, part, width), lambda i: (m, i, 0, 0, 0))
     pltpu.emit_pipeline(
-        body,
-        grid=(count, 2, part // tile),
-        in_specs=[of_sum, of_matrix],
-        out_specs=[of_matrix] * 2,
-    )(summed, params, new_params, update)
+        body, grid=(count,), in_specs=[] if staged else [of_matrix], out_specs=[of_matrix] * 2
+    )(*([] if staged else [params]), new_params, update)
 
 
 def finish(m, extent, row_new, col_new, pairs, summed, params, outs, mib):
     count, _, part, width = summed.shape
-    held = () if outs is None else outs
+    staged = outs is not None
+    held = outs if staged else ()
     in_hbm = pl.BlockSpec(memory_space=pltpu.HBM)
     in_vmem = pl.BlockSpec(memory_space=pltpu.VMEM)
+    out_shape = jax.ShapeDtypeStruct(held[0].shape if staged else params.shape, f32)
     return pl.pallas_call(
-        functools.partial(finish_kernel, m, min(part, finish_rows), extent, len(pairs)),
-        in_specs=[in_vmem, in_vmem, pl.BlockSpec(memory_space=pl.ANY), in_hbm]
+        functools.partial(finish_kernel, m, extent, len(pairs), staged),
+        in_specs=[in_vmem] * 3
+        + [in_vmem if staged else in_hbm]
         + [in_vmem] * len(pairs)
         + [in_hbm] * len(held),
         out_specs=[in_hbm] * 2,
-        out_shape=[jax.ShapeDtypeStruct(params.shape, f32)] * 2,
+        out_shape=[out_shape] * 2,
         scratch_shapes=[
-            pltpu.VMEM((count, 2 * part, sublanes), f32),
+            pltpu.VMEM((count, 2 * part, lanes), f32),
             pltpu.VMEM((1, width), f32),
         ],
         input_output_aliases={4 + len(pairs) + i: i for i in range(len(held))},
@@ -347,16 +345,16 @@
     new_rows, new_columns = [], []
 
     def row_stage(m, sums):
-        cols, summed, rows_along = sums
+        cols, rows_along, summed = sums
         row_new, stats = weighted_sums(
             extent, exchange(rows_along, "col"), row_factor[m], cols, summed
         )
-        new_rows.append(row_new[:, 0].reshape(rows))
+        new_rows.append(row_new.reshape(rows))
         return row_new, pairwise_sum(stats, "row")
 
     def col_stage(m, parts):
-        col_new, pair = column_stage(extent, col_factor[m : m + 1], parts)
-        new_columns.append(col_new)
+        col_new, pair = column_stage(extent, col_factor[m].reshape(sublanes, -1), parts)
+        new_columns.append(col_new.reshape(block_cols))
         return col_new, exchange(pair, "col")
 
     flying = {}
@@ -379,7 +377,7 @@
             me, *_ = tie(me, *sent)
         if 0 <= m < mats - 1 and b == count - 1:
             row_new, stats = row_stage(m, sums)
-            last = dict(m=m, row_new=row_new, summed=sums[1])
+            last = dict(m=m, row_new=row_new, summed=sums[2])
             me, stats = tie(me, stats)
         if since == 5:
             stats, me = tie(stats, me)
@@ -388,17 +386,19 @@
                 last["m"], extent, last["row_new"], col_new, pairs, last["summed"], blocked, outs, 36
             )
             me, *outs = tie(me, *outs)
+        if j == total_blocks - 1:
+            me, last_params = tie(me, blocked[mats - 1])
 
     row_new, stats = row_stage(mats - 1, sums)
     col_new, pairs = col_stage(mats - 1, exchange(stats, "dp"))
     new_params, update = finish(
-        mats - 1, extent, row_new, col_new, pairs, sums[1], blocked, outs, 44
+        mats - 1, extent, row_new, col_new, pairs, sums[2], last_params, outs, 12
     )
     return (
         new_params.reshape(params.shape),
         update.reshape(params.shape),
         jnp.stack(new_rows),
-        jnp.concatenate(new_columns, axis=0),
+        jnp.stack(new_columns),
     )
 
 

time: 599 us -> 591 us (0.987)
  Pallas kernels: 93.9 us -> 80.7 us
  local copies, waits for them, and re-layouts: 16.7 us -> 28.4 us
  waiting for transfers between devices: 422 us -> 414 us
    pallas_call x24, Pallas kernels: 90.7 us -> 80.5 us  [the longest x20 59.8 us: step(): pl.pallas_call(functools.partial(step_kernel, takes, finishes, b, sends,...]
    ppermute x53, waiting for transfers between devices: 422 us -> 414 us  [swap(): return lax.ppermute(x, axes, [(i, i ^ mask) for i in range(size)])]
    slice x1 -> x3, local copies, waits for them, and re-layouts: 0.62 us -> 7.91 us  [the longest x1 7.86 us: per_device(): me, last_params = tie(me, blocked[mats - 1])]
    unnamed x40 -> x26, local copies, waits for them, and re-layouts: 16.1 us -> 20.5 us
  transfers between devices with their start and end apart: 53 -> 53, of which waited for: 46 -> 45; matrix products, arithmetic and copies ran while one was open for 0% -> 2% of each run, Pallas kernels for 12% -> 12%
where the time goes in v6:
time: 591 us; the launch traced here: 590 us
  waiting for transfers between devices  414 us (70%)
  Pallas kernels  80.7 us (14%)
  starting transfers between devices  65 us (11%)
  local copies, waits for them, and re-layouts  28.4 us (5%)
    ppermute x53, waiting for transfers between devices, swap(): return lax.ppermute(x, axes, [(i, i ^ mask) for i in range(size)])  414 us
    ppermute x53, starting transfers between devices, swap(): return lax.ppermute(x, axes, [(i, i ^ mask) for i in range(size)])  65 us
    pallas_call x20, Pallas kernels, step(): pl.pallas_call(functools.partial(step_kernel, takes, finishes, b, sends,...  59.8 us
    unnamed x26, local copies, waits for them, and re-layouts  20.5 us
    pallas_call x2, Pallas kernels, finish(): pl.pallas_call(functools.partial(finish_kernel, m, extent, len(pairs), st...  18.5 us
  transfers between devices with their start and end apart: 53, of which 45 were waited for; matrix products, arithmetic and copies ran while one was open for 2% of the time, Pallas kernels for 12%

profile of v6, /device:TPU:0, one launch (start us, length us, event | category | flops | bytes accessed | tf_op | source)
XLA Modules:
  0.0 589.9 jit_solution(7406464072127708549)
XLA Ops:
  9.8 8.6 %collective-permute-done.refs_1_ = f32[64,2048]{1,0:T(8,128)S(1)} collective-permute-done((f32[64,2048]{1,0:T(8,128)S(1)}, f32[64,2048]{1,0:T(8,128)S(1)}, u32[]{:S(2)}, u32[]{:S(2)}) %collective-permute-start) | collective-permute-done | bytes 524320 | tf_op jit(solution)/shard_map/ppermute | solution.py:24
  25.1 4.5 collective-permute-done.2.refs_1_
  36.3 27.0 %collective-permute-done.4.refs_1_ = f32[192,2048]{1,0:T(8,128)S(1)} collective-permute-done((f32[192,2048]{1,0:T(8,128)S(1)}, f32[192,2048]{1,0:T(8,128)S(1)}, u32[]{:S(2)}, u32[]{:S(2)}) %collective-permute-start.4) | collective-permute-done | bytes 1572896 | tf_op jit(solution)/shard_map/ppermute | solution.py:24
  70.5 26.5 %collective-permute-done.6.refs_1_ = f32[192,2048]{1,0:T(8,128)S(1)} collective-permute-done((f32[192,2048]{1,0:T(8,128)S(1)}, f32[192,2048]{1,0:T(8,128)S(1)}, u32[]{:S(2)}, u32[]{:S(2)}) %collective-permute-start.6) | collective-permute-done | bytes 1572896 | tf_op jit(solution)/shard_map/ppermute | solution.py:24
  104.2 26.5 %collective-permute-done.8.refs_1_ = f32[192,2048]{1,0:T(8,128)S(1)} collective-permute-done((f32[192,2048]{1,0:T(8,128)S(1)}, f32[192,2048]{1,0:T(8,128)S(1)}, u32[]{:S(2)}, u32[]{:S(2)}) %collective-permute-start.8) | collective-permute-done | bytes 1572896 | tf_op jit(solution)/shard_map/ppermute | solution.py:24
  138.0 26.5 %collective-permute-done.10.refs_1_ = f32[192,2048]{1,0:T(8,128)S(1)} collective-permute-done((f32[192,2048]{1,0:T(8,128)S(1)}, f32[192,2048]{1,0:T(8,128)S(1)}, u32[]{:S(2)}, u32[]{:S(2)}) %collective-permute-start.10) | collective-permute-done | bytes 1572896 | tf_op jit(solution)/shard_map/ppermute | solution.py:24
  171.7 26.5 %collective-permute-done.12.refs_1_ = f32[192,2048]{1,0:T(8,128)S(1)} collective-permute-done((f32[192,2048]{1,0:T(8,128)S(1)}, f32[192,2048]{1,0:T(8,128)S(1)}, u32[]{:S(2)}, u32[]{:S(2)}) %collective-permute-start.12) | collective-permute-done | bytes 1572896 | tf_op jit(solution)/shard_map/ppermute | solution.py:24
  205.4 26.5 %collective-permute-done.14.refs_1_ = f32[192,2048]{1,0:T(8,128)S(1)} collective-permute-done((f32[192,2048]{1,0:T(8,128)S(1)}, f32[192,2048]{1,0:T(8,128)S(1)}, u32[]{:S(2)}, u32[]{:S(2)}) %collective-permute-start.14) | collective-permute-done | bytes 1572896 | tf_op jit(solution)/shard_map/ppermute | solution.py:24
  239.1 26.5 %collective-permute-done.16.refs_1_ = f32[192,2048]{1,0:T(8,128)S(1)} collective-permute-done((f32[192,2048]{1,0:T(8,128)S(1)}, f32[192,2048]{1,0:T(8,128)S(1)}, u32[]{:S(2)}, u32[]{:S(2)}) %collective-permute-start.16) | collective-permute-done | bytes 1572896 | tf_op jit(solution)/shard_map/ppermute | solution.py:24
  272.8 26.5 %collective-permute-done.18.refs_1_ = f32[192,2048]{1,0:T(8,128)S(1)} collective-permute-done((f32[192,2048]{1,0:T(8,128)S(1)}, f32[192,2048]{1,0:T(8,128)S(1)}, u32[]{:S(2)}, u32[]{:S(2)}) %collective-permute-start.18) | collective-permute-done | bytes 1572896 | tf_op jit(solution)/shard_map/ppermute | solution.py:24
  314.6 3.6 collective-permute-start.22
  322.4 10.6 %collective-permute-done.24.refs_1_ = f32[192,2048]{1,0:T(8,128)S(1)} collective-permute-done((f32[192,2048]{1,0:T(8,128)S(1)}, f32[192,2048]{1,0:T(8,128)S(1)}, u32[]{:S(2)}, u32[]{:S(2)}) %collective-permute-start.24) | collective-permute-done | bytes 1572896 | tf_op jit(solution)/shard_map/ppermute | solution.py:24
  340.2 26.5 %collective-permute-done.26.refs_1_ = f32[192,2048]{1,0:T(8,128)S(1)} collective-permute-done((f32[192,2048]{1,0:T(8,128)S(1)}, f32[192,2048]{1,0:T(8,128)S(1)}, u32[]{:S(2)}, u32[]{:S(2)}) %collective-permute-start.26) | collective-permute-done | bytes 1572896 | tf_op jit(solution)/shard_map/ppermute | solution.py:24
  373.9 28.6 %collective-permute-done.29.refs_2_ = f32[192,2048]{1,0:T(8,128)S(1)} collective-permute-done((f32[192,2048]{1,0:T(8,128)S(1)}, f32[192,2048]{1,0:T(8,128)S(1)}, u32[]{:S(2)}, u32[]{:S(2)}) %collective-permute-start.29) | collective-permute-done | bytes 1572896 | tf_op jit(solution)/shard_map/ppermute | solution.py:24
  402.5 4.7 step.34
  410.0 25.5 %collective-permute-done.30.refs_1_ = f32[192,2048]{1,0:T(8,128)S(1)} collective-permute-done((f32[192,2048]{1,0:T(8,128)S(1)}, f32[192,2048]{1,0:T(8,128)S(1)}, u32[]{:S(2)}, u32[]{:S(2)}) %collective-permute-start.30) | collective-permute-done | bytes 1572896 | tf_op jit(solution)/shard_map/ppermute | solution.py:24
  436.2 4.7 step.35
  440.9 3.4 copy-done
  447.2 22.1 %collective-permute-done.32.refs_1_ = f32[192,2048]{1,0:T(8,128)} collective-permute-done((f32[192,2048]{1,0:T(8,128)}, f32[192,2048]{1,0:T(8,128)}, u32[]{:S(2)}, u32[]{:S(2)}) %collective-permute-start.32) | collective-permute-done | bytes 1572896 | tf_op jit(solution)/shard_map/ppermute | solution.py:24
  471.3 3.4 copy-done.1
  474.7 3.4 step.36
  491.1 3.5 copy-done.6
  494.7 11.3 %finish.2 = (f32[2,8,2,64,2048]{4,3,2,1,0:T(8,128)}, f32[2,8,2,64,2048]{4,3,2,1,0:T(8,128)}) custom-call(f32[8,128]{1,0:T(8,128)S(1)} %get-tuple-element.306.row_new, f32[8,256]{1,0:T(8,128)S(1)} %get-tuple-element.308.col_new, f32[8,2,64,2048]{3,2,1,0:T(8,128)S(1)} %copy-done.6, f32[2,8,2,64,2048]{4,3,2,1,0:T(8,128)} %bitcast.121, ...), custom_call_target="tpu_custom_call" | custom-call | flops 8388608 | bytes 33554432 | tf_op jit(solution)/shard_map/finish/pallas_call | solution.py:315
  506.0 3.5 step.37
  511.6 7.9 %slice.19 = f32[1,1024,2048]{2,1,0:T(8,128)} slice(f32[2,1024,2048]{2,1,0:T(8,128)} %param.5), slice={[1:2], [0:1024], [0:2048]} | slice | bytes 16777216 | tf_op jit(solution)/shard_map/slice | solution.py:390
  519.4 5.9 %collective-permute-done.39.refs_1_ = f32[128,2048]{1,0:T(8,128)S(1)} collective-permute-done((f32[128,2048]{1,0:T(8,128)S(1)}, f32[128,2048]{1,0:T(8,128)S(1)}, u32[]{:S(2)}, u32[]{:S(2)}) %collective-permute-start.39) | collective-permute-done | bytes 1048608 | tf_op jit(solution)/shard_map/ppermute | solution.py:24
  529.9 17.1 %collective-permute-done.41.refs_1_ = f32[128,2048]{1,0:T(8,128)S(1)} collective-permute-done((f32[128,2048]{1,0:T(8,128)S(1)}, f32[128,2048]{1,0:T(8,128)S(1)}, u32[]{:S(2)}, u32[]{:S(2)}) %collective-permute-start.41) | collective-permute-done | bytes 1048608 | tf_op jit(solution)/shard_map/ppermute | solution.py:24
  557.0 3.5 collective-permute-done.45.refs_3_
  570.5 3.6 collective-permute-start.52
  575.9 3.4 copy-done.4
  579.3 3.4 copy-done.7
  582.7 7.2 %finish.3 = (f32[2,8,2,64,2048]{4,3,2,1,0:T(8,128)}, f32[2,8,2,64,2048]{4,3,2,1,0:T(8,128)}) custom-call(f32[8,128]{1,0:T(8,128)S(1)} %get-tuple-element.343.row_new, f32[8,256]{1,0:T(8,128)S(1)} %get-tuple-element.345.col_new, f32[8,2,64,2048]{3,2,1,0:T(8,128)S(1)} %copy-done.4, ...), custom_call_target="tpu_custom_call", output_to_operand_aliasing={{0}: (8, {}), {1}: (9, {})} | custom-call | flops 8388608 | bytes 33554432 | tf_op jit(solution)/shard_map/finish/pallas_call | solution.py:315
  (136 shorter events, 156.8 us)
Async XLA Ops:
  22.9 40.4 %collective-permute-start.4 = (f32[192,2048]{1,0:T(8,128)S(1)}, f32[192,2048]{1,0:T(8,128)S(1)}, u32[]{:S(2)}, u32[]{:S(2)}) collective-permute-start(f32[192,2048]{1,0:T(8,128)S(1)} %get-tuple-element.184), channel_id=1, source_target_pairs={{0,8},{8,0},{16,24},{24,16},{1,9},{9,1},{17,25},{25,17},{2,10},{10... | collective-permute-start | bytes 4718600 | tf_op jit(solution)/shard_map/ppermute | solution.py:24
  23.1 42.4 %collective-permute-start.5 = (f32[192,2048]{1,0:T(8,128)S(1)}, f32[192,2048]{1,0:T(8,128)S(1)}, u32[]{:S(2)}, u32[]{:S(2)}) collective-permute-start(f32[192,2048]{1,0:T(8,128)S(1)} %get-tuple-element.185), channel_id=1, source_target_pairs={{0,16},{8,24},{16,0},{24,8},{1,17},{9,25},{17,1},{25,9},{2,18},{10... | collective-permute-start | bytes 4718600 | tf_op jit(solution)/shard_map/ppermute | solution.py:24
  34.2 62.8 %collective-permute-start.6 = (f32[192,2048]{1,0:T(8,128)S(1)}, f32[192,2048]{1,0:T(8,128)S(1)}, u32[]{:S(2)}, u32[]{:S(2)}) collective-permute-start(f32[192,2048]{1,0:T(8,128)S(1)} %get-tuple-element.187), channel_id=1, source_target_pairs={{0,8},{8,0},{16,24},{24,16},{1,9},{9,1},{17,25},{25,17},{2,10},{10... | collective-permute-start | bytes 4718600 | tf_op jit(solution)/shard_map/ppermute | solution.py:24
  34.3 64.8 %collective-permute-start.7 = (f32[192,2048]{1,0:T(8,128)S(1)}, f32[192,2048]{1,0:T(8,128)S(1)}, u32[]{:S(2)}, u32[]{:S(2)}) collective-permute-start(f32[192,2048]{1,0:T(8,128)S(1)} %get-tuple-element.188), channel_id=1, source_target_pairs={{0,16},{8,24},{16,0},{24,8},{1,17},{9,25},{17,1},{25,9},{2,18},{10... | collective-permute-start | bytes 4718600 | tf_op jit(solution)/shard_map/ppermute | solution.py:24
  68.4 62.3 %collective-permute-start.8 = (f32[192,2048]{1,0:T(8,128)S(1)}, f32[192,2048]{1,0:T(8,128)S(1)}, u32[]{:S(2)}, u32[]{:S(2)}) collective-permute-start(f32[192,2048]{1,0:T(8,128)S(1)} %get-tuple-element.201), channel_id=1, source_target_pairs={{0,8},{8,0},{16,24},{24,16},{1,9},{9,1},{17,25},{25,17},{2,10},{10... | collective-permute-start | bytes 4718600 | tf_op jit(solution)/shard_map/ppermute | solution.py:24
  68.5 64.3 %collective-permute-start.9 = (f32[192,2048]{1,0:T(8,128)S(1)}, f32[192,2048]{1,0:T(8,128)S(1)}, u32[]{:S(2)}, u32[]{:S(2)}) collective-permute-start(f32[192,2048]{1,0:T(8,128)S(1)} %get-tuple-element.202), channel_id=1, source_target_pairs={{0,16},{8,24},{16,0},{24,8},{1,17},{9,25},{17,1},{25,9},{2,18},{10... | collective-permute-start | bytes 4718600 | tf_op jit(solution)/shard_map/ppermute | solution.py:24
  102.1 62.3 %collective-permute-start.10 = (f32[192,2048]{1,0:T(8,128)S(1)}, f32[192,2048]{1,0:T(8,128)S(1)}, u32[]{:S(2)}, u32[]{:S(2)}) collective-permute-start(f32[192,2048]{1,0:T(8,128)S(1)} %get-tuple-element.210), channel_id=1, source_target_pairs={{0,8},{8,0},{16,24},{24,16},{1,9},{9,1},{17,25},{25,17},{2,10},{10... | collective-permute-start | bytes 4718600 | tf_op jit(solution)/shard_map/ppermute | solution.py:24
  102.2 64.3 %collective-permute-start.11 = (f32[192,2048]{1,0:T(8,128)S(1)}, f32[192,2048]{1,0:T(8,128)S(1)}, u32[]{:S(2)}, u32[]{:S(2)}) collective-permute-start(f32[192,2048]{1,0:T(8,128)S(1)} %get-tuple-element.211), channel_id=1, source_target_pairs={{0,16},{8,24},{16,0},{24,8},{1,17},{9,25},{17,1},{25,9},{2,18},{10... | collective-permute-start | bytes 4718600 | tf_op jit(solution)/shard_map/ppermute | solution.py:24
  135.8 62.3 %collective-permute-start.12 = (f32[192,2048]{1,0:T(8,128)S(1)}, f32[192,2048]{1,0:T(8,128)S(1)}, u32[]{:S(2)}, u32[]{:S(2)}) collective-permute-start(f32[192,2048]{1,0:T(8,128)S(1)} %get-tuple-element.219), channel_id=1, source_target_pairs={{0,8},{8,0},{16,24},{24,16},{1,9},{9,1},{17,25},{25,17},{2,10},{10... | collective-permute-start | bytes 4718600 | tf_op jit(solution)/shard_map/ppermute | solution.py:24
  135.9 64.3 %collective-permute-start.13 = (f32[192,2048]{1,0:T(8,128)S(1)}, f32[192,2048]{1,0:T(8,128)S(1)}, u32[]{:S(2)}, u32[]{:S(2)}) collective-permute-start(f32[192,2048]{1,0:T(8,128)S(1)} %get-tuple-element.220), channel_id=1, source_target_pairs={{0,16},{8,24},{16,0},{24,8},{1,17},{9,25},{17,1},{25,9},{2,18},{10... | collective-permute-start | bytes 4718600 | tf_op jit(solution)/shard_map/ppermute | solution.py:24
  169.5 62.3 %collective-permute-start.14 = (f32[192,2048]{1,0:T(8,128)S(1)}, f32[192,2048]{1,0:T(8,128)S(1)}, u32[]{:S(2)}, u32[]{:S(2)}) collective-permute-start(f32[192,2048]{1,0:T(8,128)S(1)} %get-tuple-element.228), channel_id=1, source_target_pairs={{0,8},{8,0},{16,24},{24,16},{1,9},{9,1},{17,25},{25,17},{2,10},{10... | collective-permute-start | bytes 4718600 | tf_op jit(solution)/shard_map/ppermute | solution.py:24
  169.6 64.3 %collective-permute-start.15 = (f32[192,2048]{1,0:T(8,128)S(1)}, f32[192,2048]{1,0:T(8,128)S(1)}, u32[]{:S(2)}, u32[]{:S(2)}) collective-permute-start(f32[192,2048]{1,0:T(8,128)S(1)} %get-tuple-element.229), channel_id=1, source_target_pairs={{0,16},{8,24},{16,0},{24,8},{1,17},{9,25},{17,1},{25,9},{2,18},{10... | collective-permute-start | bytes 4718600 | tf_op jit(solution)/shard_map/ppermute | solution.py:24
  203.2 62.3 %collective-permute-start.16 = (f32[192,2048]{1,0:T(8,128)S(1)}, f32[192,2048]{1,0:T(8,128)S(1)}, u32[]{:S(2)}, u32[]{:S(2)}) collective-permute-start(f32[192,2048]{1,0:T(8,128)S(1)} %get-tuple-element.237), channel_id=1, source_target_pairs={{0,8},{8,0},{16,24},{24,16},{1,9},{9,1},{17,25},{25,17},{2,10},{10... | collective-permute-start | bytes 4718600 | tf_op jit(solution)/shard_map/ppermute | solution.py:24
  203.4 64.3 %collective-permute-start.17 = (f32[192,2048]{1,0:T(8,128)S(1)}, f32[192,2048]{1,0:T(8,128)S(1)}, u32[]{:S(2)}, u32[]{:S(2)}) collective-permute-start(f32[192,2048]{1,0:T(8,128)S(1)} %get-tuple-element.238), channel_id=1, source_target_pairs={{0,16},{8,24},{16,0},{24,8},{1,17},{9,25},{17,1},{25,9},{2,18},{10... | collective-permute-start | bytes 4718600 | tf_op jit(solution)/shard_map/ppermute | solution.py:24
  237.0 62.3 %collective-permute-start.18 = (f32[192,2048]{1,0:T(8,128)S(1)}, f32[192,2048]{1,0:T(8,128)S(1)}, u32[]{:S(2)}, u32[]{:S(2)}) collective-permute-start(f32[192,2048]{1,0:T(8,128)S(1)} %get-tuple-element.246), channel_id=1, source_target_pairs={{0,8},{8,0},{16,24},{24,16},{1,9},{9,1},{17,25},{25,17},{2,10},{10... | collective-permute-start | bytes 4718600 | tf_op jit(solution)/shard_map/ppermute | solution.py:24
  237.1 64.3 %collective-permute-start.19 = (f32[192,2048]{1,0:T(8,128)S(1)}, f32[192,2048]{1,0:T(8,128)S(1)}, u32[]{:S(2)}, u32[]{:S(2)}) collective-permute-start(f32[192,2048]{1,0:T(8,128)S(1)} %get-tuple-element.247), channel_id=1, source_target_pairs={{0,16},{8,24},{16,0},{24,8},{1,17},{9,25},{17,1},{25,9},{2,18},{10... | collective-permute-start | bytes 4718600 | tf_op jit(solution)/shard_map/ppermute | solution.py:24
  270.7 62.3 %collective-permute-start.24 = (f32[192,2048]{1,0:T(8,128)S(1)}, f32[192,2048]{1,0:T(8,128)S(1)}, u32[]{:S(2)}, u32[]{:S(2)}) collective-permute-start(f32[192,2048]{1,0:T(8,128)S(1)} %get-tuple-element.260), channel_id=1, source_target_pairs={{0,8},{8,0},{16,24},{24,16},{1,9},{9,1},{17,25},{25,17},{2,10},{10... | collective-permute-start | bytes 4718600 | tf_op jit(solution)/shard_map/ppermute | solution.py:24
  270.8 64.3 %collective-permute-start.25 = (f32[192,2048]{1,0:T(8,128)S(1)}, f32[192,2048]{1,0:T(8,128)S(1)}, u32[]{:S(2)}, u32[]{:S(2)}) collective-permute-start(f32[192,2048]{1,0:T(8,128)S(1)} %get-tuple-element.261), channel_id=1, source_target_pairs={{0,16},{8,24},{16,0},{24,8},{1,17},{9,25},{17,1},{25,9},{2,18},{10... | collective-permute-start | bytes 4718600 | tf_op jit(solution)/shard_map/ppermute | solution.py:24
  304.4 62.3 %collective-permute-start.26 = (f32[192,2048]{1,0:T(8,128)S(1)}, f32[192,2048]{1,0:T(8,128)S(1)}, u32[]{:S(2)}, u32[]{:S(2)}) collective-permute-start(f32[192,2048]{1,0:T(8,128)S(1)} %get-tuple-element.267), channel_id=1, source_target_pairs={{0,8},{8,0},{16,24},{24,16},{1,9},{9,1},{17,25},{25,17},{2,10},{10... | collective-permute-start | bytes 4718600 | tf_op jit(solution)/shard_map/ppermute | solution.py:24
  304.5 64.3 %collective-permute-start.27 = (f32[192,2048]{1,0:T(8,128)S(1)}, f32[192,2048]{1,0:T(8,128)S(1)}, u32[]{:S(2)}, u32[]{:S(2)}) collective-permute-start(f32[192,2048]{1,0:T(8,128)S(1)} %get-tuple-element.268), channel_id=1, source_target_pairs={{0,16},{8,24},{16,0},{24,8},{1,17},{9,25},{17,1},{25,9},{2,18},{10... | collective-permute-start | bytes 4718600 | tf_op jit(solution)/shard_map/ppermute | solution.py:24
  338.1 64.4 %collective-permute-start.28 = (f32[200,2048]{1,0:T(8,128)S(1)}, f32[200,2048]{1,0:T(8,128)S(1)}, u32[]{:S(2)}, u32[]{:S(2)}) collective-permute-start(f32[200,2048]{1,0:T(8,128)S(1)} %get-tuple-element.276), channel_id=1, source_target_pairs={{0,8},{8,0},{16,24},{24,16},{1,9},{9,1},{17,25},{25,17},{2,10},{10... | collective-permute-start | bytes 4915208 | tf_op jit(solution)/shard_map/ppermute | solution.py:24
  338.2 64.3 %collective-permute-start.29 = (f32[192,2048]{1,0:T(8,128)S(1)}, f32[192,2048]{1,0:T(8,128)S(1)}, u32[]{:S(2)}, u32[]{:S(2)}) collective-permute-start(f32[192,2048]{1,0:T(8,128)S(1)} %get-tuple-element.277), channel_id=1, source_target_pairs={{0,16},{8,24},{16,0},{24,8},{1,17},{9,25},{17,1},{25,9},{2,18},{10... | collective-permute-start | bytes 4718600 | tf_op jit(solution)/shard_map/ppermute | solution.py:24
  371.8 63.7 %collective-permute-start.30 = (f32[192,2048]{1,0:T(8,128)S(1)}, f32[192,2048]{1,0:T(8,128)S(1)}, u32[]{:S(2)}, u32[]{:S(2)}) collective-permute-start(f32[192,2048]{1,0:T(8,128)S(1)} %get-tuple-element.285), channel_id=1, source_target_pairs={{0,8},{8,0},{16,24},{24,16},{1,9},{9,1},{17,25},{25,17},{2,10},{10... | collective-permute-start | bytes 4718600 | tf_op jit(solution)/shard_map/ppermute | solution.py:24
  371.9 64.3 %collective-permute-start.31 = (f32[192,2048]{1,0:T(8,128)S(1)}, f32[192,2048]{1,0:T(8,128)S(1)}, u32[]{:S(2)}, u32[]{:S(2)}) collective-permute-start(f32[192,2048]{1,0:T(8,128)S(1)} %get-tuple-element.286), channel_id=1, source_target_pairs={{0,16},{8,24},{16,0},{24,8},{1,17},{9,25},{17,1},{25,9},{2,18},{10... | collective-permute-start | bytes 4718600 | tf_op jit(solution)/shard_map/ppermute | solution.py:24
  407.2 64.1 %collective-permute-start.33 = (f32[200,2048]{1,0:T(8,128)}, f32[200,2048]{1,0:T(8,128)S(1)}, u32[]{:S(2)}, u32[]{:S(2)}) collective-permute-start(f32[200,2048]{1,0:T(8,128)} %get-tuple-element.295), channel_id=1, source_target_pairs={{0,16},{8,24},{16,0},{24,8},{1,17},{9,25},{17,1},{25,9},{2,18},{10... | collective-permute-start | bytes 4915208 | tf_op jit(solution)/shard_map/ppermute | solution.py:24
  408.7 60.6 %collective-permute-start.32 = (f32[192,2048]{1,0:T(8,128)}, f32[192,2048]{1,0:T(8,128)}, u32[]{:S(2)}, u32[]{:S(2)}) collective-permute-start(f32[192,2048]{1,0:T(8,128)} %get-tuple-element.294), channel_id=1, source_target_pairs={{0,8},{8,0},{16,24},{24,16},{1,9},{9,1},{17,25},{25,17},{2,10},{10... | collective-permute-start | bytes 4718600 | tf_op jit(solution)/shard_map/ppermute | solution.py:24
  444.2 61.7 %collective-permute-start.37 = (f32[192,2048]{1,0:T(8,128)}, f32[192,2048]{1,0:T(8,128)S(1)}, u32[]{:S(2)}, u32[]{:S(2)}) collective-permute-start(f32[192,2048]{1,0:T(8,128)} %get-tuple-element.313), channel_id=1, source_target_pairs={{0,8},{8,0},{16,24},{24,16},{1,9},{9,1},{17,25},{25,17},{2,10},{10... | collective-permute-start | bytes 4718600 | tf_op jit(solution)/shard_map/ppermute | solution.py:24
  445.7 60.3 %collective-permute-start.38 = (f32[192,2048]{1,0:T(8,128)}, f32[192,2048]{1,0:T(8,128)}, u32[]{:S(2)}, u32[]{:S(2)}) collective-permute-start(f32[192,2048]{1,0:T(8,128)} %get-tuple-element.314), channel_id=1, source_target_pairs={{0,16},{8,24},{16,0},{24,8},{1,17},{9,25},{17,1},{25,9},{2,18},{10... | collective-permute-start | bytes 4718600 | tf_op jit(solution)/shard_map/ppermute | solution.py:24
  485.9 39.4 %collective-permute-start.39 = (f32[128,2048]{1,0:T(8,128)S(1)}, f32[128,2048]{1,0:T(8,128)S(1)}, u32[]{:S(2)}, u32[]{:S(2)}) collective-permute-start(f32[128,2048]{1,0:T(8,128)S(1)} %get-tuple-element.323), channel_id=1, source_target_pairs={{0,8},{8,0},{16,24},{24,16},{1,9},{9,1},{17,25},{25,17},{2,10},{10... | collective-permute-start | bytes 3145736 | tf_op jit(solution)/shard_map/ppermute | solution.py:24
  487.6 39.8 %collective-permute-start.40 = (f32[128,2048]{1,0:T(8,128)S(1)}, f32[128,2048]{1,0:T(8,128)S(1)}, u32[]{:S(2)}, u32[]{:S(2)}) collective-permute-start(f32[128,2048]{1,0:T(8,128)S(1)} %get-tuple-element.324), channel_id=1, source_target_pairs={{0,16},{8,24},{16,0},{24,8},{1,17},{9,25},{17,1},{25,9},{2,18},{10... | collective-permute-start | bytes 3145736 | tf_op jit(solution)/shard_map/ppermute | solution.py:24
  509.5 37.6 %collective-permute-start.41 = (f32[128,2048]{1,0:T(8,128)S(1)}, f32[128,2048]{1,0:T(8,128)S(1)}, u32[]{:S(2)}, u32[]{:S(2)}) collective-permute-start(f32[128,2048]{1,0:T(8,128)S(1)} %get-tuple-element.332), channel_id=1, source_target_pairs={{0,8},{8,0},{16,24},{24,16},{1,9},{9,1},{17,25},{25,17},{2,10},{10... | collective-permute-start | bytes 3145736 | tf_op jit(solution)/shard_map/ppermute | solution.py:24
  510.1 38.4 %collective-permute-start.42 = (f32[128,2048]{1,0:T(8,128)S(1)}, f32[128,2048]{1,0:T(8,128)S(1)}, u32[]{:S(2)}, u32[]{:S(2)}) collective-permute-start(f32[128,2048]{1,0:T(8,128)S(1)} %get-tuple-element.333), channel_id=1, source_target_pairs={{0,16},{8,24},{16,0},{24,8},{1,17},{9,25},{17,1},{25,9},{2,18},{10... | collective-permute-start | bytes 3145736 | tf_op jit(solution)/shard_map/ppermute | solution.py:24
  (33 other events, 302.6 us)

commit v7 on v6

--- a/solution.py
+++ b/solution.py
@@ -25,7 +25,8 @@
 
 
 def exchange(x, axes):
-    return [x] + [swap(x, axes, mask) for mask in range(1, lax.axis_size(axes))]
+    got = [swap(x, axes, mask) for mask in reversed(range(1, lax.axis_size(axes)))]
+    return [x] + got[::-1]
 
 
 def tree_sum(got):
@@ -194,7 +195,7 @@
             scratch_shapes=scratch,
         ),
         input_output_aliases=aliases,
-        compiler_params=params_of(34),
+        compiler_params=params_of(20 if finishes else 34),
         cost_estimate=pl.CostEstimate(
             flops=part * width * 20, bytes_accessed=moved, transcendentals=0
         ),
@@ -239,7 +240,7 @@
             jax.ShapeDtypeStruct((sublanes, 2 * width // sublanes + lanes), f32),
         ],
         scratch_shapes=[pltpu.VMEM((sublanes, width), f32)],
-        compiler_params=params_of(16),
+        compiler_params=params_of(4),
         cost_estimate=pl.CostEstimate(
             flops=3 * summed.size, bytes_accessed=4 * summed.size, transcendentals=0
         ),
@@ -383,7 +384,7 @@
             stats, me = tie(stats, me)
             col_new, pairs = col_stage(last["m"], [stats])
             outs = finish(
-                last["m"], extent, last["row_new"], col_new, pairs, last["summed"], blocked, outs, 36
+                last["m"], extent, last["row_new"], col_new, pairs, last["summed"], blocked, outs, 24
             )
             me, *outs = tie(me, *outs)
         if j == total_blocks - 1:

time: 591 us -> 591 us (level)
    unnamed x26 -> x28, local copies, waits for them, and re-layouts: 20.5 us -> 26.4 us
  transfers between devices with their start and end apart: 53 -> 53, of which waited for: 45 -> 45; matrix products, arithmetic and copies ran while one was open for 2% -> 2% of each run, Pallas kernels for 12% -> 11%
where the time goes in v7:
time: 591 us; the launch traced here: 590 us
  waiting for transfers between devices  410 us (69%)
  Pallas kernels  78.1 us (13%)
  starting transfers between devices  65 us (11%)
  local copies, waits for them, and re-layouts  34.3 us (6%)
    ppermute x53, waiting for transfers between devices, swap(): return lax.ppermute(x, axes, [(i, i ^ mask) for i in range(size)])  410 us
    ppermute x53, starting transfers between devices, swap(): return lax.ppermute(x, axes, [(i, i ^ mask) for i in range(size)])  65 us
    pallas_call x20, Pallas kernels, step(): pl.pallas_call(functools.partial(step_kernel, takes, finishes, b, sends,...  61.1 us
    unnamed x28, local copies, waits for them, and re-layouts  26.4 us
    pallas_call x2, Pallas kernels, finish(): pl.pallas_call(functools.partial(finish_kernel, m, extent, len(pairs), st...  14.7 us
  transfers between devices with their start and end apart: 53, of which 45 were waited for; matrix products, arithmetic and copies ran while one was open for 2% of the time, Pallas kernels for 11%

profile of v7, /device:TPU:0, one launch (start us, length us, event | category | flops | bytes accessed | tf_op | source)
XLA Modules:
  0.0 589.9 jit_solution(12009713732203853283)
XLA Ops:
  9.8 8.6 %collective-permute-done.refs_1_ = f32[64,2048]{1,0:T(8,128)S(1)} collective-permute-done((f32[64,2048]{1,0:T(8,128)S(1)}, f32[64,2048]{1,0:T(8,128)S(1)}, u32[]{:S(2)}, u32[]{:S(2)}) %collective-permute-start) | collective-permute-done | bytes 524320 | tf_op jit(solution)/shard_map/ppermute | solution.py:24
  25.1 4.5 collective-permute-done.2.refs_1_
  36.3 27.0 %collective-permute-done.4.refs_1_ = f32[192,2048]{1,0:T(8,128)S(1)} collective-permute-done((f32[192,2048]{1,0:T(8,128)S(1)}, f32[192,2048]{1,0:T(8,128)S(1)}, u32[]{:S(2)}, u32[]{:S(2)}) %collective-permute-start.4) | collective-permute-done | bytes 1572896 | tf_op jit(solution)/shard_map/ppermute | solution.py:24
  70.5 26.5 %collective-permute-done.6.refs_1_ = f32[192,2048]{1,0:T(8,128)S(1)} collective-permute-done((f32[192,2048]{1,0:T(8,128)S(1)}, f32[192,2048]{1,0:T(8,128)S(1)}, u32[]{:S(2)}, u32[]{:S(2)}) %collective-permute-start.6) | collective-permute-done | bytes 1572896 | tf_op jit(solution)/shard_map/ppermute | solution.py:24
  104.2 26.5 %collective-permute-done.8.refs_1_ = f32[192,2048]{1,0:T(8,128)S(1)} collective-permute-done((f32[192,2048]{1,0:T(8,128)S(1)}, f32[192,2048]{1,0:T(8,128)S(1)}, u32[]{:S(2)}, u32[]{:S(2)}) %collective-permute-start.8) | collective-permute-done | bytes 1572896 | tf_op jit(solution)/shard_map/ppermute | solution.py:24
  137.9 26.5 %collective-permute-done.10.refs_1_ = f32[192,2048]{1,0:T(8,128)S(1)} collective-permute-done((f32[192,2048]{1,0:T(8,128)S(1)}, f32[192,2048]{1,0:T(8,128)S(1)}, u32[]{:S(2)}, u32[]{:S(2)}) %collective-permute-start.10) | collective-permute-done | bytes 1572896 | tf_op jit(solution)/shard_map/ppermute | solution.py:24
  171.7 26.5 %collective-permute-done.12.refs_1_ = f32[192,2048]{1,0:T(8,128)S(1)} collective-permute-done((f32[192,2048]{1,0:T(8,128)S(1)}, f32[192,2048]{1,0:T(8,128)S(1)}, u32[]{:S(2)}, u32[]{:S(2)}) %collective-permute-start.12) | collective-permute-done | bytes 1572896 | tf_op jit(solution)/shard_map/ppermute | solution.py:24
  205.4 26.5 %collective-permute-done.14.refs_1_ = f32[192,2048]{1,0:T(8,128)S(1)} collective-permute-done((f32[192,2048]{1,0:T(8,128)S(1)}, f32[192,2048]{1,0:T(8,128)S(1)}, u32[]{:S(2)}, u32[]{:S(2)}) %collective-permute-start.14) | collective-permute-done | bytes 1572896 | tf_op jit(solution)/shard_map/ppermute | solution.py:24
  239.1 26.5 %collective-permute-done.16.refs_1_ = f32[192,2048]{1,0:T(8,128)S(1)} collective-permute-done((f32[192,2048]{1,0:T(8,128)S(1)}, f32[192,2048]{1,0:T(8,128)S(1)}, u32[]{:S(2)}, u32[]{:S(2)}) %collective-permute-start.16) | collective-permute-done | bytes 1572896 | tf_op jit(solution)/shard_map/ppermute | solution.py:24
  272.8 26.5 %collective-permute-done.18.refs_1_ = f32[192,2048]{1,0:T(8,128)S(1)} collective-permute-done((f32[192,2048]{1,0:T(8,128)S(1)}, f32[192,2048]{1,0:T(8,128)S(1)}, u32[]{:S(2)}, u32[]{:S(2)}) %collective-permute-start.18) | collective-permute-done | bytes 1572896 | tf_op jit(solution)/shard_map/ppermute | solution.py:24
  314.6 3.6 collective-permute-start.22
  322.3 10.6 %collective-permute-done.24.refs_1_ = f32[192,2048]{1,0:T(8,128)S(1)} collective-permute-done((f32[192,2048]{1,0:T(8,128)S(1)}, f32[192,2048]{1,0:T(8,128)S(1)}, u32[]{:S(2)}, u32[]{:S(2)}) %collective-permute-start.24) | collective-permute-done | bytes 1572896 | tf_op jit(solution)/shard_map/ppermute | solution.py:24
  340.2 26.5 %collective-permute-done.26.refs_1_ = f32[192,2048]{1,0:T(8,128)S(1)} collective-permute-done((f32[192,2048]{1,0:T(8,128)S(1)}, f32[192,2048]{1,0:T(8,128)S(1)}, u32[]{:S(2)}, u32[]{:S(2)}) %collective-permute-start.26) | collective-permute-done | bytes 1572896 | tf_op jit(solution)/shard_map/ppermute | solution.py:24
  373.9 28.6 %collective-permute-done.29.refs_2_ = f32[192,2048]{1,0:T(8,128)S(1)} collective-permute-done((f32[192,2048]{1,0:T(8,128)S(1)}, f32[192,2048]{1,0:T(8,128)S(1)}, u32[]{:S(2)}, u32[]{:S(2)}) %collective-permute-start.29) | collective-permute-done | bytes 1572896 | tf_op jit(solution)/shard_map/ppermute | solution.py:24
  402.5 4.6 step.34
  410.0 25.5 %collective-permute-done.30.refs_1_ = f32[192,2048]{1,0:T(8,128)S(1)} collective-permute-done((f32[192,2048]{1,0:T(8,128)S(1)}, f32[192,2048]{1,0:T(8,128)S(1)}, u32[]{:S(2)}, u32[]{:S(2)}) %collective-permute-start.30) | collective-permute-done | bytes 1572896 | tf_op jit(solution)/shard_map/ppermute | solution.py:24
  436.2 4.7 step.35
  440.9 3.4 copy-done
  447.2 22.1 %collective-permute-done.32.refs_1_ = f32[192,2048]{1,0:T(8,128)} collective-permute-done((f32[192,2048]{1,0:T(8,128)}, f32[192,2048]{1,0:T(8,128)}, u32[]{:S(2)}, u32[]{:S(2)}) %collective-permute-start.32) | collective-permute-done | bytes 1572896 | tf_op jit(solution)/shard_map/ppermute | solution.py:24
  471.3 3.4 copy-done.1
  474.7 4.7 step.36
  492.4 3.5 copy-done.6
  495.9 5.9 copy-done.7
  501.8 7.5 %finish.2 = (f32[2,8,2,64,2048]{4,3,2,1,0:T(8,128)}, f32[2,8,2,64,2048]{4,3,2,1,0:T(8,128)}) custom-call(f32[8,128]{1,0:T(8,128)S(1)} %get-tuple-element.306.row_new, f32[8,256]{1,0:T(8,128)S(1)} %get-tuple-element.308.col_new, f32[8,2,64,2048]{3,2,1,0:T(8,128)S(1)} %copy-done.6, f32[2,8,2,64,2048]{4,3,2,1,0:T(8,128)S(1)} %bitcast.18, ...), custom_call_target="tpu_custom_call" | custom-call | flops 8388608 | bytes 33554432 | tf_op jit(solution)/shard_map/finish/pallas_call | solution.py:316
  509.4 3.5 step.37
  514.9 7.9 %slice.19 = f32[1,1024,2048]{2,1,0:T(8,128)} slice(f32[2,1024,2048]{2,1,0:T(8,128)} %param.5), slice={[1:2], [0:1024], [0:2048]} | slice | bytes 16777216 | tf_op jit(solution)/shard_map/slice | solution.py:391
  529.9 17.1 %collective-permute-done.41.refs_1_ = f32[128,2048]{1,0:T(8,128)S(1)} collective-permute-done((f32[128,2048]{1,0:T(8,128)S(1)}, f32[128,2048]{1,0:T(8,128)S(1)}, u32[]{:S(2)}, u32[]{:S(2)}) %collective-permute-start.41) | collective-permute-done | bytes 1048608 | tf_op jit(solution)/shard_map/ppermute | solution.py:24
  557.0 3.5 collective-permute-done.45.refs_3_
  570.5 3.6 collective-permute-start.52
  575.9 3.4 copy-done.4
  579.3 3.4 copy-done.8
  582.7 7.2 %finish.3 = (f32[2,8,2,64,2048]{4,3,2,1,0:T(8,128)}, f32[2,8,2,64,2048]{4,3,2,1,0:T(8,128)}) custom-call(f32[8,128]{1,0:T(8,128)S(1)} %get-tuple-element.343.row_new, f32[8,256]{1,0:T(8,128)S(1)} %get-tuple-element.345.col_new, f32[8,2,64,2048]{3,2,1,0:T(8,128)S(1)} %copy-done.4, ...), custom_call_target="tpu_custom_call", output_to_operand_aliasing={{0}: (8, {}), {1}: (9, {})} | custom-call | flops 8388608 | bytes 33554432 | tf_op jit(solution)/shard_map/finish/pallas_call | solution.py:316
  (138 shorter events, 159.3 us)
Async XLA Ops:
  22.9 40.4 %collective-permute-start.4 = (f32[192,2048]{1,0:T(8,128)S(1)}, f32[192,2048]{1,0:T(8,128)S(1)}, u32[]{:S(2)}, u32[]{:S(2)}) collective-permute-start(f32[192,2048]{1,0:T(8,128)S(1)} %get-tuple-element.184), channel_id=1, source_target_pairs={{0,8},{8,0},{16,24},{24,16},{1,9},{9,1},{17,25},{25,17},{2,10},{10... | collective-permute-start | bytes 4718600 | tf_op jit(solution)/shard_map/ppermute | solution.py:24
  23.1 42.4 %collective-permute-start.5 = (f32[192,2048]{1,0:T(8,128)S(1)}, f32[192,2048]{1,0:T(8,128)S(1)}, u32[]{:S(2)}, u32[]{:S(2)}) collective-permute-start(f32[192,2048]{1,0:T(8,128)S(1)} %get-tuple-element.185), channel_id=1, source_target_pairs={{0,16},{8,24},{16,0},{24,8},{1,17},{9,25},{17,1},{25,9},{2,18},{10... | collective-permute-start | bytes 4718600 | tf_op jit(solution)/shard_map/ppermute | solution.py:24
  34.2 62.8 %collective-permute-start.6 = (f32[192,2048]{1,0:T(8,128)S(1)}, f32[192,2048]{1,0:T(8,128)S(1)}, u32[]{:S(2)}, u32[]{:S(2)}) collective-permute-start(f32[192,2048]{1,0:T(8,128)S(1)} %get-tuple-element.187), channel_id=1, source_target_pairs={{0,8},{8,0},{16,24},{24,16},{1,9},{9,1},{17,25},{25,17},{2,10},{10... | collective-permute-start | bytes 4718600 | tf_op jit(solution)/shard_map/ppermute | solution.py:24
  34.3 64.8 %collective-permute-start.7 = (f32[192,2048]{1,0:T(8,128)S(1)}, f32[192,2048]{1,0:T(8,128)S(1)}, u32[]{:S(2)}, u32[]{:S(2)}) collective-permute-start(f32[192,2048]{1,0:T(8,128)S(1)} %get-tuple-element.188), channel_id=1, source_target_pairs={{0,16},{8,24},{16,0},{24,8},{1,17},{9,25},{17,1},{25,9},{2,18},{10... | collective-permute-start | bytes 4718600 | tf_op jit(solution)/shard_map/ppermute | solution.py:24
  68.4 62.3 %collective-permute-start.8 = (f32[192,2048]{1,0:T(8,128)S(1)}, f32[192,2048]{1,0:T(8,128)S(1)}, u32[]{:S(2)}, u32[]{:S(2)}) collective-permute-start(f32[192,2048]{1,0:T(8,128)S(1)} %get-tuple-element.201), channel_id=1, source_target_pairs={{0,8},{8,0},{16,24},{24,16},{1,9},{9,1},{17,25},{25,17},{2,10},{10... | collective-permute-start | bytes 4718600 | tf_op jit(solution)/shard_map/ppermute | solution.py:24
  68.5 64.3 %collective-permute-start.9 = (f32[192,2048]{1,0:T(8,128)S(1)}, f32[192,2048]{1,0:T(8,128)S(1)}, u32[]{:S(2)}, u32[]{:S(2)}) collective-permute-start(f32[192,2048]{1,0:T(8,128)S(1)} %get-tuple-element.202), channel_id=1, source_target_pairs={{0,16},{8,24},{16,0},{24,8},{1,17},{9,25},{17,1},{25,9},{2,18},{10... | collective-permute-start | bytes 4718600 | tf_op jit(solution)/shard_map/ppermute | solution.py:24
  102.1 62.3 %collective-permute-start.10 = (f32[192,2048]{1,0:T(8,128)S(1)}, f32[192,2048]{1,0:T(8,128)S(1)}, u32[]{:S(2)}, u32[]{:S(2)}) collective-permute-start(f32[192,2048]{1,0:T(8,128)S(1)} %get-tuple-element.210), channel_id=1, source_target_pairs={{0,8},{8,0},{16,24},{24,16},{1,9},{9,1},{17,25},{25,17},{2,10},{10... | collective-permute-start | bytes 4718600 | tf_op jit(solution)/shard_map/ppermute | solution.py:24
  102.2 64.3 %collective-permute-start.11 = (f32[192,2048]{1,0:T(8,128)S(1)}, f32[192,2048]{1,0:T(8,128)S(1)}, u32[]{:S(2)}, u32[]{:S(2)}) collective-permute-start(f32[192,2048]{1,0:T(8,128)S(1)} %get-tuple-element.211), channel_id=1, source_target_pairs={{0,16},{8,24},{16,0},{24,8},{1,17},{9,25},{17,1},{25,9},{2,18},{10... | collective-permute-start | bytes 4718600 | tf_op jit(solution)/shard_map/ppermute | solution.py:24
  135.8 62.3 %collective-permute-start.12 = (f32[192,2048]{1,0:T(8,128)S(1)}, f32[192,2048]{1,0:T(8,128)S(1)}, u32[]{:S(2)}, u32[]{:S(2)}) collective-permute-start(f32[192,2048]{1,0:T(8,128)S(1)} %get-tuple-element.219), channel_id=1, source_target_pairs={{0,8},{8,0},{16,24},{24,16},{1,9},{9,1},{17,25},{25,17},{2,10},{10... | collective-permute-start | bytes 4718600 | tf_op jit(solution)/shard_map/ppermute | solution.py:24
  135.9 64.3 %collective-permute-start.13 = (f32[192,2048]{1,0:T(8,128)S(1)}, f32[192,2048]{1,0:T(8,128)S(1)}, u32[]{:S(2)}, u32[]{:S(2)}) collective-permute-start(f32[192,2048]{1,0:T(8,128)S(1)} %get-tuple-element.220), channel_id=1, source_target_pairs={{0,16},{8,24},{16,0},{24,8},{1,17},{9,25},{17,1},{25,9},{2,18},{10... | collective-permute-start | bytes 4718600 | tf_op jit(solution)/shard_map/ppermute | solution.py:24
  169.5 62.3 %collective-permute-start.14 = (f32[192,2048]{1,0:T(8,128)S(1)}, f32[192,2048]{1,0:T(8,128)S(1)}, u32[]{:S(2)}, u32[]{:S(2)}) collective-permute-start(f32[192,2048]{1,0:T(8,128)S(1)} %get-tuple-element.228), channel_id=1, source_target_pairs={{0,8},{8,0},{16,24},{24,16},{1,9},{9,1},{17,25},{25,17},{2,10},{10... | collective-permute-start | bytes 4718600 | tf_op jit(solution)/shard_map/ppermute | solution.py:24
  169.6 64.3 %collective-permute-start.15 = (f32[192,2048]{1,0:T(8,128)S(1)}, f32[192,2048]{1,0:T(8,128)S(1)}, u32[]{:S(2)}, u32[]{:S(2)}) collective-permute-start(f32[192,2048]{1,0:T(8,128)S(1)} %get-tuple-element.229), channel_id=1, source_target_pairs={{0,16},{8,24},{16,0},{24,8},{1,17},{9,25},{17,1},{25,9},{2,18},{10... | collective-permute-start | bytes 4718600 | tf_op jit(solution)/shard_map/ppermute | solution.py:24
  203.2 62.3 %collective-permute-start.16 = (f32[192,2048]{1,0:T(8,128)S(1)}, f32[192,2048]{1,0:T(8,128)S(1)}, u32[]{:S(2)}, u32[]{:S(2)}) collective-permute-start(f32[192,2048]{1,0:T(8,128)S(1)} %get-tuple-element.237), channel_id=1, source_target_pairs={{0,8},{8,0},{16,24},{24,16},{1,9},{9,1},{17,25},{25,17},{2,10},{10... | collective-permute-start | bytes 4718600 | tf_op jit(solution)/shard_map/ppermute | solution.py:24
  203.3 64.3 %collective-permute-start.17 = (f32[192,2048]{1,0:T(8,128)S(1)}, f32[192,2048]{1,0:T(8,128)S(1)}, u32[]{:S(2)}, u32[]{:S(2)}) collective-permute-start(f32[192,2048]{1,0:T(8,128)S(1)} %get-tuple-element.238), channel_id=1, source_target_pairs={{0,16},{8,24},{16,0},{24,8},{1,17},{9,25},{17,1},{25,9},{2,18},{10... | collective-permute-start | bytes 4718600 | tf_op jit(solution)/shard_map/ppermute | solution.py:24
  236.9 62.3 %collective-permute-start.18 = (f32[192,2048]{1,0:T(8,128)S(1)}, f32[192,2048]{1,0:T(8,128)S(1)}, u32[]{:S(2)}, u32[]{:S(2)}) collective-permute-start(f32[192,2048]{1,0:T(8,128)S(1)} %get-tuple-element.246), channel_id=1, source_target_pairs={{0,8},{8,0},{16,24},{24,16},{1,9},{9,1},{17,25},{25,17},{2,10},{10... | collective-permute-start | bytes 4718600 | tf_op jit(solution)/shard_map/ppermute | solution.py:24
  237.1 64.3 %collective-permute-start.19 = (f32[192,2048]{1,0:T(8,128)S(1)}, f32[192,2048]{1,0:T(8,128)S(1)}, u32[]{:S(2)}, u32[]{:S(2)}) collective-permute-start(f32[192,2048]{1,0:T(8,128)S(1)} %get-tuple-element.247), channel_id=1, source_target_pairs={{0,16},{8,24},{16,0},{24,8},{1,17},{9,25},{17,1},{25,9},{2,18},{10... | collective-permute-start | bytes 4718600 | tf_op jit(solution)/shard_map/ppermute | solution.py:24
  270.7 62.3 %collective-permute-start.24 = (f32[192,2048]{1,0:T(8,128)S(1)}, f32[192,2048]{1,0:T(8,128)S(1)}, u32[]{:S(2)}, u32[]{:S(2)}) collective-permute-start(f32[192,2048]{1,0:T(8,128)S(1)} %get-tuple-element.260), channel_id=1, source_target_pairs={{0,8},{8,0},{16,24},{24,16},{1,9},{9,1},{17,25},{25,17},{2,10},{10... | collective-permute-start | bytes 4718600 | tf_op jit(solution)/shard_map/ppermute | solution.py:24
  270.8 64.3 %collective-permute-start.25 = (f32[192,2048]{1,0:T(8,128)S(1)}, f32[192,2048]{1,0:T(8,128)S(1)}, u32[]{:S(2)}, u32[]{:S(2)}) collective-permute-start(f32[192,2048]{1,0:T(8,128)S(1)} %get-tuple-element.261), channel_id=1, source_target_pairs={{0,16},{8,24},{16,0},{24,8},{1,17},{9,25},{17,1},{25,9},{2,18},{10... | collective-permute-start | bytes 4718600 | tf_op jit(solution)/shard_map/ppermute | solution.py:24
  304.4 62.3 %collective-permute-start.26 = (f32[192,2048]{1,0:T(8,128)S(1)}, f32[192,2048]{1,0:T(8,128)S(1)}, u32[]{:S(2)}, u32[]{:S(2)}) collective-permute-start(f32[192,2048]{1,0:T(8,128)S(1)} %get-tuple-element.267), channel_id=1, source_target_pairs={{0,8},{8,0},{16,24},{24,16},{1,9},{9,1},{17,25},{25,17},{2,10},{10... | collective-permute-start | bytes 4718600 | tf_op jit(solution)/shard_map/ppermute | solution.py:24
  304.5 64.3 %collective-permute-start.27 = (f32[192,2048]{1,0:T(8,128)S(1)}, f32[192,2048]{1,0:T(8,128)S(1)}, u32[]{:S(2)}, u32[]{:S(2)}) collective-permute-start(f32[192,2048]{1,0:T(8,128)S(1)} %get-tuple-element.268), channel_id=1, source_target_pairs={{0,16},{8,24},{16,0},{24,8},{1,17},{9,25},{17,1},{25,9},{2,18},{10... | collective-permute-start | bytes 4718600 | tf_op jit(solution)/shard_map/ppermute | solution.py:24
  338.1 64.4 %collective-permute-start.28 = (f32[200,2048]{1,0:T(8,128)S(1)}, f32[200,2048]{1,0:T(8,128)S(1)}, u32[]{:S(2)}, u32[]{:S(2)}) collective-permute-start(f32[200,2048]{1,0:T(8,128)S(1)} %get-tuple-element.276), channel_id=1, source_target_pairs={{0,8},{8,0},{16,24},{24,16},{1,9},{9,1},{17,25},{25,17},{2,10},{10... | collective-permute-start | bytes 4915208 | tf_op jit(solution)/shard_map/ppermute | solution.py:24
  338.2 64.3 %collective-permute-start.29 = (f32[192,2048]{1,0:T(8,128)S(1)}, f32[192,2048]{1,0:T(8,128)S(1)}, u32[]{:S(2)}, u32[]{:S(2)}) collective-permute-start(f32[192,2048]{1,0:T(8,128)S(1)} %get-tuple-element.277), channel_id=1, source_target_pairs={{0,16},{8,24},{16,0},{24,8},{1,17},{9,25},{17,1},{25,9},{2,18},{10... | collective-permute-start | bytes 4718600 | tf_op jit(solution)/shard_map/ppermute | solution.py:24
  371.8 63.7 %collective-permute-start.30 = (f32[192,2048]{1,0:T(8,128)S(1)}, f32[192,2048]{1,0:T(8,128)S(1)}, u32[]{:S(2)}, u32[]{:S(2)}) collective-permute-start(f32[192,2048]{1,0:T(8,128)S(1)} %get-tuple-element.285), channel_id=1, source_target_pairs={{0,8},{8,0},{16,24},{24,16},{1,9},{9,1},{17,25},{25,17},{2,10},{10... | collective-permute-start | bytes 4718600 | tf_op jit(solution)/shard_map/ppermute | solution.py:24
  371.9 64.3 %collective-permute-start.31 = (f32[192,2048]{1,0:T(8,128)S(1)}, f32[192,2048]{1,0:T(8,128)S(1)}, u32[]{:S(2)}, u32[]{:S(2)}) collective-permute-start(f32[192,2048]{1,0:T(8,128)S(1)} %get-tuple-element.286), channel_id=1, source_target_pairs={{0,16},{8,24},{16,0},{24,8},{1,17},{9,25},{17,1},{25,9},{2,18},{10... | collective-permute-start | bytes 4718600 | tf_op jit(solution)/shard_map/ppermute | solution.py:24
  407.1 64.2 %collective-permute-start.33 = (f32[200,2048]{1,0:T(8,128)}, f32[200,2048]{1,0:T(8,128)S(1)}, u32[]{:S(2)}, u32[]{:S(2)}) collective-permute-start(f32[200,2048]{1,0:T(8,128)} %get-tuple-element.295), channel_id=1, source_target_pairs={{0,16},{8,24},{16,0},{24,8},{1,17},{9,25},{17,1},{25,9},{2,18},{10... | collective-permute-start | bytes 4915208 | tf_op jit(solution)/shard_map/ppermute | solution.py:24
  408.6 60.7 %collective-permute-start.32 = (f32[192,2048]{1,0:T(8,128)}, f32[192,2048]{1,0:T(8,128)}, u32[]{:S(2)}, u32[]{:S(2)}) collective-permute-start(f32[192,2048]{1,0:T(8,128)} %get-tuple-element.294), channel_id=1, source_target_pairs={{0,8},{8,0},{16,24},{24,16},{1,9},{9,1},{17,25},{25,17},{2,10},{10... | collective-permute-start | bytes 4718600 | tf_op jit(solution)/shard_map/ppermute | solution.py:24
  444.2 65.1 %collective-permute-start.37 = (f32[192,2048]{1,0:T(8,128)}, f32[192,2048]{1,0:T(8,128)S(1)}, u32[]{:S(2)}, u32[]{:S(2)}) collective-permute-start(f32[192,2048]{1,0:T(8,128)} %get-tuple-element.313), channel_id=1, source_target_pairs={{0,8},{8,0},{16,24},{24,16},{1,9},{9,1},{17,25},{25,17},{2,10},{10... | collective-permute-start | bytes 4718600 | tf_op jit(solution)/shard_map/ppermute | solution.py:24
  445.7 63.7 %collective-permute-start.38 = (f32[192,2048]{1,0:T(8,128)}, f32[192,2048]{1,0:T(8,128)}, u32[]{:S(2)}, u32[]{:S(2)}) collective-permute-start(f32[192,2048]{1,0:T(8,128)} %get-tuple-element.314), channel_id=1, source_target_pairs={{0,16},{8,24},{16,0},{24,8},{1,17},{9,25},{17,1},{25,9},{2,18},{10... | collective-permute-start | bytes 4718600 | tf_op jit(solution)/shard_map/ppermute | solution.py:24
  487.2 38.2 %collective-permute-start.39 = (f32[128,2048]{1,0:T(8,128)}, f32[128,2048]{1,0:T(8,128)S(1)}, u32[]{:S(2)}, u32[]{:S(2)}) collective-permute-start(f32[128,2048]{1,0:T(8,128)} %get-tuple-element.323), channel_id=1, source_target_pairs={{0,8},{8,0},{16,24},{24,16},{1,9},{9,1},{17,25},{25,17},{2,10},{10... | collective-permute-start | bytes 3145736 | tf_op jit(solution)/shard_map/ppermute | solution.py:24
  488.9 38.6 %collective-permute-start.40 = (f32[128,2048]{1,0:T(8,128)}, f32[128,2048]{1,0:T(8,128)S(1)}, u32[]{:S(2)}, u32[]{:S(2)}) collective-permute-start(f32[128,2048]{1,0:T(8,128)} %get-tuple-element.324), channel_id=1, source_target_pairs={{0,16},{8,24},{16,0},{24,8},{1,17},{9,25},{17,1},{25,9},{2,18},{10... | collective-permute-start | bytes 3145736 | tf_op jit(solution)/shard_map/ppermute | solution.py:24
  512.8 34.2 %collective-permute-start.41 = (f32[128,2048]{1,0:T(8,128)S(1)}, f32[128,2048]{1,0:T(8,128)S(1)}, u32[]{:S(2)}, u32[]{:S(2)}) collective-permute-start(f32[128,2048]{1,0:T(8,128)S(1)} %get-tuple-element.332), channel_id=1, source_target_pairs={{0,8},{8,0},{16,24},{24,16},{1,9},{9,1},{17,25},{25,17},{2,10},{10... | collective-permute-start | bytes 3145736 | tf_op jit(solution)/shard_map/ppermute | solution.py:24
  513.4 35.0 %collective-permute-start.42 = (f32[128,2048]{1,0:T(8,128)S(1)}, f32[128,2048]{1,0:T(8,128)S(1)}, u32[]{:S(2)}, u32[]{:S(2)}) collective-permute-start(f32[128,2048]{1,0:T(8,128)S(1)} %get-tuple-element.333), channel_id=1, source_target_pairs={{0,16},{8,24},{16,0},{24,8},{1,17},{9,25},{17,1},{25,9},{2,18},{10... | collective-permute-start | bytes 3145736 | tf_op jit(solution)/shard_map/ppermute | solution.py:24
  (34 other events, 306.8 us)

commit v8 on v6

--- a/solution.py
+++ b/solution.py
@@ -25,7 +25,8 @@
 
 
 def exchange(x, axes):
-    return [x] + [swap(x, axes, mask) for mask in range(1, lax.axis_size(axes))]
+    got = [swap(x, axes, mask) for mask in reversed(range(1, lax.axis_size(axes)))]
+    return [x] + got[::-1]
 
 
 def tree_sum(got):
@@ -115,9 +116,9 @@
 
 def step(j, total_blocks, me, partials, got, sums, stats, brings, carries):
     mats, _, count, _, part, width = partials.shape
-    tile = min(tile_rows, part)
     finishes = j >= 2
     takes = 0 <= j < total_blocks
+    tile = min(tile_rows if takes else 2 * tile_rows, part)
     sends = takes
     starts = j + 2 < total_blocks
     b = (j - 2) % count
@@ -273,53 +274,49 @@
     )(factor, *parts)
 
 
-def finish_kernel(m, extent, partners, staged, row_new, col_new, summed, params, *refs):
+def finish_kernel(m, extent, partners, row_new, col_new, summed, params, *refs):
     pairs, (new_params, update, column, by_col) = refs[:partners], refs[-4:]
     count, _, part, width = summed.shape
-    row_level = pairs[0][1:2, 0:1]
-    total = tree_sum([x[0:1, 0:1] for x in pairs]) * row_level
-    spread = jnp.sqrt(total / (extent * extent))
-    factor = jnp.sqrt(row_level) / jnp.maximum(1.0, spread / clip_limit)
-    by_row = jnp.transpose(lax.rsqrt(row_new[...]) * factor)
-    for i in range(count):
-        column[i] = jnp.broadcast_to(by_row[:, i : i + 1], column.shape[1:])
-    size = width // sublanes
-    for k in range(sublanes):
-        by_col[:, k * size : (k + 1) * size] = lax.rsqrt(col_new[k : k + 1])
-
-    def body(*blocks):
+
+    def scale():
+        row_level = pairs[0][1:2, 0:1]
+        total = tree_sum([x[0:1, 0:1] for x in pairs]) * row_level
+        spread = jnp.sqrt(total / (extent * extent))
+        factor = jnp.sqrt(row_level) / jnp.maximum(1.0, spread / clip_limit)
+        by_row = jnp.transpose(lax.rsqrt(row_new[...]) * factor)
+        for i in range(count):
+            column[i] = jnp.broadcast_to(by_row[:, i : i + 1], column.shape[1:])
+        size = width // sublanes
+        for k in range(sublanes):
+            by_col[:, k * size : (k + 1) * size] = lax.rsqrt(col_new[k : k + 1])
+
+    def body(p, new_p, moved):
         i = pl.program_id(0)
-        new_p, moved = blocks[-2:]
+        pl.when(i == 0)(scale)
         for half in range(2):
             for r in range(0, part, sublanes):
                 at = half * part + r
                 mine = column[i, at : at + sublanes][:, 0:1]
                 y = summed[i, half, r : r + sublanes] * mine * by_col[...]
                 moved[half, r : r + sublanes] = y
-                p = params[i, half, r : r + sublanes] if staged else blocks[0][half, r : r + sublanes]
-                new_p[half, r : r + sublanes] = p - learn_rate * y
+                new_p[half, r : r + sublanes] = p[half, r : r + sublanes] - learn_rate * y
 
     of_matrix = pl.BlockSpec((None, None, 2, part, width), lambda i: (m, i, 0, 0, 0))
     pltpu.emit_pipeline(
-        body, grid=(count,), in_specs=[] if staged else [of_matrix], out_specs=[of_matrix] * 2
-    )(*([] if staged else [params]), new_params, update)
+        body, grid=(count,), in_specs=[of_matrix], out_specs=[of_matrix] * 2
+    )(params, new_params, update)
 
 
 def finish(m, extent, row_new, col_new, pairs, summed, params, outs, mib):
     count, _, part, width = summed.shape
-    staged = outs is not None
-    held = outs if staged else ()
+    held = () if outs is None else outs
     in_hbm = pl.BlockSpec(memory_space=pltpu.HBM)
     in_vmem = pl.BlockSpec(memory_space=pltpu.VMEM)
-    out_shape = jax.ShapeDtypeStruct(held[0].shape if staged else params.shape, f32)
     return pl.pallas_call(
-        functools.partial(finish_kernel, m, extent, len(pairs), staged),
-        in_specs=[in_vmem] * 3
-        + [in_vmem if staged else in_hbm]
-        + [in_vmem] * len(pairs)
-        + [in_hbm] * len(held),
+        functools.partial(finish_kernel, m, extent, len(pairs)),
+        in_specs=[in_vmem] * 3 + [in_hbm] + [in_vmem] * len(pairs) + [in_hbm] * len(held),
         out_specs=[in_hbm] * 2,
-        out_shape=[out_shape] * 2,
+        out_shape=[jax.ShapeDtypeStruct(params.shape, f32)] * 2,
         scratch_shapes=[
             pltpu.VMEM((count, 2 * part, lanes), f32),
             pltpu.VMEM((1, width), f32),
@@ -386,13 +383,11 @@
                 last["m"], extent, last["row_new"], col_new, pairs, last["summed"], blocked, outs, 36
             )
             me, *outs = tie(me, *outs)
-        if j == total_blocks - 1:
-            me, last_params = tie(me, blocked[mats - 1])
 
     row_new, stats = row_stage(mats - 1, sums)
     col_new, pairs = col_stage(mats - 1, exchange(stats, "dp"))
     new_params, update = finish(
-        mats - 1, extent, row_new, col_new, pairs, sums[2], last_params, outs, 12
+        mats - 1, extent, row_new, col_new, pairs, sums[2], blocked, outs, 44
     )
     return (
         new_params.reshape(params.shape),

time: 591 us -> 590 us (level)
  local copies, waits for them, and re-layouts: 28.4 us -> 17.2 us
  waiting for transfers between devices: 414 us -> 423 us
    ppermute x53, waiting for transfers between devices: 414 us -> 423 us  [swap(): return lax.ppermute(x, axes, [(i, i ^ mask) for i in range(size)])]
    slice x1 -> x0, local copies, waits for them, and re-layouts: 7.86 us -> none  [per_device(): me, last_params = tie(me, blocked[mats - 1])]
    unnamed x26 -> x24, local copies, waits for them, and re-layouts: 20.5 us -> 17.1 us
  transfers between devices with their start and end apart: 53 -> 53, of which waited for: 45 -> 45; matrix products, arithmetic and copies ran while one was open for 2% -> 0% of each run, Pallas kernels for 12% -> 11%
where the time goes in v8:
time: 590 us; the launch traced here: 589 us
  waiting for transfers between devices  423 us (72%)
  Pallas kernels  81.1 us (14%)
  starting transfers between devices  65 us (11%)
  local copies, waits for them, and re-layouts  17.2 us (3%)
    ppermute x53, waiting for transfers between devices, swap(): return lax.ppermute(x, axes, [(i, i ^ mask) for i in range(size)])  423 us
    ppermute x53, starting transfers between devices, swap(): return lax.ppermute(x, axes, [(i, i ^ mask) for i in range(size)])  65 us
    pallas_call x20, Pallas kernels, step(): pl.pallas_call(functools.partial(step_kernel, takes, finishes, b, sends,...  56.5 us
    pallas_call x2, Pallas kernels, finish(): pl.pallas_call(functools.partial(finish_kernel, m, extent, len(pairs)), i...  22.2 us
    unnamed x24, local copies, waits for them, and re-layouts  17.1 us
  transfers between devices with their start and end apart: 53, of which 45 were waited for; matrix products, arithmetic and copies ran while one was open for 0% of the time, Pallas kernels for 11%

profile of v8, /device:TPU:0, one launch (start us, length us, event | category | flops | bytes accessed | tf_op | source)
XLA Modules:
  0.0 588.7 jit_solution(5014623050401438694)
XLA Ops:
  1.7 3.0 collective-permute-start
  8.0 9.5 %collective-permute-done.refs_1_ = f32[64,2048]{1,0:T(8,128)S(1)} collective-permute-done((f32[64,2048]{1,0:T(8,128)S(1)}, f32[64,2048]{1,0:T(8,128)S(1)}, u32[]{:S(2)}, u32[]{:S(2)}) %collective-permute-start) | collective-permute-done | bytes 524320 | tf_op jit(solution)/shard_map/ppermute | solution.py:24
  24.2 4.5 collective-permute-done.2.refs_1_
  35.4 27.0 %collective-permute-done.4.refs_1_ = f32[192,2048]{1,0:T(8,128)S(1)} collective-permute-done((f32[192,2048]{1,0:T(8,128)S(1)}, f32[192,2048]{1,0:T(8,128)S(1)}, u32[]{:S(2)}, u32[]{:S(2)}) %collective-permute-start.4) | collective-permute-done | bytes 1572896 | tf_op jit(solution)/shard_map/ppermute | solution.py:24
  69.7 26.5 %collective-permute-done.6.refs_1_ = f32[192,2048]{1,0:T(8,128)S(1)} collective-permute-done((f32[192,2048]{1,0:T(8,128)S(1)}, f32[192,2048]{1,0:T(8,128)S(1)}, u32[]{:S(2)}, u32[]{:S(2)}) %collective-permute-start.6) | collective-permute-done | bytes 1572896 | tf_op jit(solution)/shard_map/ppermute | solution.py:24
  103.4 26.5 %collective-permute-done.8.refs_1_ = f32[192,2048]{1,0:T(8,128)S(1)} collective-permute-done((f32[192,2048]{1,0:T(8,128)S(1)}, f32[192,2048]{1,0:T(8,128)S(1)}, u32[]{:S(2)}, u32[]{:S(2)}) %collective-permute-start.8) | collective-permute-done | bytes 1572896 | tf_op jit(solution)/shard_map/ppermute | solution.py:24
  137.1 26.5 %collective-permute-done.10.refs_1_ = f32[192,2048]{1,0:T(8,128)S(1)} collective-permute-done((f32[192,2048]{1,0:T(8,128)S(1)}, f32[192,2048]{1,0:T(8,128)S(1)}, u32[]{:S(2)}, u32[]{:S(2)}) %collective-permute-start.10) | collective-permute-done | bytes 1572896 | tf_op jit(solution)/shard_map/ppermute | solution.py:24
  170.8 26.5 %collective-permute-done.12.refs_1_ = f32[192,2048]{1,0:T(8,128)S(1)} collective-permute-done((f32[192,2048]{1,0:T(8,128)S(1)}, f32[192,2048]{1,0:T(8,128)S(1)}, u32[]{:S(2)}, u32[]{:S(2)}) %collective-permute-start.12) | collective-permute-done | bytes 1572896 | tf_op jit(solution)/shard_map/ppermute | solution.py:24
  204.5 26.5 %collective-permute-done.14.refs_1_ = f32[192,2048]{1,0:T(8,128)S(1)} collective-permute-done((f32[192,2048]{1,0:T(8,128)S(1)}, f32[192,2048]{1,0:T(8,128)S(1)}, u32[]{:S(2)}, u32[]{:S(2)}) %collective-permute-start.14) | collective-permute-done | bytes 1572896 | tf_op jit(solution)/shard_map/ppermute | solution.py:24
  238.2 26.5 %collective-permute-done.16.refs_1_ = f32[192,2048]{1,0:T(8,128)S(1)} collective-permute-done((f32[192,2048]{1,0:T(8,128)S(1)}, f32[192,2048]{1,0:T(8,128)S(1)}, u32[]{:S(2)}, u32[]{:S(2)}) %collective-permute-start.16) | collective-permute-done | bytes 1572896 | tf_op jit(solution)/shard_map/ppermute | solution.py:24
  271.9 26.5 %collective-permute-done.18.refs_1_ = f32[192,2048]{1,0:T(8,128)S(1)} collective-permute-done((f32[192,2048]{1,0:T(8,128)S(1)}, f32[192,2048]{1,0:T(8,128)S(1)}, u32[]{:S(2)}, u32[]{:S(2)}) %collective-permute-start.18) | collective-permute-done | bytes 1572896 | tf_op jit(solution)/shard_map/ppermute | solution.py:24
  313.7 3.6 collective-permute-start.22
  321.5 10.6 %collective-permute-done.24.refs_1_ = f32[192,2048]{1,0:T(8,128)S(1)} collective-permute-done((f32[192,2048]{1,0:T(8,128)S(1)}, f32[192,2048]{1,0:T(8,128)S(1)}, u32[]{:S(2)}, u32[]{:S(2)}) %collective-permute-start.24) | collective-permute-done | bytes 1572896 | tf_op jit(solution)/shard_map/ppermute | solution.py:24
  339.3 26.5 %collective-permute-done.26.refs_1_ = f32[192,2048]{1,0:T(8,128)S(1)} collective-permute-done((f32[192,2048]{1,0:T(8,128)S(1)}, f32[192,2048]{1,0:T(8,128)S(1)}, u32[]{:S(2)}, u32[]{:S(2)}) %collective-permute-start.26) | collective-permute-done | bytes 1572896 | tf_op jit(solution)/shard_map/ppermute | solution.py:24
  373.0 28.6 %collective-permute-done.29.refs_2_ = f32[192,2048]{1,0:T(8,128)S(1)} collective-permute-done((f32[192,2048]{1,0:T(8,128)S(1)}, f32[192,2048]{1,0:T(8,128)S(1)}, u32[]{:S(2)}, u32[]{:S(2)}) %collective-permute-start.29) | collective-permute-done | bytes 1572896 | tf_op jit(solution)/shard_map/ppermute | solution.py:24
  401.6 4.7 step.34
  409.1 25.5 %collective-permute-done.30.refs_1_ = f32[192,2048]{1,0:T(8,128)S(1)} collective-permute-done((f32[192,2048]{1,0:T(8,128)S(1)}, f32[192,2048]{1,0:T(8,128)S(1)}, u32[]{:S(2)}, u32[]{:S(2)}) %collective-permute-start.30) | collective-permute-done | bytes 1572896 | tf_op jit(solution)/shard_map/ppermute | solution.py:24
  435.3 4.7 step.35
  440.0 3.4 copy-done
  446.4 22.1 %collective-permute-done.32.refs_1_ = f32[192,2048]{1,0:T(8,128)} collective-permute-done((f32[192,2048]{1,0:T(8,128)}, f32[192,2048]{1,0:T(8,128)}, u32[]{:S(2)}, u32[]{:S(2)}) %collective-permute-start.32) | collective-permute-done | bytes 1572896 | tf_op jit(solution)/shard_map/ppermute | solution.py:24
  470.4 3.4 copy-done.1
  473.8 3.4 step.36
  477.2 3.4 copy-done.2
  490.3 3.5 copy-done.6
  493.8 11.2 %finish.2 = (f32[2,8,2,64,2048]{4,3,2,1,0:T(8,128)}, f32[2,8,2,64,2048]{4,3,2,1,0:T(8,128)}) custom-call(f32[8,128]{1,0:T(8,128)S(1)} %get-tuple-element.304.row_new, f32[8,256]{1,0:T(8,128)S(1)} %get-tuple-element.306.col_new, f32[8,2,64,2048]{3,2,1,0:T(8,128)S(1)} %copy-done.6, f32[2,8,2,64,2048]{4,3,2,1,0:T(8,128)} %bitcast.119, ...), custom_call_target="tpu_custom_call" | custom-call | flops 8388608 | bytes 33554432 | tf_op jit(solution)/shard_map/finish/pallas_call | solution.py:315
  505.0 3.5 step.37
  510.6 13.9 %collective-permute-done.39.refs_1_ = f32[128,2048]{1,0:T(8,128)S(1)} collective-permute-done((f32[128,2048]{1,0:T(8,128)S(1)}, f32[128,2048]{1,0:T(8,128)S(1)}, u32[]{:S(2)}, u32[]{:S(2)}) %collective-permute-start.39) | collective-permute-done | bytes 1048608 | tf_op jit(solution)/shard_map/ppermute | solution.py:24
  528.2 17.9 %collective-permute-done.41.refs_1_ = f32[128,2048]{1,0:T(8,128)S(1)} collective-permute-done((f32[128,2048]{1,0:T(8,128)S(1)}, f32[128,2048]{1,0:T(8,128)S(1)}, u32[]{:S(2)}, u32[]{:S(2)}) %collective-permute-start.41) | collective-permute-done | bytes 1048608 | tf_op jit(solution)/shard_map/ppermute | solution.py:24
  555.4 3.5 collective-permute-done.45.refs_3_
  568.9 3.6 collective-permute-start.52
  574.3 3.4 copy-done.4
  577.6 11.0 %finish.3 = (f32[2,8,2,64,2048]{4,3,2,1,0:T(8,128)}, f32[2,8,2,64,2048]{4,3,2,1,0:T(8,128)}) custom-call(f32[8,128]{1,0:T(8,128)S(1)} %get-tuple-element.340.row_new, f32[8,256]{1,0:T(8,128)S(1)} %get-tuple-element.342.col_new, f32[8,2,64,2048]{3,2,1,0:T(8,128)S(1)} %copy-done.4, ...), custom_call_target="tpu_custom_call", output_to_operand_aliasing={{0}: (8, {}), {1}: (9, {})} | custom-call | flops 8388608 | bytes 33554432 | tf_op jit(solution)/shard_map/finish/pallas_call | solution.py:315
  (133 shorter events, 147.1 us)
Async XLA Ops:
  22.1 40.4 %collective-permute-start.4 = (f32[192,2048]{1,0:T(8,128)S(1)}, f32[192,2048]{1,0:T(8,128)S(1)}, u32[]{:S(2)}, u32[]{:S(2)}) collective-permute-start(f32[192,2048]{1,0:T(8,128)S(1)} %get-tuple-element.182), channel_id=1, source_target_pairs={{0,8},{8,0},{16,24},{24,16},{1,9},{9,1},{17,25},{25,17},{2,10},{10... | collective-permute-start | bytes 4718600 | tf_op jit(solution)/shard_map/ppermute | solution.py:24
  22.2 42.4 %collective-permute-start.5 = (f32[192,2048]{1,0:T(8,128)S(1)}, f32[192,2048]{1,0:T(8,128)S(1)}, u32[]{:S(2)}, u32[]{:S(2)}) collective-permute-start(f32[192,2048]{1,0:T(8,128)S(1)} %get-tuple-element.183), channel_id=1, source_target_pairs={{0,16},{8,24},{16,0},{24,8},{1,17},{9,25},{17,1},{25,9},{2,18},{10... | collective-permute-start | bytes 4718600 | tf_op jit(solution)/shard_map/ppermute | solution.py:24
  33.3 62.8 %collective-permute-start.6 = (f32[192,2048]{1,0:T(8,128)S(1)}, f32[192,2048]{1,0:T(8,128)S(1)}, u32[]{:S(2)}, u32[]{:S(2)}) collective-permute-start(f32[192,2048]{1,0:T(8,128)S(1)} %get-tuple-element.185), channel_id=1, source_target_pairs={{0,8},{8,0},{16,24},{24,16},{1,9},{9,1},{17,25},{25,17},{2,10},{10... | collective-permute-start | bytes 4718600 | tf_op jit(solution)/shard_map/ppermute | solution.py:24
  33.4 64.8 %collective-permute-start.7 = (f32[192,2048]{1,0:T(8,128)S(1)}, f32[192,2048]{1,0:T(8,128)S(1)}, u32[]{:S(2)}, u32[]{:S(2)}) collective-permute-start(f32[192,2048]{1,0:T(8,128)S(1)} %get-tuple-element.186), channel_id=1, source_target_pairs={{0,16},{8,24},{16,0},{24,8},{1,17},{9,25},{17,1},{25,9},{2,18},{10... | collective-permute-start | bytes 4718600 | tf_op jit(solution)/shard_map/ppermute | solution.py:24
  67.6 62.3 %collective-permute-start.8 = (f32[192,2048]{1,0:T(8,128)S(1)}, f32[192,2048]{1,0:T(8,128)S(1)}, u32[]{:S(2)}, u32[]{:S(2)}) collective-permute-start(f32[192,2048]{1,0:T(8,128)S(1)} %get-tuple-element.199), channel_id=1, source_target_pairs={{0,8},{8,0},{16,24},{24,16},{1,9},{9,1},{17,25},{25,17},{2,10},{10... | collective-permute-start | bytes 4718600 | tf_op jit(solution)/shard_map/ppermute | solution.py:24
  67.7 64.3 %collective-permute-start.9 = (f32[192,2048]{1,0:T(8,128)S(1)}, f32[192,2048]{1,0:T(8,128)S(1)}, u32[]{:S(2)}, u32[]{:S(2)}) collective-permute-start(f32[192,2048]{1,0:T(8,128)S(1)} %get-tuple-element.200), channel_id=1, source_target_pairs={{0,16},{8,24},{16,0},{24,8},{1,17},{9,25},{17,1},{25,9},{2,18},{10... | collective-permute-start | bytes 4718600 | tf_op jit(solution)/shard_map/ppermute | solution.py:24
  101.3 62.3 %collective-permute-start.10 = (f32[192,2048]{1,0:T(8,128)S(1)}, f32[192,2048]{1,0:T(8,128)S(1)}, u32[]{:S(2)}, u32[]{:S(2)}) collective-permute-start(f32[192,2048]{1,0:T(8,128)S(1)} %get-tuple-element.208), channel_id=1, source_target_pairs={{0,8},{8,0},{16,24},{24,16},{1,9},{9,1},{17,25},{25,17},{2,10},{10... | collective-permute-start | bytes 4718600 | tf_op jit(solution)/shard_map/ppermute | solution.py:24
  101.4 64.3 %collective-permute-start.11 = (f32[192,2048]{1,0:T(8,128)S(1)}, f32[192,2048]{1,0:T(8,128)S(1)}, u32[]{:S(2)}, u32[]{:S(2)}) collective-permute-start(f32[192,2048]{1,0:T(8,128)S(1)} %get-tuple-element.209), channel_id=1, source_target_pairs={{0,16},{8,24},{16,0},{24,8},{1,17},{9,25},{17,1},{25,9},{2,18},{10... | collective-permute-start | bytes 4718600 | tf_op jit(solution)/shard_map/ppermute | solution.py:24
  135.0 62.3 %collective-permute-start.12 = (f32[192,2048]{1,0:T(8,128)S(1)}, f32[192,2048]{1,0:T(8,128)S(1)}, u32[]{:S(2)}, u32[]{:S(2)}) collective-permute-start(f32[192,2048]{1,0:T(8,128)S(1)} %get-tuple-element.217), channel_id=1, source_target_pairs={{0,8},{8,0},{16,24},{24,16},{1,9},{9,1},{17,25},{25,17},{2,10},{10... | collective-permute-start | bytes 4718600 | tf_op jit(solution)/shard_map/ppermute | solution.py:24
  135.1 64.3 %collective-permute-start.13 = (f32[192,2048]{1,0:T(8,128)S(1)}, f32[192,2048]{1,0:T(8,128)S(1)}, u32[]{:S(2)}, u32[]{:S(2)}) collective-permute-start(f32[192,2048]{1,0:T(8,128)S(1)} %get-tuple-element.218), channel_id=1, source_target_pairs={{0,16},{8,24},{16,0},{24,8},{1,17},{9,25},{17,1},{25,9},{2,18},{10... | collective-permute-start | bytes 4718600 | tf_op jit(solution)/shard_map/ppermute | solution.py:24
  168.7 62.3 %collective-permute-start.14 = (f32[192,2048]{1,0:T(8,128)S(1)}, f32[192,2048]{1,0:T(8,128)S(1)}, u32[]{:S(2)}, u32[]{:S(2)}) collective-permute-start(f32[192,2048]{1,0:T(8,128)S(1)} %get-tuple-element.226), channel_id=1, source_target_pairs={{0,8},{8,0},{16,24},{24,16},{1,9},{9,1},{17,25},{25,17},{2,10},{10... | collective-permute-start | bytes 4718600 | tf_op jit(solution)/shard_map/ppermute | solution.py:24
  168.8 64.3 %collective-permute-start.15 = (f32[192,2048]{1,0:T(8,128)S(1)}, f32[192,2048]{1,0:T(8,128)S(1)}, u32[]{:S(2)}, u32[]{:S(2)}) collective-permute-start(f32[192,2048]{1,0:T(8,128)S(1)} %get-tuple-element.227), channel_id=1, source_target_pairs={{0,16},{8,24},{16,0},{24,8},{1,17},{9,25},{17,1},{25,9},{2,18},{10... | collective-permute-start | bytes 4718600 | tf_op jit(solution)/shard_map/ppermute | solution.py:24
  202.4 62.3 %collective-permute-start.16 = (f32[192,2048]{1,0:T(8,128)S(1)}, f32[192,2048]{1,0:T(8,128)S(1)}, u32[]{:S(2)}, u32[]{:S(2)}) collective-permute-start(f32[192,2048]{1,0:T(8,128)S(1)} %get-tuple-element.235), channel_id=1, source_target_pairs={{0,8},{8,0},{16,24},{24,16},{1,9},{9,1},{17,25},{25,17},{2,10},{10... | collective-permute-start | bytes 4718600 | tf_op jit(solution)/shard_map/ppermute | solution.py:24
  202.5 64.3 %collective-permute-start.17 = (f32[192,2048]{1,0:T(8,128)S(1)}, f32[192,2048]{1,0:T(8,128)S(1)}, u32[]{:S(2)}, u32[]{:S(2)}) collective-permute-start(f32[192,2048]{1,0:T(8,128)S(1)} %get-tuple-element.236), channel_id=1, source_target_pairs={{0,16},{8,24},{16,0},{24,8},{1,17},{9,25},{17,1},{25,9},{2,18},{10... | collective-permute-start | bytes 4718600 | tf_op jit(solution)/shard_map/ppermute | solution.py:24
  236.1 62.3 %collective-permute-start.18 = (f32[192,2048]{1,0:T(8,128)S(1)}, f32[192,2048]{1,0:T(8,128)S(1)}, u32[]{:S(2)}, u32[]{:S(2)}) collective-permute-start(f32[192,2048]{1,0:T(8,128)S(1)} %get-tuple-element.244), channel_id=1, source_target_pairs={{0,8},{8,0},{16,24},{24,16},{1,9},{9,1},{17,25},{25,17},{2,10},{10... | collective-permute-start | bytes 4718600 | tf_op jit(solution)/shard_map/ppermute | solution.py:24
  236.2 64.3 %collective-permute-start.19 = (f32[192,2048]{1,0:T(8,128)S(1)}, f32[192,2048]{1,0:T(8,128)S(1)}, u32[]{:S(2)}, u32[]{:S(2)}) collective-permute-start(f32[192,2048]{1,0:T(8,128)S(1)} %get-tuple-element.245), channel_id=1, source_target_pairs={{0,16},{8,24},{16,0},{24,8},{1,17},{9,25},{17,1},{25,9},{2,18},{10... | collective-permute-start | bytes 4718600 | tf_op jit(solution)/shard_map/ppermute | solution.py:24
  269.8 62.3 %collective-permute-start.24 = (f32[192,2048]{1,0:T(8,128)S(1)}, f32[192,2048]{1,0:T(8,128)S(1)}, u32[]{:S(2)}, u32[]{:S(2)}) collective-permute-start(f32[192,2048]{1,0:T(8,128)S(1)} %get-tuple-element.258), channel_id=1, source_target_pairs={{0,8},{8,0},{16,24},{24,16},{1,9},{9,1},{17,25},{25,17},{2,10},{10... | collective-permute-start | bytes 4718600 | tf_op jit(solution)/shard_map/ppermute | solution.py:24
  269.9 64.3 %collective-permute-start.25 = (f32[192,2048]{1,0:T(8,128)S(1)}, f32[192,2048]{1,0:T(8,128)S(1)}, u32[]{:S(2)}, u32[]{:S(2)}) collective-permute-start(f32[192,2048]{1,0:T(8,128)S(1)} %get-tuple-element.259), channel_id=1, source_target_pairs={{0,16},{8,24},{16,0},{24,8},{1,17},{9,25},{17,1},{25,9},{2,18},{10... | collective-permute-start | bytes 4718600 | tf_op jit(solution)/shard_map/ppermute | solution.py:24
  303.5 62.3 %collective-permute-start.26 = (f32[192,2048]{1,0:T(8,128)S(1)}, f32[192,2048]{1,0:T(8,128)S(1)}, u32[]{:S(2)}, u32[]{:S(2)}) collective-permute-start(f32[192,2048]{1,0:T(8,128)S(1)} %get-tuple-element.265), channel_id=1, source_target_pairs={{0,8},{8,0},{16,24},{24,16},{1,9},{9,1},{17,25},{25,17},{2,10},{10... | collective-permute-start | bytes 4718600 | tf_op jit(solution)/shard_map/ppermute | solution.py:24
  303.6 64.3 %collective-permute-start.27 = (f32[192,2048]{1,0:T(8,128)S(1)}, f32[192,2048]{1,0:T(8,128)S(1)}, u32[]{:S(2)}, u32[]{:S(2)}) collective-permute-start(f32[192,2048]{1,0:T(8,128)S(1)} %get-tuple-element.266), channel_id=1, source_target_pairs={{0,16},{8,24},{16,0},{24,8},{1,17},{9,25},{17,1},{25,9},{2,18},{10... | collective-permute-start | bytes 4718600 | tf_op jit(solution)/shard_map/ppermute | solution.py:24
  337.2 64.4 %collective-permute-start.28 = (f32[200,2048]{1,0:T(8,128)S(1)}, f32[200,2048]{1,0:T(8,128)S(1)}, u32[]{:S(2)}, u32[]{:S(2)}) collective-permute-start(f32[200,2048]{1,0:T(8,128)S(1)} %get-tuple-element.274), channel_id=1, source_target_pairs={{0,8},{8,0},{16,24},{24,16},{1,9},{9,1},{17,25},{25,17},{2,10},{10... | collective-permute-start | bytes 4915208 | tf_op jit(solution)/shard_map/ppermute | solution.py:24
  337.3 64.3 %collective-permute-start.29 = (f32[192,2048]{1,0:T(8,128)S(1)}, f32[192,2048]{1,0:T(8,128)S(1)}, u32[]{:S(2)}, u32[]{:S(2)}) collective-permute-start(f32[192,2048]{1,0:T(8,128)S(1)} %get-tuple-element.275), channel_id=1, source_target_pairs={{0,16},{8,24},{16,0},{24,8},{1,17},{9,25},{17,1},{25,9},{2,18},{10... | collective-permute-start | bytes 4718600 | tf_op jit(solution)/shard_map/ppermute | solution.py:24
  370.9 63.7 %collective-permute-start.30 = (f32[192,2048]{1,0:T(8,128)S(1)}, f32[192,2048]{1,0:T(8,128)S(1)}, u32[]{:S(2)}, u32[]{:S(2)}) collective-permute-start(f32[192,2048]{1,0:T(8,128)S(1)} %get-tuple-element.283), channel_id=1, source_target_pairs={{0,8},{8,0},{16,24},{24,16},{1,9},{9,1},{17,25},{25,17},{2,10},{10... | collective-permute-start | bytes 4718600 | tf_op jit(solution)/shard_map/ppermute | solution.py:24
  371.0 64.3 %collective-permute-start.31 = (f32[192,2048]{1,0:T(8,128)S(1)}, f32[192,2048]{1,0:T(8,128)S(1)}, u32[]{:S(2)}, u32[]{:S(2)}) collective-permute-start(f32[192,2048]{1,0:T(8,128)S(1)} %get-tuple-element.284), channel_id=1, source_target_pairs={{0,16},{8,24},{16,0},{24,8},{1,17},{9,25},{17,1},{25,9},{2,18},{10... | collective-permute-start | bytes 4718600 | tf_op jit(solution)/shard_map/ppermute | solution.py:24
  406.3 64.2 %collective-permute-start.33 = (f32[200,2048]{1,0:T(8,128)}, f32[200,2048]{1,0:T(8,128)S(1)}, u32[]{:S(2)}, u32[]{:S(2)}) collective-permute-start(f32[200,2048]{1,0:T(8,128)} %get-tuple-element.293), channel_id=1, source_target_pairs={{0,16},{8,24},{16,0},{24,8},{1,17},{9,25},{17,1},{25,9},{2,18},{10... | collective-permute-start | bytes 4915208 | tf_op jit(solution)/shard_map/ppermute | solution.py:24
  407.8 60.6 %collective-permute-start.32 = (f32[192,2048]{1,0:T(8,128)}, f32[192,2048]{1,0:T(8,128)}, u32[]{:S(2)}, u32[]{:S(2)}) collective-permute-start(f32[192,2048]{1,0:T(8,128)} %get-tuple-element.292), channel_id=1, source_target_pairs={{0,8},{8,0},{16,24},{24,16},{1,9},{9,1},{17,25},{25,17},{2,10},{10... | collective-permute-start | bytes 4718600 | tf_op jit(solution)/shard_map/ppermute | solution.py:24
  443.4 61.6 %collective-permute-start.37 = (f32[192,2048]{1,0:T(8,128)}, f32[192,2048]{1,0:T(8,128)S(1)}, u32[]{:S(2)}, u32[]{:S(2)}) collective-permute-start(f32[192,2048]{1,0:T(8,128)} %get-tuple-element.311), channel_id=1, source_target_pairs={{0,8},{8,0},{16,24},{24,16},{1,9},{9,1},{17,25},{25,17},{2,10},{10... | collective-permute-start | bytes 4718600 | tf_op jit(solution)/shard_map/ppermute | solution.py:24
  444.8 60.2 %collective-permute-start.38 = (f32[192,2048]{1,0:T(8,128)}, f32[192,2048]{1,0:T(8,128)}, u32[]{:S(2)}, u32[]{:S(2)}) collective-permute-start(f32[192,2048]{1,0:T(8,128)} %get-tuple-element.312), channel_id=1, source_target_pairs={{0,16},{8,24},{16,0},{24,8},{1,17},{9,25},{17,1},{25,9},{2,18},{10... | collective-permute-start | bytes 4718600 | tf_op jit(solution)/shard_map/ppermute | solution.py:24
  485.1 39.4 %collective-permute-start.39 = (f32[128,2048]{1,0:T(8,128)S(1)}, f32[128,2048]{1,0:T(8,128)S(1)}, u32[]{:S(2)}, u32[]{:S(2)}) collective-permute-start(f32[128,2048]{1,0:T(8,128)S(1)} %get-tuple-element.320), channel_id=1, source_target_pairs={{0,8},{8,0},{16,24},{24,16},{1,9},{9,1},{17,25},{25,17},{2,10},{10... | collective-permute-start | bytes 3145736 | tf_op jit(solution)/shard_map/ppermute | solution.py:24
  486.8 39.8 %collective-permute-start.40 = (f32[128,2048]{1,0:T(8,128)S(1)}, f32[128,2048]{1,0:T(8,128)S(1)}, u32[]{:S(2)}, u32[]{:S(2)}) collective-permute-start(f32[128,2048]{1,0:T(8,128)S(1)} %get-tuple-element.321), channel_id=1, source_target_pairs={{0,16},{8,24},{16,0},{24,8},{1,17},{9,25},{17,1},{25,9},{2,18},{10... | collective-permute-start | bytes 3145736 | tf_op jit(solution)/shard_map/ppermute | solution.py:24
  508.5 37.7 %collective-permute-start.41 = (f32[128,2048]{1,0:T(8,128)S(1)}, f32[128,2048]{1,0:T(8,128)S(1)}, u32[]{:S(2)}, u32[]{:S(2)}) collective-permute-start(f32[128,2048]{1,0:T(8,128)S(1)} %get-tuple-element.329), channel_id=1, source_target_pairs={{0,8},{8,0},{16,24},{24,16},{1,9},{9,1},{17,25},{25,17},{2,10},{10... | collective-permute-start | bytes 3145736 | tf_op jit(solution)/shard_map/ppermute | solution.py:24
  509.1 38.5 %collective-permute-start.42 = (f32[128,2048]{1,0:T(8,128)S(1)}, f32[128,2048]{1,0:T(8,128)S(1)}, u32[]{:S(2)}, u32[]{:S(2)}) collective-permute-start(f32[128,2048]{1,0:T(8,128)S(1)} %get-tuple-element.330), channel_id=1, source_target_pairs={{0,16},{8,24},{16,0},{24,8},{1,17},{9,25},{17,1},{25,9},{2,18},{10... | collective-permute-start | bytes 3145736 | tf_op jit(solution)/shard_map/ppermute | solution.py:24
  (32 other events, 300.7 us)

commit v9 on v8

--- a/solution.py
+++ b/solution.py
@@ -207,45 +207,65 @@
 
 
 def weighted_kernel(extent, factor, cols, summed, *refs):
-    *totals, rows_out, stats, weighted = refs
+    *totals, rows_out, stats, weighted, column = refs
+    _, part, width = summed.shape
+    i = pl.program_id(0)
+
+    @pl.when(i == 0)
+    def _():
+        total = tree_sum([x[...] for x in totals])
+        row_new = decay_rate * factor[...] + (1.0 - decay_rate) * (total / extent + tiny_eps)
+        rows_out[...] = row_new
+        inverse = jnp.transpose(1.0 / row_new)
+        for k in range(column.shape[0]):
+            column[k] = jnp.broadcast_to(inverse[:, k : k + 1], column.shape[1:])
+        weighted[...] = jnp.zeros_like(weighted)
+
+    for r in range(0, 2 * part, sublanes):
+        half, at = divmod(r, part)
+        x = summed[half, at : at + sublanes]
+        weighted[...] += x * x * column[i, r : r + sublanes][:, 0:1]
+
+    @pl.when(i == pl.num_programs(0) - 1)
+    def _():
+        size = width // sublanes
+        for at, x in ((0, cols), (size, weighted)):
+            sums = jnp.sum(x[...], axis=0, keepdims=True)
+            for k in range(sublanes):
+                stats[k : k + 1, at : at + size] = sums[:, k * size : (k + 1) * size]
+        level = jnp.sum(jnp.sum(rows_out[...], axis=0, keepdims=True), axis=1, keepdims=True)
+        stats[:, 2 * size :] = jnp.broadcast_to(level, (sublanes, lanes))
+
+
+def weighted_sums(extent, totals, factor, cols, summed):
     count, _, part, width = summed.shape
-    total = tree_sum([x[...] for x in totals])
-    row_new = decay_rate * factor[...] + (1.0 - decay_rate) * (total / extent + tiny_eps)
-    rows_out[...] = row_new
-    inverse = jnp.transpose(1.0 / row_new)
-    weighted[...] = jnp.zeros_like(weighted)
-    for i in range(count):
-        for r in range(0, 2 * part, sublanes):
-            half, at = divmod(r, part)
-            x = summed[i, half, at : at + sublanes]
-            weighted[...] += x * x * inverse[r : r + sublanes, i : i + 1]
-    size = width // sublanes
-    for at, x in ((0, cols), (size, weighted)):
-        sums = jnp.sum(x[...], axis=0, keepdims=True)
-        for k in range(sublanes):
-            stats[k : k + 1, at : at + size] = sums[:, k * size : (k + 1) * size]
-    level = jnp.sum(jnp.sum(row_new, axis=0, keepdims=True), axis=1, keepdims=True)
-    stats[:, 2 * size :] = jnp.broadcast_to(level, (sublanes, lanes))
-
-
-def weighted_sums(extent, totals, factor, cols, summed):
-    width = summed.shape[-1]
-    in_vmem = pl.BlockSpec(memory_space=pltpu.VMEM)
+    whole = lambda *shape: pl.BlockSpec(shape, lambda i: (0,) * len(shape))
+    rows_shape = totals[0].shape
+    stats_shape = (sublanes, 2 * width // sublanes + lanes)
     return pl.pallas_call(
         functools.partial(weighted_kernel, extent),
-        in_specs=[in_vmem] * (3 + len(totals)),
-        out_specs=[in_vmem] * 2,
+        grid=(count,),
+        in_specs=[
+            whole(*rows_shape),
+            whole(*cols.shape),
+            pl.BlockSpec((None, 2, part, width), lambda i: (i, 0, 0, 0)),
+        ]
+        + [whole(*rows_shape)] * len(totals),
+        out_specs=[whole(*rows_shape), whole(*stats_shape)],
         out_shape=[
-            jax.ShapeDtypeStruct(totals[0].shape, f32),
-            jax.ShapeDtypeStruct((sublanes, 2 * width // sublanes + lanes), f32),
+            jax.ShapeDtypeStruct(rows_shape, f32),
+            jax.ShapeDtypeStruct(stats_shape, f32),
         ],
-        scratch_shapes=[pltpu.VMEM((sublanes, width), f32)],
+        scratch_shapes=[
+            pltpu.VMEM((sublanes, width), f32),
+            pltpu.VMEM((count, 2 * part, lanes), f32),
+        ],
         compiler_params=params_of(16),
         cost_estimate=pl.CostEstimate(
             flops=3 * summed.size, bytes_accessed=4 * summed.size, transcendentals=0
         ),
         name="weighted",
-    )(factor.reshape(totals[0].shape), cols, summed, *totals)
+    )(factor.reshape(rows_shape), cols, summed, *totals)
 
 
 def column_kernel(extent, factor, *refs):

time: 590 us -> 591 us (level)
  no operation moved by 1% of the time
where the time goes in v9:
time: 591 us; the launch traced here: 589 us
  waiting for transfers between devices  423 us (72%)
  Pallas kernels  82.3 us (14%)
  starting transfers between devices  64.9 us (11%)
  local copies, waits for them, and re-layouts  17.2 us (3%)
    ppermute x53, waiting for transfers between devices, swap(): return lax.ppermute(x, axes, [(i, i ^ mask) for i in range(size)])  423 us
    ppermute x53, starting transfers between devices, swap(): return lax.ppermute(x, axes, [(i, i ^ mask) for i in range(size)])  64.9 us
    pallas_call x20, Pallas kernels, step(): pl.pallas_call(functools.partial(step_kernel, takes, finishes, b, sends,...  56.5 us
    pallas_call x2, Pallas kernels, finish(): pl.pallas_call(functools.partial(finish_kernel, m, extent, len(pairs)), i...  22.2 us
    unnamed x24, local copies, waits for them, and re-layouts  17.1 us
  transfers between devices with their start and end apart: 53, of which 45 were waited for; matrix products, arithmetic and copies ran while one was open for 0% of the time, Pallas kernels for 11%

profile of v9, /device:TPU:0, one launch (start us, length us, event | category | flops | bytes accessed | tf_op | source)
XLA Modules:
  0.0 589.2 jit_solution(10248939255012841598)
XLA Ops:
  1.7 3.0 collective-permute-start
  8.0 9.5 %collective-permute-done.refs_1_ = f32[64,2048]{1,0:T(8,128)S(1)} collective-permute-done((f32[64,2048]{1,0:T(8,128)S(1)}, f32[64,2048]{1,0:T(8,128)S(1)}, u32[]{:S(2)}, u32[]{:S(2)}) %collective-permute-start) | collective-permute-done | bytes 524320 | tf_op jit(solution)/shard_map/ppermute | solution.py:24
  24.2 4.5 collective-permute-done.2.refs_1_
  35.4 27.0 %collective-permute-done.4.refs_1_ = f32[192,2048]{1,0:T(8,128)S(1)} collective-permute-done((f32[192,2048]{1,0:T(8,128)S(1)}, f32[192,2048]{1,0:T(8,128)S(1)}, u32[]{:S(2)}, u32[]{:S(2)}) %collective-permute-start.4) | collective-permute-done | bytes 1572896 | tf_op jit(solution)/shard_map/ppermute | solution.py:24
  69.7 26.5 %collective-permute-done.6.refs_1_ = f32[192,2048]{1,0:T(8,128)S(1)} collective-permute-done((f32[192,2048]{1,0:T(8,128)S(1)}, f32[192,2048]{1,0:T(8,128)S(1)}, u32[]{:S(2)}, u32[]{:S(2)}) %collective-permute-start.6) | collective-permute-done | bytes 1572896 | tf_op jit(solution)/shard_map/ppermute | solution.py:24
  103.4 26.5 %collective-permute-done.8.refs_1_ = f32[192,2048]{1,0:T(8,128)S(1)} collective-permute-done((f32[192,2048]{1,0:T(8,128)S(1)}, f32[192,2048]{1,0:T(8,128)S(1)}, u32[]{:S(2)}, u32[]{:S(2)}) %collective-permute-start.8) | collective-permute-done | bytes 1572896 | tf_op jit(solution)/shard_map/ppermute | solution.py:24
  137.1 26.5 %collective-permute-done.10.refs_1_ = f32[192,2048]{1,0:T(8,128)S(1)} collective-permute-done((f32[192,2048]{1,0:T(8,128)S(1)}, f32[192,2048]{1,0:T(8,128)S(1)}, u32[]{:S(2)}, u32[]{:S(2)}) %collective-permute-start.10) | collective-permute-done | bytes 1572896 | tf_op jit(solution)/shard_map/ppermute | solution.py:24
  170.8 26.5 %collective-permute-done.12.refs_1_ = f32[192,2048]{1,0:T(8,128)S(1)} collective-permute-done((f32[192,2048]{1,0:T(8,128)S(1)}, f32[192,2048]{1,0:T(8,128)S(1)}, u32[]{:S(2)}, u32[]{:S(2)}) %collective-permute-start.12) | collective-permute-done | bytes 1572896 | tf_op jit(solution)/shard_map/ppermute | solution.py:24
  204.5 26.5 %collective-permute-done.14.refs_1_ = f32[192,2048]{1,0:T(8,128)S(1)} collective-permute-done((f32[192,2048]{1,0:T(8,128)S(1)}, f32[192,2048]{1,0:T(8,128)S(1)}, u32[]{:S(2)}, u32[]{:S(2)}) %collective-permute-start.14) | collective-permute-done | bytes 1572896 | tf_op jit(solution)/shard_map/ppermute | solution.py:24
  238.2 26.5 %collective-permute-done.16.refs_1_ = f32[192,2048]{1,0:T(8,128)S(1)} collective-permute-done((f32[192,2048]{1,0:T(8,128)S(1)}, f32[192,2048]{1,0:T(8,128)S(1)}, u32[]{:S(2)}, u32[]{:S(2)}) %collective-permute-start.16) | collective-permute-done | bytes 1572896 | tf_op jit(solution)/shard_map/ppermute | solution.py:24
  271.9 26.5 %collective-permute-done.18.refs_1_ = f32[192,2048]{1,0:T(8,128)S(1)} collective-permute-done((f32[192,2048]{1,0:T(8,128)S(1)}, f32[192,2048]{1,0:T(8,128)S(1)}, u32[]{:S(2)}, u32[]{:S(2)}) %collective-permute-start.18) | collective-permute-done | bytes 1572896 | tf_op jit(solution)/shard_map/ppermute | solution.py:24
  313.7 3.6 collective-permute-start.22
  322.1 10.0 %collective-permute-done.24.refs_1_ = f32[192,2048]{1,0:T(8,128)S(1)} collective-permute-done((f32[192,2048]{1,0:T(8,128)S(1)}, f32[192,2048]{1,0:T(8,128)S(1)}, u32[]{:S(2)}, u32[]{:S(2)}) %collective-permute-start.24) | collective-permute-done | bytes 1572896 | tf_op jit(solution)/shard_map/ppermute | solution.py:24
  339.3 26.5 %collective-permute-done.26.refs_1_ = f32[192,2048]{1,0:T(8,128)S(1)} collective-permute-done((f32[192,2048]{1,0:T(8,128)S(1)}, f32[192,2048]{1,0:T(8,128)S(1)}, u32[]{:S(2)}, u32[]{:S(2)}) %collective-permute-start.26) | collective-permute-done | bytes 1572896 | tf_op jit(solution)/shard_map/ppermute | solution.py:24
  373.0 28.6 %collective-permute-done.29.refs_2_ = f32[192,2048]{1,0:T(8,128)S(1)} collective-permute-done((f32[192,2048]{1,0:T(8,128)S(1)}, f32[192,2048]{1,0:T(8,128)S(1)}, u32[]{:S(2)}, u32[]{:S(2)}) %collective-permute-start.29) | collective-permute-done | bytes 1572896 | tf_op jit(solution)/shard_map/ppermute | solution.py:24
  401.6 4.7 step.34
  409.1 25.5 %collective-permute-done.30.refs_1_ = f32[192,2048]{1,0:T(8,128)S(1)} collective-permute-done((f32[192,2048]{1,0:T(8,128)S(1)}, f32[192,2048]{1,0:T(8,128)S(1)}, u32[]{:S(2)}, u32[]{:S(2)}) %collective-permute-start.30) | collective-permute-done | bytes 1572896 | tf_op jit(solution)/shard_map/ppermute | solution.py:24
  435.3 4.7 step.35
  440.0 3.4 copy-done
  446.4 22.1 %collective-permute-done.32.refs_1_ = f32[192,2048]{1,0:T(8,128)} collective-permute-done((f32[192,2048]{1,0:T(8,128)}, f32[192,2048]{1,0:T(8,128)}, u32[]{:S(2)}, u32[]{:S(2)}) %collective-permute-start.32) | collective-permute-done | bytes 1572896 | tf_op jit(solution)/shard_map/ppermute | solution.py:24
  470.4 3.4 copy-done.1
  473.8 3.4 step.36
  477.2 3.4 copy-done.2
  490.3 3.5 copy-done.6
  493.8 11.2 %finish.2 = (f32[2,8,2,64,2048]{4,3,2,1,0:T(8,128)}, f32[2,8,2,64,2048]{4,3,2,1,0:T(8,128)}) custom-call(f32[8,128]{1,0:T(8,128)S(1)} %get-tuple-element.304.row_new, f32[8,256]{1,0:T(8,128)S(1)} %get-tuple-element.306.col_new, f32[8,2,64,2048]{3,2,1,0:T(8,128)S(1)} %copy-done.6, f32[2,8,2,64,2048]{4,3,2,1,0:T(8,128)} %bitcast.119, ...), custom_call_target="tpu_custom_call" | custom-call | flops 8388608 | bytes 33554432 | tf_op jit(solution)/shard_map/finish/pallas_call | solution.py:335
  505.0 3.5 step.37
  510.6 13.9 %collective-permute-done.39.refs_1_ = f32[128,2048]{1,0:T(8,128)S(1)} collective-permute-done((f32[128,2048]{1,0:T(8,128)S(1)}, f32[128,2048]{1,0:T(8,128)S(1)}, u32[]{:S(2)}, u32[]{:S(2)}) %collective-permute-start.39) | collective-permute-done | bytes 1048608 | tf_op jit(solution)/shard_map/ppermute | solution.py:24
  528.2 17.9 %collective-permute-done.41.refs_1_ = f32[128,2048]{1,0:T(8,128)S(1)} collective-permute-done((f32[128,2048]{1,0:T(8,128)S(1)}, f32[128,2048]{1,0:T(8,128)S(1)}, u32[]{:S(2)}, u32[]{:S(2)}) %collective-permute-start.41) | collective-permute-done | bytes 1048608 | tf_op jit(solution)/shard_map/ppermute | solution.py:24
  555.4 3.5 collective-permute-done.45.refs_3_
  569.4 3.6 collective-permute-start.52
  574.8 3.4 copy-done.4
  578.2 11.0 %finish.3 = (f32[2,8,2,64,2048]{4,3,2,1,0:T(8,128)}, f32[2,8,2,64,2048]{4,3,2,1,0:T(8,128)}) custom-call(f32[8,128]{1,0:T(8,128)S(1)} %get-tuple-element.340.row_new, f32[8,256]{1,0:T(8,128)S(1)} %get-tuple-element.342.col_new, f32[8,2,64,2048]{3,2,1,0:T(8,128)S(1)} %copy-done.4, ...), custom_call_target="tpu_custom_call", output_to_operand_aliasing={{0}: (8, {}), {1}: (9, {})} | custom-call | flops 8388608 | bytes 33554432 | tf_op jit(solution)/shard_map/finish/pallas_call | solution.py:335
  (133 shorter events, 148.2 us)
Async XLA Ops:
  22.1 40.4 %collective-permute-start.4 = (f32[192,2048]{1,0:T(8,128)S(1)}, f32[192,2048]{1,0:T(8,128)S(1)}, u32[]{:S(2)}, u32[]{:S(2)}) collective-permute-start(f32[192,2048]{1,0:T(8,128)S(1)} %get-tuple-element.182), channel_id=1, source_target_pairs={{0,8},{8,0},{16,24},{24,16},{1,9},{9,1},{17,25},{25,17},{2,10},{10... | collective-permute-start | bytes 4718600 | tf_op jit(solution)/shard_map/ppermute | solution.py:24
  22.2 42.4 %collective-permute-start.5 = (f32[192,2048]{1,0:T(8,128)S(1)}, f32[192,2048]{1,0:T(8,128)S(1)}, u32[]{:S(2)}, u32[]{:S(2)}) collective-permute-start(f32[192,2048]{1,0:T(8,128)S(1)} %get-tuple-element.183), channel_id=1, source_target_pairs={{0,16},{8,24},{16,0},{24,8},{1,17},{9,25},{17,1},{25,9},{2,18},{10... | collective-permute-start | bytes 4718600 | tf_op jit(solution)/shard_map/ppermute | solution.py:24
  33.3 62.8 %collective-permute-start.6 = (f32[192,2048]{1,0:T(8,128)S(1)}, f32[192,2048]{1,0:T(8,128)S(1)}, u32[]{:S(2)}, u32[]{:S(2)}) collective-permute-start(f32[192,2048]{1,0:T(8,128)S(1)} %get-tuple-element.185), channel_id=1, source_target_pairs={{0,8},{8,0},{16,24},{24,16},{1,9},{9,1},{17,25},{25,17},{2,10},{10... | collective-permute-start | bytes 4718600 | tf_op jit(solution)/shard_map/ppermute | solution.py:24
  33.4 64.8 %collective-permute-start.7 = (f32[192,2048]{1,0:T(8,128)S(1)}, f32[192,2048]{1,0:T(8,128)S(1)}, u32[]{:S(2)}, u32[]{:S(2)}) collective-permute-start(f32[192,2048]{1,0:T(8,128)S(1)} %get-tuple-element.186), channel_id=1, source_target_pairs={{0,16},{8,24},{16,0},{24,8},{1,17},{9,25},{17,1},{25,9},{2,18},{10... | collective-permute-start | bytes 4718600 | tf_op jit(solution)/shard_map/ppermute | solution.py:24
  67.6 62.3 %collective-permute-start.8 = (f32[192,2048]{1,0:T(8,128)S(1)}, f32[192,2048]{1,0:T(8,128)S(1)}, u32[]{:S(2)}, u32[]{:S(2)}) collective-permute-start(f32[192,2048]{1,0:T(8,128)S(1)} %get-tuple-element.199), channel_id=1, source_target_pairs={{0,8},{8,0},{16,24},{24,16},{1,9},{9,1},{17,25},{25,17},{2,10},{10... | collective-permute-start | bytes 4718600 | tf_op jit(solution)/shard_map/ppermute | solution.py:24
  67.7 64.3 %collective-permute-start.9 = (f32[192,2048]{1,0:T(8,128)S(1)}, f32[192,2048]{1,0:T(8,128)S(1)}, u32[]{:S(2)}, u32[]{:S(2)}) collective-permute-start(f32[192,2048]{1,0:T(8,128)S(1)} %get-tuple-element.200), channel_id=1, source_target_pairs={{0,16},{8,24},{16,0},{24,8},{1,17},{9,25},{17,1},{25,9},{2,18},{10... | collective-permute-start | bytes 4718600 | tf_op jit(solution)/shard_map/ppermute | solution.py:24
  101.3 62.3 %collective-permute-start.10 = (f32[192,2048]{1,0:T(8,128)S(1)}, f32[192,2048]{1,0:T(8,128)S(1)}, u32[]{:S(2)}, u32[]{:S(2)}) collective-permute-start(f32[192,2048]{1,0:T(8,128)S(1)} %get-tuple-element.208), channel_id=1, source_target_pairs={{0,8},{8,0},{16,24},{24,16},{1,9},{9,1},{17,25},{25,17},{2,10},{10... | collective-permute-start | bytes 4718600 | tf_op jit(solution)/shard_map/ppermute | solution.py:24
  101.4 64.3 %collective-permute-start.11 = (f32[192,2048]{1,0:T(8,128)S(1)}, f32[192,2048]{1,0:T(8,128)S(1)}, u32[]{:S(2)}, u32[]{:S(2)}) collective-permute-start(f32[192,2048]{1,0:T(8,128)S(1)} %get-tuple-element.209), channel_id=1, source_target_pairs={{0,16},{8,24},{16,0},{24,8},{1,17},{9,25},{17,1},{25,9},{2,18},{10... | collective-permute-start | bytes 4718600 | tf_op jit(solution)/shard_map/ppermute | solution.py:24
  135.0 62.3 %collective-permute-start.12 = (f32[192,2048]{1,0:T(8,128)S(1)}, f32[192,2048]{1,0:T(8,128)S(1)}, u32[]{:S(2)}, u32[]{:S(2)}) collective-permute-start(f32[192,2048]{1,0:T(8,128)S(1)} %get-tuple-element.217), channel_id=1, source_target_pairs={{0,8},{8,0},{16,24},{24,16},{1,9},{9,1},{17,25},{25,17},{2,10},{10... | collective-permute-start | bytes 4718600 | tf_op jit(solution)/shard_map/ppermute | solution.py:24
  135.1 64.3 %collective-permute-start.13 = (f32[192,2048]{1,0:T(8,128)S(1)}, f32[192,2048]{1,0:T(8,128)S(1)}, u32[]{:S(2)}, u32[]{:S(2)}) collective-permute-start(f32[192,2048]{1,0:T(8,128)S(1)} %get-tuple-element.218), channel_id=1, source_target_pairs={{0,16},{8,24},{16,0},{24,8},{1,17},{9,25},{17,1},{25,9},{2,18},{10... | collective-permute-start | bytes 4718600 | tf_op jit(solution)/shard_map/ppermute | solution.py:24
  168.7 62.3 %collective-permute-start.14 = (f32[192,2048]{1,0:T(8,128)S(1)}, f32[192,2048]{1,0:T(8,128)S(1)}, u32[]{:S(2)}, u32[]{:S(2)}) collective-permute-start(f32[192,2048]{1,0:T(8,128)S(1)} %get-tuple-element.226), channel_id=1, source_target_pairs={{0,8},{8,0},{16,24},{24,16},{1,9},{9,1},{17,25},{25,17},{2,10},{10... | collective-permute-start | bytes 4718600 | tf_op jit(solution)/shard_map/ppermute | solution.py:24
  168.8 64.3 %collective-permute-start.15 = (f32[192,2048]{1,0:T(8,128)S(1)}, f32[192,2048]{1,0:T(8,128)S(1)}, u32[]{:S(2)}, u32[]{:S(2)}) collective-permute-start(f32[192,2048]{1,0:T(8,128)S(1)} %get-tuple-element.227), channel_id=1, source_target_pairs={{0,16},{8,24},{16,0},{24,8},{1,17},{9,25},{17,1},{25,9},{2,18},{10... | collective-permute-start | bytes 4718600 | tf_op jit(solution)/shard_map/ppermute | solution.py:24
  202.4 62.3 %collective-permute-start.16 = (f32[192,2048]{1,0:T(8,128)S(1)}, f32[192,2048]{1,0:T(8,128)S(1)}, u32[]{:S(2)}, u32[]{:S(2)}) collective-permute-start(f32[192,2048]{1,0:T(8,128)S(1)} %get-tuple-element.235), channel_id=1, source_target_pairs={{0,8},{8,0},{16,24},{24,16},{1,9},{9,1},{17,25},{25,17},{2,10},{10... | collective-permute-start | bytes 4718600 | tf_op jit(solution)/shard_map/ppermute | solution.py:24
  202.5 64.3 %collective-permute-start.17 = (f32[192,2048]{1,0:T(8,128)S(1)}, f32[192,2048]{1,0:T(8,128)S(1)}, u32[]{:S(2)}, u32[]{:S(2)}) collective-permute-start(f32[192,2048]{1,0:T(8,128)S(1)} %get-tuple-element.236), channel_id=1, source_target_pairs={{0,16},{8,24},{16,0},{24,8},{1,17},{9,25},{17,1},{25,9},{2,18},{10... | collective-permute-start | bytes 4718600 | tf_op jit(solution)/shard_map/ppermute | solution.py:24
  236.1 62.3 %collective-permute-start.18 = (f32[192,2048]{1,0:T(8,128)S(1)}, f32[192,2048]{1,0:T(8,128)S(1)}, u32[]{:S(2)}, u32[]{:S(2)}) collective-permute-start(f32[192,2048]{1,0:T(8,128)S(1)} %get-tuple-element.244), channel_id=1, source_target_pairs={{0,8},{8,0},{16,24},{24,16},{1,9},{9,1},{17,25},{25,17},{2,10},{10... | collective-permute-start | bytes 4718600 | tf_op jit(solution)/shard_map/ppermute | solution.py:24
  236.2 64.3 %collective-permute-start.19 = (f32[192,2048]{1,0:T(8,128)S(1)}, f32[192,2048]{1,0:T(8,128)S(1)}, u32[]{:S(2)}, u32[]{:S(2)}) collective-permute-start(f32[192,2048]{1,0:T(8,128)S(1)} %get-tuple-element.245), channel_id=1, source_target_pairs={{0,16},{8,24},{16,0},{24,8},{1,17},{9,25},{17,1},{25,9},{2,18},{10... | collective-permute-start | bytes 4718600 | tf_op jit(solution)/shard_map/ppermute | solution.py:24
  269.8 62.3 %collective-permute-start.24 = (f32[192,2048]{1,0:T(8,128)S(1)}, f32[192,2048]{1,0:T(8,128)S(1)}, u32[]{:S(2)}, u32[]{:S(2)}) collective-permute-start(f32[192,2048]{1,0:T(8,128)S(1)} %get-tuple-element.258), channel_id=1, source_target_pairs={{0,8},{8,0},{16,24},{24,16},{1,9},{9,1},{17,25},{25,17},{2,10},{10... | collective-permute-start | bytes 4718600 | tf_op jit(solution)/shard_map/ppermute | solution.py:24
  269.9 64.3 %collective-permute-start.25 = (f32[192,2048]{1,0:T(8,128)S(1)}, f32[192,2048]{1,0:T(8,128)S(1)}, u32[]{:S(2)}, u32[]{:S(2)}) collective-permute-start(f32[192,2048]{1,0:T(8,128)S(1)} %get-tuple-element.259), channel_id=1, source_target_pairs={{0,16},{8,24},{16,0},{24,8},{1,17},{9,25},{17,1},{25,9},{2,18},{10... | collective-permute-start | bytes 4718600 | tf_op jit(solution)/shard_map/ppermute | solution.py:24
  303.5 62.3 %collective-permute-start.26 = (f32[192,2048]{1,0:T(8,128)S(1)}, f32[192,2048]{1,0:T(8,128)S(1)}, u32[]{:S(2)}, u32[]{:S(2)}) collective-permute-start(f32[192,2048]{1,0:T(8,128)S(1)} %get-tuple-element.265), channel_id=1, source_target_pairs={{0,8},{8,0},{16,24},{24,16},{1,9},{9,1},{17,25},{25,17},{2,10},{10... | collective-permute-start | bytes 4718600 | tf_op jit(solution)/shard_map/ppermute | solution.py:24
  303.6 64.3 %collective-permute-start.27 = (f32[192,2048]{1,0:T(8,128)S(1)}, f32[192,2048]{1,0:T(8,128)S(1)}, u32[]{:S(2)}, u32[]{:S(2)}) collective-permute-start(f32[192,2048]{1,0:T(8,128)S(1)} %get-tuple-element.266), channel_id=1, source_target_pairs={{0,16},{8,24},{16,0},{24,8},{1,17},{9,25},{17,1},{25,9},{2,18},{10... | collective-permute-start | bytes 4718600 | tf_op jit(solution)/shard_map/ppermute | solution.py:24
  337.2 64.4 %collective-permute-start.28 = (f32[200,2048]{1,0:T(8,128)S(1)}, f32[200,2048]{1,0:T(8,128)S(1)}, u32[]{:S(2)}, u32[]{:S(2)}) collective-permute-start(f32[200,2048]{1,0:T(8,128)S(1)} %get-tuple-element.274), channel_id=1, source_target_pairs={{0,8},{8,0},{16,24},{24,16},{1,9},{9,1},{17,25},{25,17},{2,10},{10... | collective-permute-start | bytes 4915208 | tf_op jit(solution)/shard_map/ppermute | solution.py:24
  337.3 64.3 %collective-permute-start.29 = (f32[192,2048]{1,0:T(8,128)S(1)}, f32[192,2048]{1,0:T(8,128)S(1)}, u32[]{:S(2)}, u32[]{:S(2)}) collective-permute-start(f32[192,2048]{1,0:T(8,128)S(1)} %get-tuple-element.275), channel_id=1, source_target_pairs={{0,16},{8,24},{16,0},{24,8},{1,17},{9,25},{17,1},{25,9},{2,18},{10... | collective-permute-start | bytes 4718600 | tf_op jit(solution)/shard_map/ppermute | solution.py:24
  370.9 63.7 %collective-permute-start.30 = (f32[192,2048]{1,0:T(8,128)S(1)}, f32[192,2048]{1,0:T(8,128)S(1)}, u32[]{:S(2)}, u32[]{:S(2)}) collective-permute-start(f32[192,2048]{1,0:T(8,128)S(1)} %get-tuple-element.283), channel_id=1, source_target_pairs={{0,8},{8,0},{16,24},{24,16},{1,9},{9,1},{17,25},{25,17},{2,10},{10... | collective-permute-start | bytes 4718600 | tf_op jit(solution)/shard_map/ppermute | solution.py:24
  371.0 64.3 %collective-permute-start.31 = (f32[192,2048]{1,0:T(8,128)S(1)}, f32[192,2048]{1,0:T(8,128)S(1)}, u32[]{:S(2)}, u32[]{:S(2)}) collective-permute-start(f32[192,2048]{1,0:T(8,128)S(1)} %get-tuple-element.284), channel_id=1, source_target_pairs={{0,16},{8,24},{16,0},{24,8},{1,17},{9,25},{17,1},{25,9},{2,18},{10... | collective-permute-start | bytes 4718600 | tf_op jit(solution)/shard_map/ppermute | solution.py:24
  406.3 64.2 %collective-permute-start.33 = (f32[200,2048]{1,0:T(8,128)}, f32[200,2048]{1,0:T(8,128)S(1)}, u32[]{:S(2)}, u32[]{:S(2)}) collective-permute-start(f32[200,2048]{1,0:T(8,128)} %get-tuple-element.293), channel_id=1, source_target_pairs={{0,16},{8,24},{16,0},{24,8},{1,17},{9,25},{17,1},{25,9},{2,18},{10... | collective-permute-start | bytes 4915208 | tf_op jit(solution)/shard_map/ppermute | solution.py:24
  407.8 60.6 %collective-permute-start.32 = (f32[192,2048]{1,0:T(8,128)}, f32[192,2048]{1,0:T(8,128)}, u32[]{:S(2)}, u32[]{:S(2)}) collective-permute-start(f32[192,2048]{1,0:T(8,128)} %get-tuple-element.292), channel_id=1, source_target_pairs={{0,8},{8,0},{16,24},{24,16},{1,9},{9,1},{17,25},{25,17},{2,10},{10... | collective-permute-start | bytes 4718600 | tf_op jit(solution)/shard_map/ppermute | solution.py:24
  443.4 61.6 %collective-permute-start.37 = (f32[192,2048]{1,0:T(8,128)}, f32[192,2048]{1,0:T(8,128)S(1)}, u32[]{:S(2)}, u32[]{:S(2)}) collective-permute-start(f32[192,2048]{1,0:T(8,128)} %get-tuple-element.311), channel_id=1, source_target_pairs={{0,8},{8,0},{16,24},{24,16},{1,9},{9,1},{17,25},{25,17},{2,10},{10... | collective-permute-start | bytes 4718600 | tf_op jit(solution)/shard_map/ppermute | solution.py:24
  444.8 60.2 %collective-permute-start.38 = (f32[192,2048]{1,0:T(8,128)}, f32[192,2048]{1,0:T(8,128)}, u32[]{:S(2)}, u32[]{:S(2)}) collective-permute-start(f32[192,2048]{1,0:T(8,128)} %get-tuple-element.312), channel_id=1, source_target_pairs={{0,16},{8,24},{16,0},{24,8},{1,17},{9,25},{17,1},{25,9},{2,18},{10... | collective-permute-start | bytes 4718600 | tf_op jit(solution)/shard_map/ppermute | solution.py:24
  485.1 39.4 %collective-permute-start.39 = (f32[128,2048]{1,0:T(8,128)S(1)}, f32[128,2048]{1,0:T(8,128)S(1)}, u32[]{:S(2)}, u32[]{:S(2)}) collective-permute-start(f32[128,2048]{1,0:T(8,128)S(1)} %get-tuple-element.320), channel_id=1, source_target_pairs={{0,8},{8,0},{16,24},{24,16},{1,9},{9,1},{17,25},{25,17},{2,10},{10... | collective-permute-start | bytes 3145736 | tf_op jit(solution)/shard_map/ppermute | solution.py:24
  486.8 39.8 %collective-permute-start.40 = (f32[128,2048]{1,0:T(8,128)S(1)}, f32[128,2048]{1,0:T(8,128)S(1)}, u32[]{:S(2)}, u32[]{:S(2)}) collective-permute-start(f32[128,2048]{1,0:T(8,128)S(1)} %get-tuple-element.321), channel_id=1, source_target_pairs={{0,16},{8,24},{16,0},{24,8},{1,17},{9,25},{17,1},{25,9},{2,18},{10... | collective-permute-start | bytes 3145736 | tf_op jit(solution)/shard_map/ppermute | solution.py:24
  508.5 37.7 %collective-permute-start.41 = (f32[128,2048]{1,0:T(8,128)S(1)}, f32[128,2048]{1,0:T(8,128)S(1)}, u32[]{:S(2)}, u32[]{:S(2)}) collective-permute-start(f32[128,2048]{1,0:T(8,128)S(1)} %get-tuple-element.329), channel_id=1, source_target_pairs={{0,8},{8,0},{16,24},{24,16},{1,9},{9,1},{17,25},{25,17},{2,10},{10... | collective-permute-start | bytes 3145736 | tf_op jit(solution)/shard_map/ppermute | solution.py:24
  509.1 38.5 %collective-permute-start.42 = (f32[128,2048]{1,0:T(8,128)S(1)}, f32[128,2048]{1,0:T(8,128)S(1)}, u32[]{:S(2)}, u32[]{:S(2)}) collective-permute-start(f32[128,2048]{1,0:T(8,128)S(1)} %get-tuple-element.330), channel_id=1, source_target_pairs={{0,16},{8,24},{16,0},{24,8},{1,17},{9,25},{17,1},{25,9},{2,18},{10... | collective-permute-start | bytes 3145736 | tf_op jit(solution)/shard_map/ppermute | solution.py:24
  (32 other events, 301.8 us)

commit v10 on v8

--- a/solution.py
+++ b/solution.py
@@ -249,13 +249,15 @@
 
 
 def column_kernel(extent, factor, *refs):
-    *parts, cols_out, pair = refs
+    *parts, cols_out, pair, sums = refs
     stats = tree_sum([x[...] for x in parts])
-    size = factor.shape[1]
-    col_new = decay_rate * factor[...] + (1.0 - decay_rate) * (stats[:, :size] / extent + tiny_eps)
+    size = factor.shape[1] // sublanes
+    for i in range(2):
+        for k in range(sublanes):
+            sums[i : i + 1, k * size : (k + 1) * size] = stats[k : k + 1, i * size : (i + 1) * size]
+    col_new = decay_rate * factor[...] + (1.0 - decay_rate) * (sums[0:1] / extent + tiny_eps)
     cols_out[...] = col_new
-    total = jnp.sum(stats[:, size : 2 * size] / col_new, axis=0, keepdims=True)
-    total = jnp.sum(total, axis=1, keepdims=True)
+    total = jnp.sum(sums[1:2] / col_new, axis=1, keepdims=True)
     pair[...] = stats[:, 2 * size :] / extent
     pair[0:1] = jnp.broadcast_to(total, (1, lanes))
 
@@ -269,12 +271,13 @@
             jax.ShapeDtypeStruct(factor.shape, f32),
             jax.ShapeDtypeStruct((sublanes, lanes), f32),
         ],
+        scratch_shapes=[pltpu.VMEM((sublanes, factor.shape[1]), f32)],
         compiler_params=params_of(4),
         name="column",
     )(factor, *parts)
 
 
-def finish_kernel(m, extent, partners, row_new, col_new, summed, params, *refs):
+def finish_kernel(m, extent, partners, staged, row_new, col_new, summed, params, *refs):
     pairs, (new_params, update, column, by_col) = refs[:partners], refs[-4:]
     count, _, part, width = summed.shape
 
@@ -286,11 +289,10 @@
         by_row = jnp.transpose(lax.rsqrt(row_new[...]) * factor)
         for i in range(count):
             column[i] = jnp.broadcast_to(by_row[:, i : i + 1], column.shape[1:])
-        size = width // sublanes
-        for k in range(sublanes):
-            by_col[:, k * size : (k + 1) * size] = lax.rsqrt(col_new[k : k + 1])
-
-    def body(p, new_p, moved):
+        by_col[...] = lax.rsqrt(col_new[...])
+
+    def body(*blocks):
+        new_p, moved = blocks[-2:]
         i = pl.program_id(0)
         pl.when(i == 0)(scale)
         for half in range(2):
@@ -299,24 +301,29 @@
                 mine = column[i, at : at + sublanes][:, 0:1]
                 y = summed[i, half, r : r + sublanes] * mine * by_col[...]
                 moved[half, r : r + sublanes] = y
-                new_p[half, r : r + sublanes] = p[half, r : r + sublanes] - learn_rate * y
+                p = params[i, half, r : r + sublanes] if staged else blocks[0][half, r : r + sublanes]
+                new_p[half, r : r + sublanes] = p - learn_rate * y
 
     of_matrix = pl.BlockSpec((None, None, 2, part, width), lambda i: (m, i, 0, 0, 0))
     pltpu.emit_pipeline(
-        body, grid=(count,), in_specs=[of_matrix], out_specs=[of_matrix] * 2
-    )(params, new_params, update)
+        body, grid=(count,), in_specs=[] if staged else [of_matrix], out_specs=[of_matrix] * 2
+    )(*([] if staged else [params]), new_params, update)
 
 
 def finish(m, extent, row_new, col_new, pairs, summed, params, outs, mib):
     count, _, part, width = summed.shape
     held = () if outs is None else outs
+    staged = params.ndim == summed.ndim
     in_hbm = pl.BlockSpec(memory_space=pltpu.HBM)
     in_vmem = pl.BlockSpec(memory_space=pltpu.VMEM)
     return pl.pallas_call(
-        functools.partial(finish_kernel, m, extent, len(pairs)),
-        in_specs=[in_vmem] * 3 + [in_hbm] + [in_vmem] * len(pairs) + [in_hbm] * len(held),
+        functools.partial(finish_kernel, m, extent, len(pairs), staged),
+        in_specs=[in_vmem] * 3
+        + [in_vmem if staged else in_hbm]
+        + [in_vmem] * len(pairs)
+        + [in_hbm] * len(held),
         out_specs=[in_hbm] * 2,
-        out_shape=[jax.ShapeDtypeStruct(params.shape, f32)] * 2,
+        out_shape=[jax.ShapeDtypeStruct(held[0].shape if staged else params.shape, f32)] * 2,
         scratch_shapes=[
             pltpu.VMEM((count, 2 * part, lanes), f32),
             pltpu.VMEM((1, width), f32),
@@ -350,8 +357,8 @@
         return row_new, pairwise_sum(stats, "row")
 
     def col_stage(m, parts):
-        col_new, pair = column_stage(extent, col_factor[m].reshape(sublanes, -1), parts)
-        new_columns.append(col_new.reshape(block_cols))
+        col_new, pair = column_stage(extent, col_factor[m : m + 1], parts)
+        new_columns.append(col_new)
         return col_new, exchange(pair, "col")
 
     flying = {}
@@ -383,17 +390,18 @@
                 last["m"], extent, last["row_new"], col_new, pairs, last["summed"], blocked, outs, 36
             )
             me, *outs = tie(me, *outs)
-
+        if j == total_blocks - 1:
+            me, last_params = tie(me, blocked[mats - 1])
     row_new, stats = row_stage(mats - 1, sums)
     col_new, pairs = col_stage(mats - 1, exchange(stats, "dp"))
     new_params, update = finish(
-        mats - 1, extent, row_new, col_new, pairs, sums[2], blocked, outs, 44
+        mats - 1, extent, row_new, col_new, pairs, sums[2], last_params, outs, 12
     )
     return (
         new_params.reshape(params.shape),
         update.reshape(params.shape),
         jnp.stack(new_rows),
-        jnp.stack(new_columns),
+        jnp.concatenate(new_columns, axis=0),
     )
 
 

time: 590 us -> 583 us (0.988)
  Pallas kernels: 81.1 us -> 73.7 us
  waiting for transfers between devices: 423 us -> 429 us
    unnamed x24 -> x12, local copies, waits for them, and re-layouts: 17.1 us -> 3.4 us
    slice x1 -> x2, local copies, waits for them, and re-layouts: 0.04 us -> 7.88 us  [the longest x1 7.86 us: per_device(): me, last_params = tie(me, blocked[mats - 1])]
    ppermute x53, waiting for transfers between devices: 423 us -> 429 us  [swap(): return lax.ppermute(x, axes, [(i, i ^ mask) for i in range(size)])]
  transfers between devices with their start and end apart: 53 -> 53, of which waited for: 45 -> 47; matrix products, arithmetic and copies ran while one was open for 0% -> 2% of each run, Pallas kernels for 11% -> 11%
where the time goes in v10:
time: 583 us; the launch traced here: 581 us
  waiting for transfers between devices  429 us (74%)
  Pallas kernels  73.7 us (13%)
  starting transfers between devices  65.1 us (11%)
  local copies, waits for them, and re-layouts  11.3 us (2%)
    ppermute x53, waiting for transfers between devices, swap(): return lax.ppermute(x, axes, [(i, i ^ mask) for i in range(size)])  429 us
    ppermute x53, starting transfers between devices, swap(): return lax.ppermute(x, axes, [(i, i ^ mask) for i in range(size)])  65.1 us
    pallas_call x20, Pallas kernels, step(): pl.pallas_call(functools.partial(step_kernel, takes, finishes, b, sends,...  53 us
    pallas_call x2, Pallas kernels, finish(): pl.pallas_call(functools.partial(finish_kernel, m, extent, len(pairs), st...  18.3 us
  transfers between devices with their start and end apart: 53, of which 47 were waited for; matrix products, arithmetic and copies ran while one was open for 2% of the time, Pallas kernels for 11%

profile of v10, /device:TPU:0, one launch (start us, length us, event | category | flops | bytes accessed | tf_op | source)
XLA Modules:
  0.0 581.5 jit_solution(17419079266347327951)
XLA Ops:
  1.7 3.0 collective-permute-start
  8.0 9.5 %collective-permute-done.refs_1_ = f32[64,2048]{1,0:T(8,128)S(1)} collective-permute-done((f32[64,2048]{1,0:T(8,128)S(1)}, f32[64,2048]{1,0:T(8,128)S(1)}, u32[]{:S(2)}, u32[]{:S(2)}) %collective-permute-start) | collective-permute-done | bytes 524320 | tf_op jit(solution)/shard_map/ppermute | solution.py:24
  24.2 4.5 collective-permute-done.2.refs_1_
  35.4 27.0 %collective-permute-done.4.refs_1_ = f32[192,2048]{1,0:T(8,128)S(1)} collective-permute-done((f32[192,2048]{1,0:T(8,128)S(1)}, f32[192,2048]{1,0:T(8,128)S(1)}, u32[]{:S(2)}, u32[]{:S(2)}) %collective-permute-start.4) | collective-permute-done | bytes 1572896 | tf_op jit(solution)/shard_map/ppermute | solution.py:24
  69.7 26.5 %collective-permute-done.6.refs_1_ = f32[192,2048]{1,0:T(8,128)S(1)} collective-permute-done((f32[192,2048]{1,0:T(8,128)S(1)}, f32[192,2048]{1,0:T(8,128)S(1)}, u32[]{:S(2)}, u32[]{:S(2)}) %collective-permute-start.6) | collective-permute-done | bytes 1572896 | tf_op jit(solution)/shard_map/ppermute | solution.py:24
  103.4 26.5 %collective-permute-done.8.refs_1_ = f32[192,2048]{1,0:T(8,128)S(1)} collective-permute-done((f32[192,2048]{1,0:T(8,128)S(1)}, f32[192,2048]{1,0:T(8,128)S(1)}, u32[]{:S(2)}, u32[]{:S(2)}) %collective-permute-start.8) | collective-permute-done | bytes 1572896 | tf_op jit(solution)/shard_map/ppermute | solution.py:24
  137.1 26.5 %collective-permute-done.10.refs_1_ = f32[192,2048]{1,0:T(8,128)S(1)} collective-permute-done((f32[192,2048]{1,0:T(8,128)S(1)}, f32[192,2048]{1,0:T(8,128)S(1)}, u32[]{:S(2)}, u32[]{:S(2)}) %collective-permute-start.10) | collective-permute-done | bytes 1572896 | tf_op jit(solution)/shard_map/ppermute | solution.py:24
  170.8 26.5 %collective-permute-done.12.refs_1_ = f32[192,2048]{1,0:T(8,128)S(1)} collective-permute-done((f32[192,2048]{1,0:T(8,128)S(1)}, f32[192,2048]{1,0:T(8,128)S(1)}, u32[]{:S(2)}, u32[]{:S(2)}) %collective-permute-start.12) | collective-permute-done | bytes 1572896 | tf_op jit(solution)/shard_map/ppermute | solution.py:24
  204.5 26.5 %collective-permute-done.14.refs_1_ = f32[192,2048]{1,0:T(8,128)S(1)} collective-permute-done((f32[192,2048]{1,0:T(8,128)S(1)}, f32[192,2048]{1,0:T(8,128)S(1)}, u32[]{:S(2)}, u32[]{:S(2)}) %collective-permute-start.14) | collective-permute-done | bytes 1572896 | tf_op jit(solution)/shard_map/ppermute | solution.py:24
  233.1 3.0 step.29
  238.2 26.5 %collective-permute-done.16.refs_1_ = f32[192,2048]{1,0:T(8,128)S(1)} collective-permute-done((f32[192,2048]{1,0:T(8,128)S(1)}, f32[192,2048]{1,0:T(8,128)S(1)}, u32[]{:S(2)}, u32[]{:S(2)}) %collective-permute-start.16) | collective-permute-done | bytes 1572896 | tf_op jit(solution)/shard_map/ppermute | solution.py:24
  271.9 26.5 %collective-permute-done.18.refs_1_ = f32[192,2048]{1,0:T(8,128)S(1)} collective-permute-done((f32[192,2048]{1,0:T(8,128)S(1)}, f32[192,2048]{1,0:T(8,128)S(1)}, u32[]{:S(2)}, u32[]{:S(2)}) %collective-permute-start.18) | collective-permute-done | bytes 1572896 | tf_op jit(solution)/shard_map/ppermute | solution.py:24
  313.7 3.6 collective-permute-start.22
  321.5 10.6 %collective-permute-done.24.refs_1_ = f32[192,2048]{1,0:T(8,128)S(1)} collective-permute-done((f32[192,2048]{1,0:T(8,128)S(1)}, f32[192,2048]{1,0:T(8,128)S(1)}, u32[]{:S(2)}, u32[]{:S(2)}) %collective-permute-start.24) | collective-permute-done | bytes 1572896 | tf_op jit(solution)/shard_map/ppermute | solution.py:24
  334.2 3.0 step.32
  339.3 26.5 %collective-permute-done.26.refs_1_ = f32[192,2048]{1,0:T(8,128)S(1)} collective-permute-done((f32[192,2048]{1,0:T(8,128)S(1)}, f32[192,2048]{1,0:T(8,128)S(1)}, u32[]{:S(2)}, u32[]{:S(2)}) %collective-permute-start.26) | collective-permute-done | bytes 1572896 | tf_op jit(solution)/shard_map/ppermute | solution.py:24
  367.9 3.0 step.33
  373.0 28.6 %collective-permute-done.29.refs_2_ = f32[192,2048]{1,0:T(8,128)S(1)} collective-permute-done((f32[192,2048]{1,0:T(8,128)S(1)}, f32[192,2048]{1,0:T(8,128)S(1)}, u32[]{:S(2)}, u32[]{:S(2)}) %collective-permute-start.29) | collective-permute-done | bytes 1572896 | tf_op jit(solution)/shard_map/ppermute | solution.py:24
  401.6 3.0 step.34
  407.6 27.0 %collective-permute-done.30.refs_1_ = f32[192,2048]{1,0:T(8,128)S(1)} collective-permute-done((f32[192,2048]{1,0:T(8,128)S(1)}, f32[192,2048]{1,0:T(8,128)S(1)}, u32[]{:S(2)}, u32[]{:S(2)}) %collective-permute-start.30) | collective-permute-done | bytes 1572896 | tf_op jit(solution)/shard_map/ppermute | solution.py:24
  435.3 3.0 step.35
  441.3 27.0 %collective-permute-done.32.refs_1_ = f32[192,2048]{1,0:T(8,128)S(1)} collective-permute-done((f32[192,2048]{1,0:T(8,128)S(1)}, f32[192,2048]{1,0:T(8,128)S(1)}, u32[]{:S(2)}, u32[]{:S(2)}) %collective-permute-start.32) | collective-permute-done | bytes 1572896 | tf_op jit(solution)/shard_map/ppermute | solution.py:24
  470.4 4.0 step.36
  484.1 3.4 copy-done.1
  487.5 11.1 %finish.2 = (f32[2,8,2,64,2048]{4,3,2,1,0:T(8,128)}, f32[2,8,2,64,2048]{4,3,2,1,0:T(8,128)}) custom-call(f32[8,128]{1,0:T(8,128)S(1)} %get-tuple-element.306.row_new, f32[1,2048]{1,0:T(1,128)S(1)} %get-tuple-element.308.col_new, f32[8,2,64,2048]{3,2,1,0:T(8,128)S(1)} %copy-done.1, f32[2,8,2,64,2048]{4,3,2,1,0:T(8,128)} %bitcast.113, ...), custom_call_target="tpu_custom_call" | custom-call | flops 8388608 | bytes 33554432 | tf_op jit(solution)/shard_map/finish/pallas_call | solution.py:319
  498.6 3.5 collective-permute-done.37.refs_1_
  509.0 7.9 %slice.19 = f32[1,1024,2048]{2,1,0:T(8,128)} slice(f32[2,1024,2048]{2,1,0:T(8,128)} %param.5), slice={[1:2], [0:1024], [0:2048]} | slice | bytes 16777216 | tf_op jit(solution)/shard_map/slice | solution.py:394
  516.9 7.6 %collective-permute-done.39.refs_1_ = f32[128,2048]{1,0:T(8,128)S(1)} collective-permute-done((f32[128,2048]{1,0:T(8,128)}, f32[128,2048]{1,0:T(8,128)S(1)}, u32[]{:S(2)}, u32[]{:S(2)}) %collective-permute-start.39) | collective-permute-done | bytes 1048608 | tf_op jit(solution)/shard_map/ppermute | solution.py:24
  528.2 17.9 %collective-permute-done.41.refs_1_ = f32[128,2048]{1,0:T(8,128)S(1)} collective-permute-done((f32[128,2048]{1,0:T(8,128)S(1)}, f32[128,2048]{1,0:T(8,128)S(1)}, u32[]{:S(2)}, u32[]{:S(2)}) %collective-permute-start.41) | collective-permute-done | bytes 1048608 | tf_op jit(solution)/shard_map/ppermute | solution.py:24
  555.4 3.5 collective-permute-done.45.refs_3_
  568.9 3.6 collective-permute-start.52
  574.3 7.2 %finish.3 = (f32[2,8,2,64,2048]{4,3,2,1,0:T(8,128)}, f32[2,8,2,64,2048]{4,3,2,1,0:T(8,128)}) custom-call(f32[8,128]{1,0:T(8,128)S(1)} %get-tuple-element.343.row_new, f32[1,2048]{1,0:T(1,128)S(1)} %get-tuple-element.345.col_new, f32[8,2,64,2048]{3,2,1,0:T(8,128)S(1)} %get-tuple-element.341.summed, ...), custom_call_target="tpu_custom_call", output_to_operand_aliasing={{0}: (8, {}), {1}: (9, {})} | custom-call | flops 8388608 | bytes 33554432 | tf_op jit(solution)/shard_map/finish/pallas_call | solution.py:319
  (120 shorter events, 143.1 us)
Async XLA Ops:
  22.1 40.4 %collective-permute-start.4 = (f32[192,2048]{1,0:T(8,128)S(1)}, f32[192,2048]{1,0:T(8,128)S(1)}, u32[]{:S(2)}, u32[]{:S(2)}) collective-permute-start(f32[192,2048]{1,0:T(8,128)S(1)} %get-tuple-element.184), channel_id=1, source_target_pairs={{0,8},{8,0},{16,24},{24,16},{1,9},{9,1},{17,25},{25,17},{2,10},{10... | collective-permute-start | bytes 4718600 | tf_op jit(solution)/shard_map/ppermute | solution.py:24
  22.2 42.4 %collective-permute-start.5 = (f32[192,2048]{1,0:T(8,128)S(1)}, f32[192,2048]{1,0:T(8,128)S(1)}, u32[]{:S(2)}, u32[]{:S(2)}) collective-permute-start(f32[192,2048]{1,0:T(8,128)S(1)} %get-tuple-element.185), channel_id=1, source_target_pairs={{0,16},{8,24},{16,0},{24,8},{1,17},{9,25},{17,1},{25,9},{2,18},{10... | collective-permute-start | bytes 4718600 | tf_op jit(solution)/shard_map/ppermute | solution.py:24
  33.3 62.8 %collective-permute-start.6 = (f32[192,2048]{1,0:T(8,128)S(1)}, f32[192,2048]{1,0:T(8,128)S(1)}, u32[]{:S(2)}, u32[]{:S(2)}) collective-permute-start(f32[192,2048]{1,0:T(8,128)S(1)} %get-tuple-element.187), channel_id=1, source_target_pairs={{0,8},{8,0},{16,24},{24,16},{1,9},{9,1},{17,25},{25,17},{2,10},{10... | collective-permute-start | bytes 4718600 | tf_op jit(solution)/shard_map/ppermute | solution.py:24
  33.4 64.8 %collective-permute-start.7 = (f32[192,2048]{1,0:T(8,128)S(1)}, f32[192,2048]{1,0:T(8,128)S(1)}, u32[]{:S(2)}, u32[]{:S(2)}) collective-permute-start(f32[192,2048]{1,0:T(8,128)S(1)} %get-tuple-element.188), channel_id=1, source_target_pairs={{0,16},{8,24},{16,0},{24,8},{1,17},{9,25},{17,1},{25,9},{2,18},{10... | collective-permute-start | bytes 4718600 | tf_op jit(solution)/shard_map/ppermute | solution.py:24
  67.5 62.3 %collective-permute-start.8 = (f32[192,2048]{1,0:T(8,128)S(1)}, f32[192,2048]{1,0:T(8,128)S(1)}, u32[]{:S(2)}, u32[]{:S(2)}) collective-permute-start(f32[192,2048]{1,0:T(8,128)S(1)} %get-tuple-element.201), channel_id=1, source_target_pairs={{0,8},{8,0},{16,24},{24,16},{1,9},{9,1},{17,25},{25,17},{2,10},{10... | collective-permute-start | bytes 4718600 | tf_op jit(solution)/shard_map/ppermute | solution.py:24
  67.7 64.3 %collective-permute-start.9 = (f32[192,2048]{1,0:T(8,128)S(1)}, f32[192,2048]{1,0:T(8,128)S(1)}, u32[]{:S(2)}, u32[]{:S(2)}) collective-permute-start(f32[192,2048]{1,0:T(8,128)S(1)} %get-tuple-element.202), channel_id=1, source_target_pairs={{0,16},{8,24},{16,0},{24,8},{1,17},{9,25},{17,1},{25,9},{2,18},{10... | collective-permute-start | bytes 4718600 | tf_op jit(solution)/shard_map/ppermute | solution.py:24
  101.2 62.3 %collective-permute-start.10 = (f32[192,2048]{1,0:T(8,128)S(1)}, f32[192,2048]{1,0:T(8,128)S(1)}, u32[]{:S(2)}, u32[]{:S(2)}) collective-permute-start(f32[192,2048]{1,0:T(8,128)S(1)} %get-tuple-element.210), channel_id=1, source_target_pairs={{0,8},{8,0},{16,24},{24,16},{1,9},{9,1},{17,25},{25,17},{2,10},{10... | collective-permute-start | bytes 4718600 | tf_op jit(solution)/shard_map/ppermute | solution.py:24
  101.4 64.3 %collective-permute-start.11 = (f32[192,2048]{1,0:T(8,128)S(1)}, f32[192,2048]{1,0:T(8,128)S(1)}, u32[]{:S(2)}, u32[]{:S(2)}) collective-permute-start(f32[192,2048]{1,0:T(8,128)S(1)} %get-tuple-element.211), channel_id=1, source_target_pairs={{0,16},{8,24},{16,0},{24,8},{1,17},{9,25},{17,1},{25,9},{2,18},{10... | collective-permute-start | bytes 4718600 | tf_op jit(solution)/shard_map/ppermute | solution.py:24
  135.0 62.3 %collective-permute-start.12 = (f32[192,2048]{1,0:T(8,128)S(1)}, f32[192,2048]{1,0:T(8,128)S(1)}, u32[]{:S(2)}, u32[]{:S(2)}) collective-permute-start(f32[192,2048]{1,0:T(8,128)S(1)} %get-tuple-element.219), channel_id=1, source_target_pairs={{0,8},{8,0},{16,24},{24,16},{1,9},{9,1},{17,25},{25,17},{2,10},{10... | collective-permute-start | bytes 4718600 | tf_op jit(solution)/shard_map/ppermute | solution.py:24
  135.1 64.3 %collective-permute-start.13 = (f32[192,2048]{1,0:T(8,128)S(1)}, f32[192,2048]{1,0:T(8,128)S(1)}, u32[]{:S(2)}, u32[]{:S(2)}) collective-permute-start(f32[192,2048]{1,0:T(8,128)S(1)} %get-tuple-element.220), channel_id=1, source_target_pairs={{0,16},{8,24},{16,0},{24,8},{1,17},{9,25},{17,1},{25,9},{2,18},{10... | collective-permute-start | bytes 4718600 | tf_op jit(solution)/shard_map/ppermute | solution.py:24
  168.7 62.3 %collective-permute-start.14 = (f32[192,2048]{1,0:T(8,128)S(1)}, f32[192,2048]{1,0:T(8,128)S(1)}, u32[]{:S(2)}, u32[]{:S(2)}) collective-permute-start(f32[192,2048]{1,0:T(8,128)S(1)} %get-tuple-element.228), channel_id=1, source_target_pairs={{0,8},{8,0},{16,24},{24,16},{1,9},{9,1},{17,25},{25,17},{2,10},{10... | collective-permute-start | bytes 4718600 | tf_op jit(solution)/shard_map/ppermute | solution.py:24
  168.8 64.3 %collective-permute-start.15 = (f32[192,2048]{1,0:T(8,128)S(1)}, f32[192,2048]{1,0:T(8,128)S(1)}, u32[]{:S(2)}, u32[]{:S(2)}) collective-permute-start(f32[192,2048]{1,0:T(8,128)S(1)} %get-tuple-element.229), channel_id=1, source_target_pairs={{0,16},{8,24},{16,0},{24,8},{1,17},{9,25},{17,1},{25,9},{2,18},{10... | collective-permute-start | bytes 4718600 | tf_op jit(solution)/shard_map/ppermute | solution.py:24
  202.4 62.3 %collective-permute-start.16 = (f32[192,2048]{1,0:T(8,128)S(1)}, f32[192,2048]{1,0:T(8,128)S(1)}, u32[]{:S(2)}, u32[]{:S(2)}) collective-permute-start(f32[192,2048]{1,0:T(8,128)S(1)} %get-tuple-element.237), channel_id=1, source_target_pairs={{0,8},{8,0},{16,24},{24,16},{1,9},{9,1},{17,25},{25,17},{2,10},{10... | collective-permute-start | bytes 4718600 | tf_op jit(solution)/shard_map/ppermute | solution.py:24
  202.5 64.3 %collective-permute-start.17 = (f32[192,2048]{1,0:T(8,128)S(1)}, f32[192,2048]{1,0:T(8,128)S(1)}, u32[]{:S(2)}, u32[]{:S(2)}) collective-permute-start(f32[192,2048]{1,0:T(8,128)S(1)} %get-tuple-element.238), channel_id=1, source_target_pairs={{0,16},{8,24},{16,0},{24,8},{1,17},{9,25},{17,1},{25,9},{2,18},{10... | collective-permute-start | bytes 4718600 | tf_op jit(solution)/shard_map/ppermute | solution.py:24
  236.1 62.3 %collective-permute-start.18 = (f32[192,2048]{1,0:T(8,128)S(1)}, f32[192,2048]{1,0:T(8,128)S(1)}, u32[]{:S(2)}, u32[]{:S(2)}) collective-permute-start(f32[192,2048]{1,0:T(8,128)S(1)} %get-tuple-element.246), channel_id=1, source_target_pairs={{0,8},{8,0},{16,24},{24,16},{1,9},{9,1},{17,25},{25,17},{2,10},{10... | collective-permute-start | bytes 4718600 | tf_op jit(solution)/shard_map/ppermute | solution.py:24
  236.2 64.3 %collective-permute-start.19 = (f32[192,2048]{1,0:T(8,128)S(1)}, f32[192,2048]{1,0:T(8,128)S(1)}, u32[]{:S(2)}, u32[]{:S(2)}) collective-permute-start(f32[192,2048]{1,0:T(8,128)S(1)} %get-tuple-element.247), channel_id=1, source_target_pairs={{0,16},{8,24},{16,0},{24,8},{1,17},{9,25},{17,1},{25,9},{2,18},{10... | collective-permute-start | bytes 4718600 | tf_op jit(solution)/shard_map/ppermute | solution.py:24
  269.8 62.3 %collective-permute-start.24 = (f32[192,2048]{1,0:T(8,128)S(1)}, f32[192,2048]{1,0:T(8,128)S(1)}, u32[]{:S(2)}, u32[]{:S(2)}) collective-permute-start(f32[192,2048]{1,0:T(8,128)S(1)} %get-tuple-element.260), channel_id=1, source_target_pairs={{0,8},{8,0},{16,24},{24,16},{1,9},{9,1},{17,25},{25,17},{2,10},{10... | collective-permute-start | bytes 4718600 | tf_op jit(solution)/shard_map/ppermute | solution.py:24
  269.9 64.3 %collective-permute-start.25 = (f32[192,2048]{1,0:T(8,128)S(1)}, f32[192,2048]{1,0:T(8,128)S(1)}, u32[]{:S(2)}, u32[]{:S(2)}) collective-permute-start(f32[192,2048]{1,0:T(8,128)S(1)} %get-tuple-element.261), channel_id=1, source_target_pairs={{0,16},{8,24},{16,0},{24,8},{1,17},{9,25},{17,1},{25,9},{2,18},{10... | collective-permute-start | bytes 4718600 | tf_op jit(solution)/shard_map/ppermute | solution.py:24
  303.5 62.3 %collective-permute-start.26 = (f32[192,2048]{1,0:T(8,128)S(1)}, f32[192,2048]{1,0:T(8,128)S(1)}, u32[]{:S(2)}, u32[]{:S(2)}) collective-permute-start(f32[192,2048]{1,0:T(8,128)S(1)} %get-tuple-element.267), channel_id=1, source_target_pairs={{0,8},{8,0},{16,24},{24,16},{1,9},{9,1},{17,25},{25,17},{2,10},{10... | collective-permute-start | bytes 4718600 | tf_op jit(solution)/shard_map/ppermute | solution.py:24
  303.6 64.3 %collective-permute-start.27 = (f32[192,2048]{1,0:T(8,128)S(1)}, f32[192,2048]{1,0:T(8,128)S(1)}, u32[]{:S(2)}, u32[]{:S(2)}) collective-permute-start(f32[192,2048]{1,0:T(8,128)S(1)} %get-tuple-element.268), channel_id=1, source_target_pairs={{0,16},{8,24},{16,0},{24,8},{1,17},{9,25},{17,1},{25,9},{2,18},{10... | collective-permute-start | bytes 4718600 | tf_op jit(solution)/shard_map/ppermute | solution.py:24
  337.2 64.4 %collective-permute-start.28 = (f32[200,2048]{1,0:T(8,128)S(1)}, f32[200,2048]{1,0:T(8,128)S(1)}, u32[]{:S(2)}, u32[]{:S(2)}) collective-permute-start(f32[200,2048]{1,0:T(8,128)S(1)} %get-tuple-element.276), channel_id=1, source_target_pairs={{0,8},{8,0},{16,24},{24,16},{1,9},{9,1},{17,25},{25,17},{2,10},{10... | collective-permute-start | bytes 4915208 | tf_op jit(solution)/shard_map/ppermute | solution.py:24
  337.3 64.3 %collective-permute-start.29 = (f32[192,2048]{1,0:T(8,128)S(1)}, f32[192,2048]{1,0:T(8,128)S(1)}, u32[]{:S(2)}, u32[]{:S(2)}) collective-permute-start(f32[192,2048]{1,0:T(8,128)S(1)} %get-tuple-element.277), channel_id=1, source_target_pairs={{0,16},{8,24},{16,0},{24,8},{1,17},{9,25},{17,1},{25,9},{2,18},{10... | collective-permute-start | bytes 4718600 | tf_op jit(solution)/shard_map/ppermute | solution.py:24
  370.9 63.7 %collective-permute-start.30 = (f32[192,2048]{1,0:T(8,128)S(1)}, f32[192,2048]{1,0:T(8,128)S(1)}, u32[]{:S(2)}, u32[]{:S(2)}) collective-permute-start(f32[192,2048]{1,0:T(8,128)S(1)} %get-tuple-element.285), channel_id=1, source_target_pairs={{0,8},{8,0},{16,24},{24,16},{1,9},{9,1},{17,25},{25,17},{2,10},{10... | collective-permute-start | bytes 4718600 | tf_op jit(solution)/shard_map/ppermute | solution.py:24
  371.0 64.3 %collective-permute-start.31 = (f32[192,2048]{1,0:T(8,128)S(1)}, f32[192,2048]{1,0:T(8,128)S(1)}, u32[]{:S(2)}, u32[]{:S(2)}) collective-permute-start(f32[192,2048]{1,0:T(8,128)S(1)} %get-tuple-element.286), channel_id=1, source_target_pairs={{0,16},{8,24},{16,0},{24,8},{1,17},{9,25},{17,1},{25,9},{2,18},{10... | collective-permute-start | bytes 4718600 | tf_op jit(solution)/shard_map/ppermute | solution.py:24
  404.7 65.8 %collective-permute-start.33 = (f32[200,2048]{1,0:T(8,128)S(1)}, f32[200,2048]{1,0:T(8,128)S(1)}, u32[]{:S(2)}, u32[]{:S(2)}) collective-permute-start(f32[200,2048]{1,0:T(8,128)S(1)} %get-tuple-element.295), channel_id=1, source_target_pairs={{0,16},{8,24},{16,0},{24,8},{1,17},{9,25},{17,1},{25,9},{2,18},{10... | collective-permute-start | bytes 4915208 | tf_op jit(solution)/shard_map/ppermute | solution.py:24
  406.2 62.1 %collective-permute-start.32 = (f32[192,2048]{1,0:T(8,128)S(1)}, f32[192,2048]{1,0:T(8,128)S(1)}, u32[]{:S(2)}, u32[]{:S(2)}) collective-permute-start(f32[192,2048]{1,0:T(8,128)S(1)} %get-tuple-element.294), channel_id=1, source_target_pairs={{0,8},{8,0},{16,24},{24,16},{1,9},{9,1},{17,25},{25,17},{2,10},{10... | collective-permute-start | bytes 4718600 | tf_op jit(solution)/shard_map/ppermute | solution.py:24
  438.3 63.7 %collective-permute-start.37 = (f32[192,2048]{1,0:T(8,128)S(1)}, f32[192,2048]{1,0:T(8,128)S(1)}, u32[]{:S(2)}, u32[]{:S(2)}) collective-permute-start(f32[192,2048]{1,0:T(8,128)S(1)} %get-tuple-element.313), channel_id=1, source_target_pairs={{0,8},{8,0},{16,24},{24,16},{1,9},{9,1},{17,25},{25,17},{2,10},{10... | collective-permute-start | bytes 4718600 | tf_op jit(solution)/shard_map/ppermute | solution.py:24
  439.8 64.3 %collective-permute-start.38 = (f32[192,2048]{1,0:T(8,128)S(1)}, f32[192,2048]{1,0:T(8,128)S(1)}, u32[]{:S(2)}, u32[]{:S(2)}) collective-permute-start(f32[192,2048]{1,0:T(8,128)S(1)} %get-tuple-element.314), channel_id=1, source_target_pairs={{0,16},{8,24},{16,0},{24,8},{1,17},{9,25},{17,1},{25,9},{2,18},{10... | collective-permute-start | bytes 4718600 | tf_op jit(solution)/shard_map/ppermute | solution.py:24
  478.9 45.6 %collective-permute-start.39 = (f32[128,2048]{1,0:T(8,128)}, f32[128,2048]{1,0:T(8,128)S(1)}, u32[]{:S(2)}, u32[]{:S(2)}) collective-permute-start(f32[128,2048]{1,0:T(8,128)} %get-tuple-element.323), channel_id=1, source_target_pairs={{0,8},{8,0},{16,24},{24,16},{1,9},{9,1},{17,25},{25,17},{2,10},{10... | collective-permute-start | bytes 3145736 | tf_op jit(solution)/shard_map/ppermute | solution.py:24
  480.6 46.0 %collective-permute-start.40 = (f32[128,2048]{1,0:T(8,128)}, f32[128,2048]{1,0:T(8,128)S(1)}, u32[]{:S(2)}, u32[]{:S(2)}) collective-permute-start(f32[128,2048]{1,0:T(8,128)} %get-tuple-element.324), channel_id=1, source_target_pairs={{0,16},{8,24},{16,0},{24,8},{1,17},{9,25},{17,1},{25,9},{2,18},{10... | collective-permute-start | bytes 3145736 | tf_op jit(solution)/shard_map/ppermute | solution.py:24
  506.9 39.3 %collective-permute-start.41 = (f32[128,2048]{1,0:T(8,128)S(1)}, f32[128,2048]{1,0:T(8,128)S(1)}, u32[]{:S(2)}, u32[]{:S(2)}) collective-permute-start(f32[128,2048]{1,0:T(8,128)S(1)} %get-tuple-element.332), channel_id=1, source_target_pairs={{0,8},{8,0},{16,24},{24,16},{1,9},{9,1},{17,25},{25,17},{2,10},{10... | collective-permute-start | bytes 3145736 | tf_op jit(solution)/shard_map/ppermute | solution.py:24
  507.0 40.6 %collective-permute-start.42 = (f32[128,2048]{1,0:T(8,128)S(1)}, f32[128,2048]{1,0:T(8,128)S(1)}, u32[]{:S(2)}, u32[]{:S(2)}) collective-permute-start(f32[128,2048]{1,0:T(8,128)S(1)} %get-tuple-element.333), channel_id=1, source_target_pairs={{0,16},{8,24},{16,0},{24,8},{1,17},{9,25},{17,1},{25,9},{2,18},{10... | collective-permute-start | bytes 3145736 | tf_op jit(solution)/shard_map/ppermute | solution.py:24
  (27 other events, 339.0 us)

commit v11 on v10

--- a/solution.py
+++ b/solution.py
@@ -293,20 +293,18 @@
 
     def body(*blocks):
         new_p, moved = blocks[-2:]
-        i = pl.program_id(0)
-        pl.when(i == 0)(scale)
-        for half in range(2):
-            for r in range(0, part, sublanes):
-                at = half * part + r
-                mine = column[i, at : at + sublanes][:, 0:1]
-                y = summed[i, half, r : r + sublanes] * mine * by_col[...]
-                moved[half, r : r + sublanes] = y
-                p = params[i, half, r : r + sublanes] if staged else blocks[0][half, r : r + sublanes]
-                new_p[half, r : r + sublanes] = p - learn_rate * y
-
-    of_matrix = pl.BlockSpec((None, None, 2, part, width), lambda i: (m, i, 0, 0, 0))
+        i, half = pl.program_id(0), pl.program_id(1)
+        pl.when((i == 0) & (half == 0))(scale)
+        for r in range(0, part, sublanes):
+            rows = slice(r, r + sublanes)
+            at = pl.ds(pl.multiple_of(half * part + r, sublanes), sublanes)
+            y = summed[i, half, rows] * column[i, at][:, 0:1] * by_col[...]
+            moved[rows] = y
+            new_p[rows] = (params[i, half, rows] if staged else blocks[0][rows]) - learn_rate * y
+
+    of_matrix = pl.BlockSpec((None, None, None, part, width), lambda i, h: (m, i, h, 0, 0))
     pltpu.emit_pipeline(
-        body, grid=(count,), in_specs=[] if staged else [of_matrix], out_specs=[of_matrix] * 2
+        body, grid=(count, 2), in_specs=[] if staged else [of_matrix], out_specs=[of_matrix] * 2
     )(*([] if staged else [params]), new_params, update)
 
 
@@ -351,7 +349,7 @@
     def row_stage(m, sums):
         cols, rows_along, summed = sums
         row_new, stats = weighted_sums(
-            extent, exchange(rows_along, "col"), row_factor[m], cols, summed
+            extent, [pairwise_sum(rows_along, "col")], row_factor[m], cols, summed
         )
         new_rows.append(row_new.reshape(rows))
         return row_new, pairwise_sum(stats, "row")

time: 583 us -> 587 us (level)
    ppermute x53 -> x51, starting transfers between devices: 65.1 us -> 61.3 us  [swap(): return lax.ppermute(x, axes, [(i, i ^ mask) for i in range(size)])]
    ppermute x53 -> x51, waiting for transfers between devices: 429 us -> 432 us  [swap(): return lax.ppermute(x, axes, [(i, i ^ mask) for i in range(size)])]
  transfers between devices with their start and end apart: 53 -> 51, of which waited for: 47 -> 45; matrix products, arithmetic and copies ran while one was open for 2% -> 2% of each run, Pallas kernels for 11% -> 11%
where the time goes in v11:
time: 587 us; the launch traced here: 586 us
  waiting for transfers between devices  432 us (74%)
  Pallas kernels  79.5 us (14%)
  starting transfers between devices  61.3 us (10%)
  local copies, waits for them, and re-layouts  11.3 us (2%)
    ppermute x51, waiting for transfers between devices, swap(): return lax.ppermute(x, axes, [(i, i ^ mask) for i in range(size)])  432 us
    ppermute x51, starting transfers between devices, swap(): return lax.ppermute(x, axes, [(i, i ^ mask) for i in range(size)])  61.3 us
    pallas_call x20, Pallas kernels, step(): pl.pallas_call(functools.partial(step_kernel, takes, finishes, b, sends,...  53 us
    pallas_call x2, Pallas kernels, finish(): pl.pallas_call(functools.partial(finish_kernel, m, extent, len(pairs), st...  24.1 us
  transfers between devices with their start and end apart: 51, of which 45 were waited for; matrix products, arithmetic and copies ran while one was open for 2% of the time, Pallas kernels for 11%

profile of v11, /device:TPU:0, one launch (start us, length us, event | category | flops | bytes accessed | tf_op | source)
XLA Modules:
  0.0 585.8 jit_solution(3715091281573072103)
XLA Ops:
  1.7 3.0 collective-permute-start
  8.0 9.5 %collective-permute-done.refs_1_ = f32[64,2048]{1,0:T(8,128)S(1)} collective-permute-done((f32[64,2048]{1,0:T(8,128)S(1)}, f32[64,2048]{1,0:T(8,128)S(1)}, u32[]{:S(2)}, u32[]{:S(2)}) %collective-permute-start) | collective-permute-done | bytes 524320 | tf_op jit(solution)/shard_map/ppermute | solution.py:24
  24.2 4.5 collective-permute-done.2.refs_1_
  35.4 27.0 %collective-permute-done.4.refs_1_ = f32[192,2048]{1,0:T(8,128)S(1)} collective-permute-done((f32[192,2048]{1,0:T(8,128)S(1)}, f32[192,2048]{1,0:T(8,128)S(1)}, u32[]{:S(2)}, u32[]{:S(2)}) %collective-permute-start.4) | collective-permute-done | bytes 1572896 | tf_op jit(solution)/shard_map/ppermute | solution.py:24
  64.5 3.0 step.24
  69.7 26.5 %collective-permute-done.6.refs_1_ = f32[192,2048]{1,0:T(8,128)S(1)} collective-permute-done((f32[192,2048]{1,0:T(8,128)S(1)}, f32[192,2048]{1,0:T(8,128)S(1)}, u32[]{:S(2)}, u32[]{:S(2)}) %collective-permute-start.6) | collective-permute-done | bytes 1572896 | tf_op jit(solution)/shard_map/ppermute | solution.py:24
  103.4 26.5 %collective-permute-done.8.refs_1_ = f32[192,2048]{1,0:T(8,128)S(1)} collective-permute-done((f32[192,2048]{1,0:T(8,128)S(1)}, f32[192,2048]{1,0:T(8,128)S(1)}, u32[]{:S(2)}, u32[]{:S(2)}) %collective-permute-start.8) | collective-permute-done | bytes 1572896 | tf_op jit(solution)/shard_map/ppermute | solution.py:24
  132.0 3.0 step.26
  137.1 26.5 %collective-permute-done.10.refs_1_ = f32[192,2048]{1,0:T(8,128)S(1)} collective-permute-done((f32[192,2048]{1,0:T(8,128)S(1)}, f32[192,2048]{1,0:T(8,128)S(1)}, u32[]{:S(2)}, u32[]{:S(2)}) %collective-permute-start.10) | collective-permute-done | bytes 1572896 | tf_op jit(solution)/shard_map/ppermute | solution.py:24
  170.8 26.5 %collective-permute-done.12.refs_1_ = f32[192,2048]{1,0:T(8,128)S(1)} collective-permute-done((f32[192,2048]{1,0:T(8,128)S(1)}, f32[192,2048]{1,0:T(8,128)S(1)}, u32[]{:S(2)}, u32[]{:S(2)}) %collective-permute-start.12) | collective-permute-done | bytes 1572896 | tf_op jit(solution)/shard_map/ppermute | solution.py:24
  204.5 26.5 %collective-permute-done.14.refs_1_ = f32[192,2048]{1,0:T(8,128)S(1)} collective-permute-done((f32[192,2048]{1,0:T(8,128)S(1)}, f32[192,2048]{1,0:T(8,128)S(1)}, u32[]{:S(2)}, u32[]{:S(2)}) %collective-permute-start.14) | collective-permute-done | bytes 1572896 | tf_op jit(solution)/shard_map/ppermute | solution.py:24
  233.1 3.0 step.29
  238.2 26.5 %collective-permute-done.16.refs_1_ = f32[192,2048]{1,0:T(8,128)S(1)} collective-permute-done((f32[192,2048]{1,0:T(8,128)S(1)}, f32[192,2048]{1,0:T(8,128)S(1)}, u32[]{:S(2)}, u32[]{:S(2)}) %collective-permute-start.16) | collective-permute-done | bytes 1572896 | tf_op jit(solution)/shard_map/ppermute | solution.py:24
  271.9 26.5 %collective-permute-done.18.refs_1_ = f32[192,2048]{1,0:T(8,128)S(1)} collective-permute-done((f32[192,2048]{1,0:T(8,128)S(1)}, f32[192,2048]{1,0:T(8,128)S(1)}, u32[]{:S(2)}, u32[]{:S(2)}) %collective-permute-start.18) | collective-permute-done | bytes 1572896 | tf_op jit(solution)/shard_map/ppermute | solution.py:24
  300.5 3.0 step.31
  316.1 16.0 %collective-permute-done.23.refs_1_ = f32[192,2048]{1,0:T(8,128)S(1)} collective-permute-done((f32[192,2048]{1,0:T(8,128)S(1)}, f32[192,2048]{1,0:T(8,128)S(1)}, u32[]{:S(2)}, u32[]{:S(2)}) %collective-permute-start.23) | collective-permute-done | bytes 1572896 | tf_op jit(solution)/shard_map/ppermute | solution.py:24
  334.2 3.0 step.32
  339.3 26.5 %collective-permute-done.25.refs_1_ = f32[192,2048]{1,0:T(8,128)S(1)} collective-permute-done((f32[192,2048]{1,0:T(8,128)S(1)}, f32[192,2048]{1,0:T(8,128)S(1)}, u32[]{:S(2)}, u32[]{:S(2)}) %collective-permute-start.25) | collective-permute-done | bytes 1572896 | tf_op jit(solution)/shard_map/ppermute | solution.py:24
  367.9 3.0 step.33
  373.0 28.6 %collective-permute-done.28.refs_2_ = f32[192,2048]{1,0:T(8,128)S(1)} collective-permute-done((f32[192,2048]{1,0:T(8,128)S(1)}, f32[192,2048]{1,0:T(8,128)S(1)}, u32[]{:S(2)}, u32[]{:S(2)}) %collective-permute-start.28) | collective-permute-done | bytes 1572896 | tf_op jit(solution)/shard_map/ppermute | solution.py:24
  401.6 3.0 step.34
  407.6 27.0 %collective-permute-done.29.refs_1_ = f32[192,2048]{1,0:T(8,128)S(1)} collective-permute-done((f32[192,2048]{1,0:T(8,128)S(1)}, f32[192,2048]{1,0:T(8,128)S(1)}, u32[]{:S(2)}, u32[]{:S(2)}) %collective-permute-start.29) | collective-permute-done | bytes 1572896 | tf_op jit(solution)/shard_map/ppermute | solution.py:24
  435.3 3.0 step.35
  441.3 27.0 %collective-permute-done.31.refs_1_ = f32[192,2048]{1,0:T(8,128)S(1)} collective-permute-done((f32[192,2048]{1,0:T(8,128)S(1)}, f32[192,2048]{1,0:T(8,128)S(1)}, u32[]{:S(2)}, u32[]{:S(2)}) %collective-permute-start.31) | collective-permute-done | bytes 1572896 | tf_op jit(solution)/shard_map/ppermute | solution.py:24
  470.4 4.0 step.36
  484.1 3.4 copy-done.1
  487.5 14.5 %finish.2 = (f32[2,8,2,64,2048]{4,3,2,1,0:T(8,128)}, f32[2,8,2,64,2048]{4,3,2,1,0:T(8,128)}) custom-call(f32[8,128]{1,0:T(8,128)S(1)} %get-tuple-element.306.row_new, f32[1,2048]{1,0:T(1,128)S(1)} %get-tuple-element.308.col_new, f32[8,2,64,2048]{3,2,1,0:T(8,128)S(1)} %copy-done.1, f32[2,8,2,64,2048]{4,3,2,1,0:T(8,128)} %bitcast.113, ...), custom_call_target="tpu_custom_call" | custom-call | flops 8388608 | bytes 33554432 | tf_op jit(solution)/shard_map/finish/pallas_call | solution.py:317
  509.0 7.9 %slice.19 = f32[1,1024,2048]{2,1,0:T(8,128)} slice(f32[2,1024,2048]{2,1,0:T(8,128)} %param.5), slice={[1:2], [0:1024], [0:2048]} | slice | bytes 16777216 | tf_op jit(solution)/shard_map/slice | solution.py:392
  516.9 7.6 %collective-permute-done.38.refs_1_ = f32[128,2048]{1,0:T(8,128)S(1)} collective-permute-done((f32[128,2048]{1,0:T(8,128)}, f32[128,2048]{1,0:T(8,128)S(1)}, u32[]{:S(2)}, u32[]{:S(2)}) %collective-permute-start.38) | collective-permute-done | bytes 1048608 | tf_op jit(solution)/shard_map/ppermute | solution.py:24
  528.2 17.9 %collective-permute-done.40.refs_1_ = f32[128,2048]{1,0:T(8,128)S(1)} collective-permute-done((f32[128,2048]{1,0:T(8,128)S(1)}, f32[128,2048]{1,0:T(8,128)S(1)}, u32[]{:S(2)}, u32[]{:S(2)}) %collective-permute-start.40) | collective-permute-done | bytes 1048608 | tf_op jit(solution)/shard_map/ppermute | solution.py:24
  572.7 3.5 collective-permute-done.50.refs_3_
  576.2 9.6 %finish.3 = (f32[2,8,2,64,2048]{4,3,2,1,0:T(8,128)}, f32[2,8,2,64,2048]{4,3,2,1,0:T(8,128)}) custom-call(f32[8,128]{1,0:T(8,128)S(1)} %get-tuple-element.343.row_new, f32[1,2048]{1,0:T(1,128)S(1)} %get-tuple-element.345.col_new, f32[8,2,64,2048]{3,2,1,0:T(8,128)S(1)} %get-tuple-element.341.summed, ...), custom_call_target="tpu_custom_call", output_to_operand_aliasing={{0}: (8, {}), {1}: (9, {})} | custom-call | flops 8388608 | bytes 33554432 | tf_op jit(solution)/shard_map/finish/pallas_call | solution.py:317
  (120 shorter events, 137.9 us)
Async XLA Ops:
  22.1 40.4 %collective-permute-start.4 = (f32[192,2048]{1,0:T(8,128)S(1)}, f32[192,2048]{1,0:T(8,128)S(1)}, u32[]{:S(2)}, u32[]{:S(2)}) collective-permute-start(f32[192,2048]{1,0:T(8,128)S(1)} %get-tuple-element.184), channel_id=1, source_target_pairs={{0,8},{8,0},{16,24},{24,16},{1,9},{9,1},{17,25},{25,17},{2,10},{10... | collective-permute-start | bytes 4718600 | tf_op jit(solution)/shard_map/ppermute | solution.py:24
  22.2 42.4 %collective-permute-start.5 = (f32[192,2048]{1,0:T(8,128)S(1)}, f32[192,2048]{1,0:T(8,128)S(1)}, u32[]{:S(2)}, u32[]{:S(2)}) collective-permute-start(f32[192,2048]{1,0:T(8,128)S(1)} %get-tuple-element.185), channel_id=1, source_target_pairs={{0,16},{8,24},{16,0},{24,8},{1,17},{9,25},{17,1},{25,9},{2,18},{10... | collective-permute-start | bytes 4718600 | tf_op jit(solution)/shard_map/ppermute | solution.py:24
  33.3 62.8 %collective-permute-start.6 = (f32[192,2048]{1,0:T(8,128)S(1)}, f32[192,2048]{1,0:T(8,128)S(1)}, u32[]{:S(2)}, u32[]{:S(2)}) collective-permute-start(f32[192,2048]{1,0:T(8,128)S(1)} %get-tuple-element.187), channel_id=1, source_target_pairs={{0,8},{8,0},{16,24},{24,16},{1,9},{9,1},{17,25},{25,17},{2,10},{10... | collective-permute-start | bytes 4718600 | tf_op jit(solution)/shard_map/ppermute | solution.py:24
  33.4 64.8 %collective-permute-start.7 = (f32[192,2048]{1,0:T(8,128)S(1)}, f32[192,2048]{1,0:T(8,128)S(1)}, u32[]{:S(2)}, u32[]{:S(2)}) collective-permute-start(f32[192,2048]{1,0:T(8,128)S(1)} %get-tuple-element.188), channel_id=1, source_target_pairs={{0,16},{8,24},{16,0},{24,8},{1,17},{9,25},{17,1},{25,9},{2,18},{10... | collective-permute-start | bytes 4718600 | tf_op jit(solution)/shard_map/ppermute | solution.py:24
  67.5 62.3 %collective-permute-start.8 = (f32[192,2048]{1,0:T(8,128)S(1)}, f32[192,2048]{1,0:T(8,128)S(1)}, u32[]{:S(2)}, u32[]{:S(2)}) collective-permute-start(f32[192,2048]{1,0:T(8,128)S(1)} %get-tuple-element.201), channel_id=1, source_target_pairs={{0,8},{8,0},{16,24},{24,16},{1,9},{9,1},{17,25},{25,17},{2,10},{10... | collective-permute-start | bytes 4718600 | tf_op jit(solution)/shard_map/ppermute | solution.py:24
  67.7 64.3 %collective-permute-start.9 = (f32[192,2048]{1,0:T(8,128)S(1)}, f32[192,2048]{1,0:T(8,128)S(1)}, u32[]{:S(2)}, u32[]{:S(2)}) collective-permute-start(f32[192,2048]{1,0:T(8,128)S(1)} %get-tuple-element.202), channel_id=1, source_target_pairs={{0,16},{8,24},{16,0},{24,8},{1,17},{9,25},{17,1},{25,9},{2,18},{10... | collective-permute-start | bytes 4718600 | tf_op jit(solution)/shard_map/ppermute | solution.py:24
  101.2 62.3 %collective-permute-start.10 = (f32[192,2048]{1,0:T(8,128)S(1)}, f32[192,2048]{1,0:T(8,128)S(1)}, u32[]{:S(2)}, u32[]{:S(2)}) collective-permute-start(f32[192,2048]{1,0:T(8,128)S(1)} %get-tuple-element.210), channel_id=1, source_target_pairs={{0,8},{8,0},{16,24},{24,16},{1,9},{9,1},{17,25},{25,17},{2,10},{10... | collective-permute-start | bytes 4718600 | tf_op jit(solution)/shard_map/ppermute | solution.py:24
  101.4 64.3 %collective-permute-start.11 = (f32[192,2048]{1,0:T(8,128)S(1)}, f32[192,2048]{1,0:T(8,128)S(1)}, u32[]{:S(2)}, u32[]{:S(2)}) collective-permute-start(f32[192,2048]{1,0:T(8,128)S(1)} %get-tuple-element.211), channel_id=1, source_target_pairs={{0,16},{8,24},{16,0},{24,8},{1,17},{9,25},{17,1},{25,9},{2,18},{10... | collective-permute-start | bytes 4718600 | tf_op jit(solution)/shard_map/ppermute | solution.py:24
  135.0 62.3 %collective-permute-start.12 = (f32[192,2048]{1,0:T(8,128)S(1)}, f32[192,2048]{1,0:T(8,128)S(1)}, u32[]{:S(2)}, u32[]{:S(2)}) collective-permute-start(f32[192,2048]{1,0:T(8,128)S(1)} %get-tuple-element.219), channel_id=1, source_target_pairs={{0,8},{8,0},{16,24},{24,16},{1,9},{9,1},{17,25},{25,17},{2,10},{10... | collective-permute-start | bytes 4718600 | tf_op jit(solution)/shard_map/ppermute | solution.py:24
  135.1 64.3 %collective-permute-start.13 = (f32[192,2048]{1,0:T(8,128)S(1)}, f32[192,2048]{1,0:T(8,128)S(1)}, u32[]{:S(2)}, u32[]{:S(2)}) collective-permute-start(f32[192,2048]{1,0:T(8,128)S(1)} %get-tuple-element.220), channel_id=1, source_target_pairs={{0,16},{8,24},{16,0},{24,8},{1,17},{9,25},{17,1},{25,9},{2,18},{10... | collective-permute-start | bytes 4718600 | tf_op jit(solution)/shard_map/ppermute | solution.py:24
  168.7 62.3 %collective-permute-start.14 = (f32[192,2048]{1,0:T(8,128)S(1)}, f32[192,2048]{1,0:T(8,128)S(1)}, u32[]{:S(2)}, u32[]{:S(2)}) collective-permute-start(f32[192,2048]{1,0:T(8,128)S(1)} %get-tuple-element.228), channel_id=1, source_target_pairs={{0,8},{8,0},{16,24},{24,16},{1,9},{9,1},{17,25},{25,17},{2,10},{10... | collective-permute-start | bytes 4718600 | tf_op jit(solution)/shard_map/ppermute | solution.py:24
  168.8 64.3 %collective-permute-start.15 = (f32[192,2048]{1,0:T(8,128)S(1)}, f32[192,2048]{1,0:T(8,128)S(1)}, u32[]{:S(2)}, u32[]{:S(2)}) collective-permute-start(f32[192,2048]{1,0:T(8,128)S(1)} %get-tuple-element.229), channel_id=1, source_target_pairs={{0,16},{8,24},{16,0},{24,8},{1,17},{9,25},{17,1},{25,9},{2,18},{10... | collective-permute-start | bytes 4718600 | tf_op jit(solution)/shard_map/ppermute | solution.py:24
  202.4 62.3 %collective-permute-start.16 = (f32[192,2048]{1,0:T(8,128)S(1)}, f32[192,2048]{1,0:T(8,128)S(1)}, u32[]{:S(2)}, u32[]{:S(2)}) collective-permute-start(f32[192,2048]{1,0:T(8,128)S(1)} %get-tuple-element.237), channel_id=1, source_target_pairs={{0,8},{8,0},{16,24},{24,16},{1,9},{9,1},{17,25},{25,17},{2,10},{10... | collective-permute-start | bytes 4718600 | tf_op jit(solution)/shard_map/ppermute | solution.py:24
  202.5 64.3 %collective-permute-start.17 = (f32[192,2048]{1,0:T(8,128)S(1)}, f32[192,2048]{1,0:T(8,128)S(1)}, u32[]{:S(2)}, u32[]{:S(2)}) collective-permute-start(f32[192,2048]{1,0:T(8,128)S(1)} %get-tuple-element.238), channel_id=1, source_target_pairs={{0,16},{8,24},{16,0},{24,8},{1,17},{9,25},{17,1},{25,9},{2,18},{10... | collective-permute-start | bytes 4718600 | tf_op jit(solution)/shard_map/ppermute | solution.py:24
  236.1 62.3 %collective-permute-start.18 = (f32[192,2048]{1,0:T(8,128)S(1)}, f32[192,2048]{1,0:T(8,128)S(1)}, u32[]{:S(2)}, u32[]{:S(2)}) collective-permute-start(f32[192,2048]{1,0:T(8,128)S(1)} %get-tuple-element.246), channel_id=1, source_target_pairs={{0,8},{8,0},{16,24},{24,16},{1,9},{9,1},{17,25},{25,17},{2,10},{10... | collective-permute-start | bytes 4718600 | tf_op jit(solution)/shard_map/ppermute | solution.py:24
  236.2 64.3 %collective-permute-start.19 = (f32[192,2048]{1,0:T(8,128)S(1)}, f32[192,2048]{1,0:T(8,128)S(1)}, u32[]{:S(2)}, u32[]{:S(2)}) collective-permute-start(f32[192,2048]{1,0:T(8,128)S(1)} %get-tuple-element.247), channel_id=1, source_target_pairs={{0,16},{8,24},{16,0},{24,8},{1,17},{9,25},{17,1},{25,9},{2,18},{10... | collective-permute-start | bytes 4718600 | tf_op jit(solution)/shard_map/ppermute | solution.py:24
  269.8 62.3 %collective-permute-start.23 = (f32[192,2048]{1,0:T(8,128)S(1)}, f32[192,2048]{1,0:T(8,128)S(1)}, u32[]{:S(2)}, u32[]{:S(2)}) collective-permute-start(f32[192,2048]{1,0:T(8,128)S(1)} %get-tuple-element.260), channel_id=1, source_target_pairs={{0,8},{8,0},{16,24},{24,16},{1,9},{9,1},{17,25},{25,17},{2,10},{10... | collective-permute-start | bytes 4718600 | tf_op jit(solution)/shard_map/ppermute | solution.py:24
  269.9 64.3 %collective-permute-start.24 = (f32[192,2048]{1,0:T(8,128)S(1)}, f32[192,2048]{1,0:T(8,128)S(1)}, u32[]{:S(2)}, u32[]{:S(2)}) collective-permute-start(f32[192,2048]{1,0:T(8,128)S(1)} %get-tuple-element.261), channel_id=1, source_target_pairs={{0,16},{8,24},{16,0},{24,8},{1,17},{9,25},{17,1},{25,9},{2,18},{10... | collective-permute-start | bytes 4718600 | tf_op jit(solution)/shard_map/ppermute | solution.py:24
  303.5 62.3 %collective-permute-start.25 = (f32[192,2048]{1,0:T(8,128)S(1)}, f32[192,2048]{1,0:T(8,128)S(1)}, u32[]{:S(2)}, u32[]{:S(2)}) collective-permute-start(f32[192,2048]{1,0:T(8,128)S(1)} %get-tuple-element.267), channel_id=1, source_target_pairs={{0,8},{8,0},{16,24},{24,16},{1,9},{9,1},{17,25},{25,17},{2,10},{10... | collective-permute-start | bytes 4718600 | tf_op jit(solution)/shard_map/ppermute | solution.py:24
  303.6 64.3 %collective-permute-start.26 = (f32[192,2048]{1,0:T(8,128)S(1)}, f32[192,2048]{1,0:T(8,128)S(1)}, u32[]{:S(2)}, u32[]{:S(2)}) collective-permute-start(f32[192,2048]{1,0:T(8,128)S(1)} %get-tuple-element.268), channel_id=1, source_target_pairs={{0,16},{8,24},{16,0},{24,8},{1,17},{9,25},{17,1},{25,9},{2,18},{10... | collective-permute-start | bytes 4718600 | tf_op jit(solution)/shard_map/ppermute | solution.py:24
  337.2 64.4 %collective-permute-start.27 = (f32[200,2048]{1,0:T(8,128)S(1)}, f32[200,2048]{1,0:T(8,128)S(1)}, u32[]{:S(2)}, u32[]{:S(2)}) collective-permute-start(f32[200,2048]{1,0:T(8,128)S(1)} %get-tuple-element.276), channel_id=1, source_target_pairs={{0,8},{8,0},{16,24},{24,16},{1,9},{9,1},{17,25},{25,17},{2,10},{10... | collective-permute-start | bytes 4915208 | tf_op jit(solution)/shard_map/ppermute | solution.py:24
  337.3 64.3 %collective-permute-start.28 = (f32[192,2048]{1,0:T(8,128)S(1)}, f32[192,2048]{1,0:T(8,128)S(1)}, u32[]{:S(2)}, u32[]{:S(2)}) collective-permute-start(f32[192,2048]{1,0:T(8,128)S(1)} %get-tuple-element.277), channel_id=1, source_target_pairs={{0,16},{8,24},{16,0},{24,8},{1,17},{9,25},{17,1},{25,9},{2,18},{10... | collective-permute-start | bytes 4718600 | tf_op jit(solution)/shard_map/ppermute | solution.py:24
  370.9 63.7 %collective-permute-start.29 = (f32[192,2048]{1,0:T(8,128)S(1)}, f32[192,2048]{1,0:T(8,128)S(1)}, u32[]{:S(2)}, u32[]{:S(2)}) collective-permute-start(f32[192,2048]{1,0:T(8,128)S(1)} %get-tuple-element.285), channel_id=1, source_target_pairs={{0,8},{8,0},{16,24},{24,16},{1,9},{9,1},{17,25},{25,17},{2,10},{10... | collective-permute-start | bytes 4718600 | tf_op jit(solution)/shard_map/ppermute | solution.py:24
  371.0 64.3 %collective-permute-start.30 = (f32[192,2048]{1,0:T(8,128)S(1)}, f32[192,2048]{1,0:T(8,128)S(1)}, u32[]{:S(2)}, u32[]{:S(2)}) collective-permute-start(f32[192,2048]{1,0:T(8,128)S(1)} %get-tuple-element.286), channel_id=1, source_target_pairs={{0,16},{8,24},{16,0},{24,8},{1,17},{9,25},{17,1},{25,9},{2,18},{10... | collective-permute-start | bytes 4718600 | tf_op jit(solution)/shard_map/ppermute | solution.py:24
  404.7 65.8 %collective-permute-start.32 = (f32[200,2048]{1,0:T(8,128)S(1)}, f32[200,2048]{1,0:T(8,128)S(1)}, u32[]{:S(2)}, u32[]{:S(2)}) collective-permute-start(f32[200,2048]{1,0:T(8,128)S(1)} %get-tuple-element.295), channel_id=1, source_target_pairs={{0,16},{8,24},{16,0},{24,8},{1,17},{9,25},{17,1},{25,9},{2,18},{10... | collective-permute-start | bytes 4915208 | tf_op jit(solution)/shard_map/ppermute | solution.py:24
  406.2 62.1 %collective-permute-start.31 = (f32[192,2048]{1,0:T(8,128)S(1)}, f32[192,2048]{1,0:T(8,128)S(1)}, u32[]{:S(2)}, u32[]{:S(2)}) collective-permute-start(f32[192,2048]{1,0:T(8,128)S(1)} %get-tuple-element.294), channel_id=1, source_target_pairs={{0,8},{8,0},{16,24},{24,16},{1,9},{9,1},{17,25},{25,17},{2,10},{10... | collective-permute-start | bytes 4718600 | tf_op jit(solution)/shard_map/ppermute | solution.py:24
  438.3 63.7 %collective-permute-start.36 = (f32[192,2048]{1,0:T(8,128)S(1)}, f32[192,2048]{1,0:T(8,128)S(1)}, u32[]{:S(2)}, u32[]{:S(2)}) collective-permute-start(f32[192,2048]{1,0:T(8,128)S(1)} %get-tuple-element.313), channel_id=1, source_target_pairs={{0,8},{8,0},{16,24},{24,16},{1,9},{9,1},{17,25},{25,17},{2,10},{10... | collective-permute-start | bytes 4718600 | tf_op jit(solution)/shard_map/ppermute | solution.py:24
  439.8 64.3 %collective-permute-start.37 = (f32[192,2048]{1,0:T(8,128)S(1)}, f32[192,2048]{1,0:T(8,128)S(1)}, u32[]{:S(2)}, u32[]{:S(2)}) collective-permute-start(f32[192,2048]{1,0:T(8,128)S(1)} %get-tuple-element.314), channel_id=1, source_target_pairs={{0,16},{8,24},{16,0},{24,8},{1,17},{9,25},{17,1},{25,9},{2,18},{10... | collective-permute-start | bytes 4718600 | tf_op jit(solution)/shard_map/ppermute | solution.py:24
  478.9 45.6 %collective-permute-start.38 = (f32[128,2048]{1,0:T(8,128)}, f32[128,2048]{1,0:T(8,128)S(1)}, u32[]{:S(2)}, u32[]{:S(2)}) collective-permute-start(f32[128,2048]{1,0:T(8,128)} %get-tuple-element.323), channel_id=1, source_target_pairs={{0,8},{8,0},{16,24},{24,16},{1,9},{9,1},{17,25},{25,17},{2,10},{10... | collective-permute-start | bytes 3145736 | tf_op jit(solution)/shard_map/ppermute | solution.py:24
  480.6 46.0 %collective-permute-start.39 = (f32[128,2048]{1,0:T(8,128)}, f32[128,2048]{1,0:T(8,128)S(1)}, u32[]{:S(2)}, u32[]{:S(2)}) collective-permute-start(f32[128,2048]{1,0:T(8,128)} %get-tuple-element.324), channel_id=1, source_target_pairs={{0,16},{8,24},{16,0},{24,8},{1,17},{9,25},{17,1},{25,9},{2,18},{10... | collective-permute-start | bytes 3145736 | tf_op jit(solution)/shard_map/ppermute | solution.py:24
  506.9 39.3 %collective-permute-start.40 = (f32[128,2048]{1,0:T(8,128)S(1)}, f32[128,2048]{1,0:T(8,128)S(1)}, u32[]{:S(2)}, u32[]{:S(2)}) collective-permute-start(f32[128,2048]{1,0:T(8,128)S(1)} %get-tuple-element.332), channel_id=1, source_target_pairs={{0,8},{8,0},{16,24},{24,16},{1,9},{9,1},{17,25},{25,17},{2,10},{10... | collective-permute-start | bytes 3145736 | tf_op jit(solution)/shard_map/ppermute | solution.py:24
  507.0 40.6 %collective-permute-start.41 = (f32[128,2048]{1,0:T(8,128)S(1)}, f32[128,2048]{1,0:T(8,128)S(1)}, u32[]{:S(2)}, u32[]{:S(2)}) collective-permute-start(f32[128,2048]{1,0:T(8,128)S(1)} %get-tuple-element.333), channel_id=1, source_target_pairs={{0,16},{8,24},{16,0},{24,8},{1,17},{9,25},{17,1},{25,9},{2,18},{10... | collective-permute-start | bytes 3145736 | tf_op jit(solution)/shard_map/ppermute | solution.py:24
  (25 other events, 319.8 us)

commit v12 on v11

--- a/solution.py
+++ b/solution.py
@@ -1,4 +1,5 @@
 import functools
+import itertools
 
 import jax
 import jax.numpy as jnp
@@ -293,18 +294,19 @@
 
     def body(*blocks):
         new_p, moved = blocks[-2:]
-        i, half = pl.program_id(0), pl.program_id(1)
-        pl.when((i == 0) & (half == 0))(scale)
-        for r in range(0, part, sublanes):
+        pl.when(pl.program_id(0) == 0)(scale)
+        for g, half, r in itertools.product(range(2), range(2), range(0, part, sublanes)):
+            i = 2 * pl.program_id(0) + g
             rows = slice(r, r + sublanes)
-            at = pl.ds(pl.multiple_of(half * part + r, sublanes), sublanes)
-            y = summed[i, half, rows] * column[i, at][:, 0:1] * by_col[...]
-            moved[rows] = y
-            new_p[rows] = (params[i, half, rows] if staged else blocks[0][rows]) - learn_rate * y
-
-    of_matrix = pl.BlockSpec((None, None, None, part, width), lambda i, h: (m, i, h, 0, 0))
+            at = half * part + r
+            y = summed[i, half, rows] * column[i, at : at + sublanes][:, 0:1] * by_col[...]
+            moved[g, half, rows] = y
+            p = params[i, half, rows] if staged else blocks[0][g, half, rows]
+            new_p[g, half, rows] = p - learn_rate * y
+
+    of_matrix = pl.BlockSpec((None, 2, 2, part, width), lambda i: (m, i, 0, 0, 0))
     pltpu.emit_pipeline(
-        body, grid=(count, 2), in_specs=[] if staged else [of_matrix], out_specs=[of_matrix] * 2
+        body, grid=(count // 2,), in_specs=[] if staged else [of_matrix], out_specs=[of_matrix] * 2
     )(*([] if staged else [params]), new_params, update)
 
 
@@ -349,7 +351,7 @@
     def row_stage(m, sums):
         cols, rows_along, summed = sums
         row_new, stats = weighted_sums(
-            extent, [pairwise_sum(rows_along, "col")], row_factor[m], cols, summed
+            extent, exchange(rows_along, "col"), row_factor[m], cols, summed
         )
         new_rows.append(row_new.reshape(rows))
         return row_new, pairwise_sum(stats, "row")

time: 587 us -> 582 us (level)
  Pallas kernels: 79.5 us -> 72.5 us
    pallas_call x2, Pallas kernels: 24.1 us -> 16.9 us  [finish(): pl.pallas_call(functools.partial(finish_kernel, m, extent, len(pairs), st...]
    ppermute x51 -> x53, starting transfers between devices: 61.3 us -> 65.1 us  [swap(): return lax.ppermute(x, axes, [(i, i ^ mask) for i in range(size)])]
    ppermute x51 -> x53, waiting for transfers between devices: 432 us -> 430 us  [swap(): return lax.ppermute(x, axes, [(i, i ^ mask) for i in range(size)])]
  transfers between devices with their start and end apart: 51 -> 53, of which waited for: 45 -> 47; matrix products, arithmetic and copies ran while one was open for 2% -> 2% of each run, Pallas kernels for 11% -> 11%
where the time goes in v12:
time: 582 us; the launch traced here: 581 us
  waiting for transfers between devices  430 us (74%)
  Pallas kernels  72.5 us (12%)
  starting transfers between devices  65.1 us (11%)
  local copies, waits for them, and re-layouts  11.3 us (2%)
    ppermute x53, waiting for transfers between devices, swap(): return lax.ppermute(x, axes, [(i, i ^ mask) for i in range(size)])  430 us
    ppermute x53, starting transfers between devices, swap(): return lax.ppermute(x, axes, [(i, i ^ mask) for i in range(size)])  65.1 us
    pallas_call x20, Pallas kernels, step(): pl.pallas_call(functools.partial(step_kernel, takes, finishes, b, sends,...  53.2 us
    pallas_call x2, Pallas kernels, finish(): pl.pallas_call(functools.partial(finish_kernel, m, extent, len(pairs), st...  16.9 us
  transfers between devices with their start and end apart: 53, of which 47 were waited for; matrix products, arithmetic and copies ran while one was open for 2% of the time, Pallas kernels for 11%

profile of v12, /device:TPU:0, one launch (start us, length us, event | category | flops | bytes accessed | tf_op | source)
XLA Modules:
  0.0 581.1 jit_solution(10654351419578872147)
XLA Ops:
  1.7 3.0 collective-permute-start
  8.0 9.5 %collective-permute-done.refs_1_ = f32[64,2048]{1,0:T(8,128)S(1)} collective-permute-done((f32[64,2048]{1,0:T(8,128)S(1)}, f32[64,2048]{1,0:T(8,128)S(1)}, u32[]{:S(2)}, u32[]{:S(2)}) %collective-permute-start) | collective-permute-done | bytes 524320 | tf_op jit(solution)/shard_map/ppermute | solution.py:25
  24.2 4.5 collective-permute-done.2.refs_1_
  35.4 27.0 %collective-permute-done.4.refs_1_ = f32[192,2048]{1,0:T(8,128)S(1)} collective-permute-done((f32[192,2048]{1,0:T(8,128)S(1)}, f32[192,2048]{1,0:T(8,128)S(1)}, u32[]{:S(2)}, u32[]{:S(2)}) %collective-permute-start.4) | collective-permute-done | bytes 1572896 | tf_op jit(solution)/shard_map/ppermute | solution.py:25
  69.7 26.5 %collective-permute-done.6.refs_1_ = f32[192,2048]{1,0:T(8,128)S(1)} collective-permute-done((f32[192,2048]{1,0:T(8,128)S(1)}, f32[192,2048]{1,0:T(8,128)S(1)}, u32[]{:S(2)}, u32[]{:S(2)}) %collective-permute-start.6) | collective-permute-done | bytes 1572896 | tf_op jit(solution)/shard_map/ppermute | solution.py:25
  103.4 26.5 %collective-permute-done.8.refs_1_ = f32[192,2048]{1,0:T(8,128)S(1)} collective-permute-done((f32[192,2048]{1,0:T(8,128)S(1)}, f32[192,2048]{1,0:T(8,128)S(1)}, u32[]{:S(2)}, u32[]{:S(2)}) %collective-permute-start.8) | collective-permute-done | bytes 1572896 | tf_op jit(solution)/shard_map/ppermute | solution.py:25
  137.1 26.5 %collective-permute-done.10.refs_1_ = f32[192,2048]{1,0:T(8,128)S(1)} collective-permute-done((f32[192,2048]{1,0:T(8,128)S(1)}, f32[192,2048]{1,0:T(8,128)S(1)}, u32[]{:S(2)}, u32[]{:S(2)}) %collective-permute-start.10) | collective-permute-done | bytes 1572896 | tf_op jit(solution)/shard_map/ppermute | solution.py:25
  170.8 26.5 %collective-permute-done.12.refs_1_ = f32[192,2048]{1,0:T(8,128)S(1)} collective-permute-done((f32[192,2048]{1,0:T(8,128)S(1)}, f32[192,2048]{1,0:T(8,128)S(1)}, u32[]{:S(2)}, u32[]{:S(2)}) %collective-permute-start.12) | collective-permute-done | bytes 1572896 | tf_op jit(solution)/shard_map/ppermute | solution.py:25
  204.5 26.5 %collective-permute-done.14.refs_1_ = f32[192,2048]{1,0:T(8,128)S(1)} collective-permute-done((f32[192,2048]{1,0:T(8,128)S(1)}, f32[192,2048]{1,0:T(8,128)S(1)}, u32[]{:S(2)}, u32[]{:S(2)}) %collective-permute-start.14) | collective-permute-done | bytes 1572896 | tf_op jit(solution)/shard_map/ppermute | solution.py:25
  233.1 3.0 step.29
  238.2 26.5 %collective-permute-done.16.refs_1_ = f32[192,2048]{1,0:T(8,128)S(1)} collective-permute-done((f32[192,2048]{1,0:T(8,128)S(1)}, f32[192,2048]{1,0:T(8,128)S(1)}, u32[]{:S(2)}, u32[]{:S(2)}) %collective-permute-start.16) | collective-permute-done | bytes 1572896 | tf_op jit(solution)/shard_map/ppermute | solution.py:25
  271.9 26.5 %collective-permute-done.18.refs_1_ = f32[192,2048]{1,0:T(8,128)S(1)} collective-permute-done((f32[192,2048]{1,0:T(8,128)S(1)}, f32[192,2048]{1,0:T(8,128)S(1)}, u32[]{:S(2)}, u32[]{:S(2)}) %collective-permute-start.18) | collective-permute-done | bytes 1572896 | tf_op jit(solution)/shard_map/ppermute | solution.py:25
  313.7 3.6 collective-permute-start.22
  321.5 10.6 %collective-permute-done.24.refs_1_ = f32[192,2048]{1,0:T(8,128)S(1)} collective-permute-done((f32[192,2048]{1,0:T(8,128)S(1)}, f32[192,2048]{1,0:T(8,128)S(1)}, u32[]{:S(2)}, u32[]{:S(2)}) %collective-permute-start.24) | collective-permute-done | bytes 1572896 | tf_op jit(solution)/shard_map/ppermute | solution.py:25
  334.2 3.0 step.32
  339.3 26.5 %collective-permute-done.26.refs_1_ = f32[192,2048]{1,0:T(8,128)S(1)} collective-permute-done((f32[192,2048]{1,0:T(8,128)S(1)}, f32[192,2048]{1,0:T(8,128)S(1)}, u32[]{:S(2)}, u32[]{:S(2)}) %collective-permute-start.26) | collective-permute-done | bytes 1572896 | tf_op jit(solution)/shard_map/ppermute | solution.py:25
  367.9 3.0 step.33
  373.0 28.6 %collective-permute-done.29.refs_2_ = f32[192,2048]{1,0:T(8,128)S(1)} collective-permute-done((f32[192,2048]{1,0:T(8,128)S(1)}, f32[192,2048]{1,0:T(8,128)S(1)}, u32[]{:S(2)}, u32[]{:S(2)}) %collective-permute-start.29) | collective-permute-done | bytes 1572896 | tf_op jit(solution)/shard_map/ppermute | solution.py:25
  401.6 3.0 step.34
  407.6 27.0 %collective-permute-done.30.refs_1_ = f32[192,2048]{1,0:T(8,128)S(1)} collective-permute-done((f32[192,2048]{1,0:T(8,128)S(1)}, f32[192,2048]{1,0:T(8,128)S(1)}, u32[]{:S(2)}, u32[]{:S(2)}) %collective-permute-start.30) | collective-permute-done | bytes 1572896 | tf_op jit(solution)/shard_map/ppermute | solution.py:25
  435.3 3.0 step.35
  441.3 27.0 %collective-permute-done.32.refs_1_ = f32[192,2048]{1,0:T(8,128)S(1)} collective-permute-done((f32[192,2048]{1,0:T(8,128)S(1)}, f32[192,2048]{1,0:T(8,128)S(1)}, u32[]{:S(2)}, u32[]{:S(2)}) %collective-permute-start.32) | collective-permute-done | bytes 1572896 | tf_op jit(solution)/shard_map/ppermute | solution.py:25
  470.4 4.0 step.36
  484.1 3.4 copy-done.1
  487.5 10.2 %finish.2 = (f32[2,8,2,64,2048]{4,3,2,1,0:T(8,128)}, f32[2,8,2,64,2048]{4,3,2,1,0:T(8,128)}) custom-call(f32[8,128]{1,0:T(8,128)S(1)} %get-tuple-element.306.row_new, f32[1,2048]{1,0:T(1,128)S(1)} %get-tuple-element.308.col_new, f32[8,2,64,2048]{3,2,1,0:T(8,128)S(1)} %copy-done.1, f32[2,8,2,64,2048]{4,3,2,1,0:T(8,128)} %bitcast.113, ...), custom_call_target="tpu_custom_call" | custom-call | flops 8388608 | bytes 33554432 | tf_op jit(solution)/shard_map/finish/pallas_call | solution.py:319
  497.8 4.3 collective-permute-done.37.refs_1_
  509.0 7.9 %slice.19 = f32[1,1024,2048]{2,1,0:T(8,128)} slice(f32[2,1024,2048]{2,1,0:T(8,128)} %param.5), slice={[1:2], [0:1024], [0:2048]} | slice | bytes 16777216 | tf_op jit(solution)/shard_map/slice | solution.py:394
  516.9 7.6 %collective-permute-done.39.refs_1_ = f32[128,2048]{1,0:T(8,128)S(1)} collective-permute-done((f32[128,2048]{1,0:T(8,128)}, f32[128,2048]{1,0:T(8,128)S(1)}, u32[]{:S(2)}, u32[]{:S(2)}) %collective-permute-start.39) | collective-permute-done | bytes 1048608 | tf_op jit(solution)/shard_map/ppermute | solution.py:25
  528.2 17.9 %collective-permute-done.41.refs_1_ = f32[128,2048]{1,0:T(8,128)S(1)} collective-permute-done((f32[128,2048]{1,0:T(8,128)S(1)}, f32[128,2048]{1,0:T(8,128)S(1)}, u32[]{:S(2)}, u32[]{:S(2)}) %collective-permute-start.41) | collective-permute-done | bytes 1048608 | tf_op jit(solution)/shard_map/ppermute | solution.py:25
  555.5 3.5 collective-permute-done.45.refs_3_
  569.0 3.6 collective-permute-start.52
  574.5 6.6 %finish.3 = (f32[2,8,2,64,2048]{4,3,2,1,0:T(8,128)}, f32[2,8,2,64,2048]{4,3,2,1,0:T(8,128)}) custom-call(f32[8,128]{1,0:T(8,128)S(1)} %get-tuple-element.343.row_new, f32[1,2048]{1,0:T(1,128)S(1)} %get-tuple-element.345.col_new, f32[8,2,64,2048]{3,2,1,0:T(8,128)S(1)} %get-tuple-element.341.summed, ...), custom_call_target="tpu_custom_call", output_to_operand_aliasing={{0}: (8, {}), {1}: (9, {})} | custom-call | flops 8388608 | bytes 33554432 | tf_op jit(solution)/shard_map/finish/pallas_call | solution.py:319
  (120 shorter events, 143.3 us)
Async XLA Ops:
  22.1 40.4 %collective-permute-start.4 = (f32[192,2048]{1,0:T(8,128)S(1)}, f32[192,2048]{1,0:T(8,128)S(1)}, u32[]{:S(2)}, u32[]{:S(2)}) collective-permute-start(f32[192,2048]{1,0:T(8,128)S(1)} %get-tuple-element.184), channel_id=1, source_target_pairs={{0,8},{8,0},{16,24},{24,16},{1,9},{9,1},{17,25},{25,17},{2,10},{10... | collective-permute-start | bytes 4718600 | tf_op jit(solution)/shard_map/ppermute | solution.py:25
  22.2 42.4 %collective-permute-start.5 = (f32[192,2048]{1,0:T(8,128)S(1)}, f32[192,2048]{1,0:T(8,128)S(1)}, u32[]{:S(2)}, u32[]{:S(2)}) collective-permute-start(f32[192,2048]{1,0:T(8,128)S(1)} %get-tuple-element.185), channel_id=1, source_target_pairs={{0,16},{8,24},{16,0},{24,8},{1,17},{9,25},{17,1},{25,9},{2,18},{10... | collective-permute-start | bytes 4718600 | tf_op jit(solution)/shard_map/ppermute | solution.py:25
  33.3 62.8 %collective-permute-start.6 = (f32[192,2048]{1,0:T(8,128)S(1)}, f32[192,2048]{1,0:T(8,128)S(1)}, u32[]{:S(2)}, u32[]{:S(2)}) collective-permute-start(f32[192,2048]{1,0:T(8,128)S(1)} %get-tuple-element.187), channel_id=1, source_target_pairs={{0,8},{8,0},{16,24},{24,16},{1,9},{9,1},{17,25},{25,17},{2,10},{10... | collective-permute-start | bytes 4718600 | tf_op jit(solution)/shard_map/ppermute | solution.py:25
  33.4 64.8 %collective-permute-start.7 = (f32[192,2048]{1,0:T(8,128)S(1)}, f32[192,2048]{1,0:T(8,128)S(1)}, u32[]{:S(2)}, u32[]{:S(2)}) collective-permute-start(f32[192,2048]{1,0:T(8,128)S(1)} %get-tuple-element.188), channel_id=1, source_target_pairs={{0,16},{8,24},{16,0},{24,8},{1,17},{9,25},{17,1},{25,9},{2,18},{10... | collective-permute-start | bytes 4718600 | tf_op jit(solution)/shard_map/ppermute | solution.py:25
  67.5 62.3 %collective-permute-start.8 = (f32[192,2048]{1,0:T(8,128)S(1)}, f32[192,2048]{1,0:T(8,128)S(1)}, u32[]{:S(2)}, u32[]{:S(2)}) collective-permute-start(f32[192,2048]{1,0:T(8,128)S(1)} %get-tuple-element.201), channel_id=1, source_target_pairs={{0,8},{8,0},{16,24},{24,16},{1,9},{9,1},{17,25},{25,17},{2,10},{10... | collective-permute-start | bytes 4718600 | tf_op jit(solution)/shard_map/ppermute | solution.py:25
  67.7 64.3 %collective-permute-start.9 = (f32[192,2048]{1,0:T(8,128)S(1)}, f32[192,2048]{1,0:T(8,128)S(1)}, u32[]{:S(2)}, u32[]{:S(2)}) collective-permute-start(f32[192,2048]{1,0:T(8,128)S(1)} %get-tuple-element.202), channel_id=1, source_target_pairs={{0,16},{8,24},{16,0},{24,8},{1,17},{9,25},{17,1},{25,9},{2,18},{10... | collective-permute-start | bytes 4718600 | tf_op jit(solution)/shard_map/ppermute | solution.py:25
  101.2 62.3 %collective-permute-start.10 = (f32[192,2048]{1,0:T(8,128)S(1)}, f32[192,2048]{1,0:T(8,128)S(1)}, u32[]{:S(2)}, u32[]{:S(2)}) collective-permute-start(f32[192,2048]{1,0:T(8,128)S(1)} %get-tuple-element.210), channel_id=1, source_target_pairs={{0,8},{8,0},{16,24},{24,16},{1,9},{9,1},{17,25},{25,17},{2,10},{10... | collective-permute-start | bytes 4718600 | tf_op jit(solution)/shard_map/ppermute | solution.py:25
  101.4 64.3 %collective-permute-start.11 = (f32[192,2048]{1,0:T(8,128)S(1)}, f32[192,2048]{1,0:T(8,128)S(1)}, u32[]{:S(2)}, u32[]{:S(2)}) collective-permute-start(f32[192,2048]{1,0:T(8,128)S(1)} %get-tuple-element.211), channel_id=1, source_target_pairs={{0,16},{8,24},{16,0},{24,8},{1,17},{9,25},{17,1},{25,9},{2,18},{10... | collective-permute-start | bytes 4718600 | tf_op jit(solution)/shard_map/ppermute | solution.py:25
  135.0 62.3 %collective-permute-start.12 = (f32[192,2048]{1,0:T(8,128)S(1)}, f32[192,2048]{1,0:T(8,128)S(1)}, u32[]{:S(2)}, u32[]{:S(2)}) collective-permute-start(f32[192,2048]{1,0:T(8,128)S(1)} %get-tuple-element.219), channel_id=1, source_target_pairs={{0,8},{8,0},{16,24},{24,16},{1,9},{9,1},{17,25},{25,17},{2,10},{10... | collective-permute-start | bytes 4718600 | tf_op jit(solution)/shard_map/ppermute | solution.py:25
  135.1 64.3 %collective-permute-start.13 = (f32[192,2048]{1,0:T(8,128)S(1)}, f32[192,2048]{1,0:T(8,128)S(1)}, u32[]{:S(2)}, u32[]{:S(2)}) collective-permute-start(f32[192,2048]{1,0:T(8,128)S(1)} %get-tuple-element.220), channel_id=1, source_target_pairs={{0,16},{8,24},{16,0},{24,8},{1,17},{9,25},{17,1},{25,9},{2,18},{10... | collective-permute-start | bytes 4718600 | tf_op jit(solution)/shard_map/ppermute | solution.py:25
  168.7 62.3 %collective-permute-start.14 = (f32[192,2048]{1,0:T(8,128)S(1)}, f32[192,2048]{1,0:T(8,128)S(1)}, u32[]{:S(2)}, u32[]{:S(2)}) collective-permute-start(f32[192,2048]{1,0:T(8,128)S(1)} %get-tuple-element.228), channel_id=1, source_target_pairs={{0,8},{8,0},{16,24},{24,16},{1,9},{9,1},{17,25},{25,17},{2,10},{10... | collective-permute-start | bytes 4718600 | tf_op jit(solution)/shard_map/ppermute | solution.py:25
  168.8 64.3 %collective-permute-start.15 = (f32[192,2048]{1,0:T(8,128)S(1)}, f32[192,2048]{1,0:T(8,128)S(1)}, u32[]{:S(2)}, u32[]{:S(2)}) collective-permute-start(f32[192,2048]{1,0:T(8,128)S(1)} %get-tuple-element.229), channel_id=1, source_target_pairs={{0,16},{8,24},{16,0},{24,8},{1,17},{9,25},{17,1},{25,9},{2,18},{10... | collective-permute-start | bytes 4718600 | tf_op jit(solution)/shard_map/ppermute | solution.py:25
  202.4 62.3 %collective-permute-start.16 = (f32[192,2048]{1,0:T(8,128)S(1)}, f32[192,2048]{1,0:T(8,128)S(1)}, u32[]{:S(2)}, u32[]{:S(2)}) collective-permute-start(f32[192,2048]{1,0:T(8,128)S(1)} %get-tuple-element.237), channel_id=1, source_target_pairs={{0,8},{8,0},{16,24},{24,16},{1,9},{9,1},{17,25},{25,17},{2,10},{10... | collective-permute-start | bytes 4718600 | tf_op jit(solution)/shard_map/ppermute | solution.py:25
  202.5 64.3 %collective-permute-start.17 = (f32[192,2048]{1,0:T(8,128)S(1)}, f32[192,2048]{1,0:T(8,128)S(1)}, u32[]{:S(2)}, u32[]{:S(2)}) collective-permute-start(f32[192,2048]{1,0:T(8,128)S(1)} %get-tuple-element.238), channel_id=1, source_target_pairs={{0,16},{8,24},{16,0},{24,8},{1,17},{9,25},{17,1},{25,9},{2,18},{10... | collective-permute-start | bytes 4718600 | tf_op jit(solution)/shard_map/ppermute | solution.py:25
  236.1 62.3 %collective-permute-start.18 = (f32[192,2048]{1,0:T(8,128)S(1)}, f32[192,2048]{1,0:T(8,128)S(1)}, u32[]{:S(2)}, u32[]{:S(2)}) collective-permute-start(f32[192,2048]{1,0:T(8,128)S(1)} %get-tuple-element.246), channel_id=1, source_target_pairs={{0,8},{8,0},{16,24},{24,16},{1,9},{9,1},{17,25},{25,17},{2,10},{10... | collective-permute-start | bytes 4718600 | tf_op jit(solution)/shard_map/ppermute | solution.py:25
  236.2 64.3 %collective-permute-start.19 = (f32[192,2048]{1,0:T(8,128)S(1)}, f32[192,2048]{1,0:T(8,128)S(1)}, u32[]{:S(2)}, u32[]{:S(2)}) collective-permute-start(f32[192,2048]{1,0:T(8,128)S(1)} %get-tuple-element.247), channel_id=1, source_target_pairs={{0,16},{8,24},{16,0},{24,8},{1,17},{9,25},{17,1},{25,9},{2,18},{10... | collective-permute-start | bytes 4718600 | tf_op jit(solution)/shard_map/ppermute | solution.py:25
  269.8 62.3 %collective-permute-start.24 = (f32[192,2048]{1,0:T(8,128)S(1)}, f32[192,2048]{1,0:T(8,128)S(1)}, u32[]{:S(2)}, u32[]{:S(2)}) collective-permute-start(f32[192,2048]{1,0:T(8,128)S(1)} %get-tuple-element.260), channel_id=1, source_target_pairs={{0,8},{8,0},{16,24},{24,16},{1,9},{9,1},{17,25},{25,17},{2,10},{10... | collective-permute-start | bytes 4718600 | tf_op jit(solution)/shard_map/ppermute | solution.py:25
  269.9 64.3 %collective-permute-start.25 = (f32[192,2048]{1,0:T(8,128)S(1)}, f32[192,2048]{1,0:T(8,128)S(1)}, u32[]{:S(2)}, u32[]{:S(2)}) collective-permute-start(f32[192,2048]{1,0:T(8,128)S(1)} %get-tuple-element.261), channel_id=1, source_target_pairs={{0,16},{8,24},{16,0},{24,8},{1,17},{9,25},{17,1},{25,9},{2,18},{10... | collective-permute-start | bytes 4718600 | tf_op jit(solution)/shard_map/ppermute | solution.py:25
  303.5 62.3 %collective-permute-start.26 = (f32[192,2048]{1,0:T(8,128)S(1)}, f32[192,2048]{1,0:T(8,128)S(1)}, u32[]{:S(2)}, u32[]{:S(2)}) collective-permute-start(f32[192,2048]{1,0:T(8,128)S(1)} %get-tuple-element.267), channel_id=1, source_target_pairs={{0,8},{8,0},{16,24},{24,16},{1,9},{9,1},{17,25},{25,17},{2,10},{10... | collective-permute-start | bytes 4718600 | tf_op jit(solution)/shard_map/ppermute | solution.py:25
  303.6 64.3 %collective-permute-start.27 = (f32[192,2048]{1,0:T(8,128)S(1)}, f32[192,2048]{1,0:T(8,128)S(1)}, u32[]{:S(2)}, u32[]{:S(2)}) collective-permute-start(f32[192,2048]{1,0:T(8,128)S(1)} %get-tuple-element.268), channel_id=1, source_target_pairs={{0,16},{8,24},{16,0},{24,8},{1,17},{9,25},{17,1},{25,9},{2,18},{10... | collective-permute-start | bytes 4718600 | tf_op jit(solution)/shard_map/ppermute | solution.py:25
  337.2 64.4 %collective-permute-start.28 = (f32[200,2048]{1,0:T(8,128)S(1)}, f32[200,2048]{1,0:T(8,128)S(1)}, u32[]{:S(2)}, u32[]{:S(2)}) collective-permute-start(f32[200,2048]{1,0:T(8,128)S(1)} %get-tuple-element.276), channel_id=1, source_target_pairs={{0,8},{8,0},{16,24},{24,16},{1,9},{9,1},{17,25},{25,17},{2,10},{10... | collective-permute-start | bytes 4915208 | tf_op jit(solution)/shard_map/ppermute | solution.py:25
  337.3 64.3 %collective-permute-start.29 = (f32[192,2048]{1,0:T(8,128)S(1)}, f32[192,2048]{1,0:T(8,128)S(1)}, u32[]{:S(2)}, u32[]{:S(2)}) collective-permute-start(f32[192,2048]{1,0:T(8,128)S(1)} %get-tuple-element.277), channel_id=1, source_target_pairs={{0,16},{8,24},{16,0},{24,8},{1,17},{9,25},{17,1},{25,9},{2,18},{10... | collective-permute-start | bytes 4718600 | tf_op jit(solution)/shard_map/ppermute | solution.py:25
  370.9 63.7 %collective-permute-start.30 = (f32[192,2048]{1,0:T(8,128)S(1)}, f32[192,2048]{1,0:T(8,128)S(1)}, u32[]{:S(2)}, u32[]{:S(2)}) collective-permute-start(f32[192,2048]{1,0:T(8,128)S(1)} %get-tuple-element.285), channel_id=1, source_target_pairs={{0,8},{8,0},{16,24},{24,16},{1,9},{9,1},{17,25},{25,17},{2,10},{10... | collective-permute-start | bytes 4718600 | tf_op jit(solution)/shard_map/ppermute | solution.py:25
  371.0 64.3 %collective-permute-start.31 = (f32[192,2048]{1,0:T(8,128)S(1)}, f32[192,2048]{1,0:T(8,128)S(1)}, u32[]{:S(2)}, u32[]{:S(2)}) collective-permute-start(f32[192,2048]{1,0:T(8,128)S(1)} %get-tuple-element.286), channel_id=1, source_target_pairs={{0,16},{8,24},{16,0},{24,8},{1,17},{9,25},{17,1},{25,9},{2,18},{10... | collective-permute-start | bytes 4718600 | tf_op jit(solution)/shard_map/ppermute | solution.py:25
  404.7 65.8 %collective-permute-start.33 = (f32[200,2048]{1,0:T(8,128)S(1)}, f32[200,2048]{1,0:T(8,128)S(1)}, u32[]{:S(2)}, u32[]{:S(2)}) collective-permute-start(f32[200,2048]{1,0:T(8,128)S(1)} %get-tuple-element.295), channel_id=1, source_target_pairs={{0,16},{8,24},{16,0},{24,8},{1,17},{9,25},{17,1},{25,9},{2,18},{10... | collective-permute-start | bytes 4915208 | tf_op jit(solution)/shard_map/ppermute | solution.py:25
  406.2 62.1 %collective-permute-start.32 = (f32[192,2048]{1,0:T(8,128)S(1)}, f32[192,2048]{1,0:T(8,128)S(1)}, u32[]{:S(2)}, u32[]{:S(2)}) collective-permute-start(f32[192,2048]{1,0:T(8,128)S(1)} %get-tuple-element.294), channel_id=1, source_target_pairs={{0,8},{8,0},{16,24},{24,16},{1,9},{9,1},{17,25},{25,17},{2,10},{10... | collective-permute-start | bytes 4718600 | tf_op jit(solution)/shard_map/ppermute | solution.py:25
  438.3 63.7 %collective-permute-start.37 = (f32[192,2048]{1,0:T(8,128)S(1)}, f32[192,2048]{1,0:T(8,128)S(1)}, u32[]{:S(2)}, u32[]{:S(2)}) collective-permute-start(f32[192,2048]{1,0:T(8,128)S(1)} %get-tuple-element.313), channel_id=1, source_target_pairs={{0,8},{8,0},{16,24},{24,16},{1,9},{9,1},{17,25},{25,17},{2,10},{10... | collective-permute-start | bytes 4718600 | tf_op jit(solution)/shard_map/ppermute | solution.py:25
  439.8 64.3 %collective-permute-start.38 = (f32[192,2048]{1,0:T(8,128)S(1)}, f32[192,2048]{1,0:T(8,128)S(1)}, u32[]{:S(2)}, u32[]{:S(2)}) collective-permute-start(f32[192,2048]{1,0:T(8,128)S(1)} %get-tuple-element.314), channel_id=1, source_target_pairs={{0,16},{8,24},{16,0},{24,8},{1,17},{9,25},{17,1},{25,9},{2,18},{10... | collective-permute-start | bytes 4718600 | tf_op jit(solution)/shard_map/ppermute | solution.py:25
  478.9 45.6 %collective-permute-start.39 = (f32[128,2048]{1,0:T(8,128)}, f32[128,2048]{1,0:T(8,128)S(1)}, u32[]{:S(2)}, u32[]{:S(2)}) collective-permute-start(f32[128,2048]{1,0:T(8,128)} %get-tuple-element.323), channel_id=1, source_target_pairs={{0,8},{8,0},{16,24},{24,16},{1,9},{9,1},{17,25},{25,17},{2,10},{10... | collective-permute-start | bytes 3145736 | tf_op jit(solution)/shard_map/ppermute | solution.py:25
  480.6 46.0 %collective-permute-start.40 = (f32[128,2048]{1,0:T(8,128)}, f32[128,2048]{1,0:T(8,128)S(1)}, u32[]{:S(2)}, u32[]{:S(2)}) collective-permute-start(f32[128,2048]{1,0:T(8,128)} %get-tuple-element.324), channel_id=1, source_target_pairs={{0,16},{8,24},{16,0},{24,8},{1,17},{9,25},{17,1},{25,9},{2,18},{10... | collective-permute-start | bytes 3145736 | tf_op jit(solution)/shard_map/ppermute | solution.py:25
  506.9 39.3 %collective-permute-start.41 = (f32[128,2048]{1,0:T(8,128)S(1)}, f32[128,2048]{1,0:T(8,128)S(1)}, u32[]{:S(2)}, u32[]{:S(2)}) collective-permute-start(f32[128,2048]{1,0:T(8,128)S(1)} %get-tuple-element.332), channel_id=1, source_target_pairs={{0,8},{8,0},{16,24},{24,16},{1,9},{9,1},{17,25},{25,17},{2,10},{10... | collective-permute-start | bytes 3145736 | tf_op jit(solution)/shard_map/ppermute | solution.py:25
  507.0 40.6 %collective-permute-start.42 = (f32[128,2048]{1,0:T(8,128)S(1)}, f32[128,2048]{1,0:T(8,128)S(1)}, u32[]{:S(2)}, u32[]{:S(2)}) collective-permute-start(f32[128,2048]{1,0:T(8,128)S(1)} %get-tuple-element.333), channel_id=1, source_target_pairs={{0,16},{8,24},{16,0},{24,8},{1,17},{9,25},{17,1},{25,9},{2,18},{10... | collective-permute-start | bytes 3145736 | tf_op jit(solution)/shard_map/ppermute | solution.py:25
  (27 other events, 339.3 us)
